TPU v7x, 32 devices: a whole 2x2x4 slice. The times are simulated.
32 devices in a mesh: head: 4 (over y, core), seq: 8 (over z, x).
Axes of the slice: x: 2, y: 2, z: 4, core: 2. Of those that a mesh axis runs over, the one named last changes fastest.
Arguments:
- layer_input: bfloat16 [1024, 4096], P('seq', 'head'), may hold values from -6 to 6
- receptance: bfloat16 [1024, 4096], P('seq', 'head'), may hold values from -6 to 6
- key_act: bfloat16 [1024, 4096], P('seq', 'head'), may hold values from -0.75 to 0.75
- value_act: bfloat16 [1024, 4096], P('seq', 'head'), may hold values from -6 to 6
- attention_result_sensitivity: bfloat16 [1024, 4096], P('seq', 'head'), may hold values from -0.625 to 0.625
- time_first: float32 [64, 64], P('head'), may hold values from -1 to 1
- decay_exponent_base: float32 [4096], P('head'), may hold values from -9 to -3.4
- decay_shift_mix: float32 [4096], P('head'), may hold values from 0 to 1
- mix_rkv: float32 [3, 4096], replicated, may hold values from 0 to 1
- decay_adapter_down: float32 [4096, 128], P('head'), may hold values from -0.09375 to 0.09375
- decay_adapter_up: float32 [128, 4096], P(None, 'head'), may hold values from -1 to 1
- proj_weights: bfloat16 [3, 4096, 4096], P(None, 'seq', 'head'), may hold values from -0.09375 to 0.09375
Outputs:
- stratum_source_sensitivity: bfloat16 [1024, 4096], P('seq', 'head')
- decay_down_grad: float32 [4096, 128], P('head')
- decay_up_grad: float32 [128, 4096], P(None, 'head')
- decay_base_grad: float32 [4096], P('head')
- time_first_grad: float32 [64, 64], P('head')
All inputs are finite; a program needn't handle non-finite values.
Results may differ from a plain program's by a relative error of at most 0.018.
Values may be sent and summed in bfloat16 or wider, within the bound.
No kernel may reach another device: no remote copies, remote signals or barrier semaphores. Data moves between devices by JAX's collectives and lax.ppermute only.
A program may use at most 128 MiB of HBM per device.

v0:
```python
from functools import partial

import jax
import jax.numpy as jnp
from jax import lax
from jax.sharding import PartitionSpec as P

BLOCK = 32


EXACT_ARITHMETIC = lax.Precision.HIGHEST


def shifted(block, axis, distance):
    devices = range(lax.axis_size(axis))
    route = [(i - distance, i) for i in devices if i - distance in devices]
    return lax.ppermute(block, axis, route)


def entering(part, axis, combine, identity, reverse):
    count = lax.axis_size(axis)
    place = lax.axis_index(axis)
    ahead = count - 1 - place if reverse else place
    gathered = jax.tree.map(lambda a: lax.all_gather(a, axis), part)
    state = jax.tree.map(lambda a, e: jnp.zeros_like(a) + jnp.asarray(e, a.dtype), part, identity)

    def one(step, state):
        source = count - 1 - step if reverse else step
        return combine(
            state, jax.tree.map(lambda a: lax.dynamic_index_in_dim(a, source, 0, False), gathered)
        )

    return lax.fori_loop(0, ahead, one, state)


def link(earlier, later):
    return (earlier[0] + later[0], later[1] + jnp.exp(later[0])[..., None] * earlier[1])


def block_terms(gate_matrix, lookup_matrix, payload_matrix, grads_out, fading_natural_scale):
    cumul = jnp.cumsum(fading_natural_scale, axis=1)
    before = cumul - fading_natural_scale
    final = cumul[:, -1]
    to_end = jnp.exp(final[:, None] - cumul)
    state_part = jnp.einsum(
        "bshi,bshj->bhij", lookup_matrix * to_end, payload_matrix, precision=EXACT_ARITHMETIC
    )
    grad_part = jnp.einsum(
        "bshi,bshj->bhij", gate_matrix * jnp.exp(before), grads_out, precision=EXACT_ARITHMETIC
    )
    return (cumul, before, final, state_part, grad_part)


def sensitivity_each_segment(initial_reward, sequence_entries):
    (
        gate_matrix,
        lookup_matrix,
        payload_matrix,
        grads_out,
        cumul,
        before,
        final,
        state_in,
        grad_in,
        state_part,
    ) = sequence_entries
    length = gate_matrix.shape[0]
    positions = jnp.arange(length)
    lower = positions[:, None] > positions[None, :]
    strict_up = (positions[:, None] < positions[None, :]).astype(jnp.float32)
    upper = (positions[:, None] <= positions[None, :]).astype(jnp.float32)
    spread = jnp.where(lower[:, :, None, None], before[:, None] - cumul[None, :], -jnp.inf)
    decays = jnp.exp(spread)
    pairs = jnp.einsum("thj,shj->tsh", grads_out, payload_matrix, precision=EXACT_ARITHMETIC)
    scores = jnp.einsum(
        "tshi,thi,shi->tsh", decays, gate_matrix, lookup_matrix, precision=EXACT_ARITHMETIC
    )
    to_end = jnp.exp(final[None] - cumul)
    gate_memory_product = jnp.einsum(
        "tshi,tsh,shi->thi", decays, pairs, lookup_matrix, precision=EXACT_ARITHMETIC
    )
    gate_memory_product = gate_memory_product + jnp.exp(before) * jnp.einsum(
        "hij,thj->thi", state_in, grads_out, precision=EXACT_ARITHMETIC
    )
    cumulative_lookup_memory = jnp.einsum(
        "tshi,tsh,thi->shi", decays, pairs, gate_matrix, precision=EXACT_ARITHMETIC
    )
    cumulative_lookup_memory = cumulative_lookup_memory + to_end * jnp.einsum(
        "hij,shj->shi", grad_in, payload_matrix, precision=EXACT_ARITHMETIC
    )
    val_state = jnp.einsum("tsh,thj->shj", scores, grads_out, precision=EXACT_ARITHMETIC)
    val_state = val_state + jnp.einsum(
        "shi,hij->shj", lookup_matrix * to_end, grad_in, precision=EXACT_ARITHMETIC
    )
    self_pair_contribution = jnp.sum(grads_out * payload_matrix, -1)[..., None]
    scaled_contributions = jnp.sum(gate_matrix * initial_reward * lookup_matrix, -1)[..., None]
    gate_sensitivity = gate_memory_product + initial_reward * lookup_matrix * self_pair_contribution
    lookup_sensitivity = (
        cumulative_lookup_memory + initial_reward * gate_matrix * self_pair_contribution
    )
    payload_sensitivity = val_state + scaled_contributions * grads_out
    reward_sensitivity = jnp.sum(gate_matrix * lookup_matrix * self_pair_contribution, 0)
    state_out = jnp.exp(final)[..., None] * state_in + state_part
    at_end = jnp.sum(grad_in * state_out, -1)
    fading_scale_sensitivity = jnp.einsum(
        "ts,shi->thi", strict_up, gate_matrix * gate_memory_product, precision=EXACT_ARITHMETIC
    )
    fading_scale_sensitivity = (
        fading_scale_sensitivity
        - jnp.einsum(
            "ts,shi->thi",
            upper,
            lookup_matrix * cumulative_lookup_memory,
            precision=EXACT_ARITHMETIC,
        )
        + at_end[None]
    )
    return (
        gate_sensitivity,
        lookup_sensitivity,
        payload_sensitivity,
        fading_scale_sensitivity,
        reward_sensitivity,
    )


def per_device(
    layer_input,
    receptance,
    key_act,
    value_act,
    attention_result_sensitivity,
    time_first,
    decay_exponent_base,
    decay_shift_mix,
    mix_rkv,
    decay_adapter_down,
    decay_adapter_up,
    proj_weights,
):
    tok_rows, group_columns = layer_input.shape
    heads_dev, head_size = time_first.shape
    features = layer_input.astype(jnp.float32)
    carried_row = shifted(layer_input[tok_rows - 1 :], "seq", 1).astype(jnp.float32)
    previous = jnp.concatenate([carried_row, features[:-1]], 0)
    decay_input = features + decay_shift_mix * (previous - features)
    adapter_preactivation = lax.psum(
        jnp.dot(decay_input, decay_adapter_down, precision=EXACT_ARITHMETIC), "head"
    )
    adapter_middle = jnp.tanh(adapter_preactivation)
    fading_natural_scale = -jnp.exp(
        decay_exponent_base + jnp.dot(adapter_middle, decay_adapter_up, precision=EXACT_ARITHMETIC)
    )
    count = tok_rows // BLOCK

    def blocked(array):
        return array.astype(jnp.float32).reshape(count, BLOCK, heads_dev, head_size)

    gate_matrix = blocked(receptance)
    lookup_matrix = blocked(key_act)
    payload_matrix = blocked(value_act)
    grads_out = blocked(attention_result_sensitivity)
    cumul, before, final, state_part, grad_part = block_terms(
        gate_matrix, lookup_matrix, payload_matrix, grads_out, blocked(fading_natural_scale)
    )
    zero_state = jnp.zeros((heads_dev, head_size, head_size), jnp.float32)
    zero_decay = jnp.zeros((heads_dev, head_size), jnp.float32)

    def carry_step(carry, sequence_entries):
        running, decay_sum = carry
        block_final, block_term = sequence_entries
        updated = (jnp.exp(block_final)[..., None] * running + block_term, decay_sum + block_final)
        return (updated, (running, decay_sum))

    (local_state, device_decay), (starts_local, starts_decay) = lax.scan(
        carry_step, (zero_state, zero_decay), (final, state_part)
    )
    (local_grad, unused), (ends_local, ends_decay) = lax.scan(
        carry_step, (zero_state, zero_decay), (final, grad_part), reverse=True
    )
    incoming = entering((device_decay, local_state), "seq", link, (zero_decay, zero_state), False)[
        1
    ]
    outgoing = entering((device_decay, local_grad), "seq", link, (zero_decay, zero_state), True)[1]
    starts = starts_local + jnp.exp(starts_decay)[..., None] * incoming[None]
    ends = ends_local + jnp.exp(ends_decay)[..., None] * outgoing[None]
    (
        gate_sensitivity,
        lookup_sensitivity,
        payload_sensitivity,
        fading_scale_sensitivity,
        reward_each_segment,
    ) = lax.map(
        partial(sensitivity_each_segment, time_first),
        (
            gate_matrix,
            lookup_matrix,
            payload_matrix,
            grads_out,
            cumul,
            before,
            final,
            starts,
            ends,
            state_part,
        ),
    )
    device_reward = jnp.sum(reward_each_segment, 0)

    def flatten(array):
        return array.reshape(tok_rows, group_columns)

    preactivation_gradient = flatten(fading_scale_sensitivity) * fading_natural_scale
    device_raising_matrix = jnp.dot(
        adapter_middle.T, preactivation_gradient, precision=EXACT_ARITHMETIC
    )
    device_fading_floor = jnp.sum(preactivation_gradient, 0)
    raising_matrix_sensitivity, floor_rate_sensitivity, reward_sensitivity = lax.psum(
        (device_raising_matrix, device_fading_floor, device_reward), "seq"
    )
    middle_gradient = lax.psum(
        jnp.dot(preactivation_gradient, decay_adapter_up.T, precision=EXACT_ARITHMETIC), "head"
    ) * (1.0 - adapter_middle * adapter_middle)
    down_local = jnp.dot(decay_input.T, middle_gradient, precision=EXACT_ARITHMETIC)
    lowering_matrix_sensitivity = lax.psum(down_local, "seq")
    decay_input_gradient = jnp.dot(
        middle_gradient, decay_adapter_down.T, precision=EXACT_ARITHMETIC
    )
    projected = jnp.stack(
        [flatten(gate_sensitivity), flatten(lookup_sensitivity), flatten(payload_sensitivity)]
    ).astype(jnp.bfloat16)
    terms = jnp.einsum(
        "mtc,mnc->mtn",
        projected,
        lax.all_gather(proj_weights, "seq", axis=1, tiled=True),
        preferred_element_type=jnp.float32,
    )
    own_piece = jnp.sum((1.0 - mix_rkv)[:, None, :] * terms, 0)
    prior_piece = jnp.sum(mix_rkv[:, None, :] * terms, 0)
    gradient_portions = jnp.stack([own_piece, prior_piece])
    token_offset = lax.axis_index("head") * group_columns
    adapter_terms = jnp.stack(
        [(1.0 - decay_shift_mix) * decay_input_gradient, decay_shift_mix * decay_input_gradient]
    )
    current_token = lax.dynamic_slice_in_dim(gradient_portions, token_offset, group_columns, 2)
    gradient_portions = lax.dynamic_update_slice_in_dim(
        gradient_portions, current_token + adapter_terms, token_offset, 2
    )
    own_portion = gradient_portions[0]
    previous_portion = gradient_portions[1]
    next_first = shifted(previous_portion[0:1], "seq", -1)
    group_term = own_portion + jnp.concatenate([previous_portion[1:], next_first], 0)
    stratum_source_sensitivity = lax.psum_scatter(
        group_term.astype(jnp.bfloat16), "head", scatter_dimension=1, tiled=True
    )
    return (
        stratum_source_sensitivity,
        lowering_matrix_sensitivity,
        raising_matrix_sensitivity,
        floor_rate_sensitivity,
        reward_sensitivity,
    )


def solution(mesh):
    return jax.shard_map(
        per_device,
        mesh=mesh,
        in_specs=(
            P("seq", "head"),
            P("seq", "head"),
            P("seq", "head"),
            P("seq", "head"),
            P("seq", "head"),
            P("head", None),
            P("head"),
            P("head"),
            P(),
            P("head", None),
            P(None, "head"),
            P(None, "seq", "head"),
        ),
        out_specs=(P("seq", "head"), P("head", None), P(None, "head"), P("head"), P("head", None)),
        check_vma=False,
    )
```

profile of v0, /device:TPU:4, one launch (start us, length us, event | category | flops | bytes accessed | tf_op | source)
XLA Modules:
  0.0 1034.5 jit_solution(13745320511566497413)
XLA Ops:
  19.7 27.3 %all-reduce.6.cloned.1.call-done = f32[128,128]{1,0:T(8,128)} async-done(((f32[128,128]{1,0:T(8,128)}), f32[128,128]{1,0:T(8,128)}) %all-reduce.6.cloned.1.call-update) | async-done | bytes 65552 | tf_op jit(solution)/shard_map/psum | solution.py:147
  58.3 8.9 while.85
  72.9 4.8 while.86
  81.9 31.1 %all-gather.1 = f32[128,64]{1,0:T(8,128)S(1)} all-gather(f32[16,64]{1,0:T(8,128)S(1)} %get-tuple-element.410), channel_id=3, replica_groups=mesh['head'=4,'seq'=8] {'seq'}, dimensions={0}, use_global_device_ids=true | all-gather | bytes 36864 | tf_op jit(solution)/shard_map/all_gather | solution.py:24
  113.0 30.4 %all-gather.9.cloned.1.call-done = f32[128,64,64]{2,1,0:T(8,128)} async-done(((f32[16,64,64]{2,1,0:T(8,128)}), f32[128,64,64]{2,1,0:T(8,128)}) %all-gather.9.cloned.1.call-update) | async-done | bytes 2097168 | tf_op jit(solution)/shard_map/all_gather | solution.py:24
  143.5 74.1 %all-gather.11.cloned.1.call-done = f32[128,64,64]{2,1,0:T(8,128)} async-done(((f32[16,64,64]{2,1,0:T(8,128)}), f32[128,64,64]{2,1,0:T(8,128)}) %all-gather.11.cloned.1.call-update) | async-done | bytes 2097168 | tf_op jit(solution)/shard_map/all_gather | solution.py:24
  217.6 9.6 while.83
  228.0 4.0 multiply_add_fusion
  232.0 168.3 %while.84 = (s32[]{:T(128)}, bf16[4,32,16,64]{3,1,2,0:T(8,128)(2,1)}, bf16[4,32,16,64]{3,1,2,0:T(8,128)(2,1)}, bf16[4,32,16,64]{3,1,2,0:T(8,128)(2,1)}, f32[4,32...) while((s32[]{:T(128)}, ...), condition=%wide.region_15.16_spmd, body=%wide.region_10.15_spmd.sunk | while | flops 153158720 | bytes 30696820 | solution.py:193
  237.6 4.1 multiply_reduce_fusion.11
  251.2 17.6 %fusion.123 = f32[32,16,1,32]{3,2,1,0:T(1,128)S(1)} fusion(f32[32,16,64,32]{2,1,3,0:T(8,128)S(1)} %multiply_bitcast_fusion.4, f32[32,16,64,1]{2,0,1,3:T(8,128)S(1)} %get-tuple-element.893), kind=kOutput, calls=%fused_computation.15.clone.1 | convolution fusion | flops 12582912 | bytes 4390912 | tf_op jit(solution)/shard_map/while/body/eval_jaxpr/tshi,thi,shi->tsh/dot_general | solution.py:75
  279.6 4.1 multiply_reduce_fusion.11
  293.1 17.6 %fusion.123 = f32[32,16,1,32]{3,2,1,0:T(1,128)S(1)} fusion(f32[32,16,64,32]{2,1,3,0:T(8,128)S(1)} %multiply_bitcast_fusion.4, f32[32,16,64,1]{2,0,1,3:T(8,128)S(1)} %get-tuple-element.893), kind=kOutput, calls=%fused_computation.15.clone.1 | convolution fusion | flops 12582912 | bytes 4390912 | tf_op jit(solution)/shard_map/while/body/eval_jaxpr/tshi,thi,shi->tsh/dot_general | solution.py:75
  321.5 4.1 multiply_reduce_fusion.11
  335.1 17.6 %fusion.123 = f32[32,16,1,32]{3,2,1,0:T(1,128)S(1)} fusion(f32[32,16,64,32]{2,1,3,0:T(8,128)S(1)} %multiply_bitcast_fusion.4, f32[32,16,64,1]{2,0,1,3:T(8,128)S(1)} %get-tuple-element.893), kind=kOutput, calls=%fused_computation.15.clone.1 | convolution fusion | flops 12582912 | bytes 4390912 | tf_op jit(solution)/shard_map/while/body/eval_jaxpr/tshi,thi,shi->tsh/dot_general | solution.py:75
  363.5 4.1 multiply_reduce_fusion.11
  377.1 17.6 %fusion.123 = f32[32,16,1,32]{3,2,1,0:T(1,128)S(1)} fusion(f32[32,16,64,32]{2,1,3,0:T(8,128)S(1)} %multiply_bitcast_fusion.4, f32[32,16,64,1]{2,0,1,3:T(8,128)S(1)} %get-tuple-element.893), kind=kOutput, calls=%fused_computation.15.clone.1 | convolution fusion | flops 12582912 | bytes 4390912 | tf_op jit(solution)/shard_map/while/body/eval_jaxpr/tshi,thi,shi->tsh/dot_general | solution.py:75
  410.7 20.9 %all-reduce.8.cloned.1.call-done = f32[128,128]{1,0:T(8,128)} async-done(((f32[128,128]{1,0:T(8,128)}), f32[128,128]{1,0:T(8,128)}) %all-reduce.8.cloned.1.call-update) | async-done | bytes 65552 | tf_op jit(solution)/shard_map/psum | solution.py:221
  435.0 479.8 %all-gather.7.cloned.1.call-done = bf16[3,4096,1024]{2,1,0:T(8,128)(2,1)} async-done(((bf16[3,512,1024]{2,1,0:T(8,128)(2,1)}), bf16[3,4096,1024]{2,1,0:T(8,128)(2,1)}) %all-gather.7.cloned.1.call-update) | async-done | bytes 25165840 | tf_op jit(solution)/shard_map/all_gather | solution.py:235
  914.8 15.9 %multiply_reduce_fusion.4 = (f32[128,4096]{1,0:T(8,128)}, f32[128,4096]{1,0:T(8,128)}) fusion(f32[3,4096]{1,0:T(4,128)} %broadcast_subtract_fusion, f32[3,4096]{1,0:T(4,128)} %param.30, bf16[3,4096,1024]{2,1,0:T(8,128)(2,1)} %all-gather.7.cloned.1.call-done, bf16[1,128,1024]{2,1,0:T(8,128)(2,1)S(1)} %stack_reshape.14, ...), kind=kOutput, calls=%fused_computation.97 | convolution fusion | flops 3227254784 | bytes 30244864 | tf_op jit(solution)/shard_map/mtc,mnc->mtn/dot_general | solution.py:232
  935.9 4.1 collective-permute-done.1
  941.4 35.5 %all-reduce = (f32[1024]{0:T(1024)}, f32[16,64]{1,0:T(8,128)}) all-reduce(f32[1024]{0:T(1024)S(1)} %multiply_reduce_fusion.5, f32[16,64]{1,0:T(8,128)S(1)} %reduce_sum.75), channel_id=1, replica_groups=mesh['head'=4,'seq'=8] {'seq'}, use_global_device_ids=true, to_apply=%region_23.24 | all-reduce | flops 2048 | bytes 16384 | tf_op jit(solution)/shard_map/psum | solution.py:218
  976.9 20.3 %all-reduce.10.cloned.1.call-done = (f32[1024,128]{1,0:T(8,128)}, f32[128,1024]{1,0:T(8,128)}) async-done(((f32[1024,128]{1,0:T(8,128)}, f32[128,1024]{1,0:T(8,128)}), (f32[1024,128]{1,0:T(8,128)}, f32[128,1024]{1,0:T(8,128)})) %all-reduce.10.cloned.1.call-update) | async-done | bytes 1048592 | tf_op jit(solution)/shard_map/psum | solution.py:225
  997.2 26.5 %reduce-scatter.2.cloned.1.call-done = bf16[128,1024]{1,0:T(8,128)(2,1)} async-done(((bf16[128,4096]{1,0:T(8,128)(2,1)}), bf16[128,1024]{1,0:T(8,128)(2,1)}) %reduce-scatter.2.cloned.1.call-update) | async-done | bytes 262160 | tf_op jit(solution)/shard_map/reduce_scatter | solution.py:253
  (320 shorter events, 161.0 us)
Async XLA Ops:
  7.2 6.1 copy-start
  7.2 8.6 copy-start.27
  7.2 8.9 copy-start.28
  7.2 39.8 %all-reduce.6.cloned.1.call-start = ((), (), s32[]{:S(2)}) async-start(), calls=%async_computation.1 | async-start | bytes 131072 | tf_op jit(solution)/shard_map/psum | solution.py:147
  8.0 4.7 collective-permute-start
  15.7 127.7 %all-gather.9.cloned.1.call-start = ((), (), s32[]{:S(2)}) async-start(), calls=%async_computation.5 | async-start | bytes 4718592 | tf_op jit(solution)/shard_map/all_gather | solution.py:24
  15.8 31.2 %copy-start.37 = (f32[1024]{0:T(1024)S(1)}, f32[1024]{0:T(1024)}, u32[]{:S(2)}) copy-start(f32[1024]{0:T(1024)} %param.28) | copy-start | bytes 12292
  16.1 35.4 %copy-start.9 = (f32[4,32,16,64]{3,2,1,0:T(8,128)}, f32[4,32,16,64]{3,2,1,0:T(8,128)S(1)}, u32[]{:S(2)}) copy-start(f32[4,32,16,64]{3,2,1,0:T(8,128)S(1)} %reshape.116) | copy-start | bytes 1572868
  68.0 149.6 %all-gather.11.cloned.1.call-start = ((), (), s32[]{:S(2)}) async-start(), calls=%async_computation.6 | async-start | bytes 4718592 | tf_op jit(solution)/shard_map/all_gather | solution.py:24
  78.6 353.0 %all-reduce.8.cloned.1.call-start = ((), (), s32[]{:S(2)}) async-start(), calls=%async_computation.3 | async-start | bytes 131072 | tf_op jit(solution)/shard_map/psum | solution.py:221
  242.7 5.3 copy-start.21
  284.7 5.3 copy-start.21
  284.7 5.3 copy-start.24
  326.6 5.3 copy-start.21
  326.6 5.3 copy-start.24
  368.6 5.3 copy-start.21
  404.5 510.3 %all-gather.7.cloned.1.call-start = ((), (), s32[]{:S(2)}) async-start(), calls=%async_computation.2 | async-start | bytes 28311552 | tf_op jit(solution)/shard_map/all_gather | solution.py:235
  405.1 592.1 %all-reduce.10.cloned.1.call-start = ((), (), s32[]{:S(2)}) async-start(), calls=%async_computation.7 | async-start | bytes 2097152 | tf_op jit(solution)/shard_map/psum | solution.py:225
  407.3 24.3 %copy-start.17 = (f32[127,1024]{1,0:T(8,128)S(1)}, f32[127,1024]{1,0:T(8,128)}, u32[]{:S(2)}) copy-start(f32[127,1024]{1,0:T(8,128)} %copy-done.16) | copy-start | bytes 1560580
  407.3 24.3 %copy-start.18 = (bf16[128,1024]{1,0:T(8,128)(2,1)S(1)}, bf16[128,1024]{1,0:T(8,128)(2,1)}, u32[]{:S(2)}) copy-start(bf16[128,1024]{1,0:T(8,128)(2,1)} %param.22) | copy-start | bytes 786436
  410.7 504.1 %copy-start.31 = (bf16[1,128,1024]{2,1,0:T(8,128)(2,1)S(1)}, bf16[1,128,1024]{2,1,0:T(8,128)(2,1)}, u32[]{:S(2)}) copy-start(bf16[1,128,1024]{2,1,0:T(8,128)(2,1)} %stack_reshape.12) | copy-start | bytes 786436
  434.3 589.4 %reduce-scatter.2.cloned.1.call-start = ((), (), s32[]{:S(2)}) async-start(), calls=%async_computation.4 | async-start | bytes 1310720 | tf_op jit(solution)/shard_map/reduce_scatter | solution.py:253
  934.4 5.6 collective-permute-start.1
  935.9 5.4 copy-start.34
  (41 other events, 108.8 us)
Sparse Core Ops, SparseCore 0:
  15.8 31.1 all-reduce.5
  68.1 75.1 all-gather.8
  145.7 71.8 all-gather.10
  404.6 26.9 all-reduce.7
  433.0 481.7 all-gather.6
  918.8 78.4 all-reduce.9
  1000.5 23.2 reduce-scatter.1
where the time goes:
time: 1050 us; the launch traced here: 1030 us
  waiting for transfers between devices  684 us (65%)
  matrix products  123 us (12%)
  other arithmetic  90.1 us (9%)
  blocking collectives  66.6 us (6%)
  local copies, waits for them, and re-layouts  49 us (5%)
  between operations  14.9 us (1%)
    all_gather x1, waiting for transfers between devices, per_device(): lax.all_gather(proj_weights, 'seq', axis=1, tiled=True)  480 us
    all_gather x2, waiting for transfers between devices, entering(): gathered = jax.tree.map(lambda a: lax.all_gather(a, axis), part)  104 us
    dot_general x4, matrix products, sensitivity_each_segment(): jnp.einsum('tshi,thi,shi->tsh', decays, gate_matrix, lookup_matrix, preci...  70.5 us
    psum x1, blocking collectives, per_device(): lax.psum((device_raising_matrix, device_fading_floor, device_reward), 'seq')  35.5 us
    while x8, other arithmetic  32.2 us
    all_gather x1, blocking collectives, entering(): gathered = jax.tree.map(lambda a: lax.all_gather(a, axis), part)  31.1 us
    psum x1, waiting for transfers between devices, per_device(): lax.psum(jnp.dot(decay_input, decay_adapter_down, precision=EXACT_ARITHME...  27.3 us
    reduce_scatter x1, waiting for transfers between devices, per_device(): lax.psum_scatter(group_term.astype(jnp.bfloat16), 'head', scatter_dimensi...  26.5 us
  transfers between devices with their start and end apart: 9, of which 9 were waited for; matrix products, arithmetic and copies ran while one was open for 5% of the time, Pallas kernels for 0%

commit v1 on v0

v1 whole, which is shorter than its diff:
```python
import jax
import jax.numpy as jnp
import numpy as np
from jax import lax
from jax.experimental import pallas as pl
from jax.experimental.pallas import tpu as pltpu
from jax.sharding import PartitionSpec as P

F32 = jnp.float32
BF16 = jnp.bfloat16
EXACT = lax.Precision.HIGHEST
PAIR = 128
NN = (((1,), (0,)), ((), ()))
NT = (((1,), (1,)), ((), ()))
TN = (((0,), (0,)), ((), ()))


def mm(a, b, dims=NN):
    return lax.dot_general(a, b, dims, preferred_element_type=F32)


def halves(a):
    hi = a.astype(BF16)
    return hi, (a - hi.astype(F32)).astype(BF16)


def low_lanes(shape, half):
    return lax.broadcasted_iota(jnp.int32, shape, len(shape) - 1) < half


def block_rows(a, half):
    low = low_lanes(a.shape, half)
    zero = jnp.zeros_like(a)
    return jnp.concatenate([jnp.where(low, a, zero), jnp.where(low, zero, a)], 0)


def fold(a, half):
    rows = a.shape[0] // 2
    return jnp.where(low_lanes((rows, a.shape[1]), half), a[:rows], a[rows:])


def sum_matrix(rows):
    t = np.arange(rows)
    both = np.concatenate([t[:, None] > t[None, :], t[:, None] < t[None, :]], 0)
    return np.concatenate([both, both], 1).astype(np.float32)


def level_matrix(rows):
    t = np.arange(rows)
    parts = []
    m = 1
    while m < rows:
        mid = (t // (2 * m)) * 2 * m + m
        right = t >= mid
        u = t[None, :]
        take_right = (u >= mid[:, None]) & (u < t[:, None])
        take_left = (u > t[:, None]) & (u < mid[:, None])
        parts.append(np.where(right[:, None], take_right, take_left))
        m *= 2
    both = np.concatenate(parts, 0)
    return np.concatenate([both, both], 1).astype(np.float32)


def cumulative_matrix(rows):
    t = np.arange(rows)
    strict = (t[:, None] < t[None, :]).astype(np.float32)
    full = (t[:, None] <= t[None, :]).astype(np.float32)
    return np.concatenate([strict, strict, -full, -full], 1)


def decay_kernel(head, count, *refs):
    pres = refs[:count]
    base, up, r, k, v, dy, sums, lora, lora_t, w_out, end, st, gt = refs[count:]
    rows = r.shape[0]
    total = pres[0][...]
    for pre in pres[1:]:
        total = total + pre[...]
    mid = jnp.tanh(total)
    lora[...] = mid
    lora_t[...] = mid.T.astype(BF16)
    w = -jnp.exp(
        base[...] + lax.dot_general(mid, up[...], NN, precision=EXACT, preferred_element_type=F32)
    )
    w_out[...] = w
    hi, lo = halves(w)
    args = mm(sums[...], jnp.concatenate([hi, lo], 0))
    before, after = args[:rows], args[rows:]
    end[...] = before[rows - 1 :] + w[rows - 1 :]
    kf = (k[...].astype(F32) * jnp.exp(after)).astype(BF16)
    rb = (r[...].astype(F32) * jnp.exp(before)).astype(BF16)
    for p in range(r.shape[1] // PAIR):
        cols = slice(p * PAIR, (p + 1) * PAIR)
        st[:, cols] = fold(mm(v[:, cols], kf[:, cols], TN), head)
        gt[:, cols] = fold(mm(dy[:, cols], rb[:, cols], TN), head)


def inner_kernel(head, r, k, v, dy, w, u, levels, gr_out, gk_out, gv_out, self_out, du_out):
    rows = r.shape[0]
    rf, kf = r[...].astype(F32), k[...].astype(F32)
    vf, dyf = v[...].astype(F32), dy[...].astype(F32)
    hi, lo = halves(w[...])
    decay = jnp.exp(mm(levels[...], jnp.concatenate([hi, lo], 0)))
    row = lax.broadcasted_iota(jnp.int32, (rows, PAIR), 0)
    row2 = lax.broadcasted_iota(jnp.int32, (rows, 2 * rows), 0)
    col2 = lax.broadcasted_iota(jnp.int32, (rows, 2 * rows), 1)
    apart = row2 ^ (col2 & (rows - 1))
    dydy = block_rows(dy[...], head)
    pairs = mm(dy[...], block_rows(v[...], head), NT)
    pairs_t = mm(v[...], dydy, NT)
    gr = jnp.zeros((rows, PAIR), F32)
    gk = jnp.zeros((rows, PAIR), F32)
    scores_t = jnp.zeros((rows, 2 * rows), F32)
    m, level = 1, 0
    while m < rows:
        d = decay[level * rows : (level + 1) * rows]
        right = (row & m) != 0
        rd = jnp.where(right, rf * d, 0.0).astype(BF16)
        kd = jnp.where(right, 0.0, kf * d).astype(BF16)
        kk, rr = block_rows(kd, head), block_rows(rd, head)
        near = apart < 2 * m
        a = mm(kd, rr, NT)
        scores_t = scores_t + jnp.where(near, a, 0.0)
        here = jnp.where(near, pairs, 0.0).astype(BF16)
        here_t = jnp.where(near, pairs_t, 0.0).astype(BF16)
        gr = gr + jnp.where(right, d * mm(here, kk), 0.0)
        gk = gk + jnp.where(right, 0.0, d * mm(here_t, rr))
        m, level = 2 * m, level + 1
    lane_r = lax.broadcasted_iota(jnp.int32, (2 * PAIR, PAIR), 0) & (PAIR - 1)
    lane_c = lax.broadcasted_iota(jnp.int32, (2 * PAIR, PAIR), 1)
    ones = jnp.where((lane_r < head) == (lane_c < head), 1.0, 0.0).astype(BF16)
    sh, sl = halves(dyf * vf)
    own = mm(jnp.concatenate([sh, sl], 1), ones)
    bh, bl = halves(rf * u[...] * kf)
    bonus = mm(jnp.concatenate([bh, bl], 1), ones)
    gr_out[...] = gr
    gk_out[...] = gk
    gv_out[...] = mm(scores_t.astype(BF16), dydy) + bonus * dyf
    self_out[...] = own
    du_out[...] = jnp.sum(rf * kf * own, 0, keepdims=True)


def outer_kernel(
    head, r, k, v, dy, w, u, gr0, gk0, gv0, own, st_in, gt_in, st, end, up, lora_t, sums, cums,
    proj, up_grad, base_grad, mid_grad,
):
    rows = r.shape[0]
    rf, kf = r[...].astype(F32), k[...].astype(F32)
    wv = w[...]
    hi, lo = halves(wv)
    decay = jnp.exp(mm(sums[...], jnp.concatenate([hi, lo], 0)))
    eb, ee = decay[:rows], decay[rows:]
    sb = block_rows(st_in[...].astype(BF16), head)
    gb = block_rows(gt_in[...].astype(BF16), head)
    gr = gr0[...] + eb * mm(dy[...], sb)
    gk = gk0[...] + ee * mm(v[...], gb)
    gv = gv0[...] + mm((kf * ee).astype(BF16), gb, NT)
    at_end = jnp.sum(gt_in[...] * (jnp.exp(end[...]) * st_in[...] + st[...]), 0, keepdims=True)
    ah, al = halves(rf * gr)
    bh, bl = halves(kf * gk)
    gl = mm(cums[...], jnp.concatenate([ah, al, bh, bl], 0)) + at_end
    gp = gl * wv
    s = own[...] * u[...]
    proj[0] = (gr + kf * s).astype(BF16)
    proj[1] = (gk + rf * s).astype(BF16)
    proj[2] = gv.astype(BF16)
    gpb = gp.astype(BF16)
    up_grad[...] = mm(lora_t[...], gpb)
    base_grad[...] = jnp.sum(gp, 0, keepdims=True)

    @pl.when(pl.program_id(0) == 0)
    def _():
        mid_grad[...] = jnp.zeros_like(mid_grad)

    mid_grad[...] += mm(gpb, up[...].astype(BF16), NT)


def project_kernel(ring, tiles, place, *refs):
    blocks = refs[:ring]
    edge, w_own, w_far, mix, out = refs[ring:]
    rows = blocks[0].shape[1]
    step = pl.program_id(0)

    def product(weights):
        ms = [mix[m : m + 1, :] for m in range(3)]
        tail = sum(ms[m] * mm(edge[m], weights[m], NT) for m in range(3))
        for q in range(ring):
            own = prior = None
            for m in range(3):
                term = mm(blocks[q][m], weights[m], NT)
                later = ms[m] * term
                own = term - later if m == 0 else own + (term - later)
                prior = later if m == 0 else prior + later
            last = lax.broadcasted_iota(jnp.int32, prior.shape, 0) == rows - 1
            moved = jnp.where(last, tail[q : q + 1], pltpu.roll(prior, rows - 1, 0))
            slot = lax.rem(place[1] - q - place[2] + 2 * ring, ring)
            out[slot] = (own + moved).astype(BF16)

    @pl.when(step < tiles)
    def _():
        product(w_own)

    @pl.when(step >= tiles)
    def _():
        product(w_far)


def per_device(
    layer_input, receptance, key_act, value_act, attention_result_sensitivity, time_first,
    decay_exponent_base, decay_shift_mix, mix_rkv, decay_adapter_down, decay_adapter_up, proj_weights,
):
    rows, cols = layer_input.shape
    heads, head = time_first.shape
    rank = decay_adapter_down.shape[1]
    n_seq, n_head = lax.axis_size("seq"), lax.axis_size("head")
    inner = n_seq // n_head
    ring = n_seq // inner
    pairs = cols // PAIR
    seq, hd = lax.axis_index("seq"), lax.axis_index("head")
    r, k, v, dy = receptance, key_act, value_act, attention_result_sensitivity

    def shift(a, distance):
        return lax.ppermute(
            a, "seq", [(i - distance, i) for i in range(n_seq) if 0 <= i - distance < n_seq]
        )

    def head_parts(a):
        return [a] + [
            lax.ppermute(a, "head", [(i, (i + d) % n_head) for i in range(n_head)])
            for d in range(1, n_head)
        ]

    weights_far = lax.ppermute(proj_weights, "seq", [(i, i ^ 1) for i in range(n_seq)])

    carried = shift(layer_input[rows - 1 :], 1).astype(F32)
    features = layer_input.astype(F32)
    previous = jnp.concatenate([carried, features[:-1]], 0)
    decay_input = features + decay_shift_mix * (previous - features)
    pres = head_parts(jnp.dot(decay_input, decay_adapter_down, precision=EXACT))

    sums = jnp.asarray(sum_matrix(rows), BF16)
    levels = jnp.asarray(level_matrix(rows), BF16)
    cums = jnp.asarray(cumulative_matrix(rows), BF16)
    u = time_first.reshape(1, cols)

    def shape(s, t=F32):
        return jax.ShapeDtypeStruct(s, t)

    lora, lora_t, w, end, st, gt = pl.pallas_call(
        lambda *refs: decay_kernel(head, n_head, *refs),
        out_shape=[
            shape((rows, rank)), shape((rank, rows), BF16), shape((rows, cols)), shape((1, cols)),
            shape((head, cols)), shape((head, cols)),
        ],
        compiler_params=pltpu.CompilerParams(vmem_limit_bytes=32 * 2**20),
        name="decay_and_states",
    )(*pres, decay_exponent_base.reshape(1, cols), decay_adapter_up, r, k, v, dy, sums)

    def col_block(n):
        return pl.BlockSpec((n, PAIR), lambda p: (0, p))

    def whole(s):
        return pl.BlockSpec(s, lambda p: (0,) * len(s))

    tok = col_block(rows)
    gr0, gk0, gv0, own, du = pl.pallas_call(
        lambda *refs: inner_kernel(head, *refs),
        grid=(pairs,),
        in_specs=[tok] * 5 + [col_block(1), whole(levels.shape)],
        out_specs=[tok] * 4 + [col_block(1)],
        out_shape=[shape((rows, cols))] * 4 + [shape((1, cols))],
        compiler_params=pltpu.CompilerParams(vmem_limit_bytes=32 * 2**20),
        name="inside_chunk",
    )(r, k, v, dy, w, u, levels)

    def pack(state, decay):
        hi, lo = halves(decay)
        eight = (8, cols)
        return jnp.concatenate(
            [state.astype(BF16), jnp.broadcast_to(hi, eight), jnp.broadcast_to(lo, eight)], 0
        )

    def scan(state, sign):
        entry, entry_decay = jnp.zeros_like(state), jnp.zeros_like(end)
        run, run_decay = state, end
        d = 1
        while d < n_seq:
            got = shift(pack(run, run_decay), sign * d).astype(F32)
            got_state, got_decay = got[:head], got[head : head + 1] + got[head + 8 : head + 9]
            entry = got_state * jnp.exp(entry_decay) + entry
            entry_decay = entry_decay + got_decay
            run = entry * jnp.exp(end) + state
            run_decay = entry_decay + end
            d *= 2
        return entry

    st_in = scan(st, 1)
    gt_in = scan(gt, -1)

    proj, up_grad, base_grad, mid_grad = pl.pallas_call(
        lambda *refs: outer_kernel(head, *refs),
        grid=(pairs,),
        in_specs=[tok] * 5 + [col_block(1)] + [tok] * 4 + [col_block(head)] * 3
        + [col_block(1), col_block(rank), whole((rank, rows)), whole(sums.shape), whole(cums.shape)],
        out_specs=[
            pl.BlockSpec((3, rows, PAIR), lambda p: (0, 0, p)), col_block(rank), col_block(1),
            whole((rows, rank)),
        ],
        out_shape=[
            shape((3, rows, cols), BF16), shape((rank, cols)), shape((1, cols)), shape((rows, rank)),
        ],
        compiler_params=pltpu.CompilerParams(vmem_limit_bytes=32 * 2**20),
        name="across_chunks",
    )(r, k, v, dy, w, u, gr0, gk0, gv0, own, st_in, gt_in, st, end, decay_adapter_up, lora_t, sums, cums)

    def around(step):
        return [(i, (i + inner * step) % n_seq) for i in range(n_seq)]

    blocks = [proj]
    for _ in range(ring - 1):
        blocks.append(lax.ppermute(blocks[-1], "seq", around(1)))
    first = proj[:, :1]
    edges = []
    for q in range(ring):
        route = [
            (s + 1, (s + inner * q) % n_seq) for s in range(n_seq) if s + 1 < n_seq
        ]
        edges.append(lax.ppermute(first, "seq", route))
    pad = -ring % 16
    edge = jnp.concatenate(edges + [jnp.zeros((3, pad, cols), BF16)], 1)

    up_grad, base_grad, du = lax.psum((up_grad, base_grad, du), "seq")
    mid_grad = sum(head_parts(mid_grad)) * (1.0 - lora * lora)
    down_grad = lax.psum(jnp.dot(decay_input.T, mid_grad, precision=EXACT), "seq")
    grad_in = jnp.dot(mid_grad, decay_adapter_down.T, precision=EXACT)
    grad_next = jnp.concatenate([grad_in[1:], shift(grad_in[:1], -1)], 0)
    adapter_term = (1.0 - decay_shift_mix) * grad_in + decay_shift_mix * grad_next

    far_rows = proj_weights.shape[1]
    tile = min(far_rows, 256)
    tiles = far_rows // tile

    def column(i, place):
        side = jnp.where(i < tiles, place[0], 1 - place[0])
        return side * tiles + lax.rem(i, tiles)

    place = jnp.stack([lax.rem(seq, inner), seq // inner, hd]).astype(jnp.int32)
    partial_out = pl.pallas_call(
        lambda *refs: project_kernel(ring, tiles, *refs),
        grid_spec=pltpu.PrefetchScalarGridSpec(
            num_scalar_prefetch=1,
            grid=(inner * tiles,),
            in_specs=[pl.BlockSpec((3, rows, cols), lambda i, place: (0, 0, 0))] * ring
            + [
                pl.BlockSpec(edge.shape, lambda i, place: (0, 0, 0)),
                pl.BlockSpec((3, tile, cols), lambda i, place: (0, jnp.minimum(i, tiles - 1), 0)),
                pl.BlockSpec((3, tile, cols), lambda i, place: (0, jnp.maximum(i - tiles, 0), 0)),
                pl.BlockSpec(
                    (3, tile), lambda i, place: (0, place[1] * inner * tiles + column(i, place))
                ),
            ],
            out_specs=pl.BlockSpec((ring, rows, tile), lambda i, place: (0, 0, column(i, place))),
        ),
        out_shape=shape((ring, rows, cols), BF16),
        compiler_params=pltpu.CompilerParams(vmem_limit_bytes=40 * 2**20),
        name="projections",
    )(place, *blocks, edge, proj_weights, weights_far, mix_rkv)

    total = partial_out[0].astype(F32)
    for d in range(1, n_head):
        got = lax.ppermute(
            partial_out[d], "head", [(i, (i + d) % n_head) for i in range(n_head)]
        )
        total = total + got.astype(F32)
    swap = [
        (h * n_seq + z * inner + x, z * n_seq + h * inner + x)
        for h in range(n_head) for z in range(ring) for x in range(inner)
    ]
    summed = lax.ppermute(total.astype(BF16), ("head", "seq"), swap)
    result = (summed.astype(F32) + adapter_term).astype(BF16)
    return (result, down_grad, up_grad, base_grad.reshape(cols), du.reshape(heads, head))


def solution(mesh):
    return jax.shard_map(
        per_device,
        mesh=mesh,
        in_specs=(
            P("seq", "head"), P("seq", "head"), P("seq", "head"), P("seq", "head"), P("seq", "head"),
            P("head", None), P("head"), P("head"), P(), P("head", None), P(None, "head"),
            P(None, "seq", "head"),
        ),
        out_specs=(P("seq", "head"), P("head", None), P(None, "head"), P("head"), P("head", None)),
        check_vma=False,
    )
```

time: 1050 us -> 277 us (0.26); the launches traced: 1030 us -> 274 us
  waiting for transfers between devices: 684 us -> 113 us
  matrix products: 123 us -> 4.13 us
  other arithmetic: 90.1 us -> 7.71 us
  starting transfers between devices: 4.96 us -> 48.2 us
  Pallas kernels: 0 us -> 30 us
  local copies, waits for them, and re-layouts: 49 us -> 19.3 us
  blocking collectives: 66.6 us -> 37.3 us
    all_gather x3 -> x0, waiting for transfers between devices: 584 us -> none  [the longest x1 480 us: per_device(): lax.all_gather(proj_weights, 'seq', axis=1, tiled=True)]
    dot_general x41 -> x3, matrix products: 123 us -> 4.13 us  [the longest x1 1.82 us: per_device(): jnp.dot(decay_input.T, mid_grad, precision=EXACT)]
    ppermute x2 -> x26, waiting for transfers between devices: 4.44 us -> 80.9 us  [the longest x3 39.4 us: per_device(): blocks.append(lax.ppermute(blocks[-1], 'seq', around(1)))]
    ppermute x2 -> x26, starting transfers between devices: 4.68 us -> 48.2 us  [the longest x8 24.2 us: shift(): lax.ppermute(a, 'seq', [(i - distance, i) for i in range(n_seq) if 0 <= i...]
    psum x3 -> x1, waiting for transfers between devices: 68.5 us -> 31.7 us  [per_device(): lax.psum(jnp.dot(decay_input.T, mid_grad, precision=EXACT), 'seq')]
    while x8 -> x0, other arithmetic: 32.2 us -> none
    all_gather x1 -> x0, blocking collectives: 31.1 us -> none  [entering(): gathered = jax.tree.map(lambda a: lax.all_gather(a, axis), part)]
    pallas_call x0 -> x4, Pallas kernels: none -> 30 us  [the longest x1 13.3 us: per_device(): pl.pallas_call(lambda *refs: project_kernel(ring, tiles, *refs), grid_spe...]
  transfers between devices with their start and end apart: 9 -> 27, of which waited for: 9 -> 19; matrix products, arithmetic and copies ran while one was open for 5% -> 5% of each run, Pallas kernels for 0% -> 6%
where the time goes in v1:
time: 277 us; the launch traced here: 274 us
  waiting for transfers between devices  113 us (41%)
  starting transfers between devices  48.2 us (17%)
  blocking collectives  37.3 us (13%)
  Pallas kernels  30 us (11%)
  local copies, waits for them, and re-layouts  19.3 us (7%)
  between operations  14.7 us (5%)
  other arithmetic  7.71 us (3%)
  matrix products  4.13 us (1%)
    ppermute x3, waiting for transfers between devices, per_device(): blocks.append(lax.ppermute(blocks[-1], 'seq', around(1)))  39.4 us
    psum x1, blocking collectives, per_device(): up_grad, base_grad, du = lax.psum((up_grad, base_grad, du), 'seq')  37.3 us
    psum x1, waiting for transfers between devices, per_device(): lax.psum(jnp.dot(decay_input.T, mid_grad, precision=EXACT), 'seq')  31.7 us
    ppermute x8, starting transfers between devices, shift(): lax.ppermute(a, 'seq', [(i - distance, i) for i in range(n_seq) if 0 <= i...  24.2 us
    unnamed x76, local copies, waits for them, and re-layouts  14.3 us
    ppermute x4, waiting for transfers between devices, per_device(): edges.append(lax.ppermute(first, 'seq', route))  14 us
    ppermute x8, waiting for transfers between devices, shift(): lax.ppermute(a, 'seq', [(i - distance, i) for i in range(n_seq) if 0 <= i...  13.9 us
    pallas_call x1, Pallas kernels, per_device(): pl.pallas_call(lambda *refs: project_kernel(ring, tiles, *refs), grid_spe...  13.3 us
  transfers between devices with their start and end apart: 27, of which 19 were waited for; matrix products, arithmetic and copies ran while one was open for 5% of the time, Pallas kernels for 6%

profile of v1, /device:TPU:4, one launch (start us, length us, event | category | flops | bytes accessed | tf_op | source)
XLA Modules:
  0.0 274.0 jit_solution(9017175817436515437)
XLA Ops:
  8.0 3.4 %collective-permute-start = (bf16[1,1024]{1,0:T(2,128)(2,1)S(1)}, bf16[1,1024]{1,0:T(2,128)(2,1)S(1)}, u32[]{:S(2)}, u32[]{:S(2)}) collective-permute-start(bf16[1,1024]{1,0:T(2,128)(2,1)S(1)} %slice.75), channel_id=1, source_target_pairs={{0,1},{1,2},{2,3},{3,4},{4,5},{5,6},{6,7},{8,9},{9,10},{10,11},{11... | collective-permute-start | bytes 6152 | tf_op jit(solution)/shard_map/ppermute | solution.py:222
  16.5 1.8 collective-permute-done.1.refs_1_
  28.6 5.0 %collective-permute-start.4 = (bf16[80,1024]{1,0:T(8,128)(2,1)S(1)}, bf16[80,1024]{1,0:T(8,128)(2,1)S(1)}, u32[]{:S(2)}, u32[]{:S(2)}) collective-permute-start(bf16[80,1024]{1,0:T(8,128)(2,1)S(1)} %get-tuple-element.64), channel_id=1, source_target_pairs={{0,1},{1,2},{2,3},{3,4},{4,5},{5,6},{6,7},{8,9},{9,10},{10,11},{11... | collective-permute-start | bytes 491528 | tf_op jit(solution)/shard_map/ppermute | solution.py:222
  33.5 2.8 %collective-permute-done.7 = bf16[80,1024]{1,0:T(8,128)(2,1)S(1)} collective-permute-done((bf16[80,1024]{1,0:T(8,128)(2,1)S(1)}, bf16[80,1024]{1,0:T(8,128)(2,1)S(1)}, u32[]{:S(2)}, u32[]{:S(2)}) %collective-permute-start.7) | collective-permute-done | bytes 163872 | tf_op jit(solution)/shard_map/ppermute | solution.py:222
  36.4 3.6 %collective-permute-done.4 = bf16[80,1024]{1,0:T(8,128)(2,1)S(1)} collective-permute-done((bf16[80,1024]{1,0:T(8,128)(2,1)S(1)}, bf16[80,1024]{1,0:T(8,128)(2,1)S(1)}, u32[]{:S(2)}, u32[]{:S(2)}) %collective-permute-start.4) | collective-permute-done | bytes 163872 | tf_op jit(solution)/shard_map/ppermute | solution.py:222
  40.3 4.5 %collective-permute-start.5 = (bf16[80,1024]{1,0:T(8,128)(2,1)S(1)}, bf16[80,1024]{1,0:T(8,128)(2,1)S(1)}, u32[]{:S(2)}, u32[]{:S(2)}) collective-permute-start(bf16[80,1024]{1,0:T(8,128)(2,1)S(1)} %pad_maximum_fusion.4), channel_id=1, source_target_pairs={{0,2},{1,3},{2,4},{3,5},{4,6},{5,7},{8,10},{9,11},{10,12},{11,13},... | collective-permute-start | bytes 491528 | tf_op jit(solution)/shard_map/ppermute | solution.py:222
  48.4 5.5 %collective-permute-done.8 = bf16[80,1024]{1,0:T(8,128)(2,1)S(1)} collective-permute-done((bf16[80,1024]{1,0:T(8,128)(2,1)S(1)}, bf16[80,1024]{1,0:T(8,128)(2,1)S(1)}, u32[]{:S(2)}, u32[]{:S(2)}) %collective-permute-start.8) | collective-permute-done | bytes 163872 | tf_op jit(solution)/shard_map/ppermute | solution.py:222
  58.8 7.9 %inside_chunk.1 = (f32[128,1024]{1,0:T(8,128)S(1)}, f32[128,1024]{1,0:T(8,128)S(1)}, f32[128,1024]{1,0:T(8,128)S(1)}, f32[128,1024]{1,0:T(8,128)S(1)}, f32[1,1024]{1,0:T(1,128)S(1)}) custom-call(bf16[128,1024]{1,0:T(8,128)(2,1)S(1)} %copy-done.2, bf16[128,1024]{1,0:T(8,128)(2,1)S(1)} %copy-done.4, bf16[128,1024]{1,0:T(8,128)(2,1)S(1)} %copy-done.6, ...), custom_call_target="tpu_custom_call" | custom-call | tf_op jit(solution)/shard_map/inside_chunk/pallas_call | solution.py:265
  69.0 6.1 %collective-permute-start.6 = (bf16[80,1024]{1,0:T(8,128)(2,1)S(1)}, bf16[80,1024]{1,0:T(8,128)(2,1)S(1)}, u32[]{:S(2)}, u32[]{:S(2)}) collective-permute-start(bf16[80,1024]{1,0:T(8,128)(2,1)S(1)} %pad_maximum_fusion.5), channel_id=1, source_target_pairs={{0,4},{1,5},{2,6},{3,7},{8,12},{9,13},{10,14},{11,15},{16,20},{17,... | collective-permute-start | bytes 491528 | tf_op jit(solution)/shard_map/ppermute | solution.py:222
  78.1 7.7 %across_chunks.1 = (bf16[3,128,1024]{2,1,0:T(8,128)(2,1)S(1)}, f32[128,1024]{1,0:T(8,128)}, f32[1,1024]{1,0:T(1,128)S(1)}, f32[128,128]{1,0:T(8,128)S(1)}) custom-call(bf16[128,1024]{1,0:T(8,128)(2,1)S(1)} %copy-done.2, bf16[128,1024]{1,0:T(8,128)(2,1)S(1)} %copy-done.4, bf16[128,1024]{1,0:T(8,128)(2,1)S(1)} %copy-done.6, bf16[128,1024]{1,0:T(8,128)(2,1)S(1)} %copy-done.8, ...), custom_call_target="tpu_custom_call" | custom-call | tf_op jit(solution)/shard_map/across_chunks/pallas_call | solution.py:299
  85.8 4.1 %collective-permute-start.10 = (bf16[3,128,1024]{2,1,0:T(8,128)(2,1)S(1)}, bf16[3,128,1024]{2,1,0:T(8,128)(2,1)S(1)}, u32[]{:S(2)}, u32[]{:S(2)}) collective-permute-start(bf16[3,128,1024]{2,1,0:T(8,128)(2,1)S(1)} %get-tuple-element.29.refs_1_), channel_id=1, source_target_pairs={{0,2},{1,3},{2,4},{3,5},{4,6},{5,7},{6,0},{7,1},{8,10},{9,11},{10,... | collective-permute-start | bytes 2359304 | tf_op jit(solution)/shard_map/ppermute | solution.py:320
  89.9 19.7 %collective-permute-done.10.refs_2_ = bf16[3,128,1024]{2,1,0:T(8,128)(2,1)S(1)} collective-permute-done((bf16[3,128,1024]{2,1,0:T(8,128)(2,1)S(1)}, bf16[3,128,1024]{2,1,0:T(8,128)(2,1)S(1)}, u32[]{:S(2)}, u32[]{:S(2)}) %collective-permute-start.10) | collective-permute-done | bytes 786464 | tf_op jit(solution)/shard_map/ppermute | solution.py:320
  109.6 19.7 %collective-permute-done.11.refs_3_ = bf16[3,128,1024]{2,1,0:T(8,128)(2,1)S(1)} collective-permute-done((bf16[3,128,1024]{2,1,0:T(8,128)(2,1)S(1)}, bf16[3,128,1024]{2,1,0:T(8,128)(2,1)S(1)}, u32[]{:S(2)}, u32[]{:S(2)}) %collective-permute-start.11) | collective-permute-done | bytes 786464 | tf_op jit(solution)/shard_map/ppermute | solution.py:320
  137.1 10.5 %collective-permute-done.14 = bf16[3,1,1024]{2,1,0:T(2,128)(2,1)S(1)} collective-permute-done((bf16[3,1,1024]{2,1,0:T(2,128)(2,1)S(1)}, bf16[3,1,1024]{2,1,0:T(2,128)(2,1)S(1)}, u32[]{:S(2)}, u32[]{:S(2)}) %collective-permute-start.14) | collective-permute-done | bytes 6176 | tf_op jit(solution)/shard_map/ppermute | solution.py:327
  155.8 13.3 %projections.1 = bf16[4,128,1024]{2,1,0:T(8,128)(2,1)S(1)} custom-call(s32[3]{0:T(128)S(1)} %pad_add_fusion.refs_0_, bf16[3,128,1024]{2,1,0:T(8,128)(2,1)S(1)} %copy-done.12, bf16[3,128,1024]{2,1,0:T(8,128)(2,1)S(1)} %collective-permute-done.10.refs_2_, bf16[3,128,1024]{2,1,0:T(8,128)(2,1)S(1)} %collective-permute-done.11.refs_3_, ...), custom_call_target="tpu_custom_call" | custom-call | tf_op jit(solution)/shard_map/projections/pallas_call | solution.py:347
  171.2 1.8 fusion.10
  173.0 3.7 %collective-permute-done.18 = bf16[128,1024]{1,0:T(8,128)(2,1)S(1)} collective-permute-done((bf16[128,1024]{1,0:T(8,128)(2,1)S(1)}, bf16[128,1024]{1,0:T(8,128)(2,1)S(1)}, u32[]{:S(2)}, u32[]{:S(2)}) %collective-permute-start.18) | collective-permute-done | bytes 262176 | tf_op jit(solution)/shard_map/ppermute | solution.py:370
  176.7 2.2 collective-permute-done.19
  178.9 2.4 collective-permute-done.20
  181.5 8.7 %collective-permute-start.21 = (bf16[128,1024]{1,0:T(8,128)(2,1)S(1)}, bf16[128,1024]{1,0:T(8,128)(2,1)S(1)}, u32[]{:S(2)}, u32[]{:S(2)}) collective-permute-start(bf16[128,1024]{1,0:T(8,128)(2,1)S(1)} %fusion.7), channel_id=1, source_target_pairs={{0,0},{1,1},{2,8},{3,9},{4,16},{5,17},{6,24},{7,25},{8,2},{9,3},{1... | collective-permute-start | bytes 786440 | tf_op jit(solution)/shard_map/ppermute | solution.py:378
  193.5 37.3 %all-reduce = (f32[1024]{0:T(1024)}, f32[16,64]{1,0:T(8,128)}) all-reduce(f32[1024]{0:T(1024)S(1)} %bitcast.26, f32[16,64]{1,0:T(8,128)S(1)} %reshape.29), channel_id=1, replica_groups=mesh['head'=4,'seq'=8] {'seq'}, use_global_device_ids=true, to_apply=%region_2.0 | all-reduce | flops 2048 | bytes 16384 | tf_op jit(solution)/shard_map/psum | solution.py:331
  231.7 31.7 %all-reduce.4.cloned.1.call-done = (f32[1024,128]{1,0:T(8,128)}, f32[128,1024]{1,0:T(8,128)}) async-done(((f32[1024,128]{1,0:T(8,128)}, f32[128,1024]{1,0:T(8,128)}), (f32[1024,128]{1,0:T(8,128)}, f32[128,1024]{1,0:T(8,128)})) %all-reduce.4.cloned.1.call-update) | async-done | bytes 1048592 | tf_op jit(solution)/shard_map/psum | solution.py:333
  263.4 1.9 copy.22
  265.3 1.9 copy.23
  (166 shorter events, 52.1 us)
Async XLA Ops:
  7.2 256.3 %all-reduce.4.cloned.1.call-start = ((), (), s32[]{:S(2)}) async-start(), calls=%async_computation | async-start | bytes 2097152 | tf_op jit(solution)/shard_map/psum | solution.py:333
  8.0 4.7 %collective-permute-start = (bf16[1,1024]{1,0:T(2,128)(2,1)S(1)}, bf16[1,1024]{1,0:T(2,128)(2,1)S(1)}, u32[]{:S(2)}, u32[]{:S(2)}) collective-permute-start(bf16[1,1024]{1,0:T(2,128)(2,1)S(1)} %slice.75), channel_id=1, source_target_pairs={{0,1},{1,2},{2,3},{3,4},{4,5},{5,6},{6,7},{8,9},{9,10},{10,11},{11... | collective-permute-start | bytes 6152 | tf_op jit(solution)/shard_map/ppermute | solution.py:222
  14.5 5.0 %collective-permute-start.2 = (f32[128,128]{1,0:T(8,128)S(1)}, f32[128,128]{1,0:T(8,128)S(1)}, u32[]{:S(2)}, u32[]{:S(2)}) collective-permute-start(f32[128,128]{1,0:T(8,128)S(1)} %fusion.12.refs_0_), channel_id=1, source_target_pairs={{0,16},{8,24},{16,0},{24,8},{1,17},{9,25},{17,1},{25,9},{2,18},{10... | collective-permute-start | bytes 196616 | tf_op jit(solution)/shard_map/ppermute | solution.py:228
  15.1 4.4 %collective-permute-start.3 = (f32[128,128]{1,0:T(8,128)S(1)}, f32[128,128]{1,0:T(8,128)S(1)}, u32[]{:S(2)}, u32[]{:S(2)}) collective-permute-start(f32[128,128]{1,0:T(8,128)S(1)} %fusion.12.refs_0_), channel_id=1, source_target_pairs={{0,24},{8,0},{16,8},{24,16},{1,25},{9,1},{17,9},{25,17},{2,26},{10... | collective-permute-start | bytes 196616 | tf_op jit(solution)/shard_map/ppermute | solution.py:228
  27.2 9.2 %collective-permute-start.7 = (bf16[80,1024]{1,0:T(8,128)(2,1)S(1)}, bf16[80,1024]{1,0:T(8,128)(2,1)S(1)}, u32[]{:S(2)}, u32[]{:S(2)}) collective-permute-start(bf16[80,1024]{1,0:T(8,128)(2,1)S(1)} %get-tuple-element.65), channel_id=1, source_target_pairs={{1,0},{2,1},{3,2},{4,3},{5,4},{6,5},{7,6},{9,8},{10,9},{11,10},{12... | collective-permute-start | bytes 491528 | tf_op jit(solution)/shard_map/ppermute | solution.py:222
  28.6 11.5 %collective-permute-start.4 = (bf16[80,1024]{1,0:T(8,128)(2,1)S(1)}, bf16[80,1024]{1,0:T(8,128)(2,1)S(1)}, u32[]{:S(2)}, u32[]{:S(2)}) collective-permute-start(bf16[80,1024]{1,0:T(8,128)(2,1)S(1)} %get-tuple-element.64), channel_id=1, source_target_pairs={{0,1},{1,2},{2,3},{3,4},{4,5},{5,6},{6,7},{8,9},{9,10},{10,11},{11... | collective-permute-start | bytes 491528 | tf_op jit(solution)/shard_map/ppermute | solution.py:222
  40.3 7.4 %collective-permute-start.5 = (bf16[80,1024]{1,0:T(8,128)(2,1)S(1)}, bf16[80,1024]{1,0:T(8,128)(2,1)S(1)}, u32[]{:S(2)}, u32[]{:S(2)}) collective-permute-start(bf16[80,1024]{1,0:T(8,128)(2,1)S(1)} %pad_maximum_fusion.4), channel_id=1, source_target_pairs={{0,2},{1,3},{2,4},{3,5},{4,6},{5,7},{8,10},{9,11},{10,12},{11,13},... | collective-permute-start | bytes 491528 | tf_op jit(solution)/shard_map/ppermute | solution.py:222
  44.8 108.7 %collective-permute-start.17 = (bf16[3,512,1024]{2,1,0:T(8,128)(2,1)}, bf16[3,512,1024]{2,1,0:T(8,128)(2,1)}, u32[]{:S(2)}, u32[]{:S(2)}) collective-permute-start(bf16[3,512,1024]{2,1,0:T(8,128)(2,1)} %refs_6_.4), channel_id=1, source_target_pairs={{0,1},{1,0},{2,3},{3,2},{4,5},{5,4},{6,7},{7,6},{8,9},{9,8},{10,11... | collective-permute-start | bytes 9437192 | tf_op jit(solution)/shard_map/ppermute | solution.py:232
  46.3 7.5 %collective-permute-start.8 = (bf16[80,1024]{1,0:T(8,128)(2,1)S(1)}, bf16[80,1024]{1,0:T(8,128)(2,1)S(1)}, u32[]{:S(2)}, u32[]{:S(2)}) collective-permute-start(bf16[80,1024]{1,0:T(8,128)(2,1)S(1)} %pad_maximum_fusion.6), channel_id=1, source_target_pairs={{2,0},{3,1},{4,2},{5,3},{6,4},{7,5},{10,8},{11,9},{12,10},{13,11},... | collective-permute-start | bytes 491528 | tf_op jit(solution)/shard_map/ppermute | solution.py:222
  56.7 18.5 %collective-permute-start.9 = (bf16[80,1024]{1,0:T(8,128)(2,1)}, bf16[80,1024]{1,0:T(8,128)(2,1)}, u32[]{:S(2)}, u32[]{:S(2)}) collective-permute-start(bf16[80,1024]{1,0:T(8,128)(2,1)} %pad_maximum_fusion.7), channel_id=1, source_target_pairs={{4,0},{5,1},{6,2},{7,3},{12,8},{13,9},{14,10},{15,11},{20,16},{21,... | collective-permute-start | bytes 491528 | tf_op jit(solution)/shard_map/ppermute | solution.py:222
  69.0 9.0 %collective-permute-start.6 = (bf16[80,1024]{1,0:T(8,128)(2,1)S(1)}, bf16[80,1024]{1,0:T(8,128)(2,1)S(1)}, u32[]{:S(2)}, u32[]{:S(2)}) collective-permute-start(bf16[80,1024]{1,0:T(8,128)(2,1)S(1)} %pad_maximum_fusion.5), channel_id=1, source_target_pairs={{0,4},{1,5},{2,6},{3,7},{8,12},{9,13},{10,14},{11,15},{16,20},{17,... | collective-permute-start | bytes 491528 | tf_op jit(solution)/shard_map/ppermute | solution.py:222
  85.8 23.8 %collective-permute-start.10 = (bf16[3,128,1024]{2,1,0:T(8,128)(2,1)S(1)}, bf16[3,128,1024]{2,1,0:T(8,128)(2,1)S(1)}, u32[]{:S(2)}, u32[]{:S(2)}) collective-permute-start(bf16[3,128,1024]{2,1,0:T(8,128)(2,1)S(1)} %get-tuple-element.29.refs_1_), channel_id=1, source_target_pairs={{0,2},{1,3},{2,4},{3,5},{4,6},{5,7},{6,0},{7,1},{8,10},{9,11},{10,... | collective-permute-start | bytes 2359304 | tf_op jit(solution)/shard_map/ppermute | solution.py:320
  109.6 19.7 %collective-permute-start.11 = (bf16[3,128,1024]{2,1,0:T(8,128)(2,1)S(1)}, bf16[3,128,1024]{2,1,0:T(8,128)(2,1)S(1)}, u32[]{:S(2)}, u32[]{:S(2)}) collective-permute-start(bf16[3,128,1024]{2,1,0:T(8,128)(2,1)S(1)} %collective-permute-done.10.refs_2_), channel_id=1, source_target_pairs={{0,2},{1,3},{2,4},{3,5},{4,6},{5,7},{6,0},{7,1},{8,10},{9,11},{10,... | collective-permute-start | bytes 2359304 | tf_op jit(solution)/shard_map/ppermute | solution.py:320
  129.3 23.4 %collective-permute-start.12 = (bf16[3,128,1024]{2,1,0:T(8,128)(2,1)S(1)}, bf16[3,128,1024]{2,1,0:T(8,128)(2,1)S(1)}, u32[]{:S(2)}, u32[]{:S(2)}) collective-permute-start(bf16[3,128,1024]{2,1,0:T(8,128)(2,1)S(1)} %collective-permute-done.11.refs_3_), channel_id=1, source_target_pairs={{0,2},{1,3},{2,4},{3,5},{4,6},{5,7},{6,0},{7,1},{8,10},{9,11},{10,... | collective-permute-start | bytes 2359304 | tf_op jit(solution)/shard_map/ppermute | solution.py:320
  130.2 5.6 %collective-permute-start.13 = (bf16[3,1,1024]{2,1,0:T(2,128)(2,1)S(1)}, bf16[3,1,1024]{2,1,0:T(2,128)(2,1)S(1)}, u32[]{:S(2)}, u32[]{:S(2)}) collective-permute-start(bf16[3,1,1024]{2,1,0:T(2,128)(2,1)S(1)} %slice.93), channel_id=1, source_target_pairs={{1,0},{2,1},{3,2},{4,3},{5,4},{6,5},{7,6},{9,8},{10,9},{11,10},{12... | collective-permute-start | bytes 18440 | tf_op jit(solution)/shard_map/ppermute | solution.py:327
  131.5 16.0 %collective-permute-start.14 = (bf16[3,1,1024]{2,1,0:T(2,128)(2,1)S(1)}, bf16[3,1,1024]{2,1,0:T(2,128)(2,1)S(1)}, u32[]{:S(2)}, u32[]{:S(2)}) collective-permute-start(bf16[3,1,1024]{2,1,0:T(2,128)(2,1)S(1)} %slice.93), channel_id=1, source_target_pairs={{1,2},{2,3},{3,4},{4,5},{5,6},{6,7},{7,0},{9,10},{10,11},{11,12},{... | collective-permute-start | bytes 18440 | tf_op jit(solution)/shard_map/ppermute | solution.py:327
  132.8 15.0 %collective-permute-start.15 = (bf16[3,1,1024]{2,1,0:T(2,128)(2,1)S(1)}, bf16[3,1,1024]{2,1,0:T(2,128)(2,1)S(1)}, u32[]{:S(2)}, u32[]{:S(2)}) collective-permute-start(bf16[3,1,1024]{2,1,0:T(2,128)(2,1)S(1)} %slice.93), channel_id=1, source_target_pairs={{1,4},{2,5},{3,6},{4,7},{5,0},{6,1},{7,2},{9,12},{10,13},{11,14},{... | collective-permute-start | bytes 18440 | tf_op jit(solution)/shard_map/ppermute | solution.py:327
  135.8 14.1 %collective-permute-start.16 = (bf16[3,1,1024]{2,1,0:T(2,128)(2,1)S(1)}, bf16[3,1,1024]{2,1,0:T(2,128)(2,1)S(1)}, u32[]{:S(2)}, u32[]{:S(2)}) collective-permute-start(bf16[3,1,1024]{2,1,0:T(2,128)(2,1)S(1)} %slice.93), channel_id=1, source_target_pairs={{1,6},{2,7},{3,0},{4,1},{5,2},{6,3},{7,4},{9,14},{10,15},{11,8},{1... | collective-permute-start | bytes 18440 | tf_op jit(solution)/shard_map/ppermute | solution.py:327
  147.7 4.9 %collective-permute-start.23 = (f32[128,128]{1,0:T(8,128)S(1)}, f32[128,128]{1,0:T(8,128)S(1)}, u32[]{:S(2)}, u32[]{:S(2)}) collective-permute-start(f32[128,128]{1,0:T(8,128)S(1)} %get-tuple-element.30), channel_id=1, source_target_pairs={{0,16},{8,24},{16,0},{24,8},{1,17},{9,25},{17,1},{25,9},{2,18},{10... | collective-permute-start | bytes 196616 | tf_op jit(solution)/shard_map/ppermute | solution.py:228
  169.2 7.6 %collective-permute-start.18 = (bf16[128,1024]{1,0:T(8,128)(2,1)S(1)}, bf16[128,1024]{1,0:T(8,128)(2,1)S(1)}, u32[]{:S(2)}, u32[]{:S(2)}) collective-permute-start(bf16[128,1024]{1,0:T(8,128)(2,1)S(1)} %get-tuple-element.61), channel_id=1, source_target_pairs={{0,8},{8,16},{16,24},{24,0},{1,9},{9,17},{17,25},{25,1},{2,10},{10... | collective-permute-start | bytes 786440 | tf_op jit(solution)/shard_map/ppermute | solution.py:370
  169.7 9.2 %collective-permute-start.19 = (bf16[128,1024]{1,0:T(8,128)(2,1)S(1)}, bf16[128,1024]{1,0:T(8,128)(2,1)S(1)}, u32[]{:S(2)}, u32[]{:S(2)}) collective-permute-start(bf16[128,1024]{1,0:T(8,128)(2,1)S(1)} %get-tuple-element.63), channel_id=1, source_target_pairs={{0,16},{8,24},{16,0},{24,8},{1,17},{9,25},{17,1},{25,9},{2,18},{10... | collective-permute-start | bytes 786440 | tf_op jit(solution)/shard_map/ppermute | solution.py:370
  170.6 10.8 %collective-permute-start.20 = (bf16[128,1024]{1,0:T(8,128)(2,1)S(1)}, bf16[128,1024]{1,0:T(8,128)(2,1)S(1)}, u32[]{:S(2)}, u32[]{:S(2)}) collective-permute-start(bf16[128,1024]{1,0:T(8,128)(2,1)S(1)} %get-tuple-element.62), channel_id=1, source_target_pairs={{0,24},{8,0},{16,8},{24,16},{1,25},{9,1},{17,9},{25,17},{2,26},{10... | collective-permute-start | bytes 786440 | tf_op jit(solution)/shard_map/ppermute | solution.py:370
  181.5 49.3 %collective-permute-start.21 = (bf16[128,1024]{1,0:T(8,128)(2,1)S(1)}, bf16[128,1024]{1,0:T(8,128)(2,1)S(1)}, u32[]{:S(2)}, u32[]{:S(2)}) collective-permute-start(bf16[128,1024]{1,0:T(8,128)(2,1)S(1)} %fusion.7), channel_id=1, source_target_pairs={{0,0},{1,1},{2,8},{3,9},{4,16},{5,17},{6,24},{7,25},{8,2},{9,3},{1... | collective-permute-start | bytes 786440 | tf_op jit(solution)/shard_map/ppermute | solution.py:378
  190.9 39.9 %collective-permute-start.25 = (f32[1,1024]{1,0:T(1,128)S(1)}, f32[1,1024]{1,0:T(1,128)S(1)}, u32[]{:S(2)}, u32[]{:S(2)}) collective-permute-start(f32[1,1024]{1,0:T(1,128)S(1)} %slice.120), channel_id=1, source_target_pairs={{1,0},{2,1},{3,2},{4,3},{5,4},{6,5},{7,6},{9,8},{10,9},{11,10},{12... | collective-permute-start | bytes 12296 | tf_op jit(solution)/shard_map/ppermute | solution.py:222
  (40 other events, 578.8 us)
Sparse Core Ops, SparseCore 0:
  173.1 90.2 all-reduce.3

commit v2 on v1

v2 whole, which is shorter than its diff:
```python
import jax
import jax.numpy as jnp
import numpy as np
from jax import lax
from jax.experimental import pallas as pl
from jax.experimental.pallas import tpu as pltpu
from jax.sharding import PartitionSpec as P

F32 = jnp.float32
BF16 = jnp.bfloat16
PAIR = 128
VMEM = 56 * 2**20
NN = (((1,), (0,)), ((), ()))
NT = (((1,), (1,)), ((), ()))
TN = (((0,), (0,)), ((), ()))


def mm(a, b, dims=NN):
    return lax.dot_general(a, b, dims, preferred_element_type=F32)


def halves(a):
    hi = a.astype(BF16)
    return hi, (a - hi.astype(F32)).astype(BF16)


def low_lanes(shape, half):
    return lax.broadcasted_iota(jnp.int32, shape, len(shape) - 1) < half


def block_rows(a, half):
    low = low_lanes(a.shape, half)
    zero = jnp.zeros_like(a)
    return jnp.concatenate([jnp.where(low, a, zero), jnp.where(low, zero, a)], 0)


def fold(a, half):
    rows = a.shape[0] // 2
    return jnp.where(low_lanes((rows, a.shape[1]), half), a[:rows], a[rows:])


def sum_matrix(rows):
    t = np.arange(rows)
    both = np.concatenate([t[:, None] > t[None, :], t[:, None] < t[None, :]], 0)
    return np.concatenate([both, both], 1).astype(np.float32)


def level_matrix(rows):
    t = np.arange(rows)
    parts = []
    m = 1
    while m < rows:
        mid = (t // (2 * m)) * 2 * m + m
        right = t >= mid
        u = t[None, :]
        take_right = (u >= mid[:, None]) & (u < t[:, None])
        take_left = (u > t[:, None]) & (u < mid[:, None])
        parts.append(np.where(right[:, None], take_right, take_left))
        m *= 2
    both = np.concatenate(parts, 0)
    return np.concatenate([both, both], 1).astype(np.float32)


def cumulative_matrix(rows):
    t = np.arange(rows)
    strict = (t[:, None] < t[None, :]).astype(np.float32)
    full = (t[:, None] <= t[None, :]).astype(np.float32)
    return np.concatenate([strict, strict, -full, -full], 1)


def split_rows(a):
    hi, lo = halves(a)
    return jnp.broadcast_to(hi, (8, a.shape[1])), jnp.broadcast_to(lo, (8, a.shape[1]))


def joined(msg, at):
    return msg[at : at + 1].astype(F32) + msg[at + 8 : at + 9].astype(F32)


def mm3(a, b, dims=NN):
    ah, al = halves(a)
    bh, bl = halves(b)
    return mm(ah, bh, dims) + (mm(ah, bl, dims) + mm(al, bh, dims))


def mixed_input(x, carried, mix):
    features = x[...].astype(F32)
    row = lax.broadcasted_iota(jnp.int32, features.shape, 0)
    previous = jnp.where(row == 0, carried[...].astype(F32), pltpu.roll(features, 1, 0))
    return features + mix[...] * (previous - features)


def adapter_kernel(x, carried, mix, down, pre):
    pre[...] = mm3(mixed_input(x, carried, mix), down[...])


def decay_kernel(head, count, *refs):
    pres = refs[:count]
    base, up, r, k, v, dy, sums, lora, lora_t, w_out, eb, ee, end, st, msg = refs[count:]
    rows = r.shape[0]
    total = pres[0][...]
    for pre in pres[1:]:
        total = total + pre[...]
    mid = jnp.tanh(total)
    lora[...] = mid
    lora_t[...] = mid.T.astype(BF16)
    w = -jnp.exp(base[...] + mm3(mid, up[...]))
    w_out[...] = w
    hi, lo = halves(w)
    args = mm(sums[...], jnp.concatenate([hi, lo], 0))
    before, after = args[:rows], args[rows:]
    final = before[rows - 1 :] + w[rows - 1 :]
    end[...] = final
    from_start, to_end = jnp.exp(before), jnp.exp(after)
    eb[...] = from_start
    ee[...] = to_end
    kf = (k[...].astype(F32) * to_end).astype(BF16)
    rb = (r[...].astype(F32) * from_start).astype(BF16)
    for p in range(r.shape[1] // PAIR):
        cols = slice(p * PAIR, (p + 1) * PAIR)
        state = fold(mm(v[:, cols], kf[:, cols], TN), head)
        st[:, cols] = state
        msg[:head, cols] = state.astype(BF16)
        msg[head : 2 * head, cols] = fold(mm(dy[:, cols], rb[:, cols], TN), head).astype(BF16)
    msg[2 * head : 2 * head + 8], msg[2 * head + 8 :] = split_rows(final)


def pair_kernel(head, ring, place, own, far, *outs):
    late = place[0] == 1
    dec_own, dec_far = joined(own, 2 * head), joined(far, 2 * head)
    eo, ef = jnp.exp(dec_own), jnp.exp(dec_far)
    st_own, st_far = own[:head].astype(F32), far[:head].astype(F32)
    gt_own, gt_far = own[head : 2 * head].astype(F32), far[head : 2 * head].astype(F32)
    state = jnp.where(late, st_own + eo * st_far, st_far + ef * st_own).astype(BF16)
    grad = jnp.where(late, gt_far + ef * gt_own, gt_own + eo * gt_far).astype(BF16)
    hi, lo = split_rows(dec_own + dec_far)
    for d in range(1, ring):
        out = outs[d - 1]
        ahead = place[1] + d < ring

        @pl.when(ahead)
        def _():
            out[:head] = state

        @pl.when(jnp.logical_not(ahead))
        def _():
            out[:head] = grad

        out[head : head + 8] = hi
        out[head + 8 :] = lo


def inner_kernel(head, r, k, v, dy, w, u, levels, gr_out, gk_out, gv_out, self_out, du_out):
    rows, width = r.shape
    row = lax.broadcasted_iota(jnp.int32, (rows, PAIR), 0)
    row2 = lax.broadcasted_iota(jnp.int32, (rows, 2 * rows), 0)
    col2 = lax.broadcasted_iota(jnp.int32, (rows, 2 * rows), 1)
    apart = row2 ^ (col2 & (rows - 1))
    lane_r = lax.broadcasted_iota(jnp.int32, (2 * PAIR, PAIR), 0) & (PAIR - 1)
    lane_c = lax.broadcasted_iota(jnp.int32, (2 * PAIR, PAIR), 1)
    ones = jnp.where((lane_r < head) == (lane_c < head), 1.0, 0.0).astype(BF16)
    hi, lo = halves(w[...])
    decay = jnp.exp(mm(levels[...], jnp.concatenate([hi, lo], 0)))
    for p in range(width // PAIR):
        cols = slice(p * PAIR, (p + 1) * PAIR)
        rf, kf = r[:, cols].astype(F32), k[:, cols].astype(F32)
        vf, dyf = v[:, cols].astype(F32), dy[:, cols].astype(F32)
        dydy = block_rows(dy[:, cols], head)
        pairs = mm(dy[:, cols], block_rows(v[:, cols], head), NT)
        pairs_t = mm(v[:, cols], dydy, NT)
        gr = jnp.zeros((rows, PAIR), F32)
        gk = jnp.zeros((rows, PAIR), F32)
        scores_t = jnp.zeros((rows, 2 * rows), F32)
        m, level = 1, 0
        while m < rows:
            d = decay[level * rows : (level + 1) * rows, cols]
            right = (row & m) != 0
            rd = jnp.where(right, rf * d, 0.0).astype(BF16)
            kd = jnp.where(right, 0.0, kf * d).astype(BF16)
            kk, rr = block_rows(kd, head), block_rows(rd, head)
            near = apart < 2 * m
            a = mm(kd, rr, NT)
            scores_t = scores_t + jnp.where(near, a, 0.0)
            here = jnp.where(near, pairs, 0.0).astype(BF16)
            here_t = jnp.where(near, pairs_t, 0.0).astype(BF16)
            gr = gr + jnp.where(right, d * mm(here, kk), 0.0)
            gk = gk + jnp.where(right, 0.0, d * mm(here_t, rr))
            m, level = 2 * m, level + 1
        sh, sl = halves(dyf * vf)
        own = mm(jnp.concatenate([sh, sl], 1), ones)
        bh, bl = halves(rf * u[:, cols] * kf)
        bonus = mm(jnp.concatenate([bh, bl], 1), ones)
        gr_out[:, cols] = gr
        gk_out[:, cols] = gk
        gv_out[:, cols] = mm(scores_t.astype(BF16), dydy) + bonus * dyf
        self_out[:, cols] = own
        du_out[:, cols] = jnp.sum(rf * kf * own, 0, keepdims=True)


def outer_kernel(
    head, ring, place, r, k, v, dy, eb, ee, u, gr0, gk0, gv0, own, st, end, far, *refs
):
    msgs = refs[: ring - 1]
    proj, r_gr, k_gk, at_end = refs[ring - 1 :]
    width = r.shape[1]
    late, z = place[0] == 1, place[1]
    zero = jnp.zeros((head, width), F32)
    nothing = jnp.zeros((1, width), F32)
    state, grad, past, future = zero, zero, nothing, nothing
    for d in range(1, ring):
        msg = msgs[d - 1]
        live = d <= z
        state = state + jnp.where(live, jnp.exp(past) * msg[:head].astype(F32), 0.0)
        past = past + jnp.where(live, joined(msg, head), 0.0)
    for d in range(ring - 1, 0, -1):
        msg = msgs[d - 1]
        live = d > z
        grad = grad + jnp.where(live, jnp.exp(future) * msg[:head].astype(F32), 0.0)
        future = future + jnp.where(live, joined(msg, head), 0.0)
    ef = jnp.exp(joined(far, 2 * head))
    st_in = jnp.where(late, far[:head].astype(F32) + ef * state, state)
    gt_in = jnp.where(late, grad, far[head : 2 * head].astype(F32) + ef * grad)
    at_end[...] = jnp.sum(gt_in * (jnp.exp(end[...]) * st_in + st[...]), 0, keepdims=True)
    sb, gb = st_in.astype(BF16), gt_in.astype(BF16)
    for p in range(width // PAIR):
        cols = slice(p * PAIR, (p + 1) * PAIR)
        grads = block_rows(gb[:, cols], head)
        rf, kf = r[:, cols].astype(F32), k[:, cols].astype(F32)
        after = ee[:, cols]
        gr = gr0[:, cols] + eb[:, cols] * mm(dy[:, cols], block_rows(sb[:, cols], head))
        gk = gk0[:, cols] + after * mm(v[:, cols], grads)
        gv = gv0[:, cols] + mm((kf * after).astype(BF16), grads, NT)
        s = own[:, cols] * u[:, cols]
        proj[0, :, cols] = (gr + kf * s).astype(BF16)
        proj[1, :, cols] = (gk + rf * s).astype(BF16)
        proj[2, :, cols] = gv.astype(BF16)
        r_gr[:, cols] = rf * gr
        k_gk[:, cols] = kf * gk


def decay_grad_kernel(w, r_gr, k_gk, at_end, up, lora_t, cums, up_grad, base_grad, mid_grad):
    ah, al = halves(r_gr[...])
    bh, bl = halves(k_gk[...])
    gp = (mm(cums[...], jnp.concatenate([ah, al, bh, bl], 0)) + at_end[...]) * w[...]
    gpb = gp.astype(BF16)
    up_grad[...] = mm(lora_t[...], gpb)
    base_grad[...] = jnp.sum(gp, 0, keepdims=True)
    mid_grad[...] = mm(gpb, up[...].astype(BF16), NT)


def middle_kernel(count, place, x, carried, mix, down, lora, *refs):
    mids, sides, (keep, send, grad_in) = refs[:count], refs[count:-3], refs[-3:]
    total = mids[0][...]
    for part in mids[1:]:
        total = total + part[...]
    mid = total * (1.0 - lora[...] * lora[...])
    grad_in[...] = mm3(mid, down[...], NT)
    down_grad = mm3(mid.T, mixed_input(x, carried, mix))
    rank, half = mid.shape[1], x.shape[1] // 2
    wide = (8, half)
    late = place[0] == 1

    def choose(low, high, at, size):
        keep[at : at + size] = jnp.where(late, high, low).astype(BF16)
        send[at : at + size] = jnp.where(late, low, high).astype(BF16)

    up_low, up_high, base_low, base_high, du_low, du_high = [ref[...] for ref in sides]
    choose(up_low, up_high, 0, rank)
    choose(down_grad[:, :half], down_grad[:, half:], rank, rank)
    for at, low, high in ((0, base_low, base_high), (8, du_low, du_high)):
        choose(jnp.broadcast_to(low, wide), jnp.broadcast_to(high, wide), 2 * rank + at, 8)


def finish_kernel(rank, place, mine, theirs, up, down, base, du):
    late = place[0] == 1
    half = mine.shape[1]
    a, b = mine[...].astype(F32), theirs[...].astype(F32)
    for at, value in ((0, jnp.where(late, b, a)), (half, jnp.where(late, a, b))):
        here = slice(at, at + half)
        up[:, here] = value[:rank]
        down[here] = value[rank : 2 * rank].T
        base[:, here] = value[2 * rank : 2 * rank + 1]
        du[:, here] = value[2 * rank + 8 : 2 * rank + 9]


def project_kernel(count, ring, place, *refs):
    lows, highs = refs[:count], refs[count : 2 * count]
    w_own, w_far0, w_far1, mix = refs[2 * count : 2 * count + 4]
    rest, (own, prior, low_tail, high_tail) = refs[2 * count + 4 : -4], refs[-4:]
    final = count == 1
    done, outs = (rest[: ring - 1], rest[ring - 1 :]) if final else ((), rest)
    rows, width = lows[0].shape[1:]
    side, m = pl.program_id(0), pl.program_id(1)
    mains = count * rows

    @pl.when(m == 0)
    def _():
        for ref in (own, prior, low_tail, high_tail):
            ref[...] = jnp.zeros_like(ref)

    def product(pieces):
        tails = [high[0, rows:] for high in highs]
        low = jnp.concatenate([low[0] for low in lows] + tails, 0)
        high = jnp.concatenate([high[0, :rows] for high in highs] + tails, 0)
        lane = lax.broadcasted_iota(jnp.int32, mix.shape, 1)
        weight = jnp.sum(jnp.where(lane == m, mix[...], 0.0), 1, keepdims=True)
        at = 0
        for piece in pieces:
            size = piece.shape[1]
            here = slice(at, at + size)
            a = mm(piece[0, :, :width], low, NT)
            b = mm(piece[0, :, width:], high, NT)
            term = a[:, :mains] + b[:, :mains]
            later = weight[here] * term
            own[here] += term - later
            prior[here] += later
            low_tail[here] += weight[here] * a[:, mains:]
            high_tail[here] += weight[here] * b[:, mains:]
            at += size

    @pl.when(side == 0)
    def _():
        product([w_own])

    @pl.when(side == 1)
    def _():
        product([w_far0, w_far1])

    @pl.when(m == 2)
    def _():
        last = lax.broadcasted_iota(jnp.int32, (own.shape[0], rows), 1) == rows - 1
        for q in range(count):
            here = slice(q * rows, (q + 1) * rows)
            tail = low_tail[:, 16 * q : 16 * q + 1] + high_tail[:, 16 * q + 1 : 16 * q + 2]
            moved = jnp.where(last, tail, pltpu.roll(prior[:, here], rows - 1, 1))
            value = (own[:, here] + moved).T.astype(BF16)
            if not final:
                outs[q][...] = value
        if final:
            for d in range(ring):
                wanted = lax.rem(place[1] - place[2] - d + 2 * ring, ring)
                for q in range(ring):

                    @pl.when(wanted == q)
                    def _():
                        outs[d][...] = value if q == ring - 1 else done[q][...]


def per_device(
    layer_input, receptance, key_act, value_act, attention_result_sensitivity, time_first,
    decay_exponent_base, decay_shift_mix, mix_rkv, decay_adapter_down, decay_adapter_up, proj_weights,
):
    rows, cols = layer_input.shape
    heads, head = time_first.shape
    rank = decay_adapter_down.shape[1]
    n_seq, n_head = lax.axis_size("seq"), lax.axis_size("head")
    inner = n_seq // n_head
    ring = n_seq // inner
    pairs = cols // PAIR
    parts = 2
    part_cols = cols // parts
    block = min(part_cols, 2 * PAIR)
    seq, hd = lax.axis_index("seq"), lax.axis_index("head")
    place = jnp.stack([lax.rem(seq, inner), seq // inner, hd]).astype(jnp.int32)
    r, k, v, dy = receptance, key_act, value_act, attention_result_sensitivity
    params = pltpu.CompilerParams(vmem_limit_bytes=VMEM)

    def shape(s, t=F32):
        return jax.ShapeDtypeStruct(s, t)

    def work(us):
        return pl.CostEstimate(flops=0, transcendentals=0, bytes_accessed=int(us * 3.5e6))

    def shift(a, distance):
        return lax.ppermute(
            a, "seq", [(i - distance, i) for i in range(n_seq) if 0 <= i - distance < n_seq]
        )

    def around(a, step):
        return lax.ppermute(a, "seq", [(i, (i + inner * step) % n_seq) for i in range(n_seq)])

    def partner(a):
        return lax.ppermute(a, "seq", [(i, i ^ 1) for i in range(n_seq)])

    def head_shift(a, d):
        return lax.ppermute(a, "head", [(i, (i + d) % n_head) for i in range(n_head)])

    def head_parts(a):
        return [a] + [head_shift(a, d) for d in range(1, n_head)]

    weight_rows = proj_weights.shape[1]
    cut = max(weight_rows * 3 // 8, 16)
    mix_here = lax.dynamic_slice_in_dim(mix_rkv, place[1] * cols, cols, 1).T
    carried, u, place, mix_here, *pieces = lax.optimization_barrier(
        (
            shift(layer_input[rows - 1 :], 1), time_first.reshape(1, cols), place, mix_here,
            proj_weights[:, :cut], proj_weights[:, cut:],
        )
    )
    shift_mix = decay_shift_mix.reshape(1, cols)
    pre = pl.pallas_call(
        adapter_kernel,
        out_shape=shape((rows, rank)),
        compiler_params=params,
        cost_estimate=work(1.5),
        name="adapter_input",
    )(layer_input, carried, shift_mix, decay_adapter_down)
    pres = head_parts(pre)

    sums = jnp.asarray(sum_matrix(rows), BF16)
    levels = jnp.asarray(level_matrix(rows), BF16)
    cums = jnp.asarray(cumulative_matrix(rows), BF16)
    far_rows = 2 * head + 16

    lora, lora_t, w, eb, ee, end, st, msg = pl.pallas_call(
        lambda *refs: decay_kernel(head, n_head, *refs),
        out_shape=[
            shape((rows, rank)), shape((rank, rows), BF16), *[shape((rows, cols))] * 3, shape((1, cols)),
            shape((head, cols)), shape((far_rows, cols), BF16),
        ],
        compiler_params=params,
        cost_estimate=work(3),
        name="decay_and_states",
    )(*pres, decay_exponent_base.reshape(1, cols), decay_adapter_up, r, k, v, dy, sums)

    smem = pl.BlockSpec(memory_space=pltpu.SMEM)
    vmem = pl.BlockSpec(memory_space=pltpu.VMEM)
    def col_block(n, width=block, offset=0):
        return pl.BlockSpec((n, width), lambda p, *_: (0, p + offset))

    def whole(s):
        return pl.BlockSpec(s, lambda p, *_: (0,) * len(s))

    steps = part_cols // block
    here = col_block(rows)

    def inside(part):
        at = lambda n: col_block(n, block, part * steps)
        return pl.pallas_call(
            lambda *refs: inner_kernel(head, *refs),
            grid=(steps,),
            in_specs=[at(rows)] * 5 + [at(1), whole(levels.shape)],
            out_specs=[here] * 4 + [col_block(1)],
            out_shape=[shape((rows, part_cols))] * 4 + [shape((1, part_cols))],
            compiler_params=params,
            cost_estimate=work(4),
            name="inside_chunk",
        )(r, k, v, dy, w, u, levels)

    inner_parts = [inside(part) for part in range(parts)]
    far, pieces[0], inner_parts[0] = lax.optimization_barrier(
        (partner(msg), pieces[0], inner_parts[0])
    )
    far0 = partner(pieces[0])
    out_msgs = pl.pallas_call(
        lambda *refs: pair_kernel(head, ring, *refs),
        in_specs=[smem, vmem, vmem],
        out_shape=[shape((head + 16, cols), BF16)] * (ring - 1),
        compiler_params=params,
        cost_estimate=work(1.5),
        name="pair_states",
    )(place, msg, far)
    msgs = [around(m, d + 1) for d, m in enumerate(out_msgs)]

    outer = []
    for part in range(parts):
        at = lambda n: col_block(n, block, part * steps)
        outer.append(
            pl.pallas_call(
                lambda *refs: outer_kernel(head, ring, *refs),
                grid=(steps,),
                in_specs=[smem] + [at(rows)] * 6 + [at(1)] + [here] * 4
                + [at(head), at(1), at(far_rows)] + [at(head + 16)] * (ring - 1),
                out_specs=[pl.BlockSpec((3, rows, block), lambda p: (0, 0, p)), here, here, col_block(1)],
                out_shape=[
                    shape((3, rows, part_cols), BF16), shape((rows, part_cols)),
                    shape((rows, part_cols)), shape((1, part_cols)),
                ],
                compiler_params=params,
                cost_estimate=work(3),
                name="across_chunks",
            )(place, r, k, v, dy, eb, ee, u, *inner_parts[part][:4], st, end, far, *msgs)
        )
    projs = [o[0] for o in outer]

    first, far0 = lax.optimization_barrier((jnp.concatenate([p[:, :1] for p in projs], 1), far0))
    after, pieces[1] = lax.optimization_barrier((shift(first, -1), pieces[1]))
    far1 = partner(pieces[1])
    pad = jnp.zeros((3, 16 - parts, part_cols), BF16)
    lows, highs = [projs[0]], [jnp.concatenate([projs[1], after, pad], 1)]

    ups, bases, mid_parts = [], [], []
    for part in range(parts):
        at = lambda n: pl.BlockSpec((n, part_cols), lambda p: (0, part))
        up_grad, base_grad, mid_grad = pl.pallas_call(
            decay_grad_kernel,
            grid=(1,),
            in_specs=[at(rows), *[whole((rows, part_cols))] * 2, whole((1, part_cols)), at(rank)]
            + [whole((rank, rows)), whole(cums.shape)],
            out_specs=[whole((rank, part_cols)), whole((1, part_cols)), whole((rows, rank))],
            out_shape=[shape((rank, part_cols)), shape((1, part_cols)), shape((rows, rank))],
            compiler_params=params,
            cost_estimate=work(2),
            name="decay_gradient",
        )(w, *outer[part][1:], decay_adapter_up, lora_t, cums)
        ups.append(up_grad)
        bases.append(base_grad)
        mid_parts.append(mid_grad)
    mid_grad = sum(mid_parts)

    mids = head_parts(mid_grad)
    dus = [part[4] for part in inner_parts]
    keep, send, grad_in = pl.pallas_call(
        lambda *refs: middle_kernel(n_head, *refs),
        in_specs=[smem] + [vmem] * (5 + n_head + 3 * parts),
        out_shape=[shape((2 * rank + 16, part_cols), BF16)] * 2 + [shape((rows, cols))],
        compiler_params=params,
        cost_estimate=work(3),
        name="adapter_grads",
    )(
        place, layer_input, carried, shift_mix, decay_adapter_down, lora, *mids, *ups, *bases, *dus
    )

    for step in range(ring - 1):
        low, high = around(lows[-1], 1), around(highs[-1], 1)
        if step == 0:
            low, keep, send = lax.optimization_barrier((low, keep, send))
        lows.append(low)
        highs.append(high)

    def add(a, b):
        return (a.astype(F32) + b.astype(F32)).astype(BF16)

    token_sums = add(keep, partner(send))
    b = 1
    while b < ring:
        route = [(i, ((i // inner) ^ b) * inner + i % inner) for i in range(n_seq)]
        token_sums = add(token_sums, lax.ppermute(token_sums, "seq", route))
        b *= 2
    up_grad, down_grad, base_grad, du = pl.pallas_call(
        lambda *refs: finish_kernel(rank, *refs),
        in_specs=[smem, vmem, vmem],
        out_shape=[shape((rank, cols)), shape((cols, rank)), shape((1, cols)), shape((1, cols))],
        compiler_params=params,
        cost_estimate=work(2),
        name="token_sums",
    )(place, token_sums, partner(token_sums))

    grad_next = jnp.concatenate([grad_in[1:], shift(grad_in[:1], -1)], 0)
    adapter_term = (1.0 - decay_shift_mix) * grad_in + decay_shift_mix * grad_next

    def column(i, place):
        return jnp.where(i == 0, place[0], 1 - place[0])

    def project(low, high, done, n_out):
        count = len(low)
        out_block = pl.BlockSpec((rows, weight_rows), lambda i, m, place: (0, column(i, place)))
        part_of = lambda a: pl.BlockSpec((1,) + a.shape[1:], lambda i, m, place: (m, 0, 0))
        far_of = lambda a: pl.BlockSpec(
            (1,) + a.shape[1:], lambda i, m, place: (jnp.where(i == 0, 0, m), 0, 0)
        )
        sums_of = lambda n: pltpu.VMEM((weight_rows, n), F32)
        return pl.pallas_call(
            lambda *refs: project_kernel(count, ring, *refs),
            grid_spec=pltpu.PrefetchScalarGridSpec(
                num_scalar_prefetch=1,
                grid=(inner, 3),
                in_specs=[part_of(a) for a in low + high]
                + [
                    pl.BlockSpec(
                        (1, weight_rows, cols), lambda i, m, place: (jnp.where(i == 0, m, 2), 0, 0)
                    ),
                    far_of(far0),
                    far_of(far1),
                    pl.BlockSpec((weight_rows, 3), lambda i, m, place: (column(i, place), 0)),
                ]
                + [out_block] * len(done),
                out_specs=[out_block] * n_out,
                scratch_shapes=[
                    sums_of(count * rows), sums_of(count * rows), sums_of(16 * count), sums_of(16 * count),
                ],
            ),
            out_shape=[shape((rows, cols), BF16)] * n_out,
            compiler_params=params,
            cost_estimate=work(5),
            name="projections",
        )(place, *low, *high, proj_weights, far0, far1, mix_here, *done)

    done = project(lows[:-1], highs[:-1], [], ring - 1)
    sends = project(lows[-1:], highs[-1:], done, ring)
    total = sends[0].astype(F32)
    for d in range(1, n_head):
        total = total + head_shift(sends[d], d).astype(F32)
    swap = [
        (h * n_seq + z * inner + x, z * n_seq + h * inner + x)
        for h in range(n_head) for z in range(ring) for x in range(inner)
    ]
    summed = lax.ppermute(total.astype(BF16), ("head", "seq"), swap)
    result = (summed.astype(F32) + adapter_term).astype(BF16)
    return (result, down_grad, up_grad, base_grad.reshape(cols), du.reshape(heads, head))


def solution(mesh):
    return jax.shard_map(
        per_device,
        mesh=mesh,
        in_specs=(
            P("seq", "head"), P("seq", "head"), P("seq", "head"), P("seq", "head"), P("seq", "head"),
            P("head", None), P("head"), P("head"), P(), P("head", None), P(None, "head"),
            P(None, "seq", "head"),
        ),
        out_specs=(P("seq", "head"), P("head", None), P(None, "head"), P("head"), P("head", None)),
        check_vma=False,
    )
```

time: 277 us -> 198 us (0.71)
  blocking collectives: 37.3 us -> 0 us
  waiting for transfers between devices: 113 us -> 83.5 us
  Pallas kernels: 30 us -> 55.2 us
  between operations: 14.7 us -> 1.06 us
  starting transfers between devices: 48.2 us -> 37.4 us
  local copies, waits for them, and re-layouts: 19.3 us -> 13.9 us
  matrix products: 4.13 us -> 0 us
    psum x1 -> x0, blocking collectives: 37.3 us -> none  [per_device(): up_grad, base_grad, du = lax.psum((up_grad, base_grad, du), 'seq')]
    psum x1 -> x0, waiting for transfers between devices: 31.7 us -> none  [per_device(): lax.psum(jnp.dot(decay_input.T, mid_grad, precision=EXACT), 'seq')]
    pallas_call x3 -> x12, Pallas kernels: 28.9 us -> 51.7 us  [the longest x2 21.2 us: project(): pl.pallas_call(lambda *refs: project_kernel(count, ring, *refs), grid_spe...]
    ppermute x8 -> x3, starting transfers between devices: 24.2 us -> 5.96 us  [shift(): lax.ppermute(a, 'seq', [(i - distance, i) for i in range(n_seq) if 0 <= i...]
    ppermute x17 -> x25, starting transfers between devices: 15.3 us -> 25.7 us  [the longest x9 11.2 us: around(): lax.ppermute(a, 'seq', [(i, (i + inner * step) % n_seq) for i in range(n_...]
    ppermute x8 -> x3, waiting for transfers between devices: 13.9 us -> 4.23 us  [shift(): lax.ppermute(a, 'seq', [(i - distance, i) for i in range(n_seq) if 0 <= i...]
    unnamed x76 -> x57, local copies, waits for them, and re-layouts: 14.3 us -> 6.59 us
    ppermute x17 -> x25, waiting for transfers between devices: 67 us -> 73.8 us  [the longest x5 29.2 us: partner(): return lax.ppermute(a, 'seq', [(i, i ^ 1) for i in range(n_seq)])]
  transfers between devices with their start and end apart: 27 -> 29, of which waited for: 19 -> 14; matrix products, arithmetic and copies ran while one was open for 5% -> 7% of each run, Pallas kernels for 6% -> 25%
where the time goes in v2:
time: 198 us; the launch traced here: 197 us
  waiting for transfers between devices  83.5 us (42%)
  Pallas kernels  55.2 us (28%)
  starting transfers between devices  37.4 us (19%)
  local copies, waits for them, and re-layouts  13.9 us (7%)
  other arithmetic  6.1 us (3%)
    ppermute x5, waiting for transfers between devices, partner(): return lax.ppermute(a, 'seq', [(i, i ^ 1) for i in range(n_seq)])  29.2 us
    pallas_call x2, Pallas kernels, project(): pl.pallas_call(lambda *refs: project_kernel(count, ring, *refs), grid_spe...  21.2 us
    ppermute x2, waiting for transfers between devices, per_device(): token_sums = add(token_sums, lax.ppermute(token_sums, 'seq', route))  21.2 us
    ppermute x9, waiting for transfers between devices, head_shift(): lax.ppermute(a, 'head', [(i, (i + d) % n_head) for i in range(n_head)])  19.2 us
    ppermute x9, starting transfers between devices, around(): lax.ppermute(a, 'seq', [(i, (i + inner * step) % n_seq) for i in range(n_...  11.2 us
    pallas_call x2, Pallas kernels, inside(): pl.pallas_call(lambda *refs: inner_kernel(head, *refs), grid=(steps,), in...  10.2 us
    ppermute x5, starting transfers between devices, partner(): return lax.ppermute(a, 'seq', [(i, i ^ 1) for i in range(n_seq)])  7.55 us
    unnamed x57, local copies, waits for them, and re-layouts  6.59 us
  transfers between devices with their start and end apart: 29, of which 14 were waited for; matrix products, arithmetic and copies ran while one was open for 7% of the time, Pallas kernels for 25%

profile of v2, /device:TPU:4, one launch (start us, length us, event | category | flops | bytes accessed | tf_op | source)
XLA Modules:
  0.0 197.1 jit_solution(16132475888725678703)
XLA Ops:
  1.4 3.4 %collective-permute-start = (bf16[1,1024]{1,0:T(2,128)(2,1)S(1)}, bf16[1,1024]{1,0:T(2,128)(2,1)S(1)}, u32[]{:S(2)}, u32[]{:S(2)}) collective-permute-start(bf16[1,1024]{1,0:T(2,128)(2,1)S(1)} %slice.21), channel_id=1, source_target_pairs={{0,1},{1,2},{2,3},{3,4},{4,5},{5,6},{6,7},{8,9},{9,10},{10,11},{11... | collective-permute-start | bytes 6152 | tf_op jit(solution)/shard_map/ppermute | solution.py:375
  18.9 3.5 %decay_and_states.1 = (f32[128,128]{1,0:T(8,128)}, bf16[128,128]{1,0:T(8,128)(2,1)}, f32[128,1024]{1,0:T(8,128)}, f32[128,1024]{1,0:T(8,128)}, f32[128,1024]{1,0...) custom-call(f32[128,128]{1,0:T(8,128)} %adapter_input.1.refs_0_, ...), custom_call_target="tpu_custom_call" | custom-call | bytes 10500000 | tf_op jit(solution)/shard_map/decay_and_states/pallas_call | solution.py:415
  24.0 5.1 %inside_chunk.2 = (f32[128,512]{1,0:T(8,128)}, f32[128,512]{1,0:T(8,128)}, f32[128,512]{1,0:T(8,128)}, f32[128,512]{1,0:T(8,128)}, f32[1,512]{1,0:T(1,128)}) custom-call(bf16[128,1024]{1,0:T(8,128)(2,1)} %refs_1_.8, bf16[128,1024]{1,0:T(8,128)(2,1)} %refs_2_.7, bf16[128,1024]{1,0:T(8,128)(2,1)} %refs_3_.8, bf16[128,1024]{1,0:T(8,128)(2,1)} %refs_4_.4, ...), custom_call_target="tpu_custom_call" | custom-call | bytes 14000000 | tf_op jit(solution)/shard_map/inside_chunk/pallas_call | solution.py:439
  29.1 3.0 %collective-permute-done.4.refs_2_.refs_14_ = bf16[144,1024]{1,0:T(8,128)(2,1)S(1)} collective-permute-done((bf16[144,1024]{1,0:T(8,128)(2,1)}, bf16[144,1024]{1,0:T(8,128)(2,1)S(1)}, u32[]{:S(2)}, u32[]{:S(2)}) %collective-permute-start.4) | collective-permute-done | bytes 294944 | tf_op jit(solution)/shard_map/ppermute | solution.py:383
  41.4 5.1 %inside_chunk.3 = (f32[128,512]{1,0:T(8,128)}, f32[128,512]{1,0:T(8,128)}, f32[128,512]{1,0:T(8,128)}, f32[128,512]{1,0:T(8,128)}, f32[1,512]{1,0:T(1,128)}) custom-call(bf16[128,1024]{1,0:T(8,128)(2,1)} %refs_1_.8, bf16[128,1024]{1,0:T(8,128)(2,1)} %refs_2_.7, bf16[128,1024]{1,0:T(8,128)(2,1)} %refs_3_.8, bf16[128,1024]{1,0:T(8,128)(2,1)} %refs_4_.4, ...), custom_call_target="tpu_custom_call" | custom-call | bytes 14000000 | tf_op jit(solution)/shard_map/inside_chunk/pallas_call | solution.py:439
  46.5 4.2 %collective-permute-done.6.refs_16_ = bf16[80,1024]{1,0:T(8,128)(2,1)S(1)} collective-permute-done((bf16[80,1024]{1,0:T(8,128)(2,1)}, bf16[80,1024]{1,0:T(8,128)(2,1)S(1)}, u32[]{:S(2)}, u32[]{:S(2)}) %collective-permute-start.6) | collective-permute-done | bytes 163872 | tf_op jit(solution)/shard_map/ppermute | solution.py:380
  51.4 2.9 %across_chunks.3 = (bf16[3,128,512]{2,1,0:T(8,128)(2,1)}, f32[128,512]{1,0:T(8,128)}, f32[128,512]{1,0:T(8,128)}, f32[1,512]{1,0:T(1,128)}) custom-call(s32[3]{0:T(128)} %pad_add_fusion.refs_0_, bf16[128,1024]{1,0:T(8,128)(2,1)} %refs_1_.8, bf16[128,1024]{1,0:T(8,128)(2,1)} %refs_2_.7, bf16[128,1024]{1,0:T(8,128)(2,1)} %refs_3_.8, ...), custom_call_target="tpu_custom_call" | custom-call | bytes 10500000 | tf_op jit(solution)/shard_map/across_chunks/pallas_call | solution.py:469
  55.0 2.9 %across_chunks.2 = (bf16[3,128,512]{2,1,0:T(8,128)(2,1)}, f32[128,512]{1,0:T(8,128)}, f32[128,512]{1,0:T(8,128)}, f32[1,512]{1,0:T(1,128)}) custom-call(s32[3]{0:T(128)} %pad_add_fusion.refs_0_, bf16[128,1024]{1,0:T(8,128)(2,1)} %refs_1_.8, bf16[128,1024]{1,0:T(8,128)(2,1)} %refs_2_.7, bf16[128,1024]{1,0:T(8,128)(2,1)} %refs_3_.8, ...), custom_call_target="tpu_custom_call" | custom-call | bytes 10500000 | tf_op jit(solution)/shard_map/across_chunks/pallas_call | solution.py:469
  61.1 4.2 %collective-permute-done.15 = bf16[3,2,512]{2,1,0:T(2,128)(2,1)S(1)} collective-permute-done((bf16[3,2,512]{2,1,0:T(2,128)(2,1)S(1)}, bf16[3,2,512]{2,1,0:T(2,128)(2,1)S(1)}, u32[]{:S(2)}, u32[]{:S(2)}) %collective-permute-start.15) | collective-permute-done | bytes 6176 | tf_op jit(solution)/shard_map/ppermute | solution.py:375
  65.3 2.5 %collective-permute-start.19 = (bf16[3,320,1024]{2,1,0:T(8,128)(2,1)S(1)}, bf16[3,320,1024]{2,1,0:T(8,128)(2,1)S(1)}, u32[]{:S(2)}, u32[]{:S(2)}) collective-permute-start(bf16[3,320,1024]{2,1,0:T(8,128)(2,1)S(1)} %slice.23), channel_id=1, source_target_pairs={{0,1},{1,0},{2,3},{3,2},{4,5},{5,4},{6,7},{7,6},{8,9},{9,8},{10,11... | collective-permute-start | bytes 5898248 | tf_op jit(solution)/shard_map/ppermute | solution.py:383
  67.9 2.2 %collective-permute-start.8 = (bf16[3,128,512]{2,1,0:T(8,128)(2,1)}, bf16[3,128,512]{2,1,0:T(8,128)(2,1)S(1)}, u32[]{:S(2)}, u32[]{:S(2)}) collective-permute-start(bf16[3,128,512]{2,1,0:T(8,128)(2,1)} %get-tuple-element.97.refs_1_), channel_id=1, source_target_pairs={{0,2},{1,3},{2,4},{3,5},{4,6},{5,7},{6,0},{7,1},{8,10},{9,11},{10,... | collective-permute-start | bytes 1179656 | tf_op jit(solution)/shard_map/ppermute | solution.py:380
  71.2 2.4 %decay_gradient.3 = (f32[128,512]{1,0:T(8,128)}, f32[1,512]{1,0:T(1,128)}, f32[128,128]{1,0:T(8,128)}) custom-call(f32[128,1024]{1,0:T(8,128)} %get-tuple-element.81.refs_4_.w, f32[128,512]{1,0:T(8,128)} %get-tuple-element.108.r_gr, f32[128,512]{1,0:T(8,128)} %get-tuple-element.109.k_gk, f32[1,512]{1,0:T(1,128)} %get-tuple-element.110.at_end, ...), custom_call_target="tpu_custom_call" | custom-call | bytes 7000000 | tf_op jit(solution)/shard_map/decay_gradient/pallas_call | solution.py:495
  73.6 2.4 %decay_gradient.2 = (f32[128,512]{1,0:T(8,128)}, f32[1,512]{1,0:T(1,128)}, f32[128,128]{1,0:T(8,128)}) custom-call(f32[128,1024]{1,0:T(8,128)} %get-tuple-element.81.refs_4_.w, f32[128,512]{1,0:T(8,128)} %get-tuple-element.99.r_gr, f32[128,512]{1,0:T(8,128)} %get-tuple-element.100.k_gk, f32[1,512]{1,0:T(1,128)} %get-tuple-element.101.at_end, ...), custom_call_target="tpu_custom_call" | custom-call | bytes 7000000 | tf_op jit(solution)/shard_map/decay_gradient/pallas_call | solution.py:495
  77.6 3.7 %collective-permute-done.10.refs_8_ = f32[128,128]{1,0:T(8,128)S(1)} collective-permute-done((f32[128,128]{1,0:T(8,128)S(1)}, f32[128,128]{1,0:T(8,128)S(1)}, u32[]{:S(2)}, u32[]{:S(2)}) %collective-permute-start.10) | collective-permute-done | bytes 65568 | tf_op jit(solution)/shard_map/ppermute | solution.py:386
  81.3 3.7 %collective-permute-done.9.refs_7_ = f32[128,128]{1,0:T(8,128)S(1)} collective-permute-done((f32[128,128]{1,0:T(8,128)S(1)}, f32[128,128]{1,0:T(8,128)S(1)}, u32[]{:S(2)}, u32[]{:S(2)}) %collective-permute-start.9) | collective-permute-done | bytes 65568 | tf_op jit(solution)/shard_map/ppermute | solution.py:386
  85.6 3.0 %adapter_grads.1 = (bf16[272,512]{1,0:T(8,128)(2,1)}, bf16[272,512]{1,0:T(8,128)(2,1)}, f32[128,1024]{1,0:T(8,128)}) custom-call(s32[3]{0:T(128)} %pad_add_fusion.refs_0_, bf16[128,1024]{1,0:T(8,128)(2,1)} %refs_1_.9, bf16[1,1024]{1,0:T(2,128)(2,1)} %copy-done.26, f32[1,1024]{1,0:T(1,128)} %bitcast.10, f32[1024,128]{1,0:T(8,128)} %refs_4_.5, ...), custom_call_target="tpu_custom_call" | custom-call | bytes 10500000 | tf_op jit(solution)/shard_map/adapter_grads/pallas_call | solution.py:513
  90.6 25.1 %collective-permute-done.25 = bf16[272,512]{1,0:T(8,128)(2,1)S(1)} collective-permute-done((bf16[272,512]{1,0:T(8,128)(2,1)}, bf16[272,512]{1,0:T(8,128)(2,1)S(1)}, u32[]{:S(2)}, u32[]{:S(2)}) %collective-permute-start.25) | collective-permute-done | bytes 278560 | tf_op jit(solution)/shard_map/ppermute | solution.py:383
  119.7 21.2 %collective-permute-done.26 = bf16[272,512]{1,0:T(8,128)(2,1)S(1)} collective-permute-done((bf16[272,512]{1,0:T(8,128)(2,1)S(1)}, bf16[272,512]{1,0:T(8,128)(2,1)S(1)}, u32[]{:S(2)}, u32[]{:S(2)}) %collective-permute-start.26) | collective-permute-done | bytes 278560 | tf_op jit(solution)/shard_map/ppermute | solution.py:538
  142.3 11.8 %projections.2 = (bf16[128,1024]{1,0:T(8,128)(2,1)}, bf16[128,1024]{1,0:T(8,128)(2,1)}, bf16[128,1024]{1,0:T(8,128)(2,1)}) custom-call(s32[3]{0:T(128)} %pad_add_fusion.refs_0_, bf16[3,128,512]{2,1,0:T(8,128)(2,1)} %get-tuple-element.97.refs_1_, bf16[3,128,512]{2,1,0:T(8,128)(2,1)} %copy-done.14, bf16[3,128,512]{2,1,0:T(8,128)(2,1)} %copy-done.15, ...), custom_call_target="tpu_custom_call" | custom-call | bytes 17500000 | tf_op jit(solution)/shard_map/projections/pallas_call | solution.py:563
  155.0 9.5 %projections.3 = (bf16[128,1024]{1,0:T(8,128)(2,1)}, bf16[128,1024]{1,0:T(8,128)(2,1)}, bf16[128,1024]{1,0:T(8,128)(2,1)}, bf16[128,1024]{1,0:T(8,128)(2,1)}) custom-call(s32[3]{0:T(128)} %pad_add_fusion.refs_0_, bf16[3,128,512]{2,1,0:T(8,128)(2,1)} %copy-done.16, bf16[3,144,512]{2,1,0:T(8,128)(2,1)} %copy-done.12, bf16[3,512,1024]{2,1,0:T(8,128)(2,1)} %refs_3_.9, ...), custom_call_target="tpu_custom_call" | custom-call | bytes 17500000 | tf_op jit(solution)/shard_map/projections/pallas_call | solution.py:563
  168.5 4.3 %collective-permute-done.20 = bf16[128,1024]{1,0:T(8,128)(2,1)S(1)} collective-permute-done((bf16[128,1024]{1,0:T(8,128)(2,1)}, bf16[128,1024]{1,0:T(8,128)(2,1)S(1)}, u32[]{:S(2)}, u32[]{:S(2)}) %collective-permute-start.20) | collective-permute-done | bytes 262176 | tf_op jit(solution)/shard_map/ppermute | solution.py:386
  174.0 3.1 %collective-permute-done.22 = bf16[128,1024]{1,0:T(8,128)(2,1)S(1)} collective-permute-done((bf16[128,1024]{1,0:T(8,128)(2,1)}, bf16[128,1024]{1,0:T(8,128)(2,1)S(1)}, u32[]{:S(2)}, u32[]{:S(2)}) %collective-permute-start.22) | collective-permute-done | bytes 262176 | tf_op jit(solution)/shard_map/ppermute | solution.py:386
  178.2 5.8 %collective-permute-start.23 = (bf16[128,1024]{1,0:T(8,128)(2,1)S(1)}, bf16[128,1024]{1,0:T(8,128)(2,1)S(1)}, u32[]{:S(2)}, u32[]{:S(2)}) collective-permute-start(bf16[128,1024]{1,0:T(8,128)(2,1)S(1)} %add_convert_fusion.3), channel_id=1, source_target_pairs={{0,0},{1,1},{2,8},{3,9},{4,16},{5,17},{6,24},{7,25},{8,2},{9,3},{1... | collective-permute-start | bytes 786440 | tf_op jit(solution)/shard_map/ppermute | solution.py:598
  190.9 5.4 %collective-permute-done.23 = bf16[128,1024]{1,0:T(8,128)(2,1)S(1)} collective-permute-done((bf16[128,1024]{1,0:T(8,128)(2,1)S(1)}, bf16[128,1024]{1,0:T(8,128)(2,1)S(1)}, u32[]{:S(2)}, u32[]{:S(2)}) %collective-permute-start.23) | collective-permute-done | bytes 262176 | tf_op jit(solution)/shard_map/ppermute | solution.py:598
  (128 shorter events, 55.6 us)
Async XLA Ops:
  1.4 8.8 %collective-permute-start = (bf16[1,1024]{1,0:T(2,128)(2,1)S(1)}, bf16[1,1024]{1,0:T(2,128)(2,1)S(1)}, u32[]{:S(2)}, u32[]{:S(2)}) collective-permute-start(bf16[1,1024]{1,0:T(2,128)(2,1)S(1)} %slice.21), channel_id=1, source_target_pairs={{0,1},{1,2},{2,3},{3,4},{4,5},{5,6},{6,7},{8,9},{9,10},{10,11},{11... | collective-permute-start | bytes 6152 | tf_op jit(solution)/shard_map/ppermute | solution.py:375
  13.1 5.1 %collective-permute-start.2 = (f32[128,128]{1,0:T(8,128)}, f32[128,128]{1,0:T(8,128)S(1)}, u32[]{:S(2)}, u32[]{:S(2)}) collective-permute-start(f32[128,128]{1,0:T(8,128)} %adapter_input.1.refs_0_), channel_id=1, source_target_pairs={{0,16},{8,24},{16,0},{24,8},{1,17},{9,25},{17,1},{25,9},{2,18},{10... | collective-permute-start | bytes 196616 | tf_op jit(solution)/shard_map/ppermute | solution.py:386
  22.4 9.8 %collective-permute-start.4 = (bf16[144,1024]{1,0:T(8,128)(2,1)}, bf16[144,1024]{1,0:T(8,128)(2,1)S(1)}, u32[]{:S(2)}, u32[]{:S(2)}) collective-permute-start(bf16[144,1024]{1,0:T(8,128)(2,1)} %get-tuple-element.79.refs_1_), channel_id=1, source_target_pairs={{0,1},{1,0},{2,3},{3,2},{4,5},{5,4},{6,7},{7,6},{8,9},{9,8},{10,11... | collective-permute-start | bytes 884744 | tf_op jit(solution)/shard_map/ppermute | solution.py:383
  32.2 27.6 %collective-permute-start.14 = (bf16[3,192,1024]{2,1,0:T(8,128)(2,1)S(1)}, bf16[3,192,1024]{2,1,0:T(8,128)(2,1)S(1)}, u32[]{:S(2)}, u32[]{:S(2)}) collective-permute-start(bf16[3,192,1024]{2,1,0:T(8,128)(2,1)S(1)} %slice.22), channel_id=1, source_target_pairs={{0,1},{1,0},{2,3},{3,2},{4,5},{5,4},{6,7},{7,6},{8,9},{9,8},{10,11... | collective-permute-start | bytes 3538952 | tf_op jit(solution)/shard_map/ppermute | solution.py:383
  35.9 10.6 %collective-permute-start.5 = (bf16[80,1024]{1,0:T(8,128)(2,1)}, bf16[80,1024]{1,0:T(8,128)(2,1)S(1)}, u32[]{:S(2)}, u32[]{:S(2)}) collective-permute-start(bf16[80,1024]{1,0:T(8,128)(2,1)} %get-tuple-element.94), channel_id=1, source_target_pairs={{0,2},{1,3},{2,4},{3,5},{4,6},{5,7},{6,0},{7,1},{8,10},{9,11},{10,... | collective-permute-start | bytes 491528 | tf_op jit(solution)/shard_map/ppermute | solution.py:380
  37.5 13.2 %collective-permute-start.6 = (bf16[80,1024]{1,0:T(8,128)(2,1)}, bf16[80,1024]{1,0:T(8,128)(2,1)S(1)}, u32[]{:S(2)}, u32[]{:S(2)}) collective-permute-start(bf16[80,1024]{1,0:T(8,128)(2,1)} %get-tuple-element.95), channel_id=1, source_target_pairs={{0,4},{1,5},{2,6},{3,7},{4,0},{5,1},{6,2},{7,3},{8,12},{9,13},{10,... | collective-permute-start | bytes 491528 | tf_op jit(solution)/shard_map/ppermute | solution.py:380
  39.2 11.5 %collective-permute-start.7 = (bf16[80,1024]{1,0:T(8,128)(2,1)}, bf16[80,1024]{1,0:T(8,128)(2,1)S(1)}, u32[]{:S(2)}, u32[]{:S(2)}) collective-permute-start(bf16[80,1024]{1,0:T(8,128)(2,1)} %get-tuple-element.96), channel_id=1, source_target_pairs={{0,6},{1,7},{2,0},{3,1},{4,2},{5,3},{6,4},{7,5},{8,14},{9,15},{10,... | collective-permute-start | bytes 491528 | tf_op jit(solution)/shard_map/ppermute | solution.py:380
  59.8 5.5 %collective-permute-start.15 = (bf16[3,2,512]{2,1,0:T(2,128)(2,1)S(1)}, bf16[3,2,512]{2,1,0:T(2,128)(2,1)S(1)}, u32[]{:S(2)}, u32[]{:S(2)}) collective-permute-start(bf16[3,2,512]{2,1,0:T(2,128)(2,1)S(1)} %pad_maximum_fusion), channel_id=1, source_target_pairs={{1,0},{2,1},{3,2},{4,3},{5,4},{6,5},{7,6},{9,8},{10,9},{11,10},{12... | collective-permute-start | bytes 18440 | tf_op jit(solution)/shard_map/ppermute | solution.py:375
  65.3 75.7 %collective-permute-start.19 = (bf16[3,320,1024]{2,1,0:T(8,128)(2,1)S(1)}, bf16[3,320,1024]{2,1,0:T(8,128)(2,1)S(1)}, u32[]{:S(2)}, u32[]{:S(2)}) collective-permute-start(bf16[3,320,1024]{2,1,0:T(8,128)(2,1)S(1)} %slice.23), channel_id=1, source_target_pairs={{0,1},{1,0},{2,3},{3,2},{4,5},{5,4},{6,7},{7,6},{8,9},{9,8},{10,11... | collective-permute-start | bytes 5898248 | tf_op jit(solution)/shard_map/ppermute | solution.py:383
  67.9 20.7 %collective-permute-start.8 = (bf16[3,128,512]{2,1,0:T(8,128)(2,1)}, bf16[3,128,512]{2,1,0:T(8,128)(2,1)S(1)}, u32[]{:S(2)}, u32[]{:S(2)}) collective-permute-start(bf16[3,128,512]{2,1,0:T(8,128)(2,1)} %get-tuple-element.97.refs_1_), channel_id=1, source_target_pairs={{0,2},{1,3},{2,4},{3,5},{4,6},{5,7},{6,0},{7,1},{8,10},{9,11},{10,... | collective-permute-start | bytes 1179656 | tf_op jit(solution)/shard_map/ppermute | solution.py:380
  70.3 19.9 %collective-permute-start.16 = (bf16[3,144,512]{2,1,0:T(8,128)(2,1)S(1)}, bf16[3,144,512]{2,1,0:T(8,128)(2,1)S(1)}, u32[]{:S(2)}, u32[]{:S(2)}) collective-permute-start(bf16[3,144,512]{2,1,0:T(8,128)(2,1)S(1)} %maximum_maximum_fusion.refs_4_), channel_id=1, source_target_pairs={{0,2},{1,3},{2,4},{3,5},{4,6},{5,7},{6,0},{7,1},{8,10},{9,11},{10,... | collective-permute-start | bytes 1327112 | tf_op jit(solution)/shard_map/ppermute | solution.py:380
  88.6 27.1 %collective-permute-start.25 = (bf16[272,512]{1,0:T(8,128)(2,1)}, bf16[272,512]{1,0:T(8,128)(2,1)S(1)}, u32[]{:S(2)}, u32[]{:S(2)}) collective-permute-start(bf16[272,512]{1,0:T(8,128)(2,1)} %get-tuple-element.138), channel_id=1, source_target_pairs={{0,1},{1,0},{2,3},{3,2},{4,5},{5,4},{6,7},{7,6},{8,9},{9,8},{10,11... | collective-permute-start | bytes 835592 | tf_op jit(solution)/shard_map/ppermute | solution.py:383
  88.7 30.3 %collective-permute-start.12 = (bf16[3,128,512]{2,1,0:T(8,128)(2,1)S(1)}, bf16[3,128,512]{2,1,0:T(8,128)(2,1)S(1)}, u32[]{:S(2)}, u32[]{:S(2)}) collective-permute-start(bf16[3,128,512]{2,1,0:T(8,128)(2,1)S(1)} %collective-permute-done.8.refs_2_), channel_id=1, source_target_pairs={{0,2},{1,3},{2,4},{3,5},{4,6},{5,7},{6,0},{7,1},{8,10},{9,11},{10,... | collective-permute-start | bytes 1179656 | tf_op jit(solution)/shard_map/ppermute | solution.py:380
  90.2 28.9 %collective-permute-start.17 = (bf16[3,144,512]{2,1,0:T(8,128)(2,1)S(1)}, bf16[3,144,512]{2,1,0:T(8,128)(2,1)S(1)}, u32[]{:S(2)}, u32[]{:S(2)}) collective-permute-start(bf16[3,144,512]{2,1,0:T(8,128)(2,1)S(1)} %collective-permute-done.16.refs_5_), channel_id=1, source_target_pairs={{0,2},{1,3},{2,4},{3,5},{4,6},{5,7},{6,0},{7,1},{8,10},{9,11},{10,... | collective-permute-start | bytes 1327112 | tf_op jit(solution)/shard_map/ppermute | solution.py:380
  116.8 24.0 %collective-permute-start.26 = (bf16[272,512]{1,0:T(8,128)(2,1)S(1)}, bf16[272,512]{1,0:T(8,128)(2,1)S(1)}, u32[]{:S(2)}, u32[]{:S(2)}) collective-permute-start(bf16[272,512]{1,0:T(8,128)(2,1)S(1)} %add_convert_fusion.2), channel_id=1, source_target_pairs={{0,2},{1,3},{2,0},{3,1},{4,6},{5,7},{6,4},{7,5},{8,10},{9,11},{10,... | collective-permute-start | bytes 835592 | tf_op jit(solution)/shard_map/ppermute | solution.py:538
  119.0 35.1 %collective-permute-start.13 = (bf16[3,128,512]{2,1,0:T(8,128)(2,1)S(1)}, bf16[3,128,512]{2,1,0:T(8,128)(2,1)S(1)}, u32[]{:S(2)}, u32[]{:S(2)}) collective-permute-start(bf16[3,128,512]{2,1,0:T(8,128)(2,1)S(1)} %collective-permute-done.12.refs_3_), channel_id=1, source_target_pairs={{0,2},{1,3},{2,4},{3,5},{4,6},{5,7},{6,0},{7,1},{8,10},{9,11},{10,... | collective-permute-start | bytes 1179656 | tf_op jit(solution)/shard_map/ppermute | solution.py:380
  119.1 35.0 %collective-permute-start.18 = (bf16[3,144,512]{2,1,0:T(8,128)(2,1)S(1)}, bf16[3,144,512]{2,1,0:T(8,128)(2,1)S(1)}, u32[]{:S(2)}, u32[]{:S(2)}) collective-permute-start(bf16[3,144,512]{2,1,0:T(8,128)(2,1)S(1)} %collective-permute-done.17.refs_6_), channel_id=1, source_target_pairs={{0,2},{1,3},{2,4},{3,5},{4,6},{5,7},{6,0},{7,1},{8,10},{9,11},{10,... | collective-permute-start | bytes 1327112 | tf_op jit(solution)/shard_map/ppermute | solution.py:380
  140.9 25.6 %collective-permute-start.27 = (bf16[272,512]{1,0:T(8,128)(2,1)S(1)}, bf16[272,512]{1,0:T(8,128)(2,1)S(1)}, u32[]{:S(2)}, u32[]{:S(2)}) collective-permute-start(bf16[272,512]{1,0:T(8,128)(2,1)S(1)} %add_convert_fusion.1), channel_id=1, source_target_pairs={{0,4},{1,5},{2,6},{3,7},{4,0},{5,1},{6,2},{7,3},{8,12},{9,13},{10,... | collective-permute-start | bytes 835592 | tf_op jit(solution)/shard_map/ppermute | solution.py:538
  164.5 8.3 %collective-permute-start.20 = (bf16[128,1024]{1,0:T(8,128)(2,1)}, bf16[128,1024]{1,0:T(8,128)(2,1)S(1)}, u32[]{:S(2)}, u32[]{:S(2)}) collective-permute-start(bf16[128,1024]{1,0:T(8,128)(2,1)} %get-tuple-element.133), channel_id=1, source_target_pairs={{0,8},{8,16},{16,24},{24,0},{1,9},{9,17},{17,25},{25,1},{2,10},{10... | collective-permute-start | bytes 786440 | tf_op jit(solution)/shard_map/ppermute | solution.py:386
  164.6 9.4 %collective-permute-start.21 = (bf16[128,1024]{1,0:T(8,128)(2,1)}, bf16[128,1024]{1,0:T(8,128)(2,1)S(1)}, u32[]{:S(2)}, u32[]{:S(2)}) collective-permute-start(bf16[128,1024]{1,0:T(8,128)(2,1)} %get-tuple-element.134), channel_id=1, source_target_pairs={{0,16},{8,24},{16,0},{24,8},{1,17},{9,25},{17,1},{25,9},{2,18},{10... | collective-permute-start | bytes 786440 | tf_op jit(solution)/shard_map/ppermute | solution.py:386
  165.1 12.0 %collective-permute-start.22 = (bf16[128,1024]{1,0:T(8,128)(2,1)}, bf16[128,1024]{1,0:T(8,128)(2,1)S(1)}, u32[]{:S(2)}, u32[]{:S(2)}) collective-permute-start(bf16[128,1024]{1,0:T(8,128)(2,1)} %get-tuple-element.135), channel_id=1, source_target_pairs={{0,24},{8,0},{16,8},{24,16},{1,25},{9,1},{17,9},{25,17},{2,26},{10... | collective-permute-start | bytes 786440 | tf_op jit(solution)/shard_map/ppermute | solution.py:386
  166.6 18.8 %collective-permute-start.28 = (bf16[272,512]{1,0:T(8,128)(2,1)S(1)}, bf16[272,512]{1,0:T(8,128)(2,1)S(1)}, u32[]{:S(2)}, u32[]{:S(2)}) collective-permute-start(bf16[272,512]{1,0:T(8,128)(2,1)S(1)} %add_convert_fusion.refs_1_), channel_id=1, source_target_pairs={{0,1},{1,0},{2,3},{3,2},{4,5},{5,4},{6,7},{7,6},{8,9},{9,8},{10,11... | collective-permute-start | bytes 835592 | tf_op jit(solution)/shard_map/ppermute | solution.py:383
  178.2 18.0 %collective-permute-start.23 = (bf16[128,1024]{1,0:T(8,128)(2,1)S(1)}, bf16[128,1024]{1,0:T(8,128)(2,1)S(1)}, u32[]{:S(2)}, u32[]{:S(2)}) collective-permute-start(bf16[128,1024]{1,0:T(8,128)(2,1)S(1)} %add_convert_fusion.3), channel_id=1, source_target_pairs={{0,0},{1,1},{2,8},{3,9},{4,16},{5,17},{6,24},{7,25},{8,2},{9,3},{1... | collective-permute-start | bytes 786440 | tf_op jit(solution)/shard_map/ppermute | solution.py:598
  184.0 6.8 %collective-permute-start.24 = (f32[1,1024]{1,0:T(1,128)S(1)}, f32[1,1024]{1,0:T(1,128)S(1)}, u32[]{:S(2)}, u32[]{:S(2)}) collective-permute-start(f32[1,1024]{1,0:T(1,128)S(1)} %slice.27), channel_id=1, source_target_pairs={{1,0},{2,1},{3,2},{4,3},{5,4},{6,5},{7,6},{9,8},{10,9},{11,10},{12... | collective-permute-start | bytes 12296 | tf_op jit(solution)/shard_map/ppermute | solution.py:375
  (33 other events, 312.8 us)

commit v3 on v2

v3 whole, which is shorter than its diff:
```python
import jax
import jax.numpy as jnp
import numpy as np
from jax import lax
from jax.experimental import pallas as pl
from jax.experimental.pallas import tpu as pltpu
from jax.sharding import PartitionSpec as P

F32 = jnp.float32
BF16 = jnp.bfloat16
PAIR = 128
VMEM = 56 * 2**20
NN = (((1,), (0,)), ((), ()))
NT = (((1,), (1,)), ((), ()))
TN = (((0,), (0,)), ((), ()))


def position():
    seq, head = lax.axis_index("seq"), lax.axis_index("head")
    inner = lax.axis_size("seq") // lax.axis_size("head")
    return lax.rem(seq, inner), lax.div(seq, inner), head


def mm(a, b, dims=NN):
    return lax.dot_general(a, b, dims, preferred_element_type=F32)


def halves(a):
    hi = a.astype(BF16)
    return hi, (a - hi.astype(F32)).astype(BF16)


def low_lanes(shape, half):
    return lax.broadcasted_iota(jnp.int32, shape, len(shape) - 1) < half


def block_rows(a, half):
    low = low_lanes(a.shape, half)
    zero = jnp.zeros_like(a)
    return jnp.concatenate([jnp.where(low, a, zero), jnp.where(low, zero, a)], 0)


def fold(a, half):
    rows = a.shape[0] // 2
    return jnp.where(low_lanes((rows, a.shape[1]), half), a[:rows], a[rows:])


def sum_matrix(rows):
    t = np.arange(rows)
    both = np.concatenate([t[:, None] > t[None, :], t[:, None] < t[None, :]], 0)
    return np.concatenate([both, both], 1).astype(np.float32)


def level_matrix(rows):
    t = np.arange(rows)
    parts = []
    m = 1
    while m < rows:
        mid = (t // (2 * m)) * 2 * m + m
        right = t >= mid
        u = t[None, :]
        take_right = (u >= mid[:, None]) & (u < t[:, None])
        take_left = (u > t[:, None]) & (u < mid[:, None])
        parts.append(np.where(right[:, None], take_right, take_left))
        m *= 2
    both = np.concatenate(parts, 0)
    return np.concatenate([both, both], 1).astype(np.float32)


def cumulative_matrix(rows):
    t = np.arange(rows)
    strict = (t[:, None] < t[None, :]).astype(np.float32)
    full = (t[:, None] <= t[None, :]).astype(np.float32)
    return np.concatenate([strict, strict, -full, -full], 1)


def split_rows(a):
    hi, lo = halves(a)
    wide = (4, a.shape[1])
    return jnp.concatenate([jnp.broadcast_to(hi, wide), jnp.broadcast_to(lo, wide)], 0)


def joined(msg, at):
    return msg[at : at + 1].astype(F32) + msg[at + 4 : at + 5].astype(F32)


def mm3(a, b, dims=NN):
    ah, al = halves(a)
    bh, bl = halves(b)
    return mm(ah, bh, dims) + (mm(ah, bl, dims) + mm(al, bh, dims))


def mixed_input(x, carried, mix):
    features = x[...].astype(F32)
    row = lax.broadcasted_iota(jnp.int32, features.shape, 0)
    previous = jnp.where(row == 0, carried[...].astype(F32), pltpu.roll(features, 1, 0))
    return features + mix[...] * (previous - features)


def copy_rows(weights, piece, at, sem):
    return pltpu.make_async_copy(weights.at[:, pl.ds(at, piece.shape[1])], piece, sem.at[0])


def adapter_kernel(x, carried, mix, down, weights, pre, piece, sem):
    copy = copy_rows(weights, piece, 0, sem)
    copy.start()
    pre[...] = mm3(mixed_input(x, carried, mix), down[...])
    copy.wait()


def decay_kernel(head, count, *refs):
    pres = refs[:count]
    base, up, r, k, v, dy, sums, lora, lora_t, w_out, end, st, msg = refs[count:]
    rows = r.shape[0]
    total = pres[0][...]
    for pre in pres[1:]:
        total = total + pre[...]
    mid = jnp.tanh(total)
    lora[...] = mid
    lora_t[...] = mid.T.astype(BF16)
    w = -jnp.exp(base[...] + mm3(mid, up[...]))
    w_out[...] = w
    hi, lo = halves(w)
    args = mm(sums[...], jnp.concatenate([hi, lo], 0))
    before, after = args[:rows], args[rows:]
    final = before[rows - 1 :] + w[rows - 1 :]
    end[...] = final
    from_start, to_end = jnp.exp(before), jnp.exp(after)
    kf = (k[...].astype(F32) * to_end).astype(BF16)
    rb = (r[...].astype(F32) * from_start).astype(BF16)
    for p in range(r.shape[1] // PAIR):
        cols = slice(p * PAIR, (p + 1) * PAIR)
        state = fold(mm(v[:, cols], kf[:, cols], TN), head)
        st[:, cols] = state
        msg[:head, cols] = state.astype(BF16)
        msg[head : 2 * head, cols] = fold(mm(dy[:, cols], rb[:, cols], TN), head).astype(BF16)
    msg[2 * head :] = split_rows(final)


def pair_kernel(head, ring, own, far, *outs):
    place = position()
    late = place[0] == 1
    dec_own, dec_far = joined(own, 2 * head), joined(far, 2 * head)
    eo, ef = jnp.exp(dec_own), jnp.exp(dec_far)
    st_own, st_far = own[:head].astype(F32), far[:head].astype(F32)
    gt_own, gt_far = own[head : 2 * head].astype(F32), far[head : 2 * head].astype(F32)
    state = jnp.where(late, st_own + eo * st_far, st_far + ef * st_own).astype(BF16)
    grad = jnp.where(late, gt_far + ef * gt_own, gt_own + eo * gt_far).astype(BF16)
    decays = split_rows(dec_own + dec_far)
    for d in range(1, ring):
        out = outs[d - 1]
        ahead = place[1] + d < ring

        @pl.when(ahead)
        def _():
            out[:head] = state

        @pl.when(jnp.logical_not(ahead))
        def _():
            out[:head] = grad

        out[head:] = decays


def inner_kernel(head, skip, r, k, v, dy, w, u, levels, sums, *refs):
    if skip:
        weights, piece, sem = refs[0], refs[8], refs[9]
        refs = refs[1:8]

        @pl.when(pl.program_id(0) == 0)
        def _():
            copy_rows(weights, piece, skip, sem).start()

        @pl.when(pl.program_id(0) == pl.num_programs(0) - 1)
        def _():
            copy_rows(weights, piece, skip, sem).wait()

    gr_out, gk_out, gv_out, self_out, eb_out, ee_out, du_out = refs
    rows, width = r.shape
    row = lax.broadcasted_iota(jnp.int32, (rows, PAIR), 0)
    row2 = lax.broadcasted_iota(jnp.int32, (rows, 2 * rows), 0)
    col2 = lax.broadcasted_iota(jnp.int32, (rows, 2 * rows), 1)
    apart = row2 ^ (col2 & (rows - 1))
    lane_r = lax.broadcasted_iota(jnp.int32, (2 * PAIR, PAIR), 0) & (PAIR - 1)
    lane_c = lax.broadcasted_iota(jnp.int32, (2 * PAIR, PAIR), 1)
    ones = jnp.where((lane_r < head) == (lane_c < head), 1.0, 0.0).astype(BF16)
    hi, lo = halves(w[...])
    both = jnp.concatenate([hi, lo], 0)
    decay = jnp.exp(mm(levels[...], both))
    ends = jnp.exp(mm(sums[...], both))
    eb_out[...], ee_out[...] = ends[:rows], ends[rows:]
    for p in range(width // PAIR):
        cols = slice(p * PAIR, (p + 1) * PAIR)
        rf, kf = r[:, cols].astype(F32), k[:, cols].astype(F32)
        vf, dyf = v[:, cols].astype(F32), dy[:, cols].astype(F32)
        dydy = block_rows(dy[:, cols], head)
        pairs = mm(dy[:, cols], block_rows(v[:, cols], head), NT)
        pairs_t = mm(v[:, cols], dydy, NT)
        gr = jnp.zeros((rows, PAIR), F32)
        gk = jnp.zeros((rows, PAIR), F32)
        scores_t = jnp.zeros((rows, 2 * rows), F32)
        m, level = 1, 0
        while m < rows:
            d = decay[level * rows : (level + 1) * rows, cols]
            right = (row & m) != 0
            rd = jnp.where(right, rf * d, 0.0).astype(BF16)
            kd = jnp.where(right, 0.0, kf * d).astype(BF16)
            kk, rr = block_rows(kd, head), block_rows(rd, head)
            near = apart < 2 * m
            a = mm(kd, rr, NT)
            scores_t = scores_t + jnp.where(near, a, 0.0)
            here = jnp.where(near, pairs, 0.0).astype(BF16)
            here_t = jnp.where(near, pairs_t, 0.0).astype(BF16)
            gr = gr + jnp.where(right, d * mm(here, kk), 0.0)
            gk = gk + jnp.where(right, 0.0, d * mm(here_t, rr))
            m, level = 2 * m, level + 1
        sh, sl = halves(dyf * vf)
        own = mm(jnp.concatenate([sh, sl], 1), ones)
        bh, bl = halves(rf * u[:, cols] * kf)
        bonus = mm(jnp.concatenate([bh, bl], 1), ones)
        gr_out[:, cols] = gr
        gk_out[:, cols] = gk
        gv_out[:, cols] = mm(scores_t.astype(BF16), dydy) + bonus * dyf
        self_out[:, cols] = own
        du_out[:, cols] = jnp.sum(rf * kf * own, 0, keepdims=True)


def outer_kernel(
    head, ring, r, k, v, dy, u, gr0, gk0, gv0, own, eb, ee, st, end, far, *refs
):
    place = position()
    msgs = refs[: ring - 1]
    proj, r_gr, k_gk, at_end = refs[ring - 1 :]
    width = r.shape[1]
    late, z = place[0] == 1, place[1]
    zero = jnp.zeros((head, width), F32)
    nothing = jnp.zeros((1, width), F32)
    state, grad, past, future = zero, zero, nothing, nothing
    for d in range(1, ring):
        msg = msgs[d - 1]
        live = d <= z
        state = state + jnp.where(live, jnp.exp(past) * msg[:head].astype(F32), 0.0)
        past = past + jnp.where(live, joined(msg, head), 0.0)
    for d in range(ring - 1, 0, -1):
        msg = msgs[d - 1]
        live = d > z
        grad = grad + jnp.where(live, jnp.exp(future) * msg[:head].astype(F32), 0.0)
        future = future + jnp.where(live, joined(msg, head), 0.0)
    ef = jnp.exp(joined(far, 2 * head))
    st_in = jnp.where(late, far[:head].astype(F32) + ef * state, state)
    gt_in = jnp.where(late, grad, far[head : 2 * head].astype(F32) + ef * grad)
    at_end[...] = jnp.sum(gt_in * (jnp.exp(end[...]) * st_in + st[...]), 0, keepdims=True)
    sb, gb = st_in.astype(BF16), gt_in.astype(BF16)
    for p in range(width // PAIR):
        cols = slice(p * PAIR, (p + 1) * PAIR)
        grads = block_rows(gb[:, cols], head)
        rf, kf = r[:, cols].astype(F32), k[:, cols].astype(F32)
        after = ee[:, cols]
        gr = gr0[:, cols] + eb[:, cols] * mm(dy[:, cols], block_rows(sb[:, cols], head))
        gk = gk0[:, cols] + after * mm(v[:, cols], grads)
        gv = gv0[:, cols] + mm((kf * after).astype(BF16), grads, NT)
        s = own[:, cols] * u[:, cols]
        proj[0, :, cols] = (gr + kf * s).astype(BF16)
        proj[1, :, cols] = (gk + rf * s).astype(BF16)
        proj[2, :, cols] = gv.astype(BF16)
        r_gr[:, cols] = rf * gr
        k_gk[:, cols] = kf * gk


def decay_grad_kernel(w, r_gr, k_gk, at_end, up, lora_t, cums, up_grad, base_grad, mid_grad):
    ah, al = halves(r_gr[...])
    bh, bl = halves(k_gk[...])
    gp = (mm(cums[...], jnp.concatenate([ah, al, bh, bl], 0)) + at_end[...]) * w[...]
    gpb = gp.astype(BF16)
    up_grad[...] = mm(lora_t[...], gpb)
    base_grad[...] = jnp.sum(gp, 0, keepdims=True)
    mid_grad[...] = mm(gpb, up[...].astype(BF16), NT)


def middle_kernel(count, x, carried, mix, down, lora, *refs):
    mids, sides, (keep, send, grad_in) = refs[:count], refs[count:-3], refs[-3:]
    total = mids[0][...]
    for part in mids[1:]:
        total = total + part[...]
    mid = total * (1.0 - lora[...] * lora[...])
    grad_in[...] = mm3(mid, down[...], NT)
    down_grad = mm3(mid.T, mixed_input(x, carried, mix))
    rank, half = mid.shape[1], x.shape[1] // 2
    wide = (8, half)
    late = position()[0] == 1

    def choose(low, high, at, size):
        keep[at : at + size] = jnp.where(late, high, low).astype(BF16)
        send[at : at + size] = jnp.where(late, low, high).astype(BF16)

    up_low, up_high, base_low, base_high, du_low, du_high = [ref[...] for ref in sides]
    choose(up_low, up_high, 0, rank)
    choose(down_grad[:, :half], down_grad[:, half:], rank, rank)
    for at, low, high in ((0, base_low, base_high), (8, du_low, du_high)):
        choose(jnp.broadcast_to(low, wide), jnp.broadcast_to(high, wide), 2 * rank + at, 8)


def finish_kernel(rank, mine, theirs, up, down, base, du):
    late = position()[0] == 1
    half = mine.shape[1]
    a, b = mine[...].astype(F32), theirs[...].astype(F32)
    for at, value in ((0, jnp.where(late, b, a)), (half, jnp.where(late, a, b))):
        here = slice(at, at + half)
        up[:, here] = value[:rank]
        down[here] = value[rank : 2 * rank].T
        for ref, row in ((base, 2 * rank), (du, 2 * rank + 8)):
            size = ref.shape[1]
            for i in range(half // size):
                to = at // size + i
                ref[to : to + 1] = value[row : row + 1, i * size : (i + 1) * size]


def project_kernel(count, ring, final, *refs):
    place = position()
    lows, highs, given, mix = refs[:count], refs[count : 2 * count], refs[2 * count : 2 * count + 3], refs[2 * count + 3]
    rest, (low, high, weights, own, prior, sem) = refs[2 * count + 4 : -6], refs[-6:]
    done, outs = (rest[:-ring], rest[-ring:]) if final else ((), rest)
    rows, width = lows[0].shape[1:]
    n = weights.shape[2]
    copies = []

    def fetch(source, target):
        copy = pltpu.make_async_copy(source, target, sem.at[len(copies)])
        copy.start()
        copies.append(copy)
        return copy

    weight_copies, block_copies = [], []
    for i in range(2):
        for m in range(3):
            if i == 0:
                weight_copies.append([fetch(given[0].at[m], weights.at[0, m])])
            else:
                first, cut = given[1].at[m], given[1].shape[1]
                weight_copies.append(
                    [
                        fetch(first, weights.at[1, m, pl.ds(0, cut)]),
                        fetch(given[2].at[m], weights.at[1, m, pl.ds(cut, n - cut)]),
                    ]
                )
            if i == 0:
                places = [pl.ds(q * rows, rows) for q in range(count)]
                block_copies.append(
                    [fetch(lows[q].at[m], low.at[m, at]) for q, at in enumerate(places)]
                    + [fetch(highs[q].at[m], high.at[m, at]) for q, at in enumerate(places)]
                )

    for i in range(2):
        column = pl.ds(pl.multiple_of((place[0] if i == 0 else 1 - place[0]) * n, n), n)
        for m in range(3):
            for copy in (block_copies[m] if i == 0 else []) + weight_copies[i * 3 + m]:
                copy.wait()
            term = mm(low[m], weights[i, m, :, :width], NT) + mm(high[m], weights[i, m, :, width:], NT)
            later = mix[m : m + 1, column] * term
            own[...] = term - later if m == 0 else own[...] + (term - later)
            prior[...] = later if m == 0 else prior[...] + later
        last = lax.broadcasted_iota(jnp.int32, (rows, n), 0) == rows - 1
        top = lax.broadcasted_iota(jnp.int32, (16, n), 0) == 0

        def store(out, q):
            here = slice(q * rows, (q + 1) * rows)
            part = prior[here]
            moved = jnp.where(last, 0.0, pltpu.roll(part, rows - 1, 0))
            out[:rows, column] = (own[here] + moved).astype(BF16)
            out[rows:, column] = jnp.where(top, part[:16], 0.0).astype(BF16)

        if not final:
            for q in range(count):
                store(outs[q], q)
            continue
        for d in range(ring):
            wanted = lax.rem(place[1] - place[2] - d + 2 * ring, ring)
            for q in range(ring):

                @pl.when(wanted == q)
                def _():
                    if q == ring - 1:
                        store(outs[d], 0)
                    else:
                        outs[d][:, column] = done[q][:, column]


def per_device(
    layer_input, receptance, key_act, value_act, attention_result_sensitivity, time_first,
    decay_exponent_base, decay_shift_mix, mix_rkv, decay_adapter_down, decay_adapter_up, proj_weights,
):
    rows, cols = layer_input.shape
    heads, head = time_first.shape
    rank = decay_adapter_down.shape[1]
    n_seq, n_head = lax.axis_size("seq"), lax.axis_size("head")
    inner = n_seq // n_head
    ring = n_seq // inner
    pairs = cols // PAIR
    parts = 2
    part_cols = cols // parts
    block = min(part_cols, 2 * PAIR)
    r, k, v, dy = receptance, key_act, value_act, attention_result_sensitivity
    params = pltpu.CompilerParams(vmem_limit_bytes=VMEM)

    def shape(s, t=F32):
        return jax.ShapeDtypeStruct(s, t)

    def work(us):
        return pl.CostEstimate(flops=0, transcendentals=0, bytes_accessed=int(us * 3.5e6))

    def shift(a, distance):
        return lax.ppermute(
            a, "seq", [(i - distance, i) for i in range(n_seq) if 0 <= i - distance < n_seq]
        )

    def around(a, step):
        return lax.ppermute(a, "seq", [(i, (i + inner * step) % n_seq) for i in range(n_seq)])

    def partner(a):
        return lax.ppermute(a, "seq", [(i, i ^ 1) for i in range(n_seq)])

    def head_shift(a, d):
        return lax.ppermute(a, "head", [(i, (i + d) % n_head) for i in range(n_head)])

    def head_parts(a):
        return [a] + [head_shift(a, d) for d in range(1, n_head)]

    def after_that(value, *others):
        return lax.optimization_barrier((value, *others))[0]

    weight_rows = proj_weights.shape[1]
    cut = weight_rows // 8
    anywhere = pl.BlockSpec(memory_space=pl.ANY)
    vmem = pl.BlockSpec(memory_space=pltpu.VMEM)

    carried = shift(layer_input[rows - 1 :], 1)
    shift_mix = decay_shift_mix.reshape(1, cols)
    pre, piece = pl.pallas_call(
        adapter_kernel,
        in_specs=[vmem] * 4 + [anywhere],
        out_specs=[vmem, anywhere],
        out_shape=[shape((rows, rank)), shape((3, cut, cols), BF16)],
        scratch_shapes=[pltpu.SemaphoreType.DMA((1,))],
        compiler_params=params,
        cost_estimate=work(1.5),
        name="adapter_input",
    )(layer_input, carried, shift_mix, decay_adapter_down, proj_weights)
    fars = [partner(piece)]
    pres = head_parts(pre)

    sums = jnp.asarray(sum_matrix(rows), BF16)
    levels = jnp.asarray(level_matrix(rows), BF16)
    cums = jnp.asarray(cumulative_matrix(rows), BF16)
    far_rows = 2 * head + 8

    lora, lora_t, w, end, st, msg = pl.pallas_call(
        lambda *refs: decay_kernel(head, n_head, *refs),
        out_shape=[
            shape((rows, rank)), shape((rank, rows), BF16), shape((rows, cols)), shape((1, cols)),
            shape((head, cols)), shape((far_rows, cols), BF16),
        ],
        compiler_params=params,
        cost_estimate=work(3),
        name="decay_and_states",
    )(*pres, decay_exponent_base.reshape(1, cols), decay_adapter_up, r, k, v, dy, sums)

    vmem = pl.BlockSpec(memory_space=pltpu.VMEM)
    u = after_that(time_first, msg).reshape(1, cols)

    def col_block(n, width=block, offset=0):
        return pl.BlockSpec((n, width), lambda p, *_: (0, p + offset))

    def whole(s):
        return pl.BlockSpec(s, lambda p, *_: (0,) * len(s))

    steps = part_cols // block
    here = col_block(rows)

    def inside(part):
        at = lambda n: col_block(n, block, part * steps)
        extra = part == 0
        return pl.pallas_call(
            lambda *refs: inner_kernel(head, cut if extra else 0, *refs),
            grid=(steps,),
            in_specs=[at(rows)] * 5 + [at(1), whole(levels.shape), whole(sums.shape)] + [anywhere] * extra,
            out_specs=[here] * 6 + [col_block(1)] + [anywhere] * extra,
            out_shape=[shape((rows, part_cols))] * 6 + [shape((1, part_cols))]
            + [shape((3, weight_rows - cut, cols), BF16)] * extra,
            scratch_shapes=[pltpu.SemaphoreType.DMA((1,))] * extra,
            compiler_params=params,
            cost_estimate=work(4),
            name="inside_chunk",
        )(r, k, v, dy, after_that(w, fars[0]) if extra else w, u, levels, sums, *[proj_weights] * extra)

    inner_parts = [inside(part) for part in range(parts)]
    far, piece, inner_parts[0] = lax.optimization_barrier(
        (partner(msg), inner_parts[0][7], inner_parts[0][:7])
    )
    fars.append(partner(piece))
    out_msgs = pl.pallas_call(
        lambda *refs: pair_kernel(head, ring, *refs),
                out_shape=[shape((head + 8, cols), BF16)] * (ring - 1),
        compiler_params=params,
        cost_estimate=work(1.5),
        name="pair_states",
    )(msg, far)
    msgs = [around(m, d + 1) for d, m in enumerate(out_msgs)]

    inner_parts[1], msgs = lax.optimization_barrier((inner_parts[1], msgs))
    outer = []
    for part in range(parts):
        at = lambda n: col_block(n, block, part * steps)
        outer.append(
            pl.pallas_call(
                lambda *refs: outer_kernel(head, ring, *refs),
                grid=(steps,),
                in_specs=[at(rows)] * 4 + [at(1)] + [here] * 6
                + [at(head), at(1), at(far_rows)] + [at(head + 8)] * (ring - 1),
                out_specs=[pl.BlockSpec((3, rows, block), lambda p: (0, 0, p)), here, here, col_block(1)],
                out_shape=[
                    shape((3, rows, part_cols), BF16), shape((rows, part_cols)),
                    shape((rows, part_cols)), shape((1, part_cols)),
                ],
                compiler_params=params,
                cost_estimate=work(3),
                name="across_chunks",
            )(r, k, v, dy, u, *inner_parts[part][:6], st, end, far, *msgs)
        )
    projs = [o[0] for o in outer]

    ups, bases, mid_parts = [], [], []
    for part in range(parts):
        at = lambda n: pl.BlockSpec((n, part_cols), lambda p: (0, part))
        up_grad, base_grad, mid_grad = pl.pallas_call(
            decay_grad_kernel,
            grid=(1,),
            in_specs=[at(rows), *[whole((rows, part_cols))] * 2, whole((1, part_cols)), at(rank)]
            + [whole((rank, rows)), whole(cums.shape)],
            out_specs=[whole((rank, part_cols)), whole((1, part_cols)), whole((rows, rank))],
            out_shape=[shape((rank, part_cols)), shape((1, part_cols)), shape((rows, rank))],
            compiler_params=params,
            cost_estimate=work(2),
            name="decay_gradient",
        )(w, *outer[part][1:], decay_adapter_up, lora_t, cums)
        ups.append(up_grad)
        bases.append(base_grad)
        mid_parts.append(mid_grad)
    mid_grad = sum(mid_parts)

    mids = head_parts(mid_grad)
    dus = [part[6] for part in inner_parts]
    keep, send, grad_in = pl.pallas_call(
        lambda *refs: middle_kernel(n_head, *refs),
        in_specs=[vmem] * (5 + n_head + 3 * parts),
        out_shape=[shape((2 * rank + 16, part_cols), BF16)] * 2 + [shape((rows, cols))],
        compiler_params=params,
        cost_estimate=work(3),
        name="adapter_grads",
    )(
        layer_input, carried, shift_mix, decay_adapter_down, lora, *mids, *ups, *bases, *dus
    )

    lows, highs = [projs[0]], [projs[1]]
    for step in range(ring - 1):
        low, high = lows[-1], highs[-1]
        lows.append(around(after_that(low, mid_grad) if step == 1 else low, 1))
        highs.append(around(high, 1))

    def add(a, b):
        return (a.astype(F32) + b.astype(F32)).astype(BF16)

    got = partner(after_that(send, lows[2]))

    mix_here = lax.dynamic_slice_in_dim(after_that(mix_rkv, *out_msgs), position()[1] * cols, cols, 1)

    tall = rows + 16

    def project(low, high, done=()):
        count, final = len(low), len(done) > 0
        return pl.pallas_call(
            lambda *refs: project_kernel(count, ring, final, *refs),
            in_specs=[anywhere] * (2 * count + 3) + [vmem] * (1 + len(done)),
            out_shape=[shape((tall, cols), BF16)] * (ring if final else count),
            scratch_shapes=[
                pltpu.VMEM((3, count * rows, part_cols), BF16),
                pltpu.VMEM((3, count * rows, part_cols), BF16),
                pltpu.VMEM((inner, 3, weight_rows, cols), BF16),
                pltpu.VMEM((count * rows, weight_rows), F32),
                pltpu.VMEM((count * rows, weight_rows), F32),
                pltpu.SemaphoreType.DMA((3 * (2 * count + 3),)),
            ],
            compiler_params=pltpu.CompilerParams(vmem_limit_bytes=24 * 2**20),
            cost_estimate=work(5),
            name="projections",
        )(*low, *high, proj_weights, *fars, mix_here, *done)

    done = project(lows[:-1], highs[:-1])
    sends = project(lows[-1:], highs[-1:], done)
    token_sums = add(keep, after_that(got, *done))
    b = 1
    while b < ring:
        route = [(i, ((i // inner) ^ b) * inner + i % inner) for i in range(n_seq)]
        got = lax.ppermute(token_sums, "seq", route)
        token_sums = add(token_sums, after_that(got, sends) if b == 1 else got)
        b *= 2
    up_grad, down_grad, base_grad, du = pl.pallas_call(
        lambda *refs: finish_kernel(rank, *refs),
                out_shape=[shape((rank, cols)), shape((cols, rank)), shape((pairs, PAIR)), shape((heads, head))],
        compiler_params=params,
        cost_estimate=work(2),
        name="token_sums",
    )(token_sums, partner(token_sums))

    total = sends[0].astype(F32)
    for d in range(1, n_head):
        total = total + head_shift(sends[d], d).astype(F32)
    swap, back = [], []
    for h in range(n_head):
        for z in range(ring):
            for x in range(inner):
                source = h * n_seq + z * inner + x
                block_at = h * inner + x
                swap.append((source, z * n_seq + block_at))
                if block_at > 0:
                    back.append((source, z * n_seq + block_at - 1))
    base_grad = base_grad.reshape(cols)
    summed = lax.ppermute(total[:rows].astype(BF16), ("head", "seq"), swap)
    edge = lax.ppermute(total[rows : rows + 1], ("head", "seq"), back)
    summed = after_that(summed, up_grad, base_grad, du)
    grad_next = jnp.concatenate([grad_in[1:], shift(grad_in[:1], -1)], 0)
    adapter_term = (1.0 - decay_shift_mix) * grad_in + decay_shift_mix * grad_next
    last = lax.broadcasted_iota(jnp.int32, (rows, 1), 0) == rows - 1
    result = (summed.astype(F32) + adapter_term + jnp.where(last, edge, 0.0)).astype(BF16)
    return (result, down_grad, up_grad, base_grad, du)


def solution(mesh):
    return jax.shard_map(
        per_device,
        mesh=mesh,
        in_specs=(
            P("seq", "head"), P("seq", "head"), P("seq", "head"), P("seq", "head"), P("seq", "head"),
            P("head", None), P("head"), P("head"), P(), P("head", None), P(None, "head"),
            P(None, "seq", "head"),
        ),
        out_specs=(P("seq", "head"), P("head", None), P(None, "head"), P("head"), P("head", None)),
        check_vma=False,
    )
```

time: 198 us -> 240 us (1.21)
  Pallas kernels: 55.2 us -> 141 us
  waiting for transfers between devices: 83.5 us -> 40.5 us
  starting transfers between devices: 37.4 us -> 42.5 us
  other arithmetic: 6.1 us -> 2.14 us
  local copies, waits for them, and re-layouts: 13.9 us -> 11.4 us
    pallas_call x8, Pallas kernels: 41.1 us -> 127 us  [the longest x2 93.4 us: inside(): pl.pallas_call(lambda *refs: inner_kernel(head, cut if extra else 0, *ref...]
    ppermute x5, waiting for transfers between devices: 29.2 us -> 1.35 us  [partner(): return lax.ppermute(a, 'seq', [(i, i ^ 1) for i in range(n_seq)])]
    ppermute x3 -> x4, waiting for transfers between devices: 26.6 us -> 1.84 us  [the longest x1 1.36 us: per_device(): summed = lax.ppermute(total[:rows].astype(BF16), ('head', 'seq'), swap)]
    ppermute x9, waiting for transfers between devices: 4.22 us -> 19.3 us  [around(): lax.ppermute(a, 'seq', [(i, (i + inner * step) % n_seq) for i in range(n_...]
    ppermute x3 -> x4, starting transfers between devices: 8.04 us -> 13.9 us  [the longest x1 5.27 us: per_device(): edge = lax.ppermute(total[rows:rows + 1], ('head', 'seq'), back)]
    slice x5 -> x3, local copies, waits for them, and re-layouts: 5.31 us -> 0.79 us  [the longest x1 0.76 us: per_device(): carried = shift(layer_input[rows - 1:], 1)]
    unnamed x57 -> x58, local copies, waits for them, and re-layouts: 6.59 us -> 9.87 us
    ppermute x3 -> x2, waiting for transfers between devices: 4.23 us -> 1.31 us  [shift(): lax.ppermute(a, 'seq', [(i - distance, i) for i in range(n_seq) if 0 <= i...]
  transfers between devices with their start and end apart: 29 -> 29, of which waited for: 14 -> 15; matrix products, arithmetic and copies ran while one was open for 7% -> 1% of each run, Pallas kernels for 25% -> 53%
where the time goes in v3:
time: 240 us; the launch traced here: 239 us
  Pallas kernels  141 us (59%)
  starting transfers between devices  42.5 us (18%)
  waiting for transfers between devices  40.5 us (17%)
  local copies, waits for them, and re-layouts  11.4 us (5%)
    pallas_call x2, Pallas kernels, inside(): pl.pallas_call(lambda *refs: inner_kernel(head, cut if extra else 0, *ref...  93.4 us
    ppermute x9, waiting for transfers between devices, around(): lax.ppermute(a, 'seq', [(i, (i + inner * step) % n_seq) for i in range(n_...  19.3 us
    ppermute x9, waiting for transfers between devices, head_shift(): lax.ppermute(a, 'head', [(i, (i + d) % n_head) for i in range(n_head)])  16.7 us
    pallas_call x1, Pallas kernels, per_device(): pl.pallas_call(adapter_kernel, in_specs=[vmem] * 4 + [anywhere], out_spec...  14.8 us
    ppermute x9, starting transfers between devices, around(): lax.ppermute(a, 'seq', [(i, (i + inner * step) % n_seq) for i in range(n_...  13.2 us
    pallas_call x2, Pallas kernels, project(): pl.pallas_call(lambda *refs: project_kernel(count, ring, final, *refs), i...  12 us
    unnamed x58, local copies, waits for them, and re-layouts  9.87 us
    ppermute x5, starting transfers between devices, partner(): return lax.ppermute(a, 'seq', [(i, i ^ 1) for i in range(n_seq)])  6.25 us
  transfers between devices with their start and end apart: 29, of which 15 were waited for; matrix products, arithmetic and copies ran while one was open for 1% of the time, Pallas kernels for 53%

profile of v3, /device:TPU:4, one launch (start us, length us, event | category | flops | bytes accessed | tf_op | source)
XLA Modules:
  0.0 238.9 jit_solution(504865489316349533)
XLA Ops:
  1.4 3.4 %collective-permute-start = (bf16[1,1024]{1,0:T(2,128)(2,1)S(1)}, bf16[1,1024]{1,0:T(2,128)(2,1)S(1)}, u32[]{:S(2)}, u32[]{:S(2)}) collective-permute-start(bf16[1,1024]{1,0:T(2,128)(2,1)S(1)} %slice.16), channel_id=1, source_target_pairs={{0,1},{1,2},{2,3},{3,4},{4,5},{5,6},{6,7},{8,9},{9,10},{10,11},{11... | collective-permute-start | bytes 6152 | tf_op jit(solution)/shard_map/ppermute | solution.py:412
  6.7 14.8 %adapter_input.1 = (f32[128,128]{1,0:T(8,128)}, bf16[3,64,1024]{2,1,0:T(8,128)(2,1)}) custom-call(bf16[128,1024]{1,0:T(8,128)(2,1)} %refs_0_.9, bf16[1,1024]{1,0:T(2,128)(2,1)} %copy-done.27, f32[1,1024]{1,0:T(1,128)} %bitcast.4, f32[1024,128]{1,0:T(8,128)} %refs_3_.9, bf16[3,512,1024]{2,1,0:T(8,128)(2,1)} %refs_2_.9), custom_call_target="tpu_custom_call" | custom-call | bytes 5250000 | tf_op jit(solution)/shard_map/adapter_input/pallas_call | solution.py:438
  21.5 2.3 collective-permute-start.5
  29.7 3.4 %decay_and_states.1 = (f32[128,128]{1,0:T(8,128)}, bf16[128,128]{1,0:T(8,128)(2,1)}, f32[128,1024]{1,0:T(8,128)}, f32[1,1024]{1,0:T(1,128)}, f32[64,1024]{1,0:T(8,128)}, /*index=5*/bf16[136,1024]{1,0:T(8,128)(2,1)}) custom-call(f32[128,128]{1,0:T(8,128)} %get-tuple-element.86.refs_0_, f32[128,128]{1,0:T(8,128)} %copy-done.22, f32[128,128]{1,0:T(8,128)} %copy-done.24, ...), custom_call_target="tpu_custom_call" | custom-call | bytes 10500000 | tf_op jit(solution)/shard_map/decay_and_states/pallas_call | solution.py:456
  33.8 88.3 %inside_chunk.2 = (f32[128,512]{1,0:T(8,128)}, f32[128,512]{1,0:T(8,128)}, f32[128,512]{1,0:T(8,128)}, f32[128,512]{1,0:T(8,128)}, f32[128,512]{1,0:T(8,128)}, /...) custom-call(bf16[128,1024]{1,0:T(8,128)(2,1)} %refs_0_.8, bf16[128,1024]{1,0:T(8,128)(2,1)} %refs_1_.7, ...), custom_call_target="tpu_custom_call" | custom-call | bytes 14000000 | tf_op jit(solution)/shard_map/inside_chunk/pallas_call | solution.py:482
  127.8 2.6 %collective-permute-start.7 = (bf16[72,1024]{1,0:T(8,128)(2,1)}, bf16[72,1024]{1,0:T(8,128)(2,1)S(1)}, u32[]{:S(2)}, u32[]{:S(2)}) collective-permute-start(bf16[72,1024]{1,0:T(8,128)(2,1)} %get-tuple-element.117), channel_id=1, source_target_pairs={{0,4},{1,5},{2,6},{3,7},{4,0},{5,1},{6,2},{7,3},{8,12},{9,13},{10,... | collective-permute-start | bytes 442376 | tf_op jit(solution)/shard_map/ppermute | solution.py:417
  131.7 5.1 %inside_chunk.3 = (f32[128,512]{1,0:T(8,128)}, f32[128,512]{1,0:T(8,128)}, f32[128,512]{1,0:T(8,128)}, f32[128,512]{1,0:T(8,128)}, f32[128,512]{1,0:T(8,128)}, /*index=5*/f32[128,512]{1,0:T(8,128)}, f32[1,512]{1,0:T(1,128)}) custom-call(bf16[128,1024]{1,0:T(8,128)(2,1)} %refs_0_.8, bf16[128,1024]{1,0:T(8,128)(2,1)} %refs_1_.7, bf16[128,1024]{1,0:T(8,128)(2,1)} %refs_2_.8, ...), custom_call_target="tpu_custom_call" | custom-call | bytes 14000000 | tf_op jit(solution)/shard_map/inside_chunk/pallas_call | solution.py:482
  136.9 4.2 %collective-permute-done.7.refs_15_ = bf16[72,1024]{1,0:T(8,128)(2,1)S(1)} collective-permute-done((bf16[72,1024]{1,0:T(8,128)(2,1)}, bf16[72,1024]{1,0:T(8,128)(2,1)S(1)}, u32[]{:S(2)}, u32[]{:S(2)}) %collective-permute-start.7) | collective-permute-done | bytes 147488 | tf_op jit(solution)/shard_map/ppermute | solution.py:417
  141.8 2.8 %across_chunks.2 = (bf16[3,128,512]{2,1,0:T(8,128)(2,1)}, f32[128,512]{1,0:T(8,128)}, f32[128,512]{1,0:T(8,128)}, f32[1,512]{1,0:T(1,128)}) custom-call(bf16[128,1024]{1,0:T(8,128)(2,1)} %refs_0_.8, bf16[128,1024]{1,0:T(8,128)(2,1)} %refs_1_.7, bf16[128,1024]{1,0:T(8,128)(2,1)} %refs_2_.8, bf16[128,1024]{1,0:T(8,128)(2,1)} %refs_3_.8, ...), custom_call_target="tpu_custom_call" | custom-call | bytes 10500000 | tf_op jit(solution)/shard_map/across_chunks/pallas_call | solution.py:514
  144.6 3.7 %collective-permute-start.9 = (bf16[3,128,512]{2,1,0:T(8,128)(2,1)}, bf16[3,128,512]{2,1,0:T(8,128)(2,1)S(1)}, u32[]{:S(2)}, u32[]{:S(2)}) collective-permute-start(bf16[3,128,512]{2,1,0:T(8,128)(2,1)} %get-tuple-element.122.refs_0_), channel_id=1, source_target_pairs={{0,2},{1,3},{2,4},{3,5},{4,6},{5,7},{6,0},{7,1},{8,10},{9,11},{10,... | collective-permute-start | bytes 1179656 | tf_op jit(solution)/shard_map/ppermute | solution.py:417
  148.2 2.8 %across_chunks.3 = (bf16[3,128,512]{2,1,0:T(8,128)(2,1)}, f32[128,512]{1,0:T(8,128)}, f32[128,512]{1,0:T(8,128)}, f32[1,512]{1,0:T(1,128)}) custom-call(bf16[128,1024]{1,0:T(8,128)(2,1)} %refs_0_.8, bf16[128,1024]{1,0:T(8,128)(2,1)} %refs_1_.7, bf16[128,1024]{1,0:T(8,128)(2,1)} %refs_2_.8, bf16[128,1024]{1,0:T(8,128)(2,1)} %refs_3_.8, ...), custom_call_target="tpu_custom_call" | custom-call | bytes 10500000 | tf_op jit(solution)/shard_map/across_chunks/pallas_call | solution.py:514
  151.2 2.5 %decay_gradient.3 = (f32[128,512]{1,0:T(8,128)}, f32[1,512]{1,0:T(1,128)}, f32[128,128]{1,0:T(8,128)}) custom-call(f32[128,1024]{1,0:T(8,128)} %get-tuple-element.91.refs_4_.w, f32[128,512]{1,0:T(8,128)} %get-tuple-element.134.r_gr, f32[128,512]{1,0:T(8,128)} %get-tuple-element.135.k_gk, f32[1,512]{1,0:T(1,128)} %get-tuple-element.136.at_end, ...), custom_call_target="tpu_custom_call" | custom-call | bytes 7000000 | tf_op jit(solution)/shard_map/decay_gradient/pallas_call | solution.py:534
  153.7 2.4 decay_gradient.2
  157.0 2.5 %collective-permute-done.9.refs_1_ = bf16[3,128,512]{2,1,0:T(8,128)(2,1)S(1)} collective-permute-done((bf16[3,128,512]{2,1,0:T(8,128)(2,1)}, bf16[3,128,512]{2,1,0:T(8,128)(2,1)S(1)}, u32[]{:S(2)}, u32[]{:S(2)}) %collective-permute-start.9) | collective-permute-done | bytes 393248 | tf_op jit(solution)/shard_map/ppermute | solution.py:417
  161.2 6.9 %collective-permute-done.12.refs_4_ = bf16[3,128,512]{2,1,0:T(8,128)(2,1)} collective-permute-done((bf16[3,128,512]{2,1,0:T(8,128)(2,1)}, bf16[3,128,512]{2,1,0:T(8,128)(2,1)}, u32[]{:S(2)}, u32[]{:S(2)}) %collective-permute-start.12) | collective-permute-done | bytes 393248 | tf_op jit(solution)/shard_map/ppermute | solution.py:417
  169.4 3.8 %collective-permute-done.21.refs_7_ = f32[128,128]{1,0:T(8,128)S(1)} collective-permute-done((f32[128,128]{1,0:T(8,128)S(1)}, f32[128,128]{1,0:T(8,128)S(1)}, u32[]{:S(2)}, u32[]{:S(2)}) %collective-permute-start.21) | collective-permute-done | bytes 65568 | tf_op jit(solution)/shard_map/ppermute | solution.py:423
  173.8 3.0 %adapter_grads.1 = (bf16[272,512]{1,0:T(8,128)(2,1)}, bf16[272,512]{1,0:T(8,128)(2,1)}, f32[128,1024]{1,0:T(8,128)}) custom-call(bf16[128,1024]{1,0:T(8,128)(2,1)} %refs_0_.9, bf16[1,1024]{1,0:T(2,128)(2,1)} %copy-done.27, f32[1,1024]{1,0:T(1,128)} %bitcast.5, f32[1024,128]{1,0:T(8,128)} %refs_3_.9, f32[128,128]{1,0:T(8,128)} %get-tuple-element.149.refs_4_, ...), custom_call_target="tpu_custom_call" | custom-call | bytes 10500000 | tf_op jit(solution)/shard_map/adapter_grads/pallas_call | solution.py:552
  179.2 4.9 %collective-permute-done.13.refs_5_ = bf16[3,128,512]{2,1,0:T(8,128)(2,1)} collective-permute-done((bf16[3,128,512]{2,1,0:T(8,128)(2,1)}, bf16[3,128,512]{2,1,0:T(8,128)(2,1)}, u32[]{:S(2)}, u32[]{:S(2)}) %collective-permute-start.13) | collective-permute-done | bytes 393248 | tf_op jit(solution)/shard_map/ppermute | solution.py:417
  190.8 7.0 %projections.2 = (bf16[144,1024]{1,0:T(8,128)(2,1)S(1)}, bf16[144,1024]{1,0:T(8,128)(2,1)S(1)}, bf16[144,1024]{1,0:T(8,128)(2,1)S(1)}) custom-call(bf16[3,128,512]{2,1,0:T(8,128)(2,1)S(1)} %copy-done.5, bf16[3,128,512]{2,1,0:T(8,128)(2,1)S(1)} %copy-done.7, bf16[3,128,512]{2,1,0:T(8,128)(2,1)S(1)} %copy-done.10, bf16[3,128,512]{2,1,0:T(8,128)(2,1)S(1)} %copy-done.8, ...), custom_call_target="tpu_custom_call" | custom-call | bytes 17500000 | tf_op jit(solution)/shard_map/projections/pallas_call | solution.py:580
  200.9 5.0 %projections.3 = (bf16[144,1024]{1,0:T(8,128)(2,1)S(1)}, bf16[144,1024]{1,0:T(8,128)(2,1)S(1)}, bf16[144,1024]{1,0:T(8,128)(2,1)S(1)}, bf16[144,1024]{1,0:T(8,128)(2,1)S(1)}) custom-call(bf16[3,128,512]{2,1,0:T(8,128)(2,1)S(1)} %collective-permute-done.11.refs_0_, bf16[3,128,512]{2,1,0:T(8,128)(2,1)S(1)} %collective-permute-done.14.refs_1_, ...), custom_call_target="tpu_custom_call" | custom-call | bytes 17500000 | tf_op jit(solution)/shard_map/projections/pallas_call | solution.py:580
  209.9 4.8 %collective-permute-done.16 = bf16[144,1024]{1,0:T(8,128)(2,1)S(1)} collective-permute-done((bf16[144,1024]{1,0:T(8,128)(2,1)S(1)}, bf16[144,1024]{1,0:T(8,128)(2,1)S(1)}, u32[]{:S(2)}, u32[]{:S(2)}) %collective-permute-start.16) | collective-permute-done | bytes 294944 | tf_op jit(solution)/shard_map/ppermute | solution.py:423
  215.9 3.7 %collective-permute-done.18 = bf16[144,1024]{1,0:T(8,128)(2,1)S(1)} collective-permute-done((bf16[144,1024]{1,0:T(8,128)(2,1)S(1)}, bf16[144,1024]{1,0:T(8,128)(2,1)S(1)}, u32[]{:S(2)}, u32[]{:S(2)}) %collective-permute-start.18) | collective-permute-done | bytes 294944 | tf_op jit(solution)/shard_map/ppermute | solution.py:423
  219.9 4.6 %collective-permute-start.19 = (bf16[128,1024]{1,0:T(8,128)(2,1)S(1)}, bf16[128,1024]{1,0:T(8,128)(2,1)S(1)}, u32[]{:S(2)}, u32[]{:S(2)}) collective-permute-start(bf16[128,1024]{1,0:T(8,128)(2,1)S(1)} %slice.24), channel_id=1, source_target_pairs={{0,0},{1,1},{2,8},{3,9},{4,16},{5,17},{6,24},{7,25},{8,2},{9,3},{1... | collective-permute-start | bytes 786440 | tf_op jit(solution)/shard_map/ppermute | solution.py:627
  226.6 5.3 %collective-permute-start.28 = (f32[1,1024]{1,0:T(1,128)S(1)}, f32[1,1024]{1,0:T(1,128)S(1)}, u32[]{:S(2)}, u32[]{:S(2)}) collective-permute-start(f32[1,1024]{1,0:T(1,128)S(1)} %slice.22), channel_id=1, source_target_pairs={{1,0},{3,8},{5,16},{7,24},{8,1},{9,2},{10,9},{11,10},{12,17},{13,1... | collective-permute-start | bytes 12296 | tf_op jit(solution)/shard_map/ppermute | solution.py:628
  (120 shorter events, 48.2 us)
Async XLA Ops:
  21.5 12.3 %collective-permute-start.5 = (bf16[3,64,1024]{2,1,0:T(8,128)(2,1)}, bf16[3,64,1024]{2,1,0:T(8,128)(2,1)S(1)}, u32[]{:S(2)}, u32[]{:S(2)}) collective-permute-start(bf16[3,64,1024]{2,1,0:T(8,128)(2,1)} %get-tuple-element.90), channel_id=1, source_target_pairs={{0,1},{1,0},{2,3},{3,2},{4,5},{5,4},{6,7},{7,6},{8,9},{9,8},{10,11... | collective-permute-start | bytes 1179656 | tf_op jit(solution)/shard_map/ppermute | solution.py:420
  23.9 5.1 %collective-permute-start.2 = (f32[128,128]{1,0:T(8,128)}, f32[128,128]{1,0:T(8,128)S(1)}, u32[]{:S(2)}, u32[]{:S(2)}) collective-permute-start(f32[128,128]{1,0:T(8,128)} %get-tuple-element.86.refs_0_), channel_id=1, source_target_pairs={{0,16},{8,24},{16,0},{24,8},{1,17},{9,25},{17,1},{25,9},{2,18},{10... | collective-permute-start | bytes 196616 | tf_op jit(solution)/shard_map/ppermute | solution.py:423
  33.0 89.1 %collective-permute-start.4 = (bf16[136,1024]{1,0:T(8,128)(2,1)}, bf16[136,1024]{1,0:T(8,128)(2,1)S(1)}, u32[]{:S(2)}, u32[]{:S(2)}) collective-permute-start(bf16[136,1024]{1,0:T(8,128)(2,1)} %get-tuple-element.87.refs_0_), channel_id=1, source_target_pairs={{0,1},{1,0},{2,3},{3,2},{4,5},{5,4},{6,7},{7,6},{8,9},{9,8},{10,11... | collective-permute-start | bytes 835592 | tf_op jit(solution)/shard_map/ppermute | solution.py:420
  122.1 63.7 %collective-permute-start.15 = (bf16[3,448,1024]{2,1,0:T(8,128)(2,1)}, bf16[3,448,1024]{2,1,0:T(8,128)(2,1)}, u32[]{:S(2)}, u32[]{:S(2)}) collective-permute-start(bf16[3,448,1024]{2,1,0:T(8,128)(2,1)} %get-tuple-element.140), channel_id=1, source_target_pairs={{0,1},{1,0},{2,3},{3,2},{4,5},{5,4},{6,7},{7,6},{8,9},{9,8},{10,11... | collective-permute-start | bytes 8257544 | tf_op jit(solution)/shard_map/ppermute | solution.py:420
  126.2 10.7 %collective-permute-start.6 = (bf16[72,1024]{1,0:T(8,128)(2,1)}, bf16[72,1024]{1,0:T(8,128)(2,1)S(1)}, u32[]{:S(2)}, u32[]{:S(2)}) collective-permute-start(bf16[72,1024]{1,0:T(8,128)(2,1)} %get-tuple-element.116), channel_id=1, source_target_pairs={{0,2},{1,3},{2,4},{3,5},{4,6},{5,7},{6,0},{7,1},{8,10},{9,11},{10,... | collective-permute-start | bytes 442376 | tf_op jit(solution)/shard_map/ppermute | solution.py:417
  127.8 13.3 %collective-permute-start.7 = (bf16[72,1024]{1,0:T(8,128)(2,1)}, bf16[72,1024]{1,0:T(8,128)(2,1)S(1)}, u32[]{:S(2)}, u32[]{:S(2)}) collective-permute-start(bf16[72,1024]{1,0:T(8,128)(2,1)} %get-tuple-element.117), channel_id=1, source_target_pairs={{0,4},{1,5},{2,6},{3,7},{4,0},{5,1},{6,2},{7,3},{8,12},{9,13},{10,... | collective-permute-start | bytes 442376 | tf_op jit(solution)/shard_map/ppermute | solution.py:417
  130.4 10.7 %collective-permute-start.8 = (bf16[72,1024]{1,0:T(8,128)(2,1)}, bf16[72,1024]{1,0:T(8,128)(2,1)S(1)}, u32[]{:S(2)}, u32[]{:S(2)}) collective-permute-start(bf16[72,1024]{1,0:T(8,128)(2,1)} %get-tuple-element.118), channel_id=1, source_target_pairs={{0,6},{1,7},{2,0},{3,1},{4,2},{5,3},{6,4},{7,5},{8,14},{9,15},{10,... | collective-permute-start | bytes 442376 | tf_op jit(solution)/shard_map/ppermute | solution.py:417
  144.6 14.9 %collective-permute-start.9 = (bf16[3,128,512]{2,1,0:T(8,128)(2,1)}, bf16[3,128,512]{2,1,0:T(8,128)(2,1)S(1)}, u32[]{:S(2)}, u32[]{:S(2)}) collective-permute-start(bf16[3,128,512]{2,1,0:T(8,128)(2,1)} %get-tuple-element.122.refs_0_), channel_id=1, source_target_pairs={{0,2},{1,3},{2,4},{3,5},{4,6},{5,7},{6,0},{7,1},{8,10},{9,11},{10,... | collective-permute-start | bytes 1179656 | tf_op jit(solution)/shard_map/ppermute | solution.py:417
  151.1 17.0 %collective-permute-start.12 = (bf16[3,128,512]{2,1,0:T(8,128)(2,1)}, bf16[3,128,512]{2,1,0:T(8,128)(2,1)}, u32[]{:S(2)}, u32[]{:S(2)}) collective-permute-start(bf16[3,128,512]{2,1,0:T(8,128)(2,1)} %get-tuple-element.139.refs_3_), channel_id=1, source_target_pairs={{0,2},{1,3},{2,4},{3,5},{4,6},{5,7},{6,0},{7,1},{8,10},{9,11},{10,... | collective-permute-start | bytes 1179656 | tf_op jit(solution)/shard_map/ppermute | solution.py:417
  159.5 17.3 %collective-permute-start.10 = (bf16[3,128,512]{2,1,0:T(8,128)(2,1)S(1)}, bf16[3,128,512]{2,1,0:T(8,128)(2,1)S(1)}, u32[]{:S(2)}, u32[]{:S(2)}) collective-permute-start(bf16[3,128,512]{2,1,0:T(8,128)(2,1)S(1)} %collective-permute-done.9.refs_1_), channel_id=1, source_target_pairs={{0,2},{1,3},{2,4},{3,5},{4,6},{5,7},{6,0},{7,1},{8,10},{9,11},{10,... | collective-permute-start | bytes 1179656 | tf_op jit(solution)/shard_map/ppermute | solution.py:417
  161.2 8.3 %collective-permute-start.20 = (f32[128,128]{1,0:T(8,128)S(1)}, f32[128,128]{1,0:T(8,128)S(1)}, u32[]{:S(2)}, u32[]{:S(2)}) collective-permute-start(f32[128,128]{1,0:T(8,128)S(1)} %add.33.refs_5_), channel_id=1, source_target_pairs={{0,8},{8,16},{16,24},{24,0},{1,9},{9,17},{17,25},{25,1},{2,10},{10... | collective-permute-start | bytes 196616 | tf_op jit(solution)/shard_map/ppermute | solution.py:423
  168.0 16.0 %collective-permute-start.13 = (bf16[3,128,512]{2,1,0:T(8,128)(2,1)}, bf16[3,128,512]{2,1,0:T(8,128)(2,1)}, u32[]{:S(2)}, u32[]{:S(2)}) collective-permute-start(bf16[3,128,512]{2,1,0:T(8,128)(2,1)} %collective-permute-done.12.refs_4_), channel_id=1, source_target_pairs={{0,2},{1,3},{2,4},{3,5},{4,6},{5,7},{6,0},{7,1},{8,10},{9,11},{10,... | collective-permute-start | bytes 1179656 | tf_op jit(solution)/shard_map/ppermute | solution.py:417
  177.6 20.1 %collective-permute-start.23 = (bf16[272,512]{1,0:T(8,128)(2,1)}, bf16[272,512]{1,0:T(8,128)(2,1)S(1)}, u32[]{:S(2)}, u32[]{:S(2)}) collective-permute-start(bf16[272,512]{1,0:T(8,128)(2,1)} %get-tuple-element.158), channel_id=1, source_target_pairs={{0,1},{1,0},{2,3},{3,2},{4,5},{5,4},{6,7},{7,6},{8,9},{9,8},{10,11... | collective-permute-start | bytes 835592 | tf_op jit(solution)/shard_map/ppermute | solution.py:420
  178.8 21.3 %collective-permute-start.11 = (bf16[3,128,512]{2,1,0:T(8,128)(2,1)}, bf16[3,128,512]{2,1,0:T(8,128)(2,1)S(1)}, u32[]{:S(2)}, u32[]{:S(2)}) collective-permute-start(bf16[3,128,512]{2,1,0:T(8,128)(2,1)} %copy-done.9), channel_id=1, source_target_pairs={{0,2},{1,3},{2,4},{3,5},{4,6},{5,7},{6,0},{7,1},{8,10},{9,11},{10,... | collective-permute-start | bytes 1179656 | tf_op jit(solution)/shard_map/ppermute | solution.py:417
  184.0 16.9 %collective-permute-start.14 = (bf16[3,128,512]{2,1,0:T(8,128)(2,1)}, bf16[3,128,512]{2,1,0:T(8,128)(2,1)S(1)}, u32[]{:S(2)}, u32[]{:S(2)}) collective-permute-start(bf16[3,128,512]{2,1,0:T(8,128)(2,1)} %collective-permute-done.13.refs_5_), channel_id=1, source_target_pairs={{0,2},{1,3},{2,4},{3,5},{4,6},{5,7},{6,0},{7,1},{8,10},{9,11},{10,... | collective-permute-start | bytes 1179656 | tf_op jit(solution)/shard_map/ppermute | solution.py:417
  197.8 10.2 %collective-permute-start.24 = (bf16[272,512]{1,0:T(8,128)(2,1)S(1)}, bf16[272,512]{1,0:T(8,128)(2,1)S(1)}, u32[]{:S(2)}, u32[]{:S(2)}) collective-permute-start(bf16[272,512]{1,0:T(8,128)(2,1)S(1)} %add_convert_fusion.2), channel_id=1, source_target_pairs={{0,2},{1,3},{2,0},{3,1},{4,6},{5,7},{6,4},{7,5},{8,10},{9,11},{10,... | collective-permute-start | bytes 835592 | tf_op jit(solution)/shard_map/ppermute | solution.py:603
  206.0 8.8 %collective-permute-start.16 = (bf16[144,1024]{1,0:T(8,128)(2,1)S(1)}, bf16[144,1024]{1,0:T(8,128)(2,1)S(1)}, u32[]{:S(2)}, u32[]{:S(2)}) collective-permute-start(bf16[144,1024]{1,0:T(8,128)(2,1)S(1)} %get-tuple-element.146), channel_id=1, source_target_pairs={{0,8},{8,16},{16,24},{24,0},{1,9},{9,17},{17,25},{25,1},{2,10},{10... | collective-permute-start | bytes 884744 | tf_op jit(solution)/shard_map/ppermute | solution.py:423
  206.0 9.9 %collective-permute-start.17 = (bf16[144,1024]{1,0:T(8,128)(2,1)S(1)}, bf16[144,1024]{1,0:T(8,128)(2,1)S(1)}, u32[]{:S(2)}, u32[]{:S(2)}) collective-permute-start(bf16[144,1024]{1,0:T(8,128)(2,1)S(1)} %get-tuple-element.147), channel_id=1, source_target_pairs={{0,16},{8,24},{16,0},{24,8},{1,17},{9,25},{17,1},{25,9},{2,18},{10... | collective-permute-start | bytes 884744 | tf_op jit(solution)/shard_map/ppermute | solution.py:423
  206.6 13.1 %collective-permute-start.18 = (bf16[144,1024]{1,0:T(8,128)(2,1)S(1)}, bf16[144,1024]{1,0:T(8,128)(2,1)S(1)}, u32[]{:S(2)}, u32[]{:S(2)}) collective-permute-start(bf16[144,1024]{1,0:T(8,128)(2,1)S(1)} %get-tuple-element.148), channel_id=1, source_target_pairs={{0,24},{8,0},{16,8},{24,16},{1,25},{9,1},{17,9},{25,17},{2,26},{10... | collective-permute-start | bytes 884744 | tf_op jit(solution)/shard_map/ppermute | solution.py:423
  208.1 16.4 %collective-permute-start.25 = (bf16[272,512]{1,0:T(8,128)(2,1)S(1)}, bf16[272,512]{1,0:T(8,128)(2,1)S(1)}, u32[]{:S(2)}, u32[]{:S(2)}) collective-permute-start(bf16[272,512]{1,0:T(8,128)(2,1)S(1)} %add_convert_fusion.1), channel_id=1, source_target_pairs={{0,4},{1,5},{2,6},{3,7},{4,0},{5,1},{6,2},{7,3},{8,12},{9,13},{10,... | collective-permute-start | bytes 835592 | tf_op jit(solution)/shard_map/ppermute | solution.py:603
  219.9 17.6 %collective-permute-start.19 = (bf16[128,1024]{1,0:T(8,128)(2,1)S(1)}, bf16[128,1024]{1,0:T(8,128)(2,1)S(1)}, u32[]{:S(2)}, u32[]{:S(2)}) collective-permute-start(bf16[128,1024]{1,0:T(8,128)(2,1)S(1)} %slice.24), channel_id=1, source_target_pairs={{0,0},{1,1},{2,8},{3,9},{4,16},{5,17},{6,24},{7,25},{8,2},{9,3},{1... | collective-permute-start | bytes 786440 | tf_op jit(solution)/shard_map/ppermute | solution.py:627
  224.6 8.7 %collective-permute-start.26 = (bf16[272,512]{1,0:T(8,128)(2,1)S(1)}, bf16[272,512]{1,0:T(8,128)(2,1)S(1)}, u32[]{:S(2)}, u32[]{:S(2)}) collective-permute-start(bf16[272,512]{1,0:T(8,128)(2,1)S(1)} %add_convert_fusion.refs_0_), channel_id=1, source_target_pairs={{0,1},{1,0},{2,3},{3,2},{4,5},{5,4},{6,7},{7,6},{8,9},{9,8},{10,11... | collective-permute-start | bytes 835592 | tf_op jit(solution)/shard_map/ppermute | solution.py:420
  225.3 12.2 %collective-permute-start.27 = (f32[1,1024]{1,0:T(1,128)S(1)}, f32[1,1024]{1,0:T(1,128)S(1)}, u32[]{:S(2)}, u32[]{:S(2)}) collective-permute-start(f32[1,1024]{1,0:T(1,128)S(1)} %slice.19), channel_id=1, source_target_pairs={{1,0},{2,1},{3,2},{4,3},{5,4},{6,5},{7,6},{9,8},{10,9},{11,10},{12... | collective-permute-start | bytes 12296 | tf_op jit(solution)/shard_map/ppermute | solution.py:412
  226.6 11.4 %collective-permute-start.28 = (f32[1,1024]{1,0:T(1,128)S(1)}, f32[1,1024]{1,0:T(1,128)S(1)}, u32[]{:S(2)}, u32[]{:S(2)}) collective-permute-start(f32[1,1024]{1,0:T(1,128)S(1)} %slice.22), channel_id=1, source_target_pairs={{1,0},{3,8},{5,16},{7,24},{8,1},{9,2},{10,9},{11,10},{12,17},{13,1... | collective-permute-start | bytes 12296 | tf_op jit(solution)/shard_map/ppermute | solution.py:628
  (34 other events, 456.6 us)

commit v4 on v3

--- a/solution.py
+++ b/solution.py
@@ -97,15 +97,23 @@
     return features + mix[...] * (previous - features)
 
 
-def copy_rows(weights, piece, at, sem):
-    return pltpu.make_async_copy(weights.at[:, pl.ds(at, piece.shape[1])], piece, sem.at[0])
-
-
-def adapter_kernel(x, carried, mix, down, weights, pre, piece, sem):
-    copy = copy_rows(weights, piece, 0, sem)
-    copy.start()
+def copy_rows(weights, piece, at, stage, sem):
+    rows = pl.ds(at, piece.shape[1])
+    into = [pltpu.make_async_copy(weights.at[m, rows], stage.at[m], sem.at[m]) for m in range(3)]
+    out = [pltpu.make_async_copy(stage.at[m], piece.at[m], sem.at[3 + m]) for m in range(3)]
+    return into, out
+
+
+def adapter_kernel(x, carried, mix, down, weights, pre, piece, stage, sem):
+    into, out = copy_rows(weights, piece, 0, stage, sem)
+    for copy in into:
+        copy.start()
+    for first, second in zip(into, out):
+        first.wait()
+        second.start()
     pre[...] = mm3(mixed_input(x, carried, mix), down[...])
-    copy.wait()
+    for copy in out:
+        copy.wait()
 
 
 def decay_kernel(head, count, *refs):
@@ -164,16 +172,21 @@
 
 def inner_kernel(head, skip, r, k, v, dy, w, u, levels, sums, *refs):
     if skip:
-        weights, piece, sem = refs[0], refs[8], refs[9]
+        weights, piece, stage, sem = refs[0], refs[8], refs[9], refs[10]
         refs = refs[1:8]
+        into, out = copy_rows(weights, piece, skip, stage, sem)
+        at_last = pl.program_id(0) == pl.num_programs(0) - 1
 
         @pl.when(pl.program_id(0) == 0)
         def _():
-            copy_rows(weights, piece, skip, sem).start()
-
-        @pl.when(pl.program_id(0) == pl.num_programs(0) - 1)
+            for copy in into:
+                copy.start()
+
+        @pl.when(at_last)
         def _():
-            copy_rows(weights, piece, skip, sem).wait()
+            for first, second in zip(into, out):
+                first.wait()
+                second.start()
 
     gr_out, gk_out, gv_out, self_out, eb_out, ee_out, du_out = refs
     rows, width = r.shape
@@ -223,6 +236,12 @@
         gv_out[:, cols] = mm(scores_t.astype(BF16), dydy) + bonus * dyf
         self_out[:, cols] = own
         du_out[:, cols] = jnp.sum(rf * kf * own, 0, keepdims=True)
+    if skip:
+
+        @pl.when(at_last)
+        def _():
+            for copy in out:
+                copy.wait()
 
 
 def outer_kernel(
@@ -440,7 +459,7 @@
         in_specs=[vmem] * 4 + [anywhere],
         out_specs=[vmem, anywhere],
         out_shape=[shape((rows, rank)), shape((3, cut, cols), BF16)],
-        scratch_shapes=[pltpu.SemaphoreType.DMA((1,))],
+        scratch_shapes=[pltpu.VMEM((3, cut, cols), BF16), pltpu.SemaphoreType.DMA((6,))],
         compiler_params=params,
         cost_estimate=work(1.5),
         name="adapter_input",
@@ -486,7 +505,9 @@
             out_specs=[here] * 6 + [col_block(1)] + [anywhere] * extra,
             out_shape=[shape((rows, part_cols))] * 6 + [shape((1, part_cols))]
             + [shape((3, weight_rows - cut, cols), BF16)] * extra,
-            scratch_shapes=[pltpu.SemaphoreType.DMA((1,))] * extra,
+            scratch_shapes=[
+                pltpu.VMEM((3, weight_rows - cut, cols), BF16), pltpu.SemaphoreType.DMA((6,)),
+            ] * extra,
             compiler_params=params,
             cost_estimate=work(4),
             name="inside_chunk",

time: 240 us -> 148 us (0.62)
  Pallas kernels: 141 us -> 48.2 us
    pallas_call x2, Pallas kernels: 93.4 us -> 11.5 us  [inside(): pl.pallas_call(lambda *refs: inner_kernel(head, cut if extra else 0, *ref...]
    pallas_call x1, Pallas kernels: 14.8 us -> 3.52 us  [per_device(): pl.pallas_call(adapter_kernel, in_specs=[vmem] * 4 + [anywhere], out_spec...]
    ppermute x5, waiting for transfers between devices: 1.35 us -> 4.47 us  [partner(): return lax.ppermute(a, 'seq', [(i, i ^ 1) for i in range(n_seq)])]
  transfers between devices with their start and end apart: 29 -> 29, of which waited for: 15 -> 17; matrix products, arithmetic and copies ran while one was open for 1% -> 1% of each run, Pallas kernels for 53% -> 30%
where the time goes in v4:
time: 148 us; the launch traced here: 147 us
  Pallas kernels  48.2 us (33%)
  waiting for transfers between devices  42.6 us (29%)
  starting transfers between devices  41.3 us (28%)
  local copies, waits for them, and re-layouts  12 us (8%)
  other arithmetic  2.14 us (1%)
    ppermute x9, waiting for transfers between devices, around(): lax.ppermute(a, 'seq', [(i, (i + inner * step) % n_seq) for i in range(n_...  18 us
    ppermute x9, waiting for transfers between devices, head_shift(): lax.ppermute(a, 'head', [(i, (i + d) % n_head) for i in range(n_head)])  16.6 us
    ppermute x9, starting transfers between devices, around(): lax.ppermute(a, 'seq', [(i, (i + inner * step) % n_seq) for i in range(n_...  14.5 us
    pallas_call x2, Pallas kernels, project(): pl.pallas_call(lambda *refs: project_kernel(count, ring, final, *refs), i...  12 us
    pallas_call x2, Pallas kernels, inside(): pl.pallas_call(lambda *refs: inner_kernel(head, cut if extra else 0, *ref...  11.5 us
    unnamed x58, local copies, waits for them, and re-layouts  10.5 us
    pallas_call x2, Pallas kernels, per_device(): pl.pallas_call(lambda *refs: outer_kernel(head, ring, *refs), grid=(steps...  5.64 us
    ppermute x5, starting transfers between devices, partner(): return lax.ppermute(a, 'seq', [(i, i ^ 1) for i in range(n_seq)])  4.93 us
  transfers between devices with their start and end apart: 29, of which 17 were waited for; matrix products, arithmetic and copies ran while one was open for 1% of the time, Pallas kernels for 30%

profile of v4, /device:TPU:4, one launch (start us, length us, event | category | flops | bytes accessed | tf_op | source)
XLA Modules:
  0.0 147.2 jit_solution(1302944973216547129)
XLA Ops:
  1.4 3.4 %collective-permute-start = (bf16[1,1024]{1,0:T(2,128)(2,1)S(1)}, bf16[1,1024]{1,0:T(2,128)(2,1)S(1)}, u32[]{:S(2)}, u32[]{:S(2)}) collective-permute-start(bf16[1,1024]{1,0:T(2,128)(2,1)S(1)} %slice.16), channel_id=1, source_target_pairs={{0,1},{1,2},{2,3},{3,4},{4,5},{5,6},{6,7},{8,9},{9,10},{10,11},{11... | collective-permute-start | bytes 6152 | tf_op jit(solution)/shard_map/ppermute | solution.py:431
  6.7 3.5 %adapter_input.1 = (f32[128,128]{1,0:T(8,128)}, bf16[3,64,1024]{2,1,0:T(8,128)(2,1)}) custom-call(bf16[128,1024]{1,0:T(8,128)(2,1)} %refs_0_.9, bf16[1,1024]{1,0:T(2,128)(2,1)} %copy-done.27, f32[1,1024]{1,0:T(1,128)} %bitcast.4, f32[1024,128]{1,0:T(8,128)} %refs_3_.9, bf16[3,512,1024]{2,1,0:T(8,128)(2,1)} %refs_2_.9), custom_call_target="tpu_custom_call" | custom-call | bytes 5250000 | tf_op jit(solution)/shard_map/adapter_input/pallas_call | solution.py:457
  18.4 3.4 %decay_and_states.1 = (f32[128,128]{1,0:T(8,128)}, bf16[128,128]{1,0:T(8,128)(2,1)}, f32[128,1024]{1,0:T(8,128)}, f32[1,1024]{1,0:T(1,128)}, f32[64,1024]{1,0:T(8,128)}, /*index=5*/bf16[136,1024]{1,0:T(8,128)(2,1)}) custom-call(f32[128,128]{1,0:T(8,128)} %get-tuple-element.86.refs_0_, f32[128,128]{1,0:T(8,128)} %copy-done.22, f32[128,128]{1,0:T(8,128)} %copy-done.24, ...), custom_call_target="tpu_custom_call" | custom-call | bytes 10500000 | tf_op jit(solution)/shard_map/decay_and_states/pallas_call | solution.py:475
  22.5 6.4 %inside_chunk.2 = (f32[128,512]{1,0:T(8,128)}, f32[128,512]{1,0:T(8,128)}, f32[128,512]{1,0:T(8,128)}, f32[128,512]{1,0:T(8,128)}, f32[128,512]{1,0:T(8,128)}, /...) custom-call(bf16[128,1024]{1,0:T(8,128)(2,1)} %refs_0_.8, bf16[128,1024]{1,0:T(8,128)(2,1)} %refs_1_.7, ...), custom_call_target="tpu_custom_call" | custom-call | bytes 14000000 | tf_op jit(solution)/shard_map/inside_chunk/pallas_call | solution.py:501
  28.9 2.6 %collective-permute-done.4.refs_1_.refs_13_ = bf16[136,1024]{1,0:T(8,128)(2,1)S(1)} collective-permute-done((bf16[136,1024]{1,0:T(8,128)(2,1)}, bf16[136,1024]{1,0:T(8,128)(2,1)S(1)}, u32[]{:S(2)}, u32[]{:S(2)}) %collective-permute-start.4) | collective-permute-done | bytes 278560 | tf_op jit(solution)/shard_map/ppermute | solution.py:439
  36.6 2.6 %collective-permute-start.7 = (bf16[72,1024]{1,0:T(8,128)(2,1)}, bf16[72,1024]{1,0:T(8,128)(2,1)S(1)}, u32[]{:S(2)}, u32[]{:S(2)}) collective-permute-start(bf16[72,1024]{1,0:T(8,128)(2,1)} %get-tuple-element.117), channel_id=1, source_target_pairs={{0,4},{1,5},{2,6},{3,7},{4,0},{5,1},{6,2},{7,3},{8,12},{9,13},{10,... | collective-permute-start | bytes 442376 | tf_op jit(solution)/shard_map/ppermute | solution.py:436
  40.5 5.1 %inside_chunk.3 = (f32[128,512]{1,0:T(8,128)}, f32[128,512]{1,0:T(8,128)}, f32[128,512]{1,0:T(8,128)}, f32[128,512]{1,0:T(8,128)}, f32[128,512]{1,0:T(8,128)}, /*index=5*/f32[128,512]{1,0:T(8,128)}, f32[1,512]{1,0:T(1,128)}) custom-call(bf16[128,1024]{1,0:T(8,128)(2,1)} %refs_0_.8, bf16[128,1024]{1,0:T(8,128)(2,1)} %refs_1_.7, bf16[128,1024]{1,0:T(8,128)(2,1)} %refs_2_.8, ...), custom_call_target="tpu_custom_call" | custom-call | bytes 14000000 | tf_op jit(solution)/shard_map/inside_chunk/pallas_call | solution.py:501
  45.6 3.4 %collective-permute-done.7.refs_15_ = bf16[72,1024]{1,0:T(8,128)(2,1)S(1)} collective-permute-done((bf16[72,1024]{1,0:T(8,128)(2,1)}, bf16[72,1024]{1,0:T(8,128)(2,1)S(1)}, u32[]{:S(2)}, u32[]{:S(2)}) %collective-permute-start.7) | collective-permute-done | bytes 147488 | tf_op jit(solution)/shard_map/ppermute | solution.py:436
  49.7 2.8 %across_chunks.2 = (bf16[3,128,512]{2,1,0:T(8,128)(2,1)}, f32[128,512]{1,0:T(8,128)}, f32[128,512]{1,0:T(8,128)}, f32[1,512]{1,0:T(1,128)}) custom-call(bf16[128,1024]{1,0:T(8,128)(2,1)} %refs_0_.8, bf16[128,1024]{1,0:T(8,128)(2,1)} %refs_1_.7, bf16[128,1024]{1,0:T(8,128)(2,1)} %refs_2_.8, bf16[128,1024]{1,0:T(8,128)(2,1)} %refs_3_.8, ...), custom_call_target="tpu_custom_call" | custom-call | bytes 10500000 | tf_op jit(solution)/shard_map/across_chunks/pallas_call | solution.py:535
  52.5 3.6 %collective-permute-start.9 = (bf16[3,128,512]{2,1,0:T(8,128)(2,1)}, bf16[3,128,512]{2,1,0:T(8,128)(2,1)S(1)}, u32[]{:S(2)}, u32[]{:S(2)}) collective-permute-start(bf16[3,128,512]{2,1,0:T(8,128)(2,1)} %get-tuple-element.122.refs_0_), channel_id=1, source_target_pairs={{0,2},{1,3},{2,4},{3,5},{4,6},{5,7},{6,0},{7,1},{8,10},{9,11},{10,... | collective-permute-start | bytes 1179656 | tf_op jit(solution)/shard_map/ppermute | solution.py:436
  56.2 2.8 %across_chunks.3 = (bf16[3,128,512]{2,1,0:T(8,128)(2,1)}, f32[128,512]{1,0:T(8,128)}, f32[128,512]{1,0:T(8,128)}, f32[1,512]{1,0:T(1,128)}) custom-call(bf16[128,1024]{1,0:T(8,128)(2,1)} %refs_0_.8, bf16[128,1024]{1,0:T(8,128)(2,1)} %refs_1_.7, bf16[128,1024]{1,0:T(8,128)(2,1)} %refs_2_.8, bf16[128,1024]{1,0:T(8,128)(2,1)} %refs_3_.8, ...), custom_call_target="tpu_custom_call" | custom-call | bytes 10500000 | tf_op jit(solution)/shard_map/across_chunks/pallas_call | solution.py:535
  59.1 2.5 %decay_gradient.3 = (f32[128,512]{1,0:T(8,128)}, f32[1,512]{1,0:T(1,128)}, f32[128,128]{1,0:T(8,128)}) custom-call(f32[128,1024]{1,0:T(8,128)} %get-tuple-element.91.refs_4_.w, f32[128,512]{1,0:T(8,128)} %get-tuple-element.134.r_gr, f32[128,512]{1,0:T(8,128)} %get-tuple-element.135.k_gk, f32[1,512]{1,0:T(1,128)} %get-tuple-element.136.at_end, ...), custom_call_target="tpu_custom_call" | custom-call | bytes 7000000 | tf_op jit(solution)/shard_map/decay_gradient/pallas_call | solution.py:555
  64.9 2.6 %collective-permute-done.9.refs_1_ = bf16[3,128,512]{2,1,0:T(8,128)(2,1)S(1)} collective-permute-done((bf16[3,128,512]{2,1,0:T(8,128)(2,1)}, bf16[3,128,512]{2,1,0:T(8,128)(2,1)S(1)}, u32[]{:S(2)}, u32[]{:S(2)}) %collective-permute-start.9) | collective-permute-done | bytes 393248 | tf_op jit(solution)/shard_map/ppermute | solution.py:436
  69.1 6.9 %collective-permute-done.12.refs_4_ = bf16[3,128,512]{2,1,0:T(8,128)(2,1)} collective-permute-done((bf16[3,128,512]{2,1,0:T(8,128)(2,1)}, bf16[3,128,512]{2,1,0:T(8,128)(2,1)}, u32[]{:S(2)}, u32[]{:S(2)}) %collective-permute-start.12) | collective-permute-done | bytes 393248 | tf_op jit(solution)/shard_map/ppermute | solution.py:436
  77.4 3.8 %collective-permute-done.21.refs_7_ = f32[128,128]{1,0:T(8,128)S(1)} collective-permute-done((f32[128,128]{1,0:T(8,128)S(1)}, f32[128,128]{1,0:T(8,128)S(1)}, u32[]{:S(2)}, u32[]{:S(2)}) %collective-permute-start.21) | collective-permute-done | bytes 65568 | tf_op jit(solution)/shard_map/ppermute | solution.py:442
  81.8 3.0 %adapter_grads.1 = (bf16[272,512]{1,0:T(8,128)(2,1)}, bf16[272,512]{1,0:T(8,128)(2,1)}, f32[128,1024]{1,0:T(8,128)}) custom-call(bf16[128,1024]{1,0:T(8,128)(2,1)} %refs_0_.9, bf16[1,1024]{1,0:T(2,128)(2,1)} %copy-done.27, f32[1,1024]{1,0:T(1,128)} %bitcast.5, f32[1024,128]{1,0:T(8,128)} %refs_3_.9, f32[128,128]{1,0:T(8,128)} %get-tuple-element.149.refs_4_, ...), custom_call_target="tpu_custom_call" | custom-call | bytes 10500000 | tf_op jit(solution)/shard_map/adapter_grads/pallas_call | solution.py:573
  86.9 4.3 %collective-permute-done.13.refs_5_ = bf16[3,128,512]{2,1,0:T(8,128)(2,1)} collective-permute-done((bf16[3,128,512]{2,1,0:T(8,128)(2,1)}, bf16[3,128,512]{2,1,0:T(8,128)(2,1)}, u32[]{:S(2)}, u32[]{:S(2)}) %collective-permute-start.13) | collective-permute-done | bytes 393248 | tf_op jit(solution)/shard_map/ppermute | solution.py:436
  91.2 2.5 %collective-permute-start.14 = (bf16[3,128,512]{2,1,0:T(8,128)(2,1)}, bf16[3,128,512]{2,1,0:T(8,128)(2,1)S(1)}, u32[]{:S(2)}, u32[]{:S(2)}) collective-permute-start(bf16[3,128,512]{2,1,0:T(8,128)(2,1)} %collective-permute-done.13.refs_5_), channel_id=1, source_target_pairs={{0,2},{1,3},{2,4},{3,5},{4,6},{5,7},{6,0},{7,1},{8,10},{9,11},{10,... | collective-permute-start | bytes 1179656 | tf_op jit(solution)/shard_map/ppermute | solution.py:436
  99.3 7.0 %projections.2 = (bf16[144,1024]{1,0:T(8,128)(2,1)S(1)}, bf16[144,1024]{1,0:T(8,128)(2,1)S(1)}, bf16[144,1024]{1,0:T(8,128)(2,1)S(1)}) custom-call(bf16[3,128,512]{2,1,0:T(8,128)(2,1)S(1)} %copy-done.5, bf16[3,128,512]{2,1,0:T(8,128)(2,1)S(1)} %copy-done.7, bf16[3,128,512]{2,1,0:T(8,128)(2,1)S(1)} %copy-done.10, bf16[3,128,512]{2,1,0:T(8,128)(2,1)S(1)} %copy-done.8, ...), custom_call_target="tpu_custom_call" | custom-call | bytes 17500000 | tf_op jit(solution)/shard_map/projections/pallas_call | solution.py:601
  108.8 5.0 %projections.3 = (bf16[144,1024]{1,0:T(8,128)(2,1)S(1)}, bf16[144,1024]{1,0:T(8,128)(2,1)S(1)}, bf16[144,1024]{1,0:T(8,128)(2,1)S(1)}, bf16[144,1024]{1,0:T(8,128)(2,1)S(1)}) custom-call(bf16[3,128,512]{2,1,0:T(8,128)(2,1)S(1)} %collective-permute-done.11.refs_0_, bf16[3,128,512]{2,1,0:T(8,128)(2,1)S(1)} %collective-permute-done.14.refs_1_, ...), custom_call_target="tpu_custom_call" | custom-call | bytes 17500000 | tf_op jit(solution)/shard_map/projections/pallas_call | solution.py:601
  117.8 4.7 %collective-permute-done.16 = bf16[144,1024]{1,0:T(8,128)(2,1)S(1)} collective-permute-done((bf16[144,1024]{1,0:T(8,128)(2,1)S(1)}, bf16[144,1024]{1,0:T(8,128)(2,1)S(1)}, u32[]{:S(2)}, u32[]{:S(2)}) %collective-permute-start.16) | collective-permute-done | bytes 294944 | tf_op jit(solution)/shard_map/ppermute | solution.py:442
  123.8 3.7 %collective-permute-done.18 = bf16[144,1024]{1,0:T(8,128)(2,1)S(1)} collective-permute-done((bf16[144,1024]{1,0:T(8,128)(2,1)S(1)}, bf16[144,1024]{1,0:T(8,128)(2,1)S(1)}, u32[]{:S(2)}, u32[]{:S(2)}) %collective-permute-start.18) | collective-permute-done | bytes 294944 | tf_op jit(solution)/shard_map/ppermute | solution.py:442
  127.7 4.8 %collective-permute-start.19 = (bf16[128,1024]{1,0:T(8,128)(2,1)S(1)}, bf16[128,1024]{1,0:T(8,128)(2,1)S(1)}, u32[]{:S(2)}, u32[]{:S(2)}) collective-permute-start(bf16[128,1024]{1,0:T(8,128)(2,1)S(1)} %slice.24), channel_id=1, source_target_pairs={{0,0},{1,1},{2,8},{3,9},{4,16},{5,17},{6,24},{7,25},{8,2},{9,3},{1... | collective-permute-start | bytes 786440 | tf_op jit(solution)/shard_map/ppermute | solution.py:648
  135.4 4.4 %collective-permute-start.28 = (f32[1,1024]{1,0:T(1,128)S(1)}, f32[1,1024]{1,0:T(1,128)S(1)}, u32[]{:S(2)}, u32[]{:S(2)}) collective-permute-start(f32[1,1024]{1,0:T(1,128)S(1)} %slice.22), channel_id=1, source_target_pairs={{1,0},{3,8},{5,16},{7,24},{8,1},{9,2},{10,9},{11,10},{12,17},{13,1... | collective-permute-start | bytes 12296 | tf_op jit(solution)/shard_map/ppermute | solution.py:649
  (120 shorter events, 51.5 us)
Async XLA Ops:
  10.2 12.3 %collective-permute-start.5 = (bf16[3,64,1024]{2,1,0:T(8,128)(2,1)}, bf16[3,64,1024]{2,1,0:T(8,128)(2,1)S(1)}, u32[]{:S(2)}, u32[]{:S(2)}) collective-permute-start(bf16[3,64,1024]{2,1,0:T(8,128)(2,1)} %get-tuple-element.90), channel_id=1, source_target_pairs={{0,1},{1,0},{2,3},{3,2},{4,5},{5,4},{6,7},{7,6},{8,9},{9,8},{10,11... | collective-permute-start | bytes 1179656 | tf_op jit(solution)/shard_map/ppermute | solution.py:439
  12.6 5.1 %collective-permute-start.2 = (f32[128,128]{1,0:T(8,128)}, f32[128,128]{1,0:T(8,128)S(1)}, u32[]{:S(2)}, u32[]{:S(2)}) collective-permute-start(f32[128,128]{1,0:T(8,128)} %get-tuple-element.86.refs_0_), channel_id=1, source_target_pairs={{0,16},{8,24},{16,0},{24,8},{1,17},{9,25},{17,1},{25,9},{2,18},{10... | collective-permute-start | bytes 196616 | tf_op jit(solution)/shard_map/ppermute | solution.py:442
  21.7 9.7 %collective-permute-start.4 = (bf16[136,1024]{1,0:T(8,128)(2,1)}, bf16[136,1024]{1,0:T(8,128)(2,1)S(1)}, u32[]{:S(2)}, u32[]{:S(2)}) collective-permute-start(bf16[136,1024]{1,0:T(8,128)(2,1)} %get-tuple-element.87.refs_0_), channel_id=1, source_target_pairs={{0,1},{1,0},{2,3},{3,2},{4,5},{5,4},{6,7},{7,6},{8,9},{9,8},{10,11... | collective-permute-start | bytes 835592 | tf_op jit(solution)/shard_map/ppermute | solution.py:439
  31.4 62.8 %collective-permute-start.15 = (bf16[3,448,1024]{2,1,0:T(8,128)(2,1)}, bf16[3,448,1024]{2,1,0:T(8,128)(2,1)}, u32[]{:S(2)}, u32[]{:S(2)}) collective-permute-start(bf16[3,448,1024]{2,1,0:T(8,128)(2,1)} %get-tuple-element.140), channel_id=1, source_target_pairs={{0,1},{1,0},{2,3},{3,2},{4,5},{5,4},{6,7},{7,6},{8,9},{9,8},{10,11... | collective-permute-start | bytes 8257544 | tf_op jit(solution)/shard_map/ppermute | solution.py:439
  34.2 11.4 %collective-permute-start.6 = (bf16[72,1024]{1,0:T(8,128)(2,1)}, bf16[72,1024]{1,0:T(8,128)(2,1)S(1)}, u32[]{:S(2)}, u32[]{:S(2)}) collective-permute-start(bf16[72,1024]{1,0:T(8,128)(2,1)} %get-tuple-element.116), channel_id=1, source_target_pairs={{0,2},{1,3},{2,4},{3,5},{4,6},{5,7},{6,0},{7,1},{8,10},{9,11},{10,... | collective-permute-start | bytes 442376 | tf_op jit(solution)/shard_map/ppermute | solution.py:436
  36.6 12.5 %collective-permute-start.7 = (bf16[72,1024]{1,0:T(8,128)(2,1)}, bf16[72,1024]{1,0:T(8,128)(2,1)S(1)}, u32[]{:S(2)}, u32[]{:S(2)}) collective-permute-start(bf16[72,1024]{1,0:T(8,128)(2,1)} %get-tuple-element.117), channel_id=1, source_target_pairs={{0,4},{1,5},{2,6},{3,7},{4,0},{5,1},{6,2},{7,3},{8,12},{9,13},{10,... | collective-permute-start | bytes 442376 | tf_op jit(solution)/shard_map/ppermute | solution.py:436
  39.1 9.9 %collective-permute-start.8 = (bf16[72,1024]{1,0:T(8,128)(2,1)}, bf16[72,1024]{1,0:T(8,128)(2,1)S(1)}, u32[]{:S(2)}, u32[]{:S(2)}) collective-permute-start(bf16[72,1024]{1,0:T(8,128)(2,1)} %get-tuple-element.118), channel_id=1, source_target_pairs={{0,6},{1,7},{2,0},{3,1},{4,2},{5,3},{6,4},{7,5},{8,14},{9,15},{10,... | collective-permute-start | bytes 442376 | tf_op jit(solution)/shard_map/ppermute | solution.py:436
  52.5 15.0 %collective-permute-start.9 = (bf16[3,128,512]{2,1,0:T(8,128)(2,1)}, bf16[3,128,512]{2,1,0:T(8,128)(2,1)S(1)}, u32[]{:S(2)}, u32[]{:S(2)}) collective-permute-start(bf16[3,128,512]{2,1,0:T(8,128)(2,1)} %get-tuple-element.122.refs_0_), channel_id=1, source_target_pairs={{0,2},{1,3},{2,4},{3,5},{4,6},{5,7},{6,0},{7,1},{8,10},{9,11},{10,... | collective-permute-start | bytes 1179656 | tf_op jit(solution)/shard_map/ppermute | solution.py:436
  59.0 17.0 %collective-permute-start.12 = (bf16[3,128,512]{2,1,0:T(8,128)(2,1)}, bf16[3,128,512]{2,1,0:T(8,128)(2,1)}, u32[]{:S(2)}, u32[]{:S(2)}) collective-permute-start(bf16[3,128,512]{2,1,0:T(8,128)(2,1)} %get-tuple-element.139.refs_3_), channel_id=1, source_target_pairs={{0,2},{1,3},{2,4},{3,5},{4,6},{5,7},{6,0},{7,1},{8,10},{9,11},{10,... | collective-permute-start | bytes 1179656 | tf_op jit(solution)/shard_map/ppermute | solution.py:436
  67.5 17.3 %collective-permute-start.10 = (bf16[3,128,512]{2,1,0:T(8,128)(2,1)S(1)}, bf16[3,128,512]{2,1,0:T(8,128)(2,1)S(1)}, u32[]{:S(2)}, u32[]{:S(2)}) collective-permute-start(bf16[3,128,512]{2,1,0:T(8,128)(2,1)S(1)} %collective-permute-done.9.refs_1_), channel_id=1, source_target_pairs={{0,2},{1,3},{2,4},{3,5},{4,6},{5,7},{6,0},{7,1},{8,10},{9,11},{10,... | collective-permute-start | bytes 1179656 | tf_op jit(solution)/shard_map/ppermute | solution.py:436
  69.1 8.2 %collective-permute-start.20 = (f32[128,128]{1,0:T(8,128)S(1)}, f32[128,128]{1,0:T(8,128)S(1)}, u32[]{:S(2)}, u32[]{:S(2)}) collective-permute-start(f32[128,128]{1,0:T(8,128)S(1)} %add.33.refs_5_), channel_id=1, source_target_pairs={{0,8},{8,16},{16,24},{24,0},{1,9},{9,17},{17,25},{25,1},{2,10},{10... | collective-permute-start | bytes 196616 | tf_op jit(solution)/shard_map/ppermute | solution.py:442
  76.1 15.2 %collective-permute-start.13 = (bf16[3,128,512]{2,1,0:T(8,128)(2,1)}, bf16[3,128,512]{2,1,0:T(8,128)(2,1)}, u32[]{:S(2)}, u32[]{:S(2)}) collective-permute-start(bf16[3,128,512]{2,1,0:T(8,128)(2,1)} %collective-permute-done.12.refs_4_), channel_id=1, source_target_pairs={{0,2},{1,3},{2,4},{3,5},{4,6},{5,7},{6,0},{7,1},{8,10},{9,11},{10,... | collective-permute-start | bytes 1179656 | tf_op jit(solution)/shard_map/ppermute | solution.py:436
  85.6 20.7 %collective-permute-start.23 = (bf16[272,512]{1,0:T(8,128)(2,1)}, bf16[272,512]{1,0:T(8,128)(2,1)S(1)}, u32[]{:S(2)}, u32[]{:S(2)}) collective-permute-start(bf16[272,512]{1,0:T(8,128)(2,1)} %get-tuple-element.158), channel_id=1, source_target_pairs={{0,1},{1,0},{2,3},{3,2},{4,5},{5,4},{6,7},{7,6},{8,9},{9,8},{10,11... | collective-permute-start | bytes 835592 | tf_op jit(solution)/shard_map/ppermute | solution.py:439
  86.6 21.4 %collective-permute-start.11 = (bf16[3,128,512]{2,1,0:T(8,128)(2,1)}, bf16[3,128,512]{2,1,0:T(8,128)(2,1)S(1)}, u32[]{:S(2)}, u32[]{:S(2)}) collective-permute-start(bf16[3,128,512]{2,1,0:T(8,128)(2,1)} %copy-done.9), channel_id=1, source_target_pairs={{0,2},{1,3},{2,4},{3,5},{4,6},{5,7},{6,0},{7,1},{8,10},{9,11},{10,... | collective-permute-start | bytes 1179656 | tf_op jit(solution)/shard_map/ppermute | solution.py:436
  91.2 17.5 %collective-permute-start.14 = (bf16[3,128,512]{2,1,0:T(8,128)(2,1)}, bf16[3,128,512]{2,1,0:T(8,128)(2,1)S(1)}, u32[]{:S(2)}, u32[]{:S(2)}) collective-permute-start(bf16[3,128,512]{2,1,0:T(8,128)(2,1)} %collective-permute-done.13.refs_5_), channel_id=1, source_target_pairs={{0,2},{1,3},{2,4},{3,5},{4,6},{5,7},{6,0},{7,1},{8,10},{9,11},{10,... | collective-permute-start | bytes 1179656 | tf_op jit(solution)/shard_map/ppermute | solution.py:436
  106.4 9.5 %collective-permute-start.24 = (bf16[272,512]{1,0:T(8,128)(2,1)S(1)}, bf16[272,512]{1,0:T(8,128)(2,1)S(1)}, u32[]{:S(2)}, u32[]{:S(2)}) collective-permute-start(bf16[272,512]{1,0:T(8,128)(2,1)S(1)} %add_convert_fusion.2), channel_id=1, source_target_pairs={{0,2},{1,3},{2,0},{3,1},{4,6},{5,7},{6,4},{7,5},{8,10},{9,11},{10,... | collective-permute-start | bytes 835592 | tf_op jit(solution)/shard_map/ppermute | solution.py:624
  113.8 8.8 %collective-permute-start.16 = (bf16[144,1024]{1,0:T(8,128)(2,1)S(1)}, bf16[144,1024]{1,0:T(8,128)(2,1)S(1)}, u32[]{:S(2)}, u32[]{:S(2)}) collective-permute-start(bf16[144,1024]{1,0:T(8,128)(2,1)S(1)} %get-tuple-element.146), channel_id=1, source_target_pairs={{0,8},{8,16},{16,24},{24,0},{1,9},{9,17},{17,25},{25,1},{2,10},{10... | collective-permute-start | bytes 884744 | tf_op jit(solution)/shard_map/ppermute | solution.py:442
  113.9 9.9 %collective-permute-start.17 = (bf16[144,1024]{1,0:T(8,128)(2,1)S(1)}, bf16[144,1024]{1,0:T(8,128)(2,1)S(1)}, u32[]{:S(2)}, u32[]{:S(2)}) collective-permute-start(bf16[144,1024]{1,0:T(8,128)(2,1)S(1)} %get-tuple-element.147), channel_id=1, source_target_pairs={{0,16},{8,24},{16,0},{24,8},{1,17},{9,25},{17,1},{25,9},{2,18},{10... | collective-permute-start | bytes 884744 | tf_op jit(solution)/shard_map/ppermute | solution.py:442
  114.4 13.1 %collective-permute-start.18 = (bf16[144,1024]{1,0:T(8,128)(2,1)S(1)}, bf16[144,1024]{1,0:T(8,128)(2,1)S(1)}, u32[]{:S(2)}, u32[]{:S(2)}) collective-permute-start(bf16[144,1024]{1,0:T(8,128)(2,1)S(1)} %get-tuple-element.148), channel_id=1, source_target_pairs={{0,24},{8,0},{16,8},{24,16},{1,25},{9,1},{17,9},{25,17},{2,26},{10... | collective-permute-start | bytes 884744 | tf_op jit(solution)/shard_map/ppermute | solution.py:442
  115.9 16.6 %collective-permute-start.25 = (bf16[272,512]{1,0:T(8,128)(2,1)S(1)}, bf16[272,512]{1,0:T(8,128)(2,1)S(1)}, u32[]{:S(2)}, u32[]{:S(2)}) collective-permute-start(bf16[272,512]{1,0:T(8,128)(2,1)S(1)} %add_convert_fusion.1), channel_id=1, source_target_pairs={{0,4},{1,5},{2,6},{3,7},{4,0},{5,1},{6,2},{7,3},{8,12},{9,13},{10,... | collective-permute-start | bytes 835592 | tf_op jit(solution)/shard_map/ppermute | solution.py:624
  127.7 18.2 %collective-permute-start.19 = (bf16[128,1024]{1,0:T(8,128)(2,1)S(1)}, bf16[128,1024]{1,0:T(8,128)(2,1)S(1)}, u32[]{:S(2)}, u32[]{:S(2)}) collective-permute-start(bf16[128,1024]{1,0:T(8,128)(2,1)S(1)} %slice.24), channel_id=1, source_target_pairs={{0,0},{1,1},{2,8},{3,9},{4,16},{5,17},{6,24},{7,25},{8,2},{9,3},{1... | collective-permute-start | bytes 786440 | tf_op jit(solution)/shard_map/ppermute | solution.py:648
  132.6 8.7 %collective-permute-start.26 = (bf16[272,512]{1,0:T(8,128)(2,1)S(1)}, bf16[272,512]{1,0:T(8,128)(2,1)S(1)}, u32[]{:S(2)}, u32[]{:S(2)}) collective-permute-start(bf16[272,512]{1,0:T(8,128)(2,1)S(1)} %add_convert_fusion.refs_0_), channel_id=1, source_target_pairs={{0,1},{1,0},{2,3},{3,2},{4,5},{5,4},{6,7},{7,6},{8,9},{9,8},{10,11... | collective-permute-start | bytes 835592 | tf_op jit(solution)/shard_map/ppermute | solution.py:439
  134.1 11.8 %collective-permute-start.27 = (f32[1,1024]{1,0:T(1,128)S(1)}, f32[1,1024]{1,0:T(1,128)S(1)}, u32[]{:S(2)}, u32[]{:S(2)}) collective-permute-start(f32[1,1024]{1,0:T(1,128)S(1)} %slice.19), channel_id=1, source_target_pairs={{1,0},{2,1},{3,2},{4,3},{5,4},{6,5},{7,6},{9,8},{10,9},{11,10},{12... | collective-permute-start | bytes 12296 | tf_op jit(solution)/shard_map/ppermute | solution.py:431
  135.4 11.0 %collective-permute-start.28 = (f32[1,1024]{1,0:T(1,128)S(1)}, f32[1,1024]{1,0:T(1,128)S(1)}, u32[]{:S(2)}, u32[]{:S(2)}) collective-permute-start(f32[1,1024]{1,0:T(1,128)S(1)} %slice.22), channel_id=1, source_target_pairs={{1,0},{3,8},{5,16},{7,24},{8,1},{9,2},{10,9},{11,10},{12,17},{13,1... | collective-permute-start | bytes 12296 | tf_op jit(solution)/shard_map/ppermute | solution.py:649
  (34 other events, 272.2 us)

commit v5 on v4

--- a/solution.py
+++ b/solution.py
@@ -10,6 +10,7 @@
 BF16 = jnp.bfloat16
 PAIR = 128
 VMEM = 56 * 2**20
+SMALL = 16 * 2**20
 NN = (((1,), (0,)), ((), ()))
 NT = (((1,), (1,)), ((), ()))
 TN = (((0,), (0,)), ((), ()))
@@ -306,6 +307,8 @@
     down_grad = mm3(mid.T, mixed_input(x, carried, mix))
     rank, half = mid.shape[1], x.shape[1] // 2
     wide = (8, half)
+    for ref in (keep, send):
+        ref[...] = jnp.zeros_like(ref)
     late = position()[0] == 1
 
     def choose(low, high, at, size):
@@ -319,19 +322,33 @@
         choose(jnp.broadcast_to(low, wide), jnp.broadcast_to(high, wide), 2 * rank + at, 8)
 
 
-def finish_kernel(rank, mine, theirs, up, down, base, du):
-    late = position()[0] == 1
+def split_kernel(ring, keep, got, *refs):
+    outs, total = refs[:-1], refs[-1]
+    total[...] = keep[...].astype(F32) + got[...].astype(F32)
+    z, chunk = position()[1], outs[0].shape[0]
+    for d, out in enumerate(outs):
+        at = pl.multiple_of(lax.rem(z + d, ring) * chunk, 8)
+        out[...] = total[pl.ds(at, chunk)].astype(out.dtype)
+
+
+def finish_kernel(rank, ring, mine, theirs, up, down, base, du, full):
+    x, z, _ = position()
+    late = x == 1
     half = mine.shape[1]
+    chunk = mine.shape[0] // ring
     a, b = mine[...].astype(F32), theirs[...].astype(F32)
-    for at, value in ((0, jnp.where(late, b, a)), (half, jnp.where(late, a, b))):
-        here = slice(at, at + half)
-        up[:, here] = value[:rank]
-        down[here] = value[rank : 2 * rank].T
-        for ref, row in ((base, 2 * rank), (du, 2 * rank + 8)):
-            size = ref.shape[1]
-            for i in range(half // size):
-                to = at // size + i
-                ref[to : to + 1] = value[row : row + 1, i * size : (i + 1) * size]
+    low, high = jnp.where(late, b, a), jnp.where(late, a, b)
+    for q in range(ring):
+        to = pl.ds(pl.multiple_of(lax.rem(z - q + ring, ring) * chunk, 8), chunk)
+        here = slice(q * chunk, (q + 1) * chunk)
+        full[to, :half] = low[here]
+        full[to, half:] = high[here]
+    up[...] = full[:rank]
+    down[...] = full[rank : 2 * rank].T
+    for ref, row in ((base, 2 * rank), (du, 2 * rank + 8)):
+        size = ref.shape[1]
+        for i in range(ref.shape[0]):
+            ref[i : i + 1] = full[row : row + 1, i * size : (i + 1) * size]
 
 
 def project_kernel(count, ring, final, *refs):
@@ -420,6 +437,7 @@
     block = min(part_cols, 2 * PAIR)
     r, k, v, dy = receptance, key_act, value_act, attention_result_sensitivity
     params = pltpu.CompilerParams(vmem_limit_bytes=VMEM)
+    small = pltpu.CompilerParams(vmem_limit_bytes=SMALL)
 
     def shape(s, t=F32):
         return jax.ShapeDtypeStruct(s, t)
@@ -568,12 +586,13 @@
         mid_parts.append(mid_grad)
     mid_grad = sum(mid_parts)
 
+    chunk = -(-(2 * rank + 16) // (8 * ring)) * 8
     mids = head_parts(mid_grad)
     dus = [part[6] for part in inner_parts]
     keep, send, grad_in = pl.pallas_call(
         lambda *refs: middle_kernel(n_head, *refs),
         in_specs=[vmem] * (5 + n_head + 3 * parts),
-        out_shape=[shape((2 * rank + 16, part_cols), BF16)] * 2 + [shape((rows, cols))],
+        out_shape=[shape((ring * chunk, part_cols), BF16)] * 2 + [shape((rows, cols))],
         compiler_params=params,
         cost_estimate=work(3),
         name="adapter_grads",
@@ -584,11 +603,9 @@
     lows, highs = [projs[0]], [projs[1]]
     for step in range(ring - 1):
         low, high = lows[-1], highs[-1]
-        lows.append(around(after_that(low, mid_grad) if step == 1 else low, 1))
+        ready = [(), (mid_grad,), (keep,)][step] if step < 3 else ()
+        lows.append(around(after_that(low, *ready), 1))
         highs.append(around(high, 1))
-
-    def add(a, b):
-        return (a.astype(F32) + b.astype(F32)).astype(BF16)
 
     got = partner(after_that(send, lows[2]))
 
@@ -600,7 +617,8 @@
         count, final = len(low), len(done) > 0
         return pl.pallas_call(
             lambda *refs: project_kernel(count, ring, final, *refs),
-            in_specs=[anywhere] * (2 * count + 3) + [vmem] * (1 + len(done)),
+            in_specs=[anywhere if final else pl.BlockSpec(memory_space=pltpu.HBM)] * (2 * count)
+            + [anywhere] * 3 + [vmem] * (1 + len(done)),
             out_shape=[shape((tall, cols), BF16)] * (ring if final else count),
             scratch_shapes=[
                 pltpu.VMEM((3, count * rows, part_cols), BF16),
@@ -617,20 +635,27 @@
 
     done = project(lows[:-1], highs[:-1])
     sends = project(lows[-1:], highs[-1:], done)
-    token_sums = add(keep, after_that(got, *done))
-    b = 1
-    while b < ring:
-        route = [(i, ((i // inner) ^ b) * inner + i % inner) for i in range(n_seq)]
-        got = lax.ppermute(token_sums, "seq", route)
-        token_sums = add(token_sums, after_that(got, sends) if b == 1 else got)
-        b *= 2
+    chunks = pl.pallas_call(
+        lambda *refs: split_kernel(ring, *refs),
+        out_shape=[shape((chunk, part_cols))] + [shape((chunk, part_cols), BF16)] * (ring - 1),
+        scratch_shapes=[pltpu.VMEM((ring * chunk, part_cols), F32)],
+        compiler_params=small,
+        cost_estimate=work(2),
+        name="token_chunks",
+    )(keep, after_that(got, *done))
+    mine = chunks[0]
+    for d in range(1, ring):
+        mine = mine + after_that(around(chunks[d], d), *sends).astype(F32)
+    mine = mine.astype(BF16)
+    mine = jnp.concatenate([mine] + [around(mine, q) for q in range(1, ring)], 0)
     up_grad, down_grad, base_grad, du = pl.pallas_call(
-        lambda *refs: finish_kernel(rank, *refs),
-                out_shape=[shape((rank, cols)), shape((cols, rank)), shape((pairs, PAIR)), shape((heads, head))],
-        compiler_params=params,
+        lambda *refs: finish_kernel(rank, ring, *refs),
+        out_shape=[shape((rank, cols)), shape((cols, rank)), shape((pairs, PAIR)), shape((heads, head))],
+        scratch_shapes=[pltpu.VMEM((ring * chunk, cols), F32)],
+        compiler_params=small,
         cost_estimate=work(2),
         name="token_sums",
-    )(token_sums, partner(token_sums))
+    )(mine, partner(mine))
 
     total = sends[0].astype(F32)
     for d in range(1, n_head):

time: 148 us -> 150 us (1.014)
  waiting for transfers between devices: 42.6 us -> 46.6 us
    ppermute x9 -> x15, waiting for transfers between devices: 18 us -> 28 us  [around(): lax.ppermute(a, 'seq', [(i, (i + inner * step) % n_seq) for i in range(n_...]
    ppermute x9, waiting for transfers between devices: 16.6 us -> 8.42 us  [head_shift(): lax.ppermute(a, 'head', [(i, (i + d) % n_head) for i in range(n_head)])]
    ppermute x9 -> x15, starting transfers between devices: 14.5 us -> 20.2 us  [around(): lax.ppermute(a, 'seq', [(i, (i + inner * step) % n_seq) for i in range(n_...]
    ppermute x1, waiting for transfers between devices: 1.75 us -> 5.59 us  [per_device(): summed = lax.ppermute(total[:rows].astype(BF16), ('head', 'seq'), swap)]
    ppermute x2 -> x0, starting transfers between devices: 3.59 us -> none  [per_device(): got = lax.ppermute(token_sums, 'seq', route)]
    ppermute x1, starting transfers between devices: 4.77 us -> 2.43 us  [per_device(): summed = lax.ppermute(total[:rows].astype(BF16), ('head', 'seq'), swap)]
    ppermute x5, waiting for transfers between devices: 4.47 us -> 2.56 us  [partner(): return lax.ppermute(a, 'seq', [(i, i ^ 1) for i in range(n_seq)])]
    unnamed x58 -> x54, local copies, waits for them, and re-layouts: 10.5 us -> 9.12 us
  transfers between devices with their start and end apart: 29 -> 33, of which waited for: 17 -> 16; matrix products, arithmetic and copies ran while one was open for 1% -> 1% of each run, Pallas kernels for 30% -> 29%
where the time goes in v5:
time: 150 us; the launch traced here: 149 us
  Pallas kernels  46.8 us (31%)
  waiting for transfers between devices  46.6 us (31%)
  starting transfers between devices  42.4 us (28%)
  local copies, waits for them, and re-layouts  10.6 us (7%)
  other arithmetic  1.99 us (1%)
    ppermute x15, waiting for transfers between devices, around(): lax.ppermute(a, 'seq', [(i, (i + inner * step) % n_seq) for i in range(n_...  28 us
    ppermute x15, starting transfers between devices, around(): lax.ppermute(a, 'seq', [(i, (i + inner * step) % n_seq) for i in range(n_...  20.2 us
    pallas_call x2, Pallas kernels, inside(): pl.pallas_call(lambda *refs: inner_kernel(head, cut if extra else 0, *ref...  11.5 us
    pallas_call x2, Pallas kernels, project(): pl.pallas_call(lambda *refs: project_kernel(count, ring, final, *refs), i...  11.3 us
    unnamed x54, local copies, waits for them, and re-layouts  9.12 us
    ppermute x9, waiting for transfers between devices, head_shift(): lax.ppermute(a, 'head', [(i, (i + d) % n_head) for i in range(n_head)])  8.42 us
    pallas_call x2, Pallas kernels, per_device(): pl.pallas_call(lambda *refs: outer_kernel(head, ring, *refs), grid=(steps...  5.66 us
    ppermute x1, waiting for transfers between devices, per_device(): summed = lax.ppermute(total[:rows].astype(BF16), ('head', 'seq'), swap)  5.59 us
  transfers between devices with their start and end apart: 33, of which 16 were waited for; matrix products, arithmetic and copies ran while one was open for 1% of the time, Pallas kernels for 29%

profile of v5, /device:TPU:4, one launch (start us, length us, event | category | flops | bytes accessed | tf_op | source)
XLA Modules:
  0.0 149.4 jit_solution(315646944455149855)
XLA Ops:
  1.4 3.4 %collective-permute-start = (bf16[1,1024]{1,0:T(2,128)(2,1)S(1)}, bf16[1,1024]{1,0:T(2,128)(2,1)S(1)}, u32[]{:S(2)}, u32[]{:S(2)}) collective-permute-start(bf16[1,1024]{1,0:T(2,128)(2,1)S(1)} %slice.16), channel_id=1, source_target_pairs={{0,1},{1,2},{2,3},{3,4},{4,5},{5,6},{6,7},{8,9},{9,10},{10,11},{11... | collective-permute-start | bytes 6152 | tf_op jit(solution)/shard_map/ppermute | solution.py:449
  6.7 3.5 %adapter_input.1 = (f32[128,128]{1,0:T(8,128)}, bf16[3,64,1024]{2,1,0:T(8,128)(2,1)}) custom-call(bf16[128,1024]{1,0:T(8,128)(2,1)} %refs_0_.9, bf16[1,1024]{1,0:T(2,128)(2,1)} %copy-done.25, f32[1,1024]{1,0:T(1,128)} %bitcast.4, f32[1024,128]{1,0:T(8,128)} %refs_3_.9, bf16[3,512,1024]{2,1,0:T(8,128)(2,1)} %refs_2_.9), custom_call_target="tpu_custom_call" | custom-call | bytes 5250000 | tf_op jit(solution)/shard_map/adapter_input/pallas_call | solution.py:475
  18.4 3.4 %decay_and_states.1 = (f32[128,128]{1,0:T(8,128)}, bf16[128,128]{1,0:T(8,128)(2,1)}, f32[128,1024]{1,0:T(8,128)}, f32[1,1024]{1,0:T(1,128)}, f32[64,1024]{1,0:T(8,128)}, /*index=5*/bf16[136,1024]{1,0:T(8,128)(2,1)}) custom-call(f32[128,128]{1,0:T(8,128)} %get-tuple-element.93.refs_0_, f32[128,128]{1,0:T(8,128)} %copy-done.20, f32[128,128]{1,0:T(8,128)} %copy-done.22, ...), custom_call_target="tpu_custom_call" | custom-call | bytes 10500000 | tf_op jit(solution)/shard_map/decay_and_states/pallas_call | solution.py:493
  22.5 6.4 %inside_chunk.2 = (f32[128,512]{1,0:T(8,128)}, f32[128,512]{1,0:T(8,128)}, f32[128,512]{1,0:T(8,128)}, f32[128,512]{1,0:T(8,128)}, f32[128,512]{1,0:T(8,128)}, /...) custom-call(bf16[128,1024]{1,0:T(8,128)(2,1)} %refs_0_.8, bf16[128,1024]{1,0:T(8,128)(2,1)} %refs_1_.7, ...), custom_call_target="tpu_custom_call" | custom-call | bytes 14000000 | tf_op jit(solution)/shard_map/inside_chunk/pallas_call | solution.py:519
  28.9 2.6 %collective-permute-done.4.refs_1_.refs_13_ = bf16[136,1024]{1,0:T(8,128)(2,1)S(1)} collective-permute-done((bf16[136,1024]{1,0:T(8,128)(2,1)}, bf16[136,1024]{1,0:T(8,128)(2,1)S(1)}, u32[]{:S(2)}, u32[]{:S(2)}) %collective-permute-start.4) | collective-permute-done | bytes 278560 | tf_op jit(solution)/shard_map/ppermute | solution.py:457
  36.6 2.6 %collective-permute-start.7 = (bf16[72,1024]{1,0:T(8,128)(2,1)}, bf16[72,1024]{1,0:T(8,128)(2,1)S(1)}, u32[]{:S(2)}, u32[]{:S(2)}) collective-permute-start(bf16[72,1024]{1,0:T(8,128)(2,1)} %get-tuple-element.124), channel_id=1, source_target_pairs={{0,4},{1,5},{2,6},{3,7},{4,0},{5,1},{6,2},{7,3},{8,12},{9,13},{10,... | collective-permute-start | bytes 442376 | tf_op jit(solution)/shard_map/ppermute | solution.py:454
  40.5 5.1 %inside_chunk.3 = (f32[128,512]{1,0:T(8,128)}, f32[128,512]{1,0:T(8,128)}, f32[128,512]{1,0:T(8,128)}, f32[128,512]{1,0:T(8,128)}, f32[128,512]{1,0:T(8,128)}, /*index=5*/f32[128,512]{1,0:T(8,128)}, f32[1,512]{1,0:T(1,128)}) custom-call(bf16[128,1024]{1,0:T(8,128)(2,1)} %refs_0_.8, bf16[128,1024]{1,0:T(8,128)(2,1)} %refs_1_.7, bf16[128,1024]{1,0:T(8,128)(2,1)} %refs_2_.8, ...), custom_call_target="tpu_custom_call" | custom-call | bytes 14000000 | tf_op jit(solution)/shard_map/inside_chunk/pallas_call | solution.py:519
  45.7 3.4 %collective-permute-done.7.refs_15_ = bf16[72,1024]{1,0:T(8,128)(2,1)S(1)} collective-permute-done((bf16[72,1024]{1,0:T(8,128)(2,1)}, bf16[72,1024]{1,0:T(8,128)(2,1)S(1)}, u32[]{:S(2)}, u32[]{:S(2)}) %collective-permute-start.7) | collective-permute-done | bytes 147488 | tf_op jit(solution)/shard_map/ppermute | solution.py:454
  49.8 2.8 %across_chunks.2 = (bf16[3,128,512]{2,1,0:T(8,128)(2,1)}, f32[128,512]{1,0:T(8,128)}, f32[128,512]{1,0:T(8,128)}, f32[1,512]{1,0:T(1,128)}) custom-call(bf16[128,1024]{1,0:T(8,128)(2,1)} %refs_0_.8, bf16[128,1024]{1,0:T(8,128)(2,1)} %refs_1_.7, bf16[128,1024]{1,0:T(8,128)(2,1)} %refs_2_.8, bf16[128,1024]{1,0:T(8,128)(2,1)} %refs_3_.8, ...), custom_call_target="tpu_custom_call" | custom-call | bytes 10500000 | tf_op jit(solution)/shard_map/across_chunks/pallas_call | solution.py:553
  52.6 3.6 %collective-permute-start.9 = (bf16[3,128,512]{2,1,0:T(8,128)(2,1)}, bf16[3,128,512]{2,1,0:T(8,128)(2,1)S(1)}, u32[]{:S(2)}, u32[]{:S(2)}) collective-permute-start(bf16[3,128,512]{2,1,0:T(8,128)(2,1)} %get-tuple-element.129.refs_0_), channel_id=1, source_target_pairs={{0,2},{1,3},{2,4},{3,5},{4,6},{5,7},{6,0},{7,1},{8,10},{9,11},{10,... | collective-permute-start | bytes 1179656 | tf_op jit(solution)/shard_map/ppermute | solution.py:454
  56.2 2.9 %across_chunks.3 = (bf16[3,128,512]{2,1,0:T(8,128)(2,1)}, f32[128,512]{1,0:T(8,128)}, f32[128,512]{1,0:T(8,128)}, f32[1,512]{1,0:T(1,128)}) custom-call(bf16[128,1024]{1,0:T(8,128)(2,1)} %refs_0_.8, bf16[128,1024]{1,0:T(8,128)(2,1)} %refs_1_.7, bf16[128,1024]{1,0:T(8,128)(2,1)} %refs_2_.8, bf16[128,1024]{1,0:T(8,128)(2,1)} %refs_3_.8, ...), custom_call_target="tpu_custom_call" | custom-call | bytes 10500000 | tf_op jit(solution)/shard_map/across_chunks/pallas_call | solution.py:553
  59.2 2.6 %decay_gradient.3 = (f32[128,512]{1,0:T(8,128)}, f32[1,512]{1,0:T(1,128)}, f32[128,128]{1,0:T(8,128)}) custom-call(f32[128,1024]{1,0:T(8,128)} %get-tuple-element.98.refs_4_.w, f32[128,512]{1,0:T(8,128)} %get-tuple-element.141.r_gr, f32[128,512]{1,0:T(8,128)} %get-tuple-element.142.k_gk, f32[1,512]{1,0:T(1,128)} %get-tuple-element.143.at_end, ...), custom_call_target="tpu_custom_call" | custom-call | bytes 7000000 | tf_op jit(solution)/shard_map/decay_gradient/pallas_call | solution.py:573
  65.0 2.5 %collective-permute-done.9.refs_1_ = bf16[3,128,512]{2,1,0:T(8,128)(2,1)S(1)} collective-permute-done((bf16[3,128,512]{2,1,0:T(8,128)(2,1)}, bf16[3,128,512]{2,1,0:T(8,128)(2,1)S(1)}, u32[]{:S(2)}, u32[]{:S(2)}) %collective-permute-start.9) | collective-permute-done | bytes 393248 | tf_op jit(solution)/shard_map/ppermute | solution.py:454
  69.2 6.8 %collective-permute-done.15.refs_4_ = bf16[3,128,512]{2,1,0:T(8,128)(2,1)S(1)} collective-permute-done((bf16[3,128,512]{2,1,0:T(8,128)(2,1)}, bf16[3,128,512]{2,1,0:T(8,128)(2,1)S(1)}, u32[]{:S(2)}, u32[]{:S(2)}) %collective-permute-start.15) | collective-permute-done | bytes 393248 | tf_op jit(solution)/shard_map/ppermute | solution.py:454
  77.3 3.3 %collective-permute-done.11.refs_6_ = f32[128,128]{1,0:T(8,128)S(1)} collective-permute-done((f32[128,128]{1,0:T(8,128)S(1)}, f32[128,128]{1,0:T(8,128)S(1)}, u32[]{:S(2)}, u32[]{:S(2)}) %collective-permute-start.11) | collective-permute-done | bytes 65568 | tf_op jit(solution)/shard_map/ppermute | solution.py:460
  83.2 3.0 %adapter_grads.1 = (bf16[288,512]{1,0:T(8,128)(2,1)}, bf16[288,512]{1,0:T(8,128)(2,1)}, f32[128,1024]{1,0:T(8,128)}) custom-call(bf16[128,1024]{1,0:T(8,128)(2,1)} %refs_0_.9, bf16[1,1024]{1,0:T(2,128)(2,1)} %copy-done.25, f32[1,1024]{1,0:T(1,128)} %bitcast.5, f32[1024,128]{1,0:T(8,128)} %refs_3_.9, f32[128,128]{1,0:T(8,128)} %get-tuple-element.146.refs_4_, ...), custom_call_target="tpu_custom_call" | custom-call | bytes 10500000 | tf_op jit(solution)/shard_map/adapter_grads/pallas_call | solution.py:592
  86.3 4.9 %collective-permute-done.16.refs_5_ = bf16[3,128,512]{2,1,0:T(8,128)(2,1)} collective-permute-done((bf16[3,128,512]{2,1,0:T(8,128)(2,1)S(1)}, bf16[3,128,512]{2,1,0:T(8,128)(2,1)}, u32[]{:S(2)}, u32[]{:S(2)}) %collective-permute-start.16) | collective-permute-done | bytes 393248 | tf_op jit(solution)/shard_map/ppermute | solution.py:454
  91.2 2.6 %collective-permute-start.17 = (bf16[3,128,512]{2,1,0:T(8,128)(2,1)}, bf16[3,128,512]{2,1,0:T(8,128)(2,1)}, u32[]{:S(2)}, u32[]{:S(2)}) collective-permute-start(bf16[3,128,512]{2,1,0:T(8,128)(2,1)} %collective-permute-done.16.refs_5_), channel_id=1, source_target_pairs={{0,2},{1,3},{2,4},{3,5},{4,6},{5,7},{6,0},{7,1},{8,10},{9,11},{10,... | collective-permute-start | bytes 1179656 | tf_op jit(solution)/shard_map/ppermute | solution.py:454
  99.8 7.0 %projections.2 = (bf16[144,1024]{1,0:T(8,128)(2,1)S(1)}, bf16[144,1024]{1,0:T(8,128)(2,1)S(1)}, bf16[144,1024]{1,0:T(8,128)(2,1)S(1)}) custom-call(bf16[3,128,512]{2,1,0:T(8,128)(2,1)S(1)} %copy-done.5, bf16[3,128,512]{2,1,0:T(8,128)(2,1)S(1)} %copy-done.7, bf16[3,128,512]{2,1,0:T(8,128)(2,1)} %collective-permute-done.10.refs_2_, ...), custom_call_target="tpu_custom_call" | custom-call | bytes 17500000 | tf_op jit(solution)/shard_map/projections/pallas_call | solution.py:618
  107.2 3.5 %collective-permute-start.25 = (bf16[72,512]{1,0:T(8,128)(2,1)S(1)}, bf16[72,512]{1,0:T(8,128)(2,1)S(1)}, u32[]{:S(2)}, u32[]{:S(2)}) collective-permute-start(bf16[72,512]{1,0:T(8,128)(2,1)S(1)} %get-tuple-element.171), channel_id=1, source_target_pairs={{0,4},{1,5},{2,6},{3,7},{4,0},{5,1},{6,2},{7,3},{8,12},{9,13},{10,... | collective-permute-start | bytes 221192 | tf_op jit(solution)/shard_map/ppermute | solution.py:454
  111.9 4.3 %projections.3 = (bf16[144,1024]{1,0:T(8,128)(2,1)S(1)}, bf16[144,1024]{1,0:T(8,128)(2,1)S(1)}, bf16[144,1024]{1,0:T(8,128)(2,1)S(1)}, bf16[144,1024]{1,0:T(8,128)(2,1)S(1)}) custom-call(bf16[3,128,512]{2,1,0:T(8,128)(2,1)} %collective-permute-done.14.refs_0_, bf16[3,128,512]{2,1,0:T(8,128)(2,1)} %collective-permute-done.17.refs_1_, ...), custom_call_target="tpu_custom_call" | custom-call | bytes 17500000 | tf_op jit(solution)/shard_map/projections/pallas_call | solution.py:618
  119.4 6.0 %collective-permute-done.27 = bf16[72,512]{1,0:T(8,128)(2,1)S(1)} collective-permute-done((bf16[72,512]{1,0:T(8,128)(2,1)S(1)}, bf16[72,512]{1,0:T(8,128)(2,1)S(1)}, u32[]{:S(2)}, u32[]{:S(2)}) %collective-permute-start.27) | collective-permute-done | bytes 73760 | tf_op jit(solution)/shard_map/ppermute | solution.py:454
  135.4 5.5 %collective-permute-start.32 = (f32[1,1024]{1,0:T(1,128)S(1)}, f32[1,1024]{1,0:T(1,128)S(1)}, u32[]{:S(2)}, u32[]{:S(2)}) collective-permute-start(f32[1,1024]{1,0:T(1,128)S(1)} %slice.22), channel_id=1, source_target_pairs={{1,0},{3,8},{5,16},{7,24},{8,1},{9,2},{10,9},{11,10},{12,17},{13,1... | collective-permute-start | bytes 12296 | tf_op jit(solution)/shard_map/ppermute | solution.py:674
  142.3 5.6 %collective-permute-done.22 = bf16[128,1024]{1,0:T(8,128)(2,1)S(1)} collective-permute-done((bf16[128,1024]{1,0:T(8,128)(2,1)S(1)}, bf16[128,1024]{1,0:T(8,128)(2,1)S(1)}, u32[]{:S(2)}, u32[]{:S(2)}) %collective-permute-start.22) | collective-permute-done | bytes 262176 | tf_op jit(solution)/shard_map/ppermute | solution.py:673
  (124 shorter events, 51.2 us)
Async XLA Ops:
  10.2 12.3 %collective-permute-start.5 = (bf16[3,64,1024]{2,1,0:T(8,128)(2,1)}, bf16[3,64,1024]{2,1,0:T(8,128)(2,1)S(1)}, u32[]{:S(2)}, u32[]{:S(2)}) collective-permute-start(bf16[3,64,1024]{2,1,0:T(8,128)(2,1)} %get-tuple-element.97), channel_id=1, source_target_pairs={{0,1},{1,0},{2,3},{3,2},{4,5},{5,4},{6,7},{7,6},{8,9},{9,8},{10,11... | collective-permute-start | bytes 1179656 | tf_op jit(solution)/shard_map/ppermute | solution.py:457
  21.8 9.7 %collective-permute-start.4 = (bf16[136,1024]{1,0:T(8,128)(2,1)}, bf16[136,1024]{1,0:T(8,128)(2,1)S(1)}, u32[]{:S(2)}, u32[]{:S(2)}) collective-permute-start(bf16[136,1024]{1,0:T(8,128)(2,1)} %get-tuple-element.94.refs_0_), channel_id=1, source_target_pairs={{0,1},{1,0},{2,3},{3,2},{4,5},{5,4},{6,7},{7,6},{8,9},{9,8},{10,11... | collective-permute-start | bytes 835592 | tf_op jit(solution)/shard_map/ppermute | solution.py:457
  31.5 63.3 %collective-permute-start.18 = (bf16[3,448,1024]{2,1,0:T(8,128)(2,1)}, bf16[3,448,1024]{2,1,0:T(8,128)(2,1)}, u32[]{:S(2)}, u32[]{:S(2)}) collective-permute-start(bf16[3,448,1024]{2,1,0:T(8,128)(2,1)} %get-tuple-element.156), channel_id=1, source_target_pairs={{0,1},{1,0},{2,3},{3,2},{4,5},{5,4},{6,7},{7,6},{8,9},{9,8},{10,11... | collective-permute-start | bytes 8257544 | tf_op jit(solution)/shard_map/ppermute | solution.py:457
  34.3 11.3 %collective-permute-start.6 = (bf16[72,1024]{1,0:T(8,128)(2,1)}, bf16[72,1024]{1,0:T(8,128)(2,1)S(1)}, u32[]{:S(2)}, u32[]{:S(2)}) collective-permute-start(bf16[72,1024]{1,0:T(8,128)(2,1)} %get-tuple-element.123), channel_id=1, source_target_pairs={{0,2},{1,3},{2,4},{3,5},{4,6},{5,7},{6,0},{7,1},{8,10},{9,11},{10,... | collective-permute-start | bytes 442376 | tf_op jit(solution)/shard_map/ppermute | solution.py:454
  36.6 12.5 %collective-permute-start.7 = (bf16[72,1024]{1,0:T(8,128)(2,1)}, bf16[72,1024]{1,0:T(8,128)(2,1)S(1)}, u32[]{:S(2)}, u32[]{:S(2)}) collective-permute-start(bf16[72,1024]{1,0:T(8,128)(2,1)} %get-tuple-element.124), channel_id=1, source_target_pairs={{0,4},{1,5},{2,6},{3,7},{4,0},{5,1},{6,2},{7,3},{8,12},{9,13},{10,... | collective-permute-start | bytes 442376 | tf_op jit(solution)/shard_map/ppermute | solution.py:454
  39.2 9.9 %collective-permute-start.8 = (bf16[72,1024]{1,0:T(8,128)(2,1)}, bf16[72,1024]{1,0:T(8,128)(2,1)S(1)}, u32[]{:S(2)}, u32[]{:S(2)}) collective-permute-start(bf16[72,1024]{1,0:T(8,128)(2,1)} %get-tuple-element.125), channel_id=1, source_target_pairs={{0,6},{1,7},{2,0},{3,1},{4,2},{5,3},{6,4},{7,5},{8,14},{9,15},{10,... | collective-permute-start | bytes 442376 | tf_op jit(solution)/shard_map/ppermute | solution.py:454
  52.6 15.0 %collective-permute-start.9 = (bf16[3,128,512]{2,1,0:T(8,128)(2,1)}, bf16[3,128,512]{2,1,0:T(8,128)(2,1)S(1)}, u32[]{:S(2)}, u32[]{:S(2)}) collective-permute-start(bf16[3,128,512]{2,1,0:T(8,128)(2,1)} %get-tuple-element.129.refs_0_), channel_id=1, source_target_pairs={{0,2},{1,3},{2,4},{3,5},{4,6},{5,7},{6,0},{7,1},{8,10},{9,11},{10,... | collective-permute-start | bytes 1179656 | tf_op jit(solution)/shard_map/ppermute | solution.py:454
  59.1 16.9 %collective-permute-start.15 = (bf16[3,128,512]{2,1,0:T(8,128)(2,1)}, bf16[3,128,512]{2,1,0:T(8,128)(2,1)S(1)}, u32[]{:S(2)}, u32[]{:S(2)}) collective-permute-start(bf16[3,128,512]{2,1,0:T(8,128)(2,1)} %get-tuple-element.155.refs_3_), channel_id=1, source_target_pairs={{0,2},{1,3},{2,4},{3,5},{4,6},{5,7},{6,0},{7,1},{8,10},{9,11},{10,... | collective-permute-start | bytes 1179656 | tf_op jit(solution)/shard_map/ppermute | solution.py:454
  67.6 18.7 %collective-permute-start.10 = (bf16[3,128,512]{2,1,0:T(8,128)(2,1)S(1)}, bf16[3,128,512]{2,1,0:T(8,128)(2,1)}, u32[]{:S(2)}, u32[]{:S(2)}) collective-permute-start(bf16[3,128,512]{2,1,0:T(8,128)(2,1)S(1)} %collective-permute-done.9.refs_1_), channel_id=1, source_target_pairs={{0,2},{1,3},{2,4},{3,5},{4,6},{5,7},{6,0},{7,1},{8,10},{9,11},{10,... | collective-permute-start | bytes 1179656 | tf_op jit(solution)/shard_map/ppermute | solution.py:454
  76.0 15.2 %collective-permute-start.16 = (bf16[3,128,512]{2,1,0:T(8,128)(2,1)S(1)}, bf16[3,128,512]{2,1,0:T(8,128)(2,1)}, u32[]{:S(2)}, u32[]{:S(2)}) collective-permute-start(bf16[3,128,512]{2,1,0:T(8,128)(2,1)S(1)} %collective-permute-done.15.refs_4_), channel_id=1, source_target_pairs={{0,2},{1,3},{2,4},{3,5},{4,6},{5,7},{6,0},{7,1},{8,10},{9,11},{10,... | collective-permute-start | bytes 1179656 | tf_op jit(solution)/shard_map/ppermute | solution.py:454
  86.2 25.7 %collective-permute-start.14 = (bf16[3,128,512]{2,1,0:T(8,128)(2,1)}, bf16[3,128,512]{2,1,0:T(8,128)(2,1)}, u32[]{:S(2)}, u32[]{:S(2)}) collective-permute-start(bf16[3,128,512]{2,1,0:T(8,128)(2,1)} %collective-permute-done.10.refs_2_), channel_id=1, source_target_pairs={{0,2},{1,3},{2,4},{3,5},{4,6},{5,7},{6,0},{7,1},{8,10},{9,11},{10,... | collective-permute-start | bytes 1179656 | tf_op jit(solution)/shard_map/ppermute | solution.py:454
  91.2 20.8 %collective-permute-start.17 = (bf16[3,128,512]{2,1,0:T(8,128)(2,1)}, bf16[3,128,512]{2,1,0:T(8,128)(2,1)}, u32[]{:S(2)}, u32[]{:S(2)}) collective-permute-start(bf16[3,128,512]{2,1,0:T(8,128)(2,1)} %collective-permute-done.16.refs_5_), channel_id=1, source_target_pairs={{0,2},{1,3},{2,4},{3,5},{4,6},{5,7},{6,0},{7,1},{8,10},{9,11},{10,... | collective-permute-start | bytes 1179656 | tf_op jit(solution)/shard_map/ppermute | solution.py:454
  93.8 13.0 %collective-permute-start.23 = (bf16[288,512]{1,0:T(8,128)(2,1)}, bf16[288,512]{1,0:T(8,128)(2,1)S(1)}, u32[]{:S(2)}, u32[]{:S(2)}) collective-permute-start(bf16[288,512]{1,0:T(8,128)(2,1)} %get-tuple-element.166), channel_id=1, source_target_pairs={{0,1},{1,0},{2,3},{3,2},{4,5},{5,4},{6,7},{7,6},{8,9},{9,8},{10,11... | collective-permute-start | bytes 884744 | tf_op jit(solution)/shard_map/ppermute | solution.py:457
  106.9 10.0 %collective-permute-start.24 = (bf16[72,512]{1,0:T(8,128)(2,1)S(1)}, bf16[72,512]{1,0:T(8,128)(2,1)S(1)}, u32[]{:S(2)}, u32[]{:S(2)}) collective-permute-start(bf16[72,512]{1,0:T(8,128)(2,1)S(1)} %get-tuple-element.169), channel_id=1, source_target_pairs={{0,2},{1,3},{2,4},{3,5},{4,6},{5,7},{6,0},{7,1},{8,10},{9,11},{10,... | collective-permute-start | bytes 221192 | tf_op jit(solution)/shard_map/ppermute | solution.py:454
  107.2 11.2 %collective-permute-start.25 = (bf16[72,512]{1,0:T(8,128)(2,1)S(1)}, bf16[72,512]{1,0:T(8,128)(2,1)S(1)}, u32[]{:S(2)}, u32[]{:S(2)}) collective-permute-start(bf16[72,512]{1,0:T(8,128)(2,1)S(1)} %get-tuple-element.171), channel_id=1, source_target_pairs={{0,4},{1,5},{2,6},{3,7},{4,0},{5,1},{6,2},{7,3},{8,12},{9,13},{10,... | collective-permute-start | bytes 221192 | tf_op jit(solution)/shard_map/ppermute | solution.py:454
  110.6 7.7 %collective-permute-start.26 = (bf16[72,512]{1,0:T(8,128)(2,1)S(1)}, bf16[72,512]{1,0:T(8,128)(2,1)S(1)}, u32[]{:S(2)}, u32[]{:S(2)}) collective-permute-start(bf16[72,512]{1,0:T(8,128)(2,1)S(1)} %get-tuple-element.173), channel_id=1, source_target_pairs={{0,6},{1,7},{2,0},{3,1},{4,2},{5,3},{6,4},{7,5},{8,14},{9,15},{10,... | collective-permute-start | bytes 221192 | tf_op jit(solution)/shard_map/ppermute | solution.py:454
  116.3 15.1 %collective-permute-start.19 = (bf16[144,1024]{1,0:T(8,128)(2,1)S(1)}, bf16[144,1024]{1,0:T(8,128)(2,1)S(1)}, u32[]{:S(2)}, u32[]{:S(2)}) collective-permute-start(bf16[144,1024]{1,0:T(8,128)(2,1)S(1)} %get-tuple-element.162), channel_id=1, source_target_pairs={{0,8},{8,16},{16,24},{24,0},{1,9},{9,17},{17,25},{25,1},{2,10},{10... | collective-permute-start | bytes 884744 | tf_op jit(solution)/shard_map/ppermute | solution.py:460
  116.4 15.0 %collective-permute-start.20 = (bf16[144,1024]{1,0:T(8,128)(2,1)S(1)}, bf16[144,1024]{1,0:T(8,128)(2,1)S(1)}, u32[]{:S(2)}, u32[]{:S(2)}) collective-permute-start(bf16[144,1024]{1,0:T(8,128)(2,1)S(1)} %get-tuple-element.163), channel_id=1, source_target_pairs={{0,16},{8,24},{16,0},{24,8},{1,17},{9,25},{17,1},{25,9},{2,18},{10... | collective-permute-start | bytes 884744 | tf_op jit(solution)/shard_map/ppermute | solution.py:460
  117.0 14.4 %collective-permute-start.21 = (bf16[144,1024]{1,0:T(8,128)(2,1)S(1)}, bf16[144,1024]{1,0:T(8,128)(2,1)S(1)}, u32[]{:S(2)}, u32[]{:S(2)}) collective-permute-start(bf16[144,1024]{1,0:T(8,128)(2,1)S(1)} %get-tuple-element.164), channel_id=1, source_target_pairs={{0,24},{8,0},{16,8},{24,16},{1,25},{9,1},{17,9},{25,17},{2,26},{10... | collective-permute-start | bytes 884744 | tf_op jit(solution)/shard_map/ppermute | solution.py:460
  119.2 8.4 %collective-permute-start.28 = (bf16[72,512]{1,0:T(8,128)(2,1)S(1)}, bf16[72,512]{1,0:T(8,128)(2,1)S(1)}, u32[]{:S(2)}, u32[]{:S(2)}) collective-permute-start(bf16[72,512]{1,0:T(8,128)(2,1)S(1)} %add_convert_fusion), channel_id=1, source_target_pairs={{0,4},{1,5},{2,6},{3,7},{4,0},{5,1},{6,2},{7,3},{8,12},{9,13},{10,... | collective-permute-start | bytes 221192 | tf_op jit(solution)/shard_map/ppermute | solution.py:454
  129.8 11.2 %collective-permute-start.30 = (bf16[288,512]{1,0:T(8,128)(2,1)S(1)}, bf16[288,512]{1,0:T(8,128)(2,1)S(1)}, u32[]{:S(2)}, u32[]{:S(2)}) collective-permute-start(bf16[288,512]{1,0:T(8,128)(2,1)S(1)} %pad_maximum_fusion.refs_0_), channel_id=1, source_target_pairs={{0,1},{1,0},{2,3},{3,2},{4,5},{5,4},{6,7},{7,6},{8,9},{9,8},{10,11... | collective-permute-start | bytes 884744 | tf_op jit(solution)/shard_map/ppermute | solution.py:457
  131.6 16.2 %collective-permute-start.22 = (bf16[128,1024]{1,0:T(8,128)(2,1)S(1)}, bf16[128,1024]{1,0:T(8,128)(2,1)S(1)}, u32[]{:S(2)}, u32[]{:S(2)}) collective-permute-start(bf16[128,1024]{1,0:T(8,128)(2,1)S(1)} %slice.24), channel_id=1, source_target_pairs={{0,0},{1,1},{2,8},{3,9},{4,16},{5,17},{6,24},{7,25},{8,2},{9,3},{1... | collective-permute-start | bytes 786440 | tf_op jit(solution)/shard_map/ppermute | solution.py:673
  134.1 13.8 %collective-permute-start.31 = (f32[1,1024]{1,0:T(1,128)S(1)}, f32[1,1024]{1,0:T(1,128)S(1)}, u32[]{:S(2)}, u32[]{:S(2)}) collective-permute-start(f32[1,1024]{1,0:T(1,128)S(1)} %slice.19), channel_id=1, source_target_pairs={{1,0},{2,1},{3,2},{4,3},{5,4},{6,5},{7,6},{9,8},{10,9},{11,10},{12... | collective-permute-start | bytes 12296 | tf_op jit(solution)/shard_map/ppermute | solution.py:449
  135.4 13.1 %collective-permute-start.32 = (f32[1,1024]{1,0:T(1,128)S(1)}, f32[1,1024]{1,0:T(1,128)S(1)}, u32[]{:S(2)}, u32[]{:S(2)}) collective-permute-start(f32[1,1024]{1,0:T(1,128)S(1)} %slice.22), channel_id=1, source_target_pairs={{1,0},{3,8},{5,16},{7,24},{8,1},{9,2},{10,9},{11,10},{12,17},{13,1... | collective-permute-start | bytes 12296 | tf_op jit(solution)/shard_map/ppermute | solution.py:674
  (36 other events, 297.5 us)

commit v6 on v4

--- a/solution.py
+++ b/solution.py
@@ -104,16 +104,8 @@
     return into, out
 
 
-def adapter_kernel(x, carried, mix, down, weights, pre, piece, stage, sem):
-    into, out = copy_rows(weights, piece, 0, stage, sem)
-    for copy in into:
-        copy.start()
-    for first, second in zip(into, out):
-        first.wait()
-        second.start()
+def adapter_kernel(x, carried, mix, down, pre):
     pre[...] = mm3(mixed_input(x, carried, mix), down[...])
-    for copy in out:
-        copy.wait()
 
 
 def decay_kernel(head, count, *refs):
@@ -448,23 +440,20 @@
         return lax.optimization_barrier((value, *others))[0]
 
     weight_rows = proj_weights.shape[1]
-    cut = weight_rows // 8
+    cut = max(weight_rows * 3 // 256, 1) * 16
     anywhere = pl.BlockSpec(memory_space=pl.ANY)
     vmem = pl.BlockSpec(memory_space=pltpu.VMEM)
 
-    carried = shift(layer_input[rows - 1 :], 1)
+    carried, piece = lax.optimization_barrier((shift(layer_input[rows - 1 :], 1), proj_weights[:, :cut]))
+    fars = [partner(piece)]
     shift_mix = decay_shift_mix.reshape(1, cols)
-    pre, piece = pl.pallas_call(
+    pre = pl.pallas_call(
         adapter_kernel,
-        in_specs=[vmem] * 4 + [anywhere],
-        out_specs=[vmem, anywhere],
-        out_shape=[shape((rows, rank)), shape((3, cut, cols), BF16)],
-        scratch_shapes=[pltpu.VMEM((3, cut, cols), BF16), pltpu.SemaphoreType.DMA((6,))],
+        out_shape=shape((rows, rank)),
         compiler_params=params,
         cost_estimate=work(1.5),
         name="adapter_input",
-    )(layer_input, carried, shift_mix, decay_adapter_down, proj_weights)
-    fars = [partner(piece)]
+    )(layer_input, carried, shift_mix, decay_adapter_down)
     pres = head_parts(pre)
 
     sums = jnp.asarray(sum_matrix(rows), BF16)
@@ -585,7 +574,7 @@
     for step in range(ring - 1):
         low, high = lows[-1], highs[-1]
         lows.append(around(after_that(low, mid_grad) if step == 1 else low, 1))
-        highs.append(around(high, 1))
+        highs.append(around(after_that(high, keep) if step == 1 else high, 1))
 
     def add(a, b):
         return (a.astype(F32) + b.astype(F32)).astype(BF16)
@@ -627,7 +616,7 @@
     up_grad, down_grad, base_grad, du = pl.pallas_call(
         lambda *refs: finish_kernel(rank, *refs),
                 out_shape=[shape((rank, cols)), shape((cols, rank)), shape((pairs, PAIR)), shape((heads, head))],
-        compiler_params=params,
+        compiler_params=pltpu.CompilerParams(vmem_limit_bytes=16 * 2**20),
         cost_estimate=work(2),
         name="token_sums",
     )(token_sums, partner(token_sums))

time: 148 us -> 146 us (0.986)
  waiting for transfers between devices: 42.6 us -> 46.4 us
  starting transfers between devices: 41.3 us -> 38 us
  Pallas kernels: 48.2 us -> 46.5 us
    ppermute x2, starting transfers between devices: 3.59 us -> 0.15 us  [per_device(): got = lax.ppermute(token_sums, 'seq', route)]
    ppermute x9, waiting for transfers between devices: 16.6 us -> 19.5 us  [head_shift(): lax.ppermute(a, 'head', [(i, (i + d) % n_head) for i in range(n_head)])]
    unnamed x58 -> x54, local copies, waits for them, and re-layouts: 10.5 us -> 8.69 us
    ppermute x1, waiting for transfers between devices: 1.75 us -> 3.27 us  [per_device(): summed = lax.ppermute(total[:rows].astype(BF16), ('head', 'seq'), swap)]
  transfers between devices with their start and end apart: 29 -> 29, of which waited for: 17 -> 19; matrix products, arithmetic and copies ran while one was open for 1% -> 2% of each run, Pallas kernels for 30% -> 32%
where the time goes in v6:
time: 146 us; the launch traced here: 145 us
  Pallas kernels  46.5 us (32%)
  waiting for transfers between devices  46.4 us (32%)
  starting transfers between devices  38 us (26%)
  local copies, waits for them, and re-layouts  11.3 us (8%)
  other arithmetic  2.14 us (1%)
    ppermute x9, waiting for transfers between devices, head_shift(): lax.ppermute(a, 'head', [(i, (i + d) % n_head) for i in range(n_head)])  19.5 us
    ppermute x9, waiting for transfers between devices, around(): lax.ppermute(a, 'seq', [(i, (i + inner * step) % n_seq) for i in range(n_...  18.9 us
    ppermute x9, starting transfers between devices, around(): lax.ppermute(a, 'seq', [(i, (i + inner * step) % n_seq) for i in range(n_...  14.3 us
    pallas_call x2, Pallas kernels, project(): pl.pallas_call(lambda *refs: project_kernel(count, ring, final, *refs), i...  12.5 us
    pallas_call x2, Pallas kernels, inside(): pl.pallas_call(lambda *refs: inner_kernel(head, cut if extra else 0, *ref...  11.5 us
    unnamed x54, local copies, waits for them, and re-layouts  8.69 us
    pallas_call x2, Pallas kernels, per_device(): pl.pallas_call(lambda *refs: outer_kernel(head, ring, *refs), grid=(steps...  5.67 us
    ppermute x5, starting transfers between devices, partner(): return lax.ppermute(a, 'seq', [(i, i ^ 1) for i in range(n_seq)])  5.65 us
  transfers between devices with their start and end apart: 29, of which 19 were waited for; matrix products, arithmetic and copies ran while one was open for 2% of the time, Pallas kernels for 32%

profile of v6, /device:TPU:4, one launch (start us, length us, event | category | flops | bytes accessed | tf_op | source)
XLA Modules:
  0.0 145.3 jit_solution(5354780943598515744)
XLA Ops:
  1.4 3.4 %collective-permute-start = (bf16[1,1024]{1,0:T(2,128)(2,1)S(1)}, bf16[1,1024]{1,0:T(2,128)(2,1)S(1)}, u32[]{:S(2)}, u32[]{:S(2)}) collective-permute-start(bf16[1,1024]{1,0:T(2,128)(2,1)S(1)} %slice.19), channel_id=1, source_target_pairs={{0,1},{1,2},{2,3},{3,4},{4,5},{5,6},{6,7},{8,9},{9,10},{10,11},{11... | collective-permute-start | bytes 6152 | tf_op jit(solution)/shard_map/ppermute | solution.py:423
  16.5 3.4 %decay_and_states.1 = (f32[128,128]{1,0:T(8,128)}, bf16[128,128]{1,0:T(8,128)(2,1)}, f32[128,1024]{1,0:T(8,128)}, f32[1,1024]{1,0:T(1,128)}, f32[64,1024]{1,0:T(8,128)}, /*index=5*/bf16[136,1024]{1,0:T(8,128)(2,1)}) custom-call(f32[128,128]{1,0:T(8,128)} %adapter_input.1.refs_0_, f32[128,128]{1,0:T(8,128)} %copy-done.21, f32[128,128]{1,0:T(8,128)} %copy-done.23, ...), custom_call_target="tpu_custom_call" | custom-call | bytes 10500000 | tf_op jit(solution)/shard_map/decay_and_states/pallas_call | solution.py:464
  21.1 6.4 %inside_chunk.2 = (f32[128,512]{1,0:T(8,128)}, f32[128,512]{1,0:T(8,128)}, f32[128,512]{1,0:T(8,128)}, f32[128,512]{1,0:T(8,128)}, f32[128,512]{1,0:T(8,128)}, /...) custom-call(bf16[128,1024]{1,0:T(8,128)(2,1)} %refs_0_.8, bf16[128,1024]{1,0:T(8,128)(2,1)} %refs_1_.7, ...), custom_call_target="tpu_custom_call" | custom-call | bytes 14000000 | tf_op jit(solution)/shard_map/inside_chunk/pallas_call | solution.py:490
  34.6 2.6 %collective-permute-start.7 = (bf16[72,1024]{1,0:T(8,128)(2,1)}, bf16[72,1024]{1,0:T(8,128)(2,1)S(1)}, u32[]{:S(2)}, u32[]{:S(2)}) collective-permute-start(bf16[72,1024]{1,0:T(8,128)(2,1)} %get-tuple-element.118), channel_id=1, source_target_pairs={{0,4},{1,5},{2,6},{3,7},{4,0},{5,1},{6,2},{7,3},{8,12},{9,13},{10,... | collective-permute-start | bytes 442376 | tf_op jit(solution)/shard_map/ppermute | solution.py:428
  38.6 5.1 %inside_chunk.3 = (f32[128,512]{1,0:T(8,128)}, f32[128,512]{1,0:T(8,128)}, f32[128,512]{1,0:T(8,128)}, f32[128,512]{1,0:T(8,128)}, f32[128,512]{1,0:T(8,128)}, /*index=5*/f32[128,512]{1,0:T(8,128)}, f32[1,512]{1,0:T(1,128)}) custom-call(bf16[128,1024]{1,0:T(8,128)(2,1)} %refs_0_.8, bf16[128,1024]{1,0:T(8,128)(2,1)} %refs_1_.7, bf16[128,1024]{1,0:T(8,128)(2,1)} %refs_2_.8, ...), custom_call_target="tpu_custom_call" | custom-call | bytes 14000000 | tf_op jit(solution)/shard_map/inside_chunk/pallas_call | solution.py:490
  43.7 3.4 %collective-permute-done.7.refs_15_ = bf16[72,1024]{1,0:T(8,128)(2,1)S(1)} collective-permute-done((bf16[72,1024]{1,0:T(8,128)(2,1)}, bf16[72,1024]{1,0:T(8,128)(2,1)S(1)}, u32[]{:S(2)}, u32[]{:S(2)}) %collective-permute-start.7) | collective-permute-done | bytes 147488 | tf_op jit(solution)/shard_map/ppermute | solution.py:428
  47.8 2.8 %across_chunks.2 = (bf16[3,128,512]{2,1,0:T(8,128)(2,1)}, f32[128,512]{1,0:T(8,128)}, f32[128,512]{1,0:T(8,128)}, f32[1,512]{1,0:T(1,128)}) custom-call(bf16[128,1024]{1,0:T(8,128)(2,1)} %refs_0_.8, bf16[128,1024]{1,0:T(8,128)(2,1)} %refs_1_.7, bf16[128,1024]{1,0:T(8,128)(2,1)} %refs_2_.8, bf16[128,1024]{1,0:T(8,128)(2,1)} %refs_3_.8, ...), custom_call_target="tpu_custom_call" | custom-call | bytes 10500000 | tf_op jit(solution)/shard_map/across_chunks/pallas_call | solution.py:524
  50.6 3.6 %collective-permute-start.9 = (bf16[3,128,512]{2,1,0:T(8,128)(2,1)}, bf16[3,128,512]{2,1,0:T(8,128)(2,1)S(1)}, u32[]{:S(2)}, u32[]{:S(2)}) collective-permute-start(bf16[3,128,512]{2,1,0:T(8,128)(2,1)} %get-tuple-element.123.refs_0_), channel_id=1, source_target_pairs={{0,2},{1,3},{2,4},{3,5},{4,6},{5,7},{6,0},{7,1},{8,10},{9,11},{10,... | collective-permute-start | bytes 1179656 | tf_op jit(solution)/shard_map/ppermute | solution.py:428
  54.2 2.9 %across_chunks.3 = (bf16[3,128,512]{2,1,0:T(8,128)(2,1)}, f32[128,512]{1,0:T(8,128)}, f32[128,512]{1,0:T(8,128)}, f32[1,512]{1,0:T(1,128)}) custom-call(bf16[128,1024]{1,0:T(8,128)(2,1)} %refs_0_.8, bf16[128,1024]{1,0:T(8,128)(2,1)} %refs_1_.7, bf16[128,1024]{1,0:T(8,128)(2,1)} %refs_2_.8, bf16[128,1024]{1,0:T(8,128)(2,1)} %refs_3_.8, ...), custom_call_target="tpu_custom_call" | custom-call | bytes 10500000 | tf_op jit(solution)/shard_map/across_chunks/pallas_call | solution.py:524
  57.2 2.6 %decay_gradient.3 = (f32[128,512]{1,0:T(8,128)}, f32[1,512]{1,0:T(1,128)}, f32[128,128]{1,0:T(8,128)}) custom-call(f32[128,1024]{1,0:T(8,128)} %get-tuple-element.92.refs_4_.w, f32[128,512]{1,0:T(8,128)} %get-tuple-element.135.r_gr, f32[128,512]{1,0:T(8,128)} %get-tuple-element.136.k_gk, f32[1,512]{1,0:T(1,128)} %get-tuple-element.137.at_end, ...), custom_call_target="tpu_custom_call" | custom-call | bytes 7000000 | tf_op jit(solution)/shard_map/decay_gradient/pallas_call | solution.py:544
  59.8 2.4 %decay_gradient.2 = (f32[128,512]{1,0:T(8,128)}, f32[1,512]{1,0:T(1,128)}, f32[128,128]{1,0:T(8,128)}) custom-call(f32[128,1024]{1,0:T(8,128)} %get-tuple-element.92.refs_4_.w, f32[128,512]{1,0:T(8,128)} %get-tuple-element.124.r_gr, f32[128,512]{1,0:T(8,128)} %get-tuple-element.125.k_gk, f32[1,512]{1,0:T(1,128)} %get-tuple-element.126.at_end, ...), custom_call_target="tpu_custom_call" | custom-call | bytes 7000000 | tf_op jit(solution)/shard_map/decay_gradient/pallas_call | solution.py:544
  63.0 2.6 %collective-permute-done.9.refs_1_ = bf16[3,128,512]{2,1,0:T(8,128)(2,1)S(1)} collective-permute-done((bf16[3,128,512]{2,1,0:T(8,128)(2,1)}, bf16[3,128,512]{2,1,0:T(8,128)(2,1)S(1)}, u32[]{:S(2)}, u32[]{:S(2)}) %collective-permute-start.9) | collective-permute-done | bytes 393248 | tf_op jit(solution)/shard_map/ppermute | solution.py:428
  67.7 3.3 %collective-permute-done.13.refs_6_ = f32[128,128]{1,0:T(8,128)S(1)} collective-permute-done((f32[128,128]{1,0:T(8,128)S(1)}, f32[128,128]{1,0:T(8,128)S(1)}, u32[]{:S(2)}, u32[]{:S(2)}) %collective-permute-start.13) | collective-permute-done | bytes 65568 | tf_op jit(solution)/shard_map/ppermute | solution.py:434
  73.5 3.0 %adapter_grads.1 = (bf16[272,512]{1,0:T(8,128)(2,1)}, bf16[272,512]{1,0:T(8,128)(2,1)}, f32[128,1024]{1,0:T(8,128)}) custom-call(bf16[128,1024]{1,0:T(8,128)(2,1)} %refs_0_.9, bf16[1,1024]{1,0:T(2,128)(2,1)} %copy-done.25, f32[1,1024]{1,0:T(1,128)} %bitcast.5, f32[1024,128]{1,0:T(8,128)} %refs_3_.9, f32[128,128]{1,0:T(8,128)} %get-tuple-element.141.refs_4_, ...), custom_call_target="tpu_custom_call" | custom-call | bytes 10500000 | tf_op jit(solution)/shard_map/adapter_grads/pallas_call | solution.py:562
  76.6 4.2 %collective-permute-done.10.refs_2_ = bf16[3,128,512]{2,1,0:T(8,128)(2,1)S(1)} collective-permute-done((bf16[3,128,512]{2,1,0:T(8,128)(2,1)S(1)}, bf16[3,128,512]{2,1,0:T(8,128)(2,1)S(1)}, u32[]{:S(2)}, u32[]{:S(2)}) %collective-permute-start.10) | collective-permute-done | bytes 393248 | tf_op jit(solution)/shard_map/ppermute | solution.py:428
  85.0 5.6 %collective-permute-done.16.refs_5_ = bf16[3,128,512]{2,1,0:T(8,128)(2,1)} collective-permute-done((bf16[3,128,512]{2,1,0:T(8,128)(2,1)}, bf16[3,128,512]{2,1,0:T(8,128)(2,1)}, u32[]{:S(2)}, u32[]{:S(2)}) %collective-permute-start.16) | collective-permute-done | bytes 393248 | tf_op jit(solution)/shard_map/ppermute | solution.py:428
  96.9 7.2 %projections.2 = (bf16[144,1024]{1,0:T(8,128)(2,1)S(1)}, bf16[144,1024]{1,0:T(8,128)(2,1)S(1)}, bf16[144,1024]{1,0:T(8,128)(2,1)S(1)}) custom-call(bf16[3,128,512]{2,1,0:T(8,128)(2,1)S(1)} %copy-done.5, bf16[3,128,512]{2,1,0:T(8,128)(2,1)S(1)} %copy-done.7, bf16[3,128,512]{2,1,0:T(8,128)(2,1)S(1)} %copy-done.10, bf16[3,128,512]{2,1,0:T(8,128)(2,1)S(1)} %copy-done.8, ...), custom_call_target="tpu_custom_call" | custom-call | bytes 17500000 | tf_op jit(solution)/shard_map/projections/pallas_call | solution.py:590
  104.3 3.2 %collective-permute-done.17.refs_1_ = bf16[3,128,512]{2,1,0:T(8,128)(2,1)S(1)} collective-permute-done((bf16[3,128,512]{2,1,0:T(8,128)(2,1)}, bf16[3,128,512]{2,1,0:T(8,128)(2,1)S(1)}, u32[]{:S(2)}, u32[]{:S(2)}) %collective-permute-start.17) | collective-permute-done | bytes 393248 | tf_op jit(solution)/shard_map/ppermute | solution.py:428
  107.5 5.3 %projections.3 = (bf16[144,1024]{1,0:T(8,128)(2,1)S(1)}, bf16[144,1024]{1,0:T(8,128)(2,1)S(1)}, bf16[144,1024]{1,0:T(8,128)(2,1)S(1)}, bf16[144,1024]{1,0:T(8,128)(2,1)S(1)}) custom-call(bf16[3,128,512]{2,1,0:T(8,128)(2,1)S(1)} %collective-permute-done.11.refs_0_, bf16[3,128,512]{2,1,0:T(8,128)(2,1)S(1)} %collective-permute-done.17.refs_1_, ...), custom_call_target="tpu_custom_call" | custom-call | bytes 17500000 | tf_op jit(solution)/shard_map/projections/pallas_call | solution.py:590
  114.8 6.8 %collective-permute-done.19 = bf16[144,1024]{1,0:T(8,128)(2,1)S(1)} collective-permute-done((bf16[144,1024]{1,0:T(8,128)(2,1)S(1)}, bf16[144,1024]{1,0:T(8,128)(2,1)S(1)}, u32[]{:S(2)}, u32[]{:S(2)}) %collective-permute-start.19) | collective-permute-done | bytes 294944 | tf_op jit(solution)/shard_map/ppermute | solution.py:434
  122.8 3.1 %collective-permute-done.21 = bf16[144,1024]{1,0:T(8,128)(2,1)S(1)} collective-permute-done((bf16[144,1024]{1,0:T(8,128)(2,1)S(1)}, bf16[144,1024]{1,0:T(8,128)(2,1)S(1)}, u32[]{:S(2)}, u32[]{:S(2)}) %collective-permute-start.21) | collective-permute-done | bytes 294944 | tf_op jit(solution)/shard_map/ppermute | solution.py:434
  126.1 3.5 %collective-permute-start.22 = (bf16[128,1024]{1,0:T(8,128)(2,1)S(1)}, bf16[128,1024]{1,0:T(8,128)(2,1)S(1)}, u32[]{:S(2)}, u32[]{:S(2)}) collective-permute-start(bf16[128,1024]{1,0:T(8,128)(2,1)S(1)} %slice.28), channel_id=1, source_target_pairs={{0,0},{1,1},{2,8},{3,9},{4,16},{5,17},{6,24},{7,25},{8,2},{9,3},{1... | collective-permute-start | bytes 786440 | tf_op jit(solution)/shard_map/ppermute | solution.py:637
  132.7 5.4 %collective-permute-start.28 = (f32[1,1024]{1,0:T(1,128)S(1)}, f32[1,1024]{1,0:T(1,128)S(1)}, u32[]{:S(2)}, u32[]{:S(2)}) collective-permute-start(f32[1,1024]{1,0:T(1,128)S(1)} %slice.26), channel_id=1, source_target_pairs={{1,0},{3,8},{5,16},{7,24},{8,1},{9,2},{10,9},{11,10},{12,17},{13,1... | collective-permute-start | bytes 12296 | tf_op jit(solution)/shard_map/ppermute | solution.py:638
  140.7 3.3 %collective-permute-done.22 = bf16[128,1024]{1,0:T(8,128)(2,1)S(1)} collective-permute-done((bf16[128,1024]{1,0:T(8,128)(2,1)S(1)}, bf16[128,1024]{1,0:T(8,128)(2,1)S(1)}, u32[]{:S(2)}, u32[]{:S(2)}) %collective-permute-start.22) | collective-permute-done | bytes 262176 | tf_op jit(solution)/shard_map/ppermute | solution.py:637
  (117 shorter events, 49.5 us)
Async XLA Ops:
  6.1 15.0 %collective-permute-start.5 = (bf16[3,96,1024]{2,1,0:T(8,128)(2,1)S(1)}, bf16[3,96,1024]{2,1,0:T(8,128)(2,1)S(1)}, u32[]{:S(2)}, u32[]{:S(2)}) collective-permute-start(bf16[3,96,1024]{2,1,0:T(8,128)(2,1)S(1)} %slice.20), channel_id=1, source_target_pairs={{0,1},{1,0},{2,3},{3,2},{4,5},{5,4},{6,7},{7,6},{8,9},{9,8},{10,11... | collective-permute-start | bytes 1769480 | tf_op jit(solution)/shard_map/ppermute | solution.py:431
  10.7 5.1 %collective-permute-start.2 = (f32[128,128]{1,0:T(8,128)}, f32[128,128]{1,0:T(8,128)S(1)}, u32[]{:S(2)}, u32[]{:S(2)}) collective-permute-start(f32[128,128]{1,0:T(8,128)} %adapter_input.1.refs_0_), channel_id=1, source_target_pairs={{0,16},{8,24},{16,0},{24,8},{1,17},{9,25},{17,1},{25,9},{2,18},{10... | collective-permute-start | bytes 196616 | tf_op jit(solution)/shard_map/ppermute | solution.py:434
  19.8 9.7 %collective-permute-start.4 = (bf16[136,1024]{1,0:T(8,128)(2,1)}, bf16[136,1024]{1,0:T(8,128)(2,1)S(1)}, u32[]{:S(2)}, u32[]{:S(2)}) collective-permute-start(bf16[136,1024]{1,0:T(8,128)(2,1)} %get-tuple-element.88.refs_0_), channel_id=1, source_target_pairs={{0,1},{1,0},{2,3},{3,2},{4,5},{5,4},{6,7},{7,6},{8,9},{9,8},{10,11... | collective-permute-start | bytes 835592 | tf_op jit(solution)/shard_map/ppermute | solution.py:431
  29.5 62.3 %collective-permute-start.18 = (bf16[3,416,1024]{2,1,0:T(8,128)(2,1)}, bf16[3,416,1024]{2,1,0:T(8,128)(2,1)}, u32[]{:S(2)}, u32[]{:S(2)}) collective-permute-start(bf16[3,416,1024]{2,1,0:T(8,128)(2,1)} %get-tuple-element.150), channel_id=1, source_target_pairs={{0,1},{1,0},{2,3},{3,2},{4,5},{5,4},{6,7},{7,6},{8,9},{9,8},{10,11... | collective-permute-start | bytes 7667720 | tf_op jit(solution)/shard_map/ppermute | solution.py:431
  32.3 11.4 %collective-permute-start.6 = (bf16[72,1024]{1,0:T(8,128)(2,1)}, bf16[72,1024]{1,0:T(8,128)(2,1)S(1)}, u32[]{:S(2)}, u32[]{:S(2)}) collective-permute-start(bf16[72,1024]{1,0:T(8,128)(2,1)} %get-tuple-element.117), channel_id=1, source_target_pairs={{0,2},{1,3},{2,4},{3,5},{4,6},{5,7},{6,0},{7,1},{8,10},{9,11},{10,... | collective-permute-start | bytes 442376 | tf_op jit(solution)/shard_map/ppermute | solution.py:428
  34.6 12.5 %collective-permute-start.7 = (bf16[72,1024]{1,0:T(8,128)(2,1)}, bf16[72,1024]{1,0:T(8,128)(2,1)S(1)}, u32[]{:S(2)}, u32[]{:S(2)}) collective-permute-start(bf16[72,1024]{1,0:T(8,128)(2,1)} %get-tuple-element.118), channel_id=1, source_target_pairs={{0,4},{1,5},{2,6},{3,7},{4,0},{5,1},{6,2},{7,3},{8,12},{9,13},{10,... | collective-permute-start | bytes 442376 | tf_op jit(solution)/shard_map/ppermute | solution.py:428
  37.2 9.9 %collective-permute-start.8 = (bf16[72,1024]{1,0:T(8,128)(2,1)}, bf16[72,1024]{1,0:T(8,128)(2,1)S(1)}, u32[]{:S(2)}, u32[]{:S(2)}) collective-permute-start(bf16[72,1024]{1,0:T(8,128)(2,1)} %get-tuple-element.119), channel_id=1, source_target_pairs={{0,6},{1,7},{2,0},{3,1},{4,2},{5,3},{6,4},{7,5},{8,14},{9,15},{10,... | collective-permute-start | bytes 442376 | tf_op jit(solution)/shard_map/ppermute | solution.py:428
  50.6 15.0 %collective-permute-start.9 = (bf16[3,128,512]{2,1,0:T(8,128)(2,1)}, bf16[3,128,512]{2,1,0:T(8,128)(2,1)S(1)}, u32[]{:S(2)}, u32[]{:S(2)}) collective-permute-start(bf16[3,128,512]{2,1,0:T(8,128)(2,1)} %get-tuple-element.123.refs_0_), channel_id=1, source_target_pairs={{0,2},{1,3},{2,4},{3,5},{4,6},{5,7},{6,0},{7,1},{8,10},{9,11},{10,... | collective-permute-start | bytes 1179656 | tf_op jit(solution)/shard_map/ppermute | solution.py:428
  57.1 19.4 %collective-permute-start.12 = (bf16[3,128,512]{2,1,0:T(8,128)(2,1)}, bf16[3,128,512]{2,1,0:T(8,128)(2,1)}, u32[]{:S(2)}, u32[]{:S(2)}) collective-permute-start(bf16[3,128,512]{2,1,0:T(8,128)(2,1)} %get-tuple-element.140.refs_3_), channel_id=1, source_target_pairs={{0,2},{1,3},{2,4},{3,5},{4,6},{5,7},{6,0},{7,1},{8,10},{9,11},{10,... | collective-permute-start | bytes 1179656 | tf_op jit(solution)/shard_map/ppermute | solution.py:428
  65.6 15.2 %collective-permute-start.10 = (bf16[3,128,512]{2,1,0:T(8,128)(2,1)S(1)}, bf16[3,128,512]{2,1,0:T(8,128)(2,1)S(1)}, u32[]{:S(2)}, u32[]{:S(2)}) collective-permute-start(bf16[3,128,512]{2,1,0:T(8,128)(2,1)S(1)} %collective-permute-done.9.refs_1_), channel_id=1, source_target_pairs={{0,2},{1,3},{2,4},{3,5},{4,6},{5,7},{6,0},{7,1},{8,10},{9,11},{10,... | collective-permute-start | bytes 1179656 | tf_op jit(solution)/shard_map/ppermute | solution.py:428
  67.2 4.9 %collective-permute-start.14 = (f32[128,128]{1,0:T(8,128)S(1)}, f32[128,128]{1,0:T(8,128)S(1)}, u32[]{:S(2)}, u32[]{:S(2)}) collective-permute-start(f32[128,128]{1,0:T(8,128)S(1)} %add.33.refs_5_), channel_id=1, source_target_pairs={{0,16},{8,24},{16,0},{24,8},{1,17},{9,25},{17,1},{25,9},{2,18},{10... | collective-permute-start | bytes 196616 | tf_op jit(solution)/shard_map/ppermute | solution.py:434
  76.5 14.1 %collective-permute-start.16 = (bf16[3,128,512]{2,1,0:T(8,128)(2,1)}, bf16[3,128,512]{2,1,0:T(8,128)(2,1)}, u32[]{:S(2)}, u32[]{:S(2)}) collective-permute-start(bf16[3,128,512]{2,1,0:T(8,128)(2,1)} %collective-permute-done.12.refs_4_), channel_id=1, source_target_pairs={{0,2},{1,3},{2,4},{3,5},{4,6},{5,7},{6,0},{7,1},{8,10},{9,11},{10,... | collective-permute-start | bytes 1179656 | tf_op jit(solution)/shard_map/ppermute | solution.py:428
  81.6 22.5 %collective-permute-start.23 = (bf16[272,512]{1,0:T(8,128)(2,1)}, bf16[272,512]{1,0:T(8,128)(2,1)S(1)}, u32[]{:S(2)}, u32[]{:S(2)}) collective-permute-start(bf16[272,512]{1,0:T(8,128)(2,1)} %get-tuple-element.160), channel_id=1, source_target_pairs={{0,1},{1,0},{2,3},{3,2},{4,5},{5,4},{6,7},{7,6},{8,9},{9,8},{10,11... | collective-permute-start | bytes 835592 | tf_op jit(solution)/shard_map/ppermute | solution.py:431
  82.7 24.7 %collective-permute-start.11 = (bf16[3,128,512]{2,1,0:T(8,128)(2,1)}, bf16[3,128,512]{2,1,0:T(8,128)(2,1)S(1)}, u32[]{:S(2)}, u32[]{:S(2)}) collective-permute-start(bf16[3,128,512]{2,1,0:T(8,128)(2,1)} %copy-done.9), channel_id=1, source_target_pairs={{0,2},{1,3},{2,4},{3,5},{4,6},{5,7},{6,0},{7,1},{8,10},{9,11},{10,... | collective-permute-start | bytes 1179656 | tf_op jit(solution)/shard_map/ppermute | solution.py:428
  90.6 16.8 %collective-permute-start.17 = (bf16[3,128,512]{2,1,0:T(8,128)(2,1)}, bf16[3,128,512]{2,1,0:T(8,128)(2,1)S(1)}, u32[]{:S(2)}, u32[]{:S(2)}) collective-permute-start(bf16[3,128,512]{2,1,0:T(8,128)(2,1)} %collective-permute-done.16.refs_5_), channel_id=1, source_target_pairs={{0,2},{1,3},{2,4},{3,5},{4,6},{5,7},{6,0},{7,1},{8,10},{9,11},{10,... | collective-permute-start | bytes 1179656 | tf_op jit(solution)/shard_map/ppermute | solution.py:428
  104.2 10.4 %collective-permute-start.24 = (bf16[272,512]{1,0:T(8,128)(2,1)S(1)}, bf16[272,512]{1,0:T(8,128)(2,1)S(1)}, u32[]{:S(2)}, u32[]{:S(2)}) collective-permute-start(bf16[272,512]{1,0:T(8,128)(2,1)S(1)} %add_convert_fusion.2), channel_id=1, source_target_pairs={{0,2},{1,3},{2,0},{3,1},{4,6},{5,7},{6,4},{7,5},{8,10},{9,11},{10,... | collective-permute-start | bytes 835592 | tf_op jit(solution)/shard_map/ppermute | solution.py:613
  112.8 8.8 %collective-permute-start.19 = (bf16[144,1024]{1,0:T(8,128)(2,1)S(1)}, bf16[144,1024]{1,0:T(8,128)(2,1)S(1)}, u32[]{:S(2)}, u32[]{:S(2)}) collective-permute-start(bf16[144,1024]{1,0:T(8,128)(2,1)S(1)} %get-tuple-element.156), channel_id=1, source_target_pairs={{0,8},{8,16},{16,24},{24,0},{1,9},{9,17},{17,25},{25,1},{2,10},{10... | collective-permute-start | bytes 884744 | tf_op jit(solution)/shard_map/ppermute | solution.py:434
  112.9 9.9 %collective-permute-start.20 = (bf16[144,1024]{1,0:T(8,128)(2,1)S(1)}, bf16[144,1024]{1,0:T(8,128)(2,1)S(1)}, u32[]{:S(2)}, u32[]{:S(2)}) collective-permute-start(bf16[144,1024]{1,0:T(8,128)(2,1)S(1)} %get-tuple-element.157), channel_id=1, source_target_pairs={{0,16},{8,24},{16,0},{24,8},{1,17},{9,25},{17,1},{25,9},{2,18},{10... | collective-permute-start | bytes 884744 | tf_op jit(solution)/shard_map/ppermute | solution.py:434
  113.2 12.7 %collective-permute-start.21 = (bf16[144,1024]{1,0:T(8,128)(2,1)S(1)}, bf16[144,1024]{1,0:T(8,128)(2,1)S(1)}, u32[]{:S(2)}, u32[]{:S(2)}) collective-permute-start(bf16[144,1024]{1,0:T(8,128)(2,1)S(1)} %get-tuple-element.158), channel_id=1, source_target_pairs={{0,24},{8,0},{16,8},{24,16},{1,25},{9,1},{17,9},{25,17},{2,26},{10... | collective-permute-start | bytes 884744 | tf_op jit(solution)/shard_map/ppermute | solution.py:434
  114.7 15.6 %collective-permute-start.25 = (bf16[272,512]{1,0:T(8,128)(2,1)S(1)}, bf16[272,512]{1,0:T(8,128)(2,1)S(1)}, u32[]{:S(2)}, u32[]{:S(2)}) collective-permute-start(bf16[272,512]{1,0:T(8,128)(2,1)S(1)} %add_convert_fusion.1), channel_id=1, source_target_pairs={{0,4},{1,5},{2,6},{3,7},{4,0},{5,1},{6,2},{7,3},{8,12},{9,13},{10,... | collective-permute-start | bytes 835592 | tf_op jit(solution)/shard_map/ppermute | solution.py:613
  126.1 17.9 %collective-permute-start.22 = (bf16[128,1024]{1,0:T(8,128)(2,1)S(1)}, bf16[128,1024]{1,0:T(8,128)(2,1)S(1)}, u32[]{:S(2)}, u32[]{:S(2)}) collective-permute-start(bf16[128,1024]{1,0:T(8,128)(2,1)S(1)} %slice.28), channel_id=1, source_target_pairs={{0,0},{1,1},{2,8},{3,9},{4,16},{5,17},{6,24},{7,25},{8,2},{9,3},{1... | collective-permute-start | bytes 786440 | tf_op jit(solution)/shard_map/ppermute | solution.py:637
  130.4 9.2 %collective-permute-start.26 = (bf16[272,512]{1,0:T(8,128)(2,1)S(1)}, bf16[272,512]{1,0:T(8,128)(2,1)S(1)}, u32[]{:S(2)}, u32[]{:S(2)}) collective-permute-start(bf16[272,512]{1,0:T(8,128)(2,1)S(1)} %add_convert_fusion.refs_0_), channel_id=1, source_target_pairs={{0,1},{1,0},{2,3},{3,2},{4,5},{5,4},{6,7},{7,6},{8,9},{9,8},{10,11... | collective-permute-start | bytes 835592 | tf_op jit(solution)/shard_map/ppermute | solution.py:431
  131.4 12.6 %collective-permute-start.27 = (f32[1,1024]{1,0:T(1,128)S(1)}, f32[1,1024]{1,0:T(1,128)S(1)}, u32[]{:S(2)}, u32[]{:S(2)}) collective-permute-start(f32[1,1024]{1,0:T(1,128)S(1)} %slice.23), channel_id=1, source_target_pairs={{1,0},{2,1},{3,2},{4,3},{5,4},{6,5},{7,6},{9,8},{10,9},{11,10},{12... | collective-permute-start | bytes 12296 | tf_op jit(solution)/shard_map/ppermute | solution.py:423
  132.7 11.7 %collective-permute-start.28 = (f32[1,1024]{1,0:T(1,128)S(1)}, f32[1,1024]{1,0:T(1,128)S(1)}, u32[]{:S(2)}, u32[]{:S(2)}) collective-permute-start(f32[1,1024]{1,0:T(1,128)S(1)} %slice.26), channel_id=1, source_target_pairs={{1,0},{3,8},{5,16},{7,24},{8,1},{9,2},{10,9},{11,10},{12,17},{13,1... | collective-permute-start | bytes 12296 | tf_op jit(solution)/shard_map/ppermute | solution.py:638
  (32 other events, 247.0 us)

commit v7 on v6

--- a/solution.py
+++ b/solution.py
@@ -385,7 +385,7 @@
                 store(outs[q], q)
             continue
         for d in range(ring):
-            wanted = lax.rem(place[1] - place[2] - d + 2 * ring, ring)
+            wanted = lax.rem(place[1] - lax.bitwise_xor(place[2], d) + ring, ring)
             for q in range(ring):
 
                 @pl.when(wanted == q)
@@ -621,9 +621,17 @@
         name="token_sums",
     )(token_sums, partner(token_sums))
 
-    total = sends[0].astype(F32)
-    for d in range(1, n_head):
-        total = total + head_shift(sends[d], d).astype(F32)
+    def across(a, bit):
+        return lax.ppermute(a, "head", [(i, i ^ bit) for i in range(n_head)])
+
+    left, bit = dict(enumerate(sends)), 1
+    while bit < n_head:
+        got = {e: across(left[e | bit], bit) for e in left if not e & bit}
+        left = {e: left[e].astype(F32) + got[e].astype(F32) for e in got}
+        bit *= 2
+        if bit < n_head:
+            left = {e: value.astype(BF16) for e, value in left.items()}
+    total = left[0]
     swap, back = [], []
     for h in range(n_head):
         for z in range(ring):

time: 146 us -> 147 us (level)
  waiting for transfers between devices: 46.4 us -> 50.1 us
  starting transfers between devices: 38 us -> 35.6 us
    ppermute x2, waiting for transfers between devices: 0.67 us -> 14.5 us  [per_device(): got = lax.ppermute(token_sums, 'seq', route)]
    ppermute x9 -> x6, waiting for transfers between devices: 19.5 us -> 8.4 us  [head_shift(): lax.ppermute(a, 'head', [(i, (i + d) % n_head) for i in range(n_head)])]
    ppermute x1, waiting for transfers between devices: 3.27 us -> 5.43 us  [per_device(): summed = lax.ppermute(total[:rows].astype(BF16), ('head', 'seq'), swap)]
    ppermute x9 -> x6, starting transfers between devices: 4.32 us -> 2.49 us  [head_shift(): lax.ppermute(a, 'head', [(i, (i + d) % n_head) for i in range(n_head)])]
    ppermute x1, starting transfers between devices: 3.48 us -> 1.92 us  [per_device(): summed = lax.ppermute(total[:rows].astype(BF16), ('head', 'seq'), swap)]
  transfers between devices with their start and end apart: 29 -> 29, of which waited for: 19 -> 16; matrix products, arithmetic and copies ran while one was open for 2% -> 2% of each run, Pallas kernels for 32% -> 32%
where the time goes in v7:
time: 147 us
  waiting for transfers between devices  50.1 us (34%)
  Pallas kernels  46.5 us (32%)
  starting transfers between devices  35.6 us (24%)
  local copies, waits for them, and re-layouts  11.3 us (8%)
  other arithmetic  2.15 us (1%)
    ppermute x9, waiting for transfers between devices, around(): lax.ppermute(a, 'seq', [(i, (i + inner * step) % n_seq) for i in range(n_...  18.9 us
    ppermute x2, waiting for transfers between devices, per_device(): got = lax.ppermute(token_sums, 'seq', route)  14.5 us
    ppermute x9, starting transfers between devices, around(): lax.ppermute(a, 'seq', [(i, (i + inner * step) % n_seq) for i in range(n_...  14.3 us
    pallas_call x2, Pallas kernels, project(): pl.pallas_call(lambda *refs: project_kernel(count, ring, final, *refs), i...  12.5 us
    pallas_call x2, Pallas kernels, inside(): pl.pallas_call(lambda *refs: inner_kernel(head, cut if extra else 0, *ref...  11.5 us
    unnamed x54, local copies, waits for them, and re-layouts  8.69 us
    ppermute x6, waiting for transfers between devices, head_shift(): lax.ppermute(a, 'head', [(i, (i + d) % n_head) for i in range(n_head)])  8.4 us
    pallas_call x2, Pallas kernels, per_device(): pl.pallas_call(lambda *refs: outer_kernel(head, ring, *refs), grid=(steps...  5.67 us
  transfers between devices with their start and end apart: 29, of which 16 were waited for; matrix products, arithmetic and copies ran while one was open for 2% of the time, Pallas kernels for 32%

profile of v7, /device:TPU:4, one launch (start us, length us, event | category | flops | bytes accessed | tf_op | source)
XLA Modules:
  0.0 146.7 jit_solution(18055563555571334105)
XLA Ops:
  1.4 3.4 %collective-permute-start = (bf16[1,1024]{1,0:T(2,128)(2,1)S(1)}, bf16[1,1024]{1,0:T(2,128)(2,1)S(1)}, u32[]{:S(2)}, u32[]{:S(2)}) collective-permute-start(bf16[1,1024]{1,0:T(2,128)(2,1)S(1)} %slice.19), channel_id=1, source_target_pairs={{0,1},{1,2},{2,3},{3,4},{4,5},{5,6},{6,7},{8,9},{9,10},{10,11},{11... | collective-permute-start | bytes 6152 | tf_op jit(solution)/shard_map/ppermute | solution.py:423
  16.5 3.4 %decay_and_states.1 = (f32[128,128]{1,0:T(8,128)}, bf16[128,128]{1,0:T(8,128)(2,1)}, f32[128,1024]{1,0:T(8,128)}, f32[1,1024]{1,0:T(1,128)}, f32[64,1024]{1,0:T(8,128)}, /*index=5*/bf16[136,1024]{1,0:T(8,128)(2,1)}) custom-call(f32[128,128]{1,0:T(8,128)} %adapter_input.1.refs_0_, f32[128,128]{1,0:T(8,128)} %copy-done.21, f32[128,128]{1,0:T(8,128)} %copy-done.23, ...), custom_call_target="tpu_custom_call" | custom-call | bytes 10500000 | tf_op jit(solution)/shard_map/decay_and_states/pallas_call | solution.py:464
  21.1 6.4 %inside_chunk.2 = (f32[128,512]{1,0:T(8,128)}, f32[128,512]{1,0:T(8,128)}, f32[128,512]{1,0:T(8,128)}, f32[128,512]{1,0:T(8,128)}, f32[128,512]{1,0:T(8,128)}, /...) custom-call(bf16[128,1024]{1,0:T(8,128)(2,1)} %refs_0_.8, bf16[128,1024]{1,0:T(8,128)(2,1)} %refs_1_.7, ...), custom_call_target="tpu_custom_call" | custom-call | bytes 14000000 | tf_op jit(solution)/shard_map/inside_chunk/pallas_call | solution.py:490
  32.3 2.3 %collective-permute-start.6 = (bf16[72,1024]{1,0:T(8,128)(2,1)}, bf16[72,1024]{1,0:T(8,128)(2,1)S(1)}, u32[]{:S(2)}, u32[]{:S(2)}) collective-permute-start(bf16[72,1024]{1,0:T(8,128)(2,1)} %get-tuple-element.117), channel_id=1, source_target_pairs={{0,2},{1,3},{2,4},{3,5},{4,6},{5,7},{6,0},{7,1},{8,10},{9,11},{10,... | collective-permute-start | bytes 442376 | tf_op jit(solution)/shard_map/ppermute | solution.py:428
  34.6 2.6 %collective-permute-start.7 = (bf16[72,1024]{1,0:T(8,128)(2,1)}, bf16[72,1024]{1,0:T(8,128)(2,1)S(1)}, u32[]{:S(2)}, u32[]{:S(2)}) collective-permute-start(bf16[72,1024]{1,0:T(8,128)(2,1)} %get-tuple-element.118), channel_id=1, source_target_pairs={{0,4},{1,5},{2,6},{3,7},{4,0},{5,1},{6,2},{7,3},{8,12},{9,13},{10,... | collective-permute-start | bytes 442376 | tf_op jit(solution)/shard_map/ppermute | solution.py:428
  38.6 5.1 %inside_chunk.3 = (f32[128,512]{1,0:T(8,128)}, f32[128,512]{1,0:T(8,128)}, f32[128,512]{1,0:T(8,128)}, f32[128,512]{1,0:T(8,128)}, f32[128,512]{1,0:T(8,128)}, /*index=5*/f32[128,512]{1,0:T(8,128)}, f32[1,512]{1,0:T(1,128)}) custom-call(bf16[128,1024]{1,0:T(8,128)(2,1)} %refs_0_.8, bf16[128,1024]{1,0:T(8,128)(2,1)} %refs_1_.7, bf16[128,1024]{1,0:T(8,128)(2,1)} %refs_2_.8, ...), custom_call_target="tpu_custom_call" | custom-call | bytes 14000000 | tf_op jit(solution)/shard_map/inside_chunk/pallas_call | solution.py:490
  43.7 3.4 %collective-permute-done.7.refs_15_ = bf16[72,1024]{1,0:T(8,128)(2,1)S(1)} collective-permute-done((bf16[72,1024]{1,0:T(8,128)(2,1)}, bf16[72,1024]{1,0:T(8,128)(2,1)S(1)}, u32[]{:S(2)}, u32[]{:S(2)}) %collective-permute-start.7) | collective-permute-done | bytes 147488 | tf_op jit(solution)/shard_map/ppermute | solution.py:428
  47.8 2.8 %across_chunks.2 = (bf16[3,128,512]{2,1,0:T(8,128)(2,1)}, f32[128,512]{1,0:T(8,128)}, f32[128,512]{1,0:T(8,128)}, f32[1,512]{1,0:T(1,128)}) custom-call(bf16[128,1024]{1,0:T(8,128)(2,1)} %refs_0_.8, bf16[128,1024]{1,0:T(8,128)(2,1)} %refs_1_.7, bf16[128,1024]{1,0:T(8,128)(2,1)} %refs_2_.8, bf16[128,1024]{1,0:T(8,128)(2,1)} %refs_3_.8, ...), custom_call_target="tpu_custom_call" | custom-call | bytes 10500000 | tf_op jit(solution)/shard_map/across_chunks/pallas_call | solution.py:524
  50.6 3.6 %collective-permute-start.9 = (bf16[3,128,512]{2,1,0:T(8,128)(2,1)}, bf16[3,128,512]{2,1,0:T(8,128)(2,1)S(1)}, u32[]{:S(2)}, u32[]{:S(2)}) collective-permute-start(bf16[3,128,512]{2,1,0:T(8,128)(2,1)} %get-tuple-element.123.refs_0_), channel_id=1, source_target_pairs={{0,2},{1,3},{2,4},{3,5},{4,6},{5,7},{6,0},{7,1},{8,10},{9,11},{10,... | collective-permute-start | bytes 1179656 | tf_op jit(solution)/shard_map/ppermute | solution.py:428
  54.2 2.9 %across_chunks.3 = (bf16[3,128,512]{2,1,0:T(8,128)(2,1)}, f32[128,512]{1,0:T(8,128)}, f32[128,512]{1,0:T(8,128)}, f32[1,512]{1,0:T(1,128)}) custom-call(bf16[128,1024]{1,0:T(8,128)(2,1)} %refs_0_.8, bf16[128,1024]{1,0:T(8,128)(2,1)} %refs_1_.7, bf16[128,1024]{1,0:T(8,128)(2,1)} %refs_2_.8, bf16[128,1024]{1,0:T(8,128)(2,1)} %refs_3_.8, ...), custom_call_target="tpu_custom_call" | custom-call | bytes 10500000 | tf_op jit(solution)/shard_map/across_chunks/pallas_call | solution.py:524
  57.2 2.6 %decay_gradient.3 = (f32[128,512]{1,0:T(8,128)}, f32[1,512]{1,0:T(1,128)}, f32[128,128]{1,0:T(8,128)}) custom-call(f32[128,1024]{1,0:T(8,128)} %get-tuple-element.92.refs_4_.w, f32[128,512]{1,0:T(8,128)} %get-tuple-element.135.r_gr, f32[128,512]{1,0:T(8,128)} %get-tuple-element.136.k_gk, f32[1,512]{1,0:T(1,128)} %get-tuple-element.137.at_end, ...), custom_call_target="tpu_custom_call" | custom-call | bytes 7000000 | tf_op jit(solution)/shard_map/decay_gradient/pallas_call | solution.py:544
  59.8 2.4 %decay_gradient.2 = (f32[128,512]{1,0:T(8,128)}, f32[1,512]{1,0:T(1,128)}, f32[128,128]{1,0:T(8,128)}) custom-call(f32[128,1024]{1,0:T(8,128)} %get-tuple-element.92.refs_4_.w, f32[128,512]{1,0:T(8,128)} %get-tuple-element.124.r_gr, f32[128,512]{1,0:T(8,128)} %get-tuple-element.125.k_gk, f32[1,512]{1,0:T(1,128)} %get-tuple-element.126.at_end, ...), custom_call_target="tpu_custom_call" | custom-call | bytes 7000000 | tf_op jit(solution)/shard_map/decay_gradient/pallas_call | solution.py:544
  63.0 2.6 %collective-permute-done.9.refs_1_ = bf16[3,128,512]{2,1,0:T(8,128)(2,1)S(1)} collective-permute-done((bf16[3,128,512]{2,1,0:T(8,128)(2,1)}, bf16[3,128,512]{2,1,0:T(8,128)(2,1)S(1)}, u32[]{:S(2)}, u32[]{:S(2)}) %collective-permute-start.9) | collective-permute-done | bytes 393248 | tf_op jit(solution)/shard_map/ppermute | solution.py:428
  67.7 3.3 %collective-permute-done.13.refs_6_ = f32[128,128]{1,0:T(8,128)S(1)} collective-permute-done((f32[128,128]{1,0:T(8,128)S(1)}, f32[128,128]{1,0:T(8,128)S(1)}, u32[]{:S(2)}, u32[]{:S(2)}) %collective-permute-start.13) | collective-permute-done | bytes 65568 | tf_op jit(solution)/shard_map/ppermute | solution.py:434
  73.5 3.0 %adapter_grads.1 = (bf16[272,512]{1,0:T(8,128)(2,1)}, bf16[272,512]{1,0:T(8,128)(2,1)}, f32[128,1024]{1,0:T(8,128)}) custom-call(bf16[128,1024]{1,0:T(8,128)(2,1)} %refs_0_.9, bf16[1,1024]{1,0:T(2,128)(2,1)} %copy-done.25, f32[1,1024]{1,0:T(1,128)} %bitcast.5, f32[1024,128]{1,0:T(8,128)} %refs_3_.9, f32[128,128]{1,0:T(8,128)} %get-tuple-element.141.refs_4_, ...), custom_call_target="tpu_custom_call" | custom-call | bytes 10500000 | tf_op jit(solution)/shard_map/adapter_grads/pallas_call | solution.py:562
  76.6 4.2 %collective-permute-done.10.refs_2_ = bf16[3,128,512]{2,1,0:T(8,128)(2,1)S(1)} collective-permute-done((bf16[3,128,512]{2,1,0:T(8,128)(2,1)S(1)}, bf16[3,128,512]{2,1,0:T(8,128)(2,1)S(1)}, u32[]{:S(2)}, u32[]{:S(2)}) %collective-permute-start.10) | collective-permute-done | bytes 393248 | tf_op jit(solution)/shard_map/ppermute | solution.py:428
  82.7 2.3 %collective-permute-start.11 = (bf16[3,128,512]{2,1,0:T(8,128)(2,1)}, bf16[3,128,512]{2,1,0:T(8,128)(2,1)S(1)}, u32[]{:S(2)}, u32[]{:S(2)}) collective-permute-start(bf16[3,128,512]{2,1,0:T(8,128)(2,1)} %copy-done.9), channel_id=1, source_target_pairs={{0,2},{1,3},{2,4},{3,5},{4,6},{5,7},{6,0},{7,1},{8,10},{9,11},{10,... | collective-permute-start | bytes 1179656 | tf_op jit(solution)/shard_map/ppermute | solution.py:428
  85.0 5.6 %collective-permute-done.16.refs_5_ = bf16[3,128,512]{2,1,0:T(8,128)(2,1)} collective-permute-done((bf16[3,128,512]{2,1,0:T(8,128)(2,1)}, bf16[3,128,512]{2,1,0:T(8,128)(2,1)}, u32[]{:S(2)}, u32[]{:S(2)}) %collective-permute-start.16) | collective-permute-done | bytes 393248 | tf_op jit(solution)/shard_map/ppermute | solution.py:428
  96.9 7.2 %projections.2 = (bf16[144,1024]{1,0:T(8,128)(2,1)S(1)}, bf16[144,1024]{1,0:T(8,128)(2,1)S(1)}, bf16[144,1024]{1,0:T(8,128)(2,1)S(1)}) custom-call(bf16[3,128,512]{2,1,0:T(8,128)(2,1)S(1)} %copy-done.5, bf16[3,128,512]{2,1,0:T(8,128)(2,1)S(1)} %copy-done.7, bf16[3,128,512]{2,1,0:T(8,128)(2,1)S(1)} %copy-done.10, bf16[3,128,512]{2,1,0:T(8,128)(2,1)S(1)} %copy-done.8, ...), custom_call_target="tpu_custom_call" | custom-call | bytes 17500000 | tf_op jit(solution)/shard_map/projections/pallas_call | solution.py:590
  104.3 3.2 %collective-permute-done.17.refs_1_ = bf16[3,128,512]{2,1,0:T(8,128)(2,1)S(1)} collective-permute-done((bf16[3,128,512]{2,1,0:T(8,128)(2,1)}, bf16[3,128,512]{2,1,0:T(8,128)(2,1)S(1)}, u32[]{:S(2)}, u32[]{:S(2)}) %collective-permute-start.17) | collective-permute-done | bytes 393248 | tf_op jit(solution)/shard_map/ppermute | solution.py:428
  107.5 5.3 %projections.3 = (bf16[144,1024]{1,0:T(8,128)(2,1)S(1)}, bf16[144,1024]{1,0:T(8,128)(2,1)S(1)}, bf16[144,1024]{1,0:T(8,128)(2,1)S(1)}, bf16[144,1024]{1,0:T(8,128)(2,1)S(1)}) custom-call(bf16[3,128,512]{2,1,0:T(8,128)(2,1)S(1)} %collective-permute-done.11.refs_0_, bf16[3,128,512]{2,1,0:T(8,128)(2,1)S(1)} %collective-permute-done.17.refs_1_, ...), custom_call_target="tpu_custom_call" | custom-call | bytes 17500000 | tf_op jit(solution)/shard_map/projections/pallas_call | solution.py:590
  114.6 14.4 %collective-permute-done.25 = bf16[272,512]{1,0:T(8,128)(2,1)S(1)} collective-permute-done((bf16[272,512]{1,0:T(8,128)(2,1)S(1)}, bf16[272,512]{1,0:T(8,128)(2,1)S(1)}, u32[]{:S(2)}, u32[]{:S(2)}) %collective-permute-start.25) | collective-permute-done | bytes 278560 | tf_op jit(solution)/shard_map/ppermute | solution.py:613
  133.6 5.0 %collective-permute-start.28 = (f32[1,1024]{1,0:T(1,128)S(1)}, f32[1,1024]{1,0:T(1,128)S(1)}, u32[]{:S(2)}, u32[]{:S(2)}) collective-permute-start(f32[1,1024]{1,0:T(1,128)S(1)} %slice.26), channel_id=1, source_target_pairs={{1,0},{3,8},{5,16},{7,24},{8,1},{9,2},{10,9},{11,10},{12,17},{13,1... | collective-permute-start | bytes 12296 | tf_op jit(solution)/shard_map/ppermute | solution.py:646
  139.8 5.4 %collective-permute-done.22 = bf16[128,1024]{1,0:T(8,128)(2,1)S(1)} collective-permute-done((bf16[128,1024]{1,0:T(8,128)(2,1)S(1)}, bf16[128,1024]{1,0:T(8,128)(2,1)S(1)}, u32[]{:S(2)}, u32[]{:S(2)}) %collective-permute-start.22) | collective-permute-done | bytes 262176 | tf_op jit(solution)/shard_map/ppermute | solution.py:645
  (118 shorter events, 43.4 us)
Async XLA Ops:
  1.4 4.7 %collective-permute-start = (bf16[1,1024]{1,0:T(2,128)(2,1)S(1)}, bf16[1,1024]{1,0:T(2,128)(2,1)S(1)}, u32[]{:S(2)}, u32[]{:S(2)}) collective-permute-start(bf16[1,1024]{1,0:T(2,128)(2,1)S(1)} %slice.19), channel_id=1, source_target_pairs={{0,1},{1,2},{2,3},{3,4},{4,5},{5,6},{6,7},{8,9},{9,10},{10,11},{11... | collective-permute-start | bytes 6152 | tf_op jit(solution)/shard_map/ppermute | solution.py:423
  6.1 15.0 %collective-permute-start.5 = (bf16[3,96,1024]{2,1,0:T(8,128)(2,1)S(1)}, bf16[3,96,1024]{2,1,0:T(8,128)(2,1)S(1)}, u32[]{:S(2)}, u32[]{:S(2)}) collective-permute-start(bf16[3,96,1024]{2,1,0:T(8,128)(2,1)S(1)} %slice.20), channel_id=1, source_target_pairs={{0,1},{1,0},{2,3},{3,2},{4,5},{5,4},{6,7},{7,6},{8,9},{9,8},{10,11... | collective-permute-start | bytes 1769480 | tf_op jit(solution)/shard_map/ppermute | solution.py:431
  10.7 5.1 %collective-permute-start.2 = (f32[128,128]{1,0:T(8,128)}, f32[128,128]{1,0:T(8,128)S(1)}, u32[]{:S(2)}, u32[]{:S(2)}) collective-permute-start(f32[128,128]{1,0:T(8,128)} %adapter_input.1.refs_0_), channel_id=1, source_target_pairs={{0,16},{8,24},{16,0},{24,8},{1,17},{9,25},{17,1},{25,9},{2,18},{10... | collective-permute-start | bytes 196616 | tf_op jit(solution)/shard_map/ppermute | solution.py:434
  19.8 9.7 %collective-permute-start.4 = (bf16[136,1024]{1,0:T(8,128)(2,1)}, bf16[136,1024]{1,0:T(8,128)(2,1)S(1)}, u32[]{:S(2)}, u32[]{:S(2)}) collective-permute-start(bf16[136,1024]{1,0:T(8,128)(2,1)} %get-tuple-element.88.refs_0_), channel_id=1, source_target_pairs={{0,1},{1,0},{2,3},{3,2},{4,5},{5,4},{6,7},{7,6},{8,9},{9,8},{10,11... | collective-permute-start | bytes 835592 | tf_op jit(solution)/shard_map/ppermute | solution.py:431
  29.5 62.3 %collective-permute-start.18 = (bf16[3,416,1024]{2,1,0:T(8,128)(2,1)}, bf16[3,416,1024]{2,1,0:T(8,128)(2,1)}, u32[]{:S(2)}, u32[]{:S(2)}) collective-permute-start(bf16[3,416,1024]{2,1,0:T(8,128)(2,1)} %get-tuple-element.150), channel_id=1, source_target_pairs={{0,1},{1,0},{2,3},{3,2},{4,5},{5,4},{6,7},{7,6},{8,9},{9,8},{10,11... | collective-permute-start | bytes 7667720 | tf_op jit(solution)/shard_map/ppermute | solution.py:431
  32.3 11.4 %collective-permute-start.6 = (bf16[72,1024]{1,0:T(8,128)(2,1)}, bf16[72,1024]{1,0:T(8,128)(2,1)S(1)}, u32[]{:S(2)}, u32[]{:S(2)}) collective-permute-start(bf16[72,1024]{1,0:T(8,128)(2,1)} %get-tuple-element.117), channel_id=1, source_target_pairs={{0,2},{1,3},{2,4},{3,5},{4,6},{5,7},{6,0},{7,1},{8,10},{9,11},{10,... | collective-permute-start | bytes 442376 | tf_op jit(solution)/shard_map/ppermute | solution.py:428
  34.6 12.5 %collective-permute-start.7 = (bf16[72,1024]{1,0:T(8,128)(2,1)}, bf16[72,1024]{1,0:T(8,128)(2,1)S(1)}, u32[]{:S(2)}, u32[]{:S(2)}) collective-permute-start(bf16[72,1024]{1,0:T(8,128)(2,1)} %get-tuple-element.118), channel_id=1, source_target_pairs={{0,4},{1,5},{2,6},{3,7},{4,0},{5,1},{6,2},{7,3},{8,12},{9,13},{10,... | collective-permute-start | bytes 442376 | tf_op jit(solution)/shard_map/ppermute | solution.py:428
  37.2 9.9 %collective-permute-start.8 = (bf16[72,1024]{1,0:T(8,128)(2,1)}, bf16[72,1024]{1,0:T(8,128)(2,1)S(1)}, u32[]{:S(2)}, u32[]{:S(2)}) collective-permute-start(bf16[72,1024]{1,0:T(8,128)(2,1)} %get-tuple-element.119), channel_id=1, source_target_pairs={{0,6},{1,7},{2,0},{3,1},{4,2},{5,3},{6,4},{7,5},{8,14},{9,15},{10,... | collective-permute-start | bytes 442376 | tf_op jit(solution)/shard_map/ppermute | solution.py:428
  50.6 15.0 %collective-permute-start.9 = (bf16[3,128,512]{2,1,0:T(8,128)(2,1)}, bf16[3,128,512]{2,1,0:T(8,128)(2,1)S(1)}, u32[]{:S(2)}, u32[]{:S(2)}) collective-permute-start(bf16[3,128,512]{2,1,0:T(8,128)(2,1)} %get-tuple-element.123.refs_0_), channel_id=1, source_target_pairs={{0,2},{1,3},{2,4},{3,5},{4,6},{5,7},{6,0},{7,1},{8,10},{9,11},{10,... | collective-permute-start | bytes 1179656 | tf_op jit(solution)/shard_map/ppermute | solution.py:428
  57.1 19.4 %collective-permute-start.12 = (bf16[3,128,512]{2,1,0:T(8,128)(2,1)}, bf16[3,128,512]{2,1,0:T(8,128)(2,1)}, u32[]{:S(2)}, u32[]{:S(2)}) collective-permute-start(bf16[3,128,512]{2,1,0:T(8,128)(2,1)} %get-tuple-element.140.refs_3_), channel_id=1, source_target_pairs={{0,2},{1,3},{2,4},{3,5},{4,6},{5,7},{6,0},{7,1},{8,10},{9,11},{10,... | collective-permute-start | bytes 1179656 | tf_op jit(solution)/shard_map/ppermute | solution.py:428
  65.6 15.2 %collective-permute-start.10 = (bf16[3,128,512]{2,1,0:T(8,128)(2,1)S(1)}, bf16[3,128,512]{2,1,0:T(8,128)(2,1)S(1)}, u32[]{:S(2)}, u32[]{:S(2)}) collective-permute-start(bf16[3,128,512]{2,1,0:T(8,128)(2,1)S(1)} %collective-permute-done.9.refs_1_), channel_id=1, source_target_pairs={{0,2},{1,3},{2,4},{3,5},{4,6},{5,7},{6,0},{7,1},{8,10},{9,11},{10,... | collective-permute-start | bytes 1179656 | tf_op jit(solution)/shard_map/ppermute | solution.py:428
  67.2 4.9 %collective-permute-start.14 = (f32[128,128]{1,0:T(8,128)S(1)}, f32[128,128]{1,0:T(8,128)S(1)}, u32[]{:S(2)}, u32[]{:S(2)}) collective-permute-start(f32[128,128]{1,0:T(8,128)S(1)} %add.33.refs_5_), channel_id=1, source_target_pairs={{0,16},{8,24},{16,0},{24,8},{1,17},{9,25},{17,1},{25,9},{2,18},{10... | collective-permute-start | bytes 196616 | tf_op jit(solution)/shard_map/ppermute | solution.py:434
  76.5 14.1 %collective-permute-start.16 = (bf16[3,128,512]{2,1,0:T(8,128)(2,1)}, bf16[3,128,512]{2,1,0:T(8,128)(2,1)}, u32[]{:S(2)}, u32[]{:S(2)}) collective-permute-start(bf16[3,128,512]{2,1,0:T(8,128)(2,1)} %collective-permute-done.12.refs_4_), channel_id=1, source_target_pairs={{0,2},{1,3},{2,4},{3,5},{4,6},{5,7},{6,0},{7,1},{8,10},{9,11},{10,... | collective-permute-start | bytes 1179656 | tf_op jit(solution)/shard_map/ppermute | solution.py:428
  81.6 22.5 %collective-permute-start.23 = (bf16[272,512]{1,0:T(8,128)(2,1)}, bf16[272,512]{1,0:T(8,128)(2,1)S(1)}, u32[]{:S(2)}, u32[]{:S(2)}) collective-permute-start(bf16[272,512]{1,0:T(8,128)(2,1)} %get-tuple-element.160), channel_id=1, source_target_pairs={{0,1},{1,0},{2,3},{3,2},{4,5},{5,4},{6,7},{7,6},{8,9},{9,8},{10,11... | collective-permute-start | bytes 835592 | tf_op jit(solution)/shard_map/ppermute | solution.py:431
  82.7 24.7 %collective-permute-start.11 = (bf16[3,128,512]{2,1,0:T(8,128)(2,1)}, bf16[3,128,512]{2,1,0:T(8,128)(2,1)S(1)}, u32[]{:S(2)}, u32[]{:S(2)}) collective-permute-start(bf16[3,128,512]{2,1,0:T(8,128)(2,1)} %copy-done.9), channel_id=1, source_target_pairs={{0,2},{1,3},{2,4},{3,5},{4,6},{5,7},{6,0},{7,1},{8,10},{9,11},{10,... | collective-permute-start | bytes 1179656 | tf_op jit(solution)/shard_map/ppermute | solution.py:428
  90.6 16.8 %collective-permute-start.17 = (bf16[3,128,512]{2,1,0:T(8,128)(2,1)}, bf16[3,128,512]{2,1,0:T(8,128)(2,1)S(1)}, u32[]{:S(2)}, u32[]{:S(2)}) collective-permute-start(bf16[3,128,512]{2,1,0:T(8,128)(2,1)} %collective-permute-done.16.refs_5_), channel_id=1, source_target_pairs={{0,2},{1,3},{2,4},{3,5},{4,6},{5,7},{6,0},{7,1},{8,10},{9,11},{10,... | collective-permute-start | bytes 1179656 | tf_op jit(solution)/shard_map/ppermute | solution.py:428
  104.2 9.2 %collective-permute-start.24 = (bf16[272,512]{1,0:T(8,128)(2,1)S(1)}, bf16[272,512]{1,0:T(8,128)(2,1)S(1)}, u32[]{:S(2)}, u32[]{:S(2)}) collective-permute-start(bf16[272,512]{1,0:T(8,128)(2,1)S(1)} %add_convert_fusion.4), channel_id=1, source_target_pairs={{0,2},{1,3},{2,0},{3,1},{4,6},{5,7},{6,4},{7,5},{8,10},{9,11},{10,... | collective-permute-start | bytes 835592 | tf_op jit(solution)/shard_map/ppermute | solution.py:613
  112.9 17.3 %collective-permute-start.19 = (bf16[144,1024]{1,0:T(8,128)(2,1)S(1)}, bf16[144,1024]{1,0:T(8,128)(2,1)S(1)}, u32[]{:S(2)}, u32[]{:S(2)}) collective-permute-start(bf16[144,1024]{1,0:T(8,128)(2,1)S(1)} %get-tuple-element.156), channel_id=1, source_target_pairs={{0,8},{8,0},{16,24},{24,16},{1,9},{9,1},{17,25},{25,17},{2,10},{10... | collective-permute-start | bytes 884744 | tf_op jit(solution)/shard_map/ppermute | solution.py:625
  113.5 15.5 %collective-permute-start.25 = (bf16[272,512]{1,0:T(8,128)(2,1)S(1)}, bf16[272,512]{1,0:T(8,128)(2,1)S(1)}, u32[]{:S(2)}, u32[]{:S(2)}) collective-permute-start(bf16[272,512]{1,0:T(8,128)(2,1)S(1)} %add_convert_fusion.3), channel_id=1, source_target_pairs={{0,4},{1,5},{2,6},{3,7},{4,0},{5,1},{6,2},{7,3},{8,12},{9,13},{10,... | collective-permute-start | bytes 835592 | tf_op jit(solution)/shard_map/ppermute | solution.py:613
  114.5 15.6 %collective-permute-start.21 = (bf16[144,1024]{1,0:T(8,128)(2,1)S(1)}, bf16[144,1024]{1,0:T(8,128)(2,1)S(1)}, u32[]{:S(2)}, u32[]{:S(2)}) collective-permute-start(bf16[144,1024]{1,0:T(8,128)(2,1)S(1)} %add_convert_fusion), channel_id=1, source_target_pairs={{0,16},{8,24},{16,0},{24,8},{1,17},{9,25},{17,1},{25,9},{2,18},{10... | collective-permute-start | bytes 884744 | tf_op jit(solution)/shard_map/ppermute | solution.py:625
  129.1 9.6 %collective-permute-start.26 = (bf16[272,512]{1,0:T(8,128)(2,1)S(1)}, bf16[272,512]{1,0:T(8,128)(2,1)S(1)}, u32[]{:S(2)}, u32[]{:S(2)}) collective-permute-start(bf16[272,512]{1,0:T(8,128)(2,1)S(1)} %add_convert_fusion.2.refs_0_), channel_id=1, source_target_pairs={{0,1},{1,0},{2,3},{3,2},{4,5},{5,4},{6,7},{7,6},{8,9},{9,8},{10,11... | collective-permute-start | bytes 835592 | tf_op jit(solution)/shard_map/ppermute | solution.py:431
  130.3 14.9 %collective-permute-start.22 = (bf16[128,1024]{1,0:T(8,128)(2,1)S(1)}, bf16[128,1024]{1,0:T(8,128)(2,1)S(1)}, u32[]{:S(2)}, u32[]{:S(2)}) collective-permute-start(bf16[128,1024]{1,0:T(8,128)(2,1)S(1)} %slice.28), channel_id=1, source_target_pairs={{0,0},{1,1},{2,8},{3,9},{4,16},{5,17},{6,24},{7,25},{8,2},{9,3},{1... | collective-permute-start | bytes 786440 | tf_op jit(solution)/shard_map/ppermute | solution.py:645
  132.3 13.0 %collective-permute-start.27 = (f32[1,1024]{1,0:T(1,128)S(1)}, f32[1,1024]{1,0:T(1,128)S(1)}, u32[]{:S(2)}, u32[]{:S(2)}) collective-permute-start(f32[1,1024]{1,0:T(1,128)S(1)} %slice.23), channel_id=1, source_target_pairs={{1,0},{2,1},{3,2},{4,3},{5,4},{6,5},{7,6},{9,8},{10,9},{11,10},{12... | collective-permute-start | bytes 12296 | tf_op jit(solution)/shard_map/ppermute | solution.py:423
  133.6 12.2 %collective-permute-start.28 = (f32[1,1024]{1,0:T(1,128)S(1)}, f32[1,1024]{1,0:T(1,128)S(1)}, u32[]{:S(2)}, u32[]{:S(2)}) collective-permute-start(f32[1,1024]{1,0:T(1,128)S(1)} %slice.26), channel_id=1, source_target_pairs={{1,0},{3,8},{5,16},{7,24},{8,1},{9,2},{10,9},{11,10},{12,17},{13,1... | collective-permute-start | bytes 12296 | tf_op jit(solution)/shard_map/ppermute | solution.py:646
  (32 other events, 245.7 us)

commit v8 on v6

--- a/solution.py
+++ b/solution.py
@@ -385,7 +385,7 @@
                 store(outs[q], q)
             continue
         for d in range(ring):
-            wanted = lax.rem(place[1] - place[2] - d + 2 * ring, ring)
+            wanted = lax.rem(place[1] - lax.bitwise_xor(place[2], d) + ring, ring)
             for q in range(ring):
 
                 @pl.when(wanted == q)
@@ -606,12 +606,23 @@
 
     done = project(lows[:-1], highs[:-1])
     sends = project(lows[-1:], highs[-1:], done)
+    def across(a, bit):
+        return lax.ppermute(a, "head", [(i, i ^ bit) for i in range(n_head)])
+
+    left, bit = dict(enumerate(sends)), 1
+    while bit < n_head:
+        came = {e: across(left[e | bit], bit) for e in left if not e & bit}
+        left = {e: left[e].astype(F32) + came[e].astype(F32) for e in came}
+        bit *= 2
+        if bit < n_head:
+            left = {e: value.astype(BF16) for e, value in left.items()}
+    total = left[0]
     token_sums = add(keep, after_that(got, *done))
     b = 1
     while b < ring:
         route = [(i, ((i // inner) ^ b) * inner + i % inner) for i in range(n_seq)]
         got = lax.ppermute(token_sums, "seq", route)
-        token_sums = add(token_sums, after_that(got, sends) if b == 1 else got)
+        token_sums = add(token_sums, after_that(got, {1: sends, 2: total}.get(b, ())))
         b *= 2
     up_grad, down_grad, base_grad, du = pl.pallas_call(
         lambda *refs: finish_kernel(rank, *refs),
@@ -621,9 +632,6 @@
         name="token_sums",
     )(token_sums, partner(token_sums))
 
-    total = sends[0].astype(F32)
-    for d in range(1, n_head):
-        total = total + head_shift(sends[d], d).astype(F32)
     swap, back = [], []
     for h in range(n_head):
         for z in range(ring):

time: 146 us -> 159 us (1.089)
  waiting for transfers between devices: 46.4 us -> 63.2 us
  starting transfers between devices: 38 us -> 35.3 us
    ppermute x2, waiting for transfers between devices: 0.67 us -> 20.6 us  [per_device(): got = lax.ppermute(token_sums, 'seq', route)]
    ppermute x9 -> x6, waiting for transfers between devices: 19.5 us -> 8.3 us  [head_shift(): lax.ppermute(a, 'head', [(i, (i + d) % n_head) for i in range(n_head)])]
    ppermute x9, waiting for transfers between devices: 18.9 us -> 23.7 us  [around(): lax.ppermute(a, 'seq', [(i, (i + inner * step) % n_seq) for i in range(n_...]
    ppermute x1, waiting for transfers between devices: 3.27 us -> 7.08 us  [per_device(): summed = lax.ppermute(total[:rows].astype(BF16), ('head', 'seq'), swap)]
    ppermute x9 -> x6, starting transfers between devices: 4.32 us -> 2.58 us  [head_shift(): lax.ppermute(a, 'head', [(i, (i + d) % n_head) for i in range(n_head)])]
    ppermute x2, starting transfers between devices: 0.15 us -> 1.87 us  [per_device(): got = lax.ppermute(token_sums, 'seq', route)]
  transfers between devices with their start and end apart: 29 -> 29, of which waited for: 19 -> 17; matrix products, arithmetic and copies ran while one was open for 2% -> 2% of each run, Pallas kernels for 32% -> 29%
where the time goes in v8:
time: 159 us
  waiting for transfers between devices  63.2 us (40%)
  Pallas kernels  45.6 us (29%)
  starting transfers between devices  35.3 us (22%)
  local copies, waits for them, and re-layouts  11.4 us (7%)
  other arithmetic  2.16 us (1%)
    ppermute x9, waiting for transfers between devices, around(): lax.ppermute(a, 'seq', [(i, (i + inner * step) % n_seq) for i in range(n_...  23.7 us
    ppermute x2, waiting for transfers between devices, per_device(): got = lax.ppermute(token_sums, 'seq', route)  20.6 us
    ppermute x9, starting transfers between devices, around(): lax.ppermute(a, 'seq', [(i, (i + inner * step) % n_seq) for i in range(n_...  13.6 us
    pallas_call x2, Pallas kernels, project(): pl.pallas_call(lambda *refs: project_kernel(count, ring, final, *refs), i...  11.6 us
    pallas_call x2, Pallas kernels, inside(): pl.pallas_call(lambda *refs: inner_kernel(head, cut if extra else 0, *ref...  11.6 us
    unnamed x54, local copies, waits for them, and re-layouts  8.74 us
    ppermute x6, waiting for transfers between devices, head_shift(): lax.ppermute(a, 'head', [(i, (i + d) % n_head) for i in range(n_head)])  8.3 us
    ppermute x1, waiting for transfers between devices, per_device(): summed = lax.ppermute(total[:rows].astype(BF16), ('head', 'seq'), swap)  7.08 us
  transfers between devices with their start and end apart: 29, of which 17 were waited for; matrix products, arithmetic and copies ran while one was open for 2% of the time, Pallas kernels for 29%

profile of v8, /device:TPU:4, one launch (start us, length us, event | category | flops | bytes accessed | tf_op | source)
XLA Modules:
  0.0 158.6 jit_solution(5550718119786169403)
XLA Ops:
  1.4 3.4 %collective-permute-start = (bf16[1,1024]{1,0:T(2,128)(2,1)S(1)}, bf16[1,1024]{1,0:T(2,128)(2,1)S(1)}, u32[]{:S(2)}, u32[]{:S(2)}) collective-permute-start(bf16[1,1024]{1,0:T(2,128)(2,1)S(1)} %slice.19), channel_id=1, source_target_pairs={{0,1},{1,2},{2,3},{3,4},{4,5},{5,6},{6,7},{8,9},{9,10},{10,11},{11... | collective-permute-start | bytes 6152 | tf_op jit(solution)/shard_map/ppermute | solution.py:423
  16.4 3.4 %decay_and_states.1 = (f32[128,128]{1,0:T(8,128)}, bf16[128,128]{1,0:T(8,128)(2,1)}, f32[128,1024]{1,0:T(8,128)}, f32[1,1024]{1,0:T(1,128)}, f32[64,1024]{1,0:T(8,128)}, /*index=5*/bf16[136,1024]{1,0:T(8,128)(2,1)}) custom-call(f32[128,128]{1,0:T(8,128)} %adapter_input.1.refs_0_, f32[128,128]{1,0:T(8,128)} %copy-done.21, f32[128,128]{1,0:T(8,128)} %copy-done.23, ...), custom_call_target="tpu_custom_call" | custom-call | bytes 10500000 | tf_op jit(solution)/shard_map/decay_and_states/pallas_call | solution.py:464
  21.1 6.4 %inside_chunk.2 = (f32[128,512]{1,0:T(8,128)}, f32[128,512]{1,0:T(8,128)}, f32[128,512]{1,0:T(8,128)}, f32[128,512]{1,0:T(8,128)}, f32[128,512]{1,0:T(8,128)}, /...) custom-call(bf16[128,1024]{1,0:T(8,128)(2,1)} %refs_0_.8, bf16[128,1024]{1,0:T(8,128)(2,1)} %refs_1_.7, ...), custom_call_target="tpu_custom_call" | custom-call | bytes 14000000 | tf_op jit(solution)/shard_map/inside_chunk/pallas_call | solution.py:490
  32.3 2.3 %collective-permute-start.6 = (bf16[72,1024]{1,0:T(8,128)(2,1)}, bf16[72,1024]{1,0:T(8,128)(2,1)S(1)}, u32[]{:S(2)}, u32[]{:S(2)}) collective-permute-start(bf16[72,1024]{1,0:T(8,128)(2,1)} %get-tuple-element.118), channel_id=1, source_target_pairs={{0,2},{1,3},{2,4},{3,5},{4,6},{5,7},{6,0},{7,1},{8,10},{9,11},{10,... | collective-permute-start | bytes 442376 | tf_op jit(solution)/shard_map/ppermute | solution.py:428
  34.6 2.6 %collective-permute-start.7 = (bf16[72,1024]{1,0:T(8,128)(2,1)}, bf16[72,1024]{1,0:T(8,128)(2,1)S(1)}, u32[]{:S(2)}, u32[]{:S(2)}) collective-permute-start(bf16[72,1024]{1,0:T(8,128)(2,1)} %get-tuple-element.119), channel_id=1, source_target_pairs={{0,4},{1,5},{2,6},{3,7},{4,0},{5,1},{6,2},{7,3},{8,12},{9,13},{10,... | collective-permute-start | bytes 442376 | tf_op jit(solution)/shard_map/ppermute | solution.py:428
  38.5 5.1 %inside_chunk.3 = (f32[128,512]{1,0:T(8,128)}, f32[128,512]{1,0:T(8,128)}, f32[128,512]{1,0:T(8,128)}, f32[128,512]{1,0:T(8,128)}, f32[128,512]{1,0:T(8,128)}, /*index=5*/f32[128,512]{1,0:T(8,128)}, f32[1,512]{1,0:T(1,128)}) custom-call(bf16[128,1024]{1,0:T(8,128)(2,1)} %refs_0_.8, bf16[128,1024]{1,0:T(8,128)(2,1)} %refs_1_.7, bf16[128,1024]{1,0:T(8,128)(2,1)} %refs_2_.8, ...), custom_call_target="tpu_custom_call" | custom-call | bytes 14000000 | tf_op jit(solution)/shard_map/inside_chunk/pallas_call | solution.py:490
  43.7 3.4 %collective-permute-done.7.refs_15_ = bf16[72,1024]{1,0:T(8,128)(2,1)S(1)} collective-permute-done((bf16[72,1024]{1,0:T(8,128)(2,1)}, bf16[72,1024]{1,0:T(8,128)(2,1)S(1)}, u32[]{:S(2)}, u32[]{:S(2)}) %collective-permute-start.7) | collective-permute-done | bytes 147488 | tf_op jit(solution)/shard_map/ppermute | solution.py:428
  47.8 2.8 %across_chunks.2 = (bf16[3,128,512]{2,1,0:T(8,128)(2,1)}, f32[128,512]{1,0:T(8,128)}, f32[128,512]{1,0:T(8,128)}, f32[1,512]{1,0:T(1,128)}) custom-call(bf16[128,1024]{1,0:T(8,128)(2,1)} %refs_0_.8, bf16[128,1024]{1,0:T(8,128)(2,1)} %refs_1_.7, bf16[128,1024]{1,0:T(8,128)(2,1)} %refs_2_.8, bf16[128,1024]{1,0:T(8,128)(2,1)} %refs_3_.8, ...), custom_call_target="tpu_custom_call" | custom-call | bytes 10500000 | tf_op jit(solution)/shard_map/across_chunks/pallas_call | solution.py:524
  50.6 3.6 %collective-permute-start.9 = (bf16[3,128,512]{2,1,0:T(8,128)(2,1)}, bf16[3,128,512]{2,1,0:T(8,128)(2,1)S(1)}, u32[]{:S(2)}, u32[]{:S(2)}) collective-permute-start(bf16[3,128,512]{2,1,0:T(8,128)(2,1)} %get-tuple-element.124.refs_0_), channel_id=1, source_target_pairs={{0,2},{1,3},{2,4},{3,5},{4,6},{5,7},{6,0},{7,1},{8,10},{9,11},{10,... | collective-permute-start | bytes 1179656 | tf_op jit(solution)/shard_map/ppermute | solution.py:428
  54.2 2.9 %across_chunks.3 = (bf16[3,128,512]{2,1,0:T(8,128)(2,1)}, f32[128,512]{1,0:T(8,128)}, f32[128,512]{1,0:T(8,128)}, f32[1,512]{1,0:T(1,128)}) custom-call(bf16[128,1024]{1,0:T(8,128)(2,1)} %refs_0_.8, bf16[128,1024]{1,0:T(8,128)(2,1)} %refs_1_.7, bf16[128,1024]{1,0:T(8,128)(2,1)} %refs_2_.8, bf16[128,1024]{1,0:T(8,128)(2,1)} %refs_3_.8, ...), custom_call_target="tpu_custom_call" | custom-call | bytes 10500000 | tf_op jit(solution)/shard_map/across_chunks/pallas_call | solution.py:524
  57.2 2.6 %decay_gradient.3 = (f32[128,512]{1,0:T(8,128)}, f32[1,512]{1,0:T(1,128)}, f32[128,128]{1,0:T(8,128)}) custom-call(f32[128,1024]{1,0:T(8,128)} %get-tuple-element.93.refs_4_.w, f32[128,512]{1,0:T(8,128)} %get-tuple-element.136.r_gr, f32[128,512]{1,0:T(8,128)} %get-tuple-element.137.k_gk, f32[1,512]{1,0:T(1,128)} %get-tuple-element.138.at_end, ...), custom_call_target="tpu_custom_call" | custom-call | bytes 7000000 | tf_op jit(solution)/shard_map/decay_gradient/pallas_call | solution.py:544
  59.7 2.4 %decay_gradient.2 = (f32[128,512]{1,0:T(8,128)}, f32[1,512]{1,0:T(1,128)}, f32[128,128]{1,0:T(8,128)}) custom-call(f32[128,1024]{1,0:T(8,128)} %get-tuple-element.93.refs_4_.w, f32[128,512]{1,0:T(8,128)} %get-tuple-element.125.r_gr, f32[128,512]{1,0:T(8,128)} %get-tuple-element.126.k_gk, f32[1,512]{1,0:T(1,128)} %get-tuple-element.127.at_end, ...), custom_call_target="tpu_custom_call" | custom-call | bytes 7000000 | tf_op jit(solution)/shard_map/decay_gradient/pallas_call | solution.py:544
  63.6 3.2 %collective-permute-done.13.refs_6_ = f32[128,128]{1,0:T(8,128)S(1)} collective-permute-done((f32[128,128]{1,0:T(8,128)S(1)}, f32[128,128]{1,0:T(8,128)S(1)}, u32[]{:S(2)}, u32[]{:S(2)}) %collective-permute-start.13) | collective-permute-done | bytes 65568 | tf_op jit(solution)/shard_map/ppermute | solution.py:434
  69.4 3.0 %adapter_grads.1 = (bf16[272,512]{1,0:T(8,128)(2,1)}, bf16[272,512]{1,0:T(8,128)(2,1)}, f32[128,1024]{1,0:T(8,128)}) custom-call(bf16[128,1024]{1,0:T(8,128)(2,1)} %refs_0_.9, bf16[1,1024]{1,0:T(2,128)(2,1)} %copy-done.25, f32[1,1024]{1,0:T(1,128)} %bitcast.5, f32[1024,128]{1,0:T(8,128)} %refs_3_.9, f32[128,128]{1,0:T(8,128)} %get-tuple-element.142.refs_4_, ...), custom_call_target="tpu_custom_call" | custom-call | bytes 10500000 | tf_op jit(solution)/shard_map/adapter_grads/pallas_call | solution.py:562
  72.4 2.3 %collective-permute-start.16 = (bf16[3,128,512]{2,1,0:T(8,128)(2,1)S(1)}, bf16[3,128,512]{2,1,0:T(8,128)(2,1)}, u32[]{:S(2)}, u32[]{:S(2)}) collective-permute-start(bf16[3,128,512]{2,1,0:T(8,128)(2,1)S(1)} %collective-permute-done.12.refs_4_), channel_id=1, source_target_pairs={{0,2},{1,3},{2,4},{3,5},{4,6},{5,7},{6,0},{7,1},{8,10},{9,11},{10,... | collective-permute-start | bytes 1179656 | tf_op jit(solution)/shard_map/ppermute | solution.py:428
  76.3 9.7 %collective-permute-done.16.refs_5_ = bf16[3,128,512]{2,1,0:T(8,128)(2,1)} collective-permute-done((bf16[3,128,512]{2,1,0:T(8,128)(2,1)S(1)}, bf16[3,128,512]{2,1,0:T(8,128)(2,1)}, u32[]{:S(2)}, u32[]{:S(2)}) %collective-permute-start.16) | collective-permute-done | bytes 393248 | tf_op jit(solution)/shard_map/ppermute | solution.py:428
  86.7 7.7 %collective-permute-done.10.refs_2_ = bf16[3,128,512]{2,1,0:T(8,128)(2,1)} collective-permute-done((bf16[3,128,512]{2,1,0:T(8,128)(2,1)S(1)}, bf16[3,128,512]{2,1,0:T(8,128)(2,1)}, u32[]{:S(2)}, u32[]{:S(2)}) %collective-permute-start.10) | collective-permute-done | bytes 393248 | tf_op jit(solution)/shard_map/ppermute | solution.py:428
  101.2 7.2 %projections.2 = (bf16[144,1024]{1,0:T(8,128)(2,1)S(1)}, bf16[144,1024]{1,0:T(8,128)(2,1)S(1)}, bf16[144,1024]{1,0:T(8,128)(2,1)S(1)}) custom-call(bf16[3,128,512]{2,1,0:T(8,128)(2,1)S(1)} %copy-done.5, bf16[3,128,512]{2,1,0:T(8,128)(2,1)S(1)} %copy-done.7, bf16[3,128,512]{2,1,0:T(8,128)(2,1)} %collective-permute-done.10.refs_2_, ...), custom_call_target="tpu_custom_call" | custom-call | bytes 17500000 | tf_op jit(solution)/shard_map/projections/pallas_call | solution.py:590
  108.5 2.9 %collective-permute-done.11.refs_0_ = bf16[3,128,512]{2,1,0:T(8,128)(2,1)} collective-permute-done((bf16[3,128,512]{2,1,0:T(8,128)(2,1)}, bf16[3,128,512]{2,1,0:T(8,128)(2,1)}, u32[]{:S(2)}, u32[]{:S(2)}) %collective-permute-start.11) | collective-permute-done | bytes 393248 | tf_op jit(solution)/shard_map/ppermute | solution.py:428
  111.3 4.4 %projections.3 = (bf16[144,1024]{1,0:T(8,128)(2,1)S(1)}, bf16[144,1024]{1,0:T(8,128)(2,1)S(1)}, bf16[144,1024]{1,0:T(8,128)(2,1)S(1)}, bf16[144,1024]{1,0:T(8,128)(2,1)S(1)}) custom-call(bf16[3,128,512]{2,1,0:T(8,128)(2,1)} %collective-permute-done.11.refs_0_, bf16[3,128,512]{2,1,0:T(8,128)(2,1)} %collective-permute-done.17.refs_1_, ...), custom_call_target="tpu_custom_call" | custom-call | bytes 17500000 | tf_op jit(solution)/shard_map/projections/pallas_call | solution.py:590
  117.8 7.2 %collective-permute-done.24 = bf16[272,512]{1,0:T(8,128)(2,1)S(1)} collective-permute-done((bf16[272,512]{1,0:T(8,128)(2,1)S(1)}, bf16[272,512]{1,0:T(8,128)(2,1)S(1)}, u32[]{:S(2)}, u32[]{:S(2)}) %collective-permute-start.24) | collective-permute-done | bytes 278560 | tf_op jit(solution)/shard_map/ppermute | solution.py:624
  126.8 13.4 %collective-permute-done.25 = bf16[272,512]{1,0:T(8,128)(2,1)S(1)} collective-permute-done((bf16[272,512]{1,0:T(8,128)(2,1)S(1)}, bf16[272,512]{1,0:T(8,128)(2,1)S(1)}, u32[]{:S(2)}, u32[]{:S(2)}) %collective-permute-start.25) | collective-permute-done | bytes 278560 | tf_op jit(solution)/shard_map/ppermute | solution.py:624
  144.7 4.3 %collective-permute-start.28 = (f32[1,1024]{1,0:T(1,128)S(1)}, f32[1,1024]{1,0:T(1,128)S(1)}, u32[]{:S(2)}, u32[]{:S(2)}) collective-permute-start(f32[1,1024]{1,0:T(1,128)S(1)} %slice.26), channel_id=1, source_target_pairs={{1,0},{3,8},{5,16},{7,24},{8,1},{9,2},{10,9},{11,10},{12,17},{13,1... | collective-permute-start | bytes 12296 | tf_op jit(solution)/shard_map/ppermute | solution.py:646
  150.2 7.1 %collective-permute-done.22 = bf16[128,1024]{1,0:T(8,128)(2,1)S(1)} collective-permute-done((bf16[128,1024]{1,0:T(8,128)(2,1)S(1)}, bf16[128,1024]{1,0:T(8,128)(2,1)S(1)}, u32[]{:S(2)}, u32[]{:S(2)}) %collective-permute-start.22) | collective-permute-done | bytes 262176 | tf_op jit(solution)/shard_map/ppermute | solution.py:645
  (118 shorter events, 44.5 us)
Async XLA Ops:
  1.4 4.7 %collective-permute-start = (bf16[1,1024]{1,0:T(2,128)(2,1)S(1)}, bf16[1,1024]{1,0:T(2,128)(2,1)S(1)}, u32[]{:S(2)}, u32[]{:S(2)}) collective-permute-start(bf16[1,1024]{1,0:T(2,128)(2,1)S(1)} %slice.19), channel_id=1, source_target_pairs={{0,1},{1,2},{2,3},{3,4},{4,5},{5,6},{6,7},{8,9},{9,10},{10,11},{11... | collective-permute-start | bytes 6152 | tf_op jit(solution)/shard_map/ppermute | solution.py:423
  6.1 14.9 %collective-permute-start.5 = (bf16[3,96,1024]{2,1,0:T(8,128)(2,1)S(1)}, bf16[3,96,1024]{2,1,0:T(8,128)(2,1)S(1)}, u32[]{:S(2)}, u32[]{:S(2)}) collective-permute-start(bf16[3,96,1024]{2,1,0:T(8,128)(2,1)S(1)} %slice.20), channel_id=1, source_target_pairs={{0,1},{1,0},{2,3},{3,2},{4,5},{5,4},{6,7},{7,6},{8,9},{9,8},{10,11... | collective-permute-start | bytes 1769480 | tf_op jit(solution)/shard_map/ppermute | solution.py:431
  10.7 5.1 %collective-permute-start.2 = (f32[128,128]{1,0:T(8,128)}, f32[128,128]{1,0:T(8,128)S(1)}, u32[]{:S(2)}, u32[]{:S(2)}) collective-permute-start(f32[128,128]{1,0:T(8,128)} %adapter_input.1.refs_0_), channel_id=1, source_target_pairs={{0,16},{8,24},{16,0},{24,8},{1,17},{9,25},{17,1},{25,9},{2,18},{10... | collective-permute-start | bytes 196616 | tf_op jit(solution)/shard_map/ppermute | solution.py:434
  19.8 9.7 %collective-permute-start.4 = (bf16[136,1024]{1,0:T(8,128)(2,1)}, bf16[136,1024]{1,0:T(8,128)(2,1)S(1)}, u32[]{:S(2)}, u32[]{:S(2)}) collective-permute-start(bf16[136,1024]{1,0:T(8,128)(2,1)} %get-tuple-element.89.refs_0_), channel_id=1, source_target_pairs={{0,1},{1,0},{2,3},{3,2},{4,5},{5,4},{6,7},{7,6},{8,9},{9,8},{10,11... | collective-permute-start | bytes 835592 | tf_op jit(solution)/shard_map/ppermute | solution.py:431
  29.5 66.6 %collective-permute-start.18 = (bf16[3,416,1024]{2,1,0:T(8,128)(2,1)}, bf16[3,416,1024]{2,1,0:T(8,128)(2,1)}, u32[]{:S(2)}, u32[]{:S(2)}) collective-permute-start(bf16[3,416,1024]{2,1,0:T(8,128)(2,1)} %get-tuple-element.151), channel_id=1, source_target_pairs={{0,1},{1,0},{2,3},{3,2},{4,5},{5,4},{6,7},{7,6},{8,9},{9,8},{10,11... | collective-permute-start | bytes 7667720 | tf_op jit(solution)/shard_map/ppermute | solution.py:431
  32.3 11.3 %collective-permute-start.6 = (bf16[72,1024]{1,0:T(8,128)(2,1)}, bf16[72,1024]{1,0:T(8,128)(2,1)S(1)}, u32[]{:S(2)}, u32[]{:S(2)}) collective-permute-start(bf16[72,1024]{1,0:T(8,128)(2,1)} %get-tuple-element.118), channel_id=1, source_target_pairs={{0,2},{1,3},{2,4},{3,5},{4,6},{5,7},{6,0},{7,1},{8,10},{9,11},{10,... | collective-permute-start | bytes 442376 | tf_op jit(solution)/shard_map/ppermute | solution.py:428
  34.6 12.5 %collective-permute-start.7 = (bf16[72,1024]{1,0:T(8,128)(2,1)}, bf16[72,1024]{1,0:T(8,128)(2,1)S(1)}, u32[]{:S(2)}, u32[]{:S(2)}) collective-permute-start(bf16[72,1024]{1,0:T(8,128)(2,1)} %get-tuple-element.119), channel_id=1, source_target_pairs={{0,4},{1,5},{2,6},{3,7},{4,0},{5,1},{6,2},{7,3},{8,12},{9,13},{10,... | collective-permute-start | bytes 442376 | tf_op jit(solution)/shard_map/ppermute | solution.py:428
  37.2 9.9 %collective-permute-start.8 = (bf16[72,1024]{1,0:T(8,128)(2,1)}, bf16[72,1024]{1,0:T(8,128)(2,1)S(1)}, u32[]{:S(2)}, u32[]{:S(2)}) collective-permute-start(bf16[72,1024]{1,0:T(8,128)(2,1)} %get-tuple-element.120), channel_id=1, source_target_pairs={{0,6},{1,7},{2,0},{3,1},{4,2},{5,3},{6,4},{7,5},{8,14},{9,15},{10,... | collective-permute-start | bytes 442376 | tf_op jit(solution)/shard_map/ppermute | solution.py:428
  50.6 21.8 %collective-permute-start.9 = (bf16[3,128,512]{2,1,0:T(8,128)(2,1)}, bf16[3,128,512]{2,1,0:T(8,128)(2,1)S(1)}, u32[]{:S(2)}, u32[]{:S(2)}) collective-permute-start(bf16[3,128,512]{2,1,0:T(8,128)(2,1)} %get-tuple-element.124.refs_0_), channel_id=1, source_target_pairs={{0,2},{1,3},{2,4},{3,5},{4,6},{5,7},{6,0},{7,1},{8,10},{9,11},{10,... | collective-permute-start | bytes 1179656 | tf_op jit(solution)/shard_map/ppermute | solution.py:428
  57.1 15.3 %collective-permute-start.12 = (bf16[3,128,512]{2,1,0:T(8,128)(2,1)}, bf16[3,128,512]{2,1,0:T(8,128)(2,1)S(1)}, u32[]{:S(2)}, u32[]{:S(2)}) collective-permute-start(bf16[3,128,512]{2,1,0:T(8,128)(2,1)} %get-tuple-element.141.refs_3_), channel_id=1, source_target_pairs={{0,2},{1,3},{2,4},{3,5},{4,6},{5,7},{6,0},{7,1},{8,10},{9,11},{10,... | collective-permute-start | bytes 1179656 | tf_op jit(solution)/shard_map/ppermute | solution.py:428
  63.1 5.0 %collective-permute-start.14 = (f32[128,128]{1,0:T(8,128)S(1)}, f32[128,128]{1,0:T(8,128)S(1)}, u32[]{:S(2)}, u32[]{:S(2)}) collective-permute-start(f32[128,128]{1,0:T(8,128)S(1)} %add.33.refs_5_), channel_id=1, source_target_pairs={{0,16},{8,24},{16,0},{24,8},{1,17},{9,25},{17,1},{25,9},{2,18},{10... | collective-permute-start | bytes 196616 | tf_op jit(solution)/shard_map/ppermute | solution.py:434
  72.4 13.6 %collective-permute-start.16 = (bf16[3,128,512]{2,1,0:T(8,128)(2,1)S(1)}, bf16[3,128,512]{2,1,0:T(8,128)(2,1)}, u32[]{:S(2)}, u32[]{:S(2)}) collective-permute-start(bf16[3,128,512]{2,1,0:T(8,128)(2,1)S(1)} %collective-permute-done.12.refs_4_), channel_id=1, source_target_pairs={{0,2},{1,3},{2,4},{3,5},{4,6},{5,7},{6,0},{7,1},{8,10},{9,11},{10,... | collective-permute-start | bytes 1179656 | tf_op jit(solution)/shard_map/ppermute | solution.py:428
  75.5 19.0 %collective-permute-start.10 = (bf16[3,128,512]{2,1,0:T(8,128)(2,1)S(1)}, bf16[3,128,512]{2,1,0:T(8,128)(2,1)}, u32[]{:S(2)}, u32[]{:S(2)}) collective-permute-start(bf16[3,128,512]{2,1,0:T(8,128)(2,1)S(1)} %collective-permute-done.9.refs_1_), channel_id=1, source_target_pairs={{0,2},{1,3},{2,4},{3,5},{4,6},{5,7},{6,0},{7,1},{8,10},{9,11},{10,... | collective-permute-start | bytes 1179656 | tf_op jit(solution)/shard_map/ppermute | solution.py:428
  86.0 22.4 %collective-permute-start.17 = (bf16[3,128,512]{2,1,0:T(8,128)(2,1)}, bf16[3,128,512]{2,1,0:T(8,128)(2,1)}, u32[]{:S(2)}, u32[]{:S(2)}) collective-permute-start(bf16[3,128,512]{2,1,0:T(8,128)(2,1)} %collective-permute-done.16.refs_5_), channel_id=1, source_target_pairs={{0,2},{1,3},{2,4},{3,5},{4,6},{5,7},{6,0},{7,1},{8,10},{9,11},{10,... | collective-permute-start | bytes 1179656 | tf_op jit(solution)/shard_map/ppermute | solution.py:428
  94.5 16.9 %collective-permute-start.11 = (bf16[3,128,512]{2,1,0:T(8,128)(2,1)}, bf16[3,128,512]{2,1,0:T(8,128)(2,1)}, u32[]{:S(2)}, u32[]{:S(2)}) collective-permute-start(bf16[3,128,512]{2,1,0:T(8,128)(2,1)} %collective-permute-done.10.refs_2_), channel_id=1, source_target_pairs={{0,2},{1,3},{2,4},{3,5},{4,6},{5,7},{6,0},{7,1},{8,10},{9,11},{10,... | collective-permute-start | bytes 1179656 | tf_op jit(solution)/shard_map/ppermute | solution.py:428
  95.2 20.8 %collective-permute-start.23 = (bf16[272,512]{1,0:T(8,128)(2,1)}, bf16[272,512]{1,0:T(8,128)(2,1)S(1)}, u32[]{:S(2)}, u32[]{:S(2)}) collective-permute-start(bf16[272,512]{1,0:T(8,128)(2,1)} %get-tuple-element.161), channel_id=1, source_target_pairs={{0,1},{1,0},{2,3},{3,2},{4,5},{5,4},{6,7},{7,6},{8,9},{9,8},{10,11... | collective-permute-start | bytes 835592 | tf_op jit(solution)/shard_map/ppermute | solution.py:431
  116.0 9.0 %collective-permute-start.24 = (bf16[272,512]{1,0:T(8,128)(2,1)S(1)}, bf16[272,512]{1,0:T(8,128)(2,1)S(1)}, u32[]{:S(2)}, u32[]{:S(2)}) collective-permute-start(bf16[272,512]{1,0:T(8,128)(2,1)S(1)} %add_convert_fusion.4), channel_id=1, source_target_pairs={{0,2},{1,3},{2,0},{3,1},{4,6},{5,7},{6,4},{7,5},{8,10},{9,11},{10,... | collective-permute-start | bytes 835592 | tf_op jit(solution)/shard_map/ppermute | solution.py:624
  116.8 9.5 %collective-permute-start.19 = (bf16[144,1024]{1,0:T(8,128)(2,1)S(1)}, bf16[144,1024]{1,0:T(8,128)(2,1)S(1)}, u32[]{:S(2)}, u32[]{:S(2)}) collective-permute-start(bf16[144,1024]{1,0:T(8,128)(2,1)S(1)} %get-tuple-element.157), channel_id=1, source_target_pairs={{0,8},{8,0},{16,24},{24,16},{1,9},{9,1},{17,25},{25,17},{2,10},{10... | collective-permute-start | bytes 884744 | tf_op jit(solution)/shard_map/ppermute | solution.py:610
  117.5 9.1 %collective-permute-start.21 = (bf16[144,1024]{1,0:T(8,128)(2,1)S(1)}, bf16[144,1024]{1,0:T(8,128)(2,1)S(1)}, u32[]{:S(2)}, u32[]{:S(2)}) collective-permute-start(bf16[144,1024]{1,0:T(8,128)(2,1)S(1)} %add_convert_fusion), channel_id=1, source_target_pairs={{0,16},{8,24},{16,0},{24,8},{1,17},{9,25},{17,1},{25,9},{2,18},{10... | collective-permute-start | bytes 884744 | tf_op jit(solution)/shard_map/ppermute | solution.py:610
  125.1 15.0 %collective-permute-start.25 = (bf16[272,512]{1,0:T(8,128)(2,1)S(1)}, bf16[272,512]{1,0:T(8,128)(2,1)S(1)}, u32[]{:S(2)}, u32[]{:S(2)}) collective-permute-start(bf16[272,512]{1,0:T(8,128)(2,1)S(1)} %add_convert_fusion.3), channel_id=1, source_target_pairs={{0,4},{1,5},{2,6},{3,7},{4,0},{5,1},{6,2},{7,3},{8,12},{9,13},{10,... | collective-permute-start | bytes 835592 | tf_op jit(solution)/shard_map/ppermute | solution.py:624
  140.2 8.8 %collective-permute-start.26 = (bf16[272,512]{1,0:T(8,128)(2,1)S(1)}, bf16[272,512]{1,0:T(8,128)(2,1)S(1)}, u32[]{:S(2)}, u32[]{:S(2)}) collective-permute-start(bf16[272,512]{1,0:T(8,128)(2,1)S(1)} %add_convert_fusion.2.refs_0_), channel_id=1, source_target_pairs={{0,1},{1,0},{2,3},{3,2},{4,5},{5,4},{6,7},{7,6},{8,9},{9,8},{10,11... | collective-permute-start | bytes 835592 | tf_op jit(solution)/shard_map/ppermute | solution.py:431
  141.4 15.9 %collective-permute-start.22 = (bf16[128,1024]{1,0:T(8,128)(2,1)S(1)}, bf16[128,1024]{1,0:T(8,128)(2,1)S(1)}, u32[]{:S(2)}, u32[]{:S(2)}) collective-permute-start(bf16[128,1024]{1,0:T(8,128)(2,1)S(1)} %slice.28), channel_id=1, source_target_pairs={{0,0},{1,1},{2,8},{3,9},{4,16},{5,17},{6,24},{7,25},{8,2},{9,3},{1... | collective-permute-start | bytes 786440 | tf_op jit(solution)/shard_map/ppermute | solution.py:645
  143.4 13.9 %collective-permute-start.27 = (f32[1,1024]{1,0:T(1,128)S(1)}, f32[1,1024]{1,0:T(1,128)S(1)}, u32[]{:S(2)}, u32[]{:S(2)}) collective-permute-start(f32[1,1024]{1,0:T(1,128)S(1)} %slice.23), channel_id=1, source_target_pairs={{1,0},{2,1},{3,2},{4,3},{5,4},{6,5},{7,6},{9,8},{10,9},{11,10},{12... | collective-permute-start | bytes 12296 | tf_op jit(solution)/shard_map/ppermute | solution.py:423
  144.7 13.1 %collective-permute-start.28 = (f32[1,1024]{1,0:T(1,128)S(1)}, f32[1,1024]{1,0:T(1,128)S(1)}, u32[]{:S(2)}, u32[]{:S(2)}) collective-permute-start(f32[1,1024]{1,0:T(1,128)S(1)} %slice.26), channel_id=1, source_target_pairs={{1,0},{3,8},{5,16},{7,24},{8,1},{9,2},{10,9},{11,10},{12,17},{13,1... | collective-permute-start | bytes 12296 | tf_op jit(solution)/shard_map/ppermute | solution.py:646
  (32 other events, 272.5 us)

commit v9 on v7

--- a/solution.py
+++ b/solution.py
@@ -607,27 +607,20 @@
     done = project(lows[:-1], highs[:-1])
     sends = project(lows[-1:], highs[-1:], done)
     token_sums = add(keep, after_that(got, *done))
-    b = 1
-    while b < ring:
+    def other_z(a, b):
         route = [(i, ((i // inner) ^ b) * inner + i % inner) for i in range(n_seq)]
-        got = lax.ppermute(token_sums, "seq", route)
-        token_sums = add(token_sums, after_that(got, sends) if b == 1 else got)
-        b *= 2
-    up_grad, down_grad, base_grad, du = pl.pallas_call(
-        lambda *refs: finish_kernel(rank, *refs),
-                out_shape=[shape((rank, cols)), shape((cols, rank)), shape((pairs, PAIR)), shape((heads, head))],
-        compiler_params=pltpu.CompilerParams(vmem_limit_bytes=16 * 2**20),
-        cost_estimate=work(2),
-        name="token_sums",
-    )(token_sums, partner(token_sums))
-
+        return lax.ppermute(a, "seq", route)
+
+    token_sums = add(token_sums, after_that(other_z(token_sums, 1), sends))
     def across(a, bit):
         return lax.ppermute(a, "head", [(i, i ^ bit) for i in range(n_head)])
 
     left, bit = dict(enumerate(sends)), 1
     while bit < n_head:
-        got = {e: across(left[e | bit], bit) for e in left if not e & bit}
-        left = {e: left[e].astype(F32) + got[e].astype(F32) for e in got}
+        came = {e: across(left[e | bit], bit) for e in left if not e & bit}
+        if bit == 1:
+            came = {e: after_that(value, token_sums) for e, value in came.items()}
+        left = {e: left[e].astype(F32) + came[e].astype(F32) for e in came}
         bit *= 2
         if bit < n_head:
             left = {e: value.astype(BF16) for e, value in left.items()}
@@ -641,9 +634,22 @@
                 swap.append((source, z * n_seq + block_at))
                 if block_at > 0:
                     back.append((source, z * n_seq + block_at - 1))
-    base_grad = base_grad.reshape(cols)
     summed = lax.ppermute(total[:rows].astype(BF16), ("head", "seq"), swap)
     edge = lax.ppermute(total[rows : rows + 1], ("head", "seq"), back)
+    b = 2
+    while b < ring:
+        got = other_z(token_sums, b)
+        token_sums = add(token_sums, after_that(got, edge) if b == 2 else got)
+        b *= 2
+    up_grad, down_grad, base_grad, du = pl.pallas_call(
+        lambda *refs: finish_kernel(rank, *refs),
+                out_shape=[shape((rank, cols)), shape((cols, rank)), shape((pairs, PAIR)), shape((heads, head))],
+        compiler_params=pltpu.CompilerParams(vmem_limit_bytes=16 * 2**20),
+        cost_estimate=work(2),
+        name="token_sums",
+    )(token_sums, partner(token_sums))
+
+    base_grad = base_grad.reshape(cols)
     summed = after_that(summed, up_grad, base_grad, du)
     grad_next = jnp.concatenate([grad_in[1:], shift(grad_in[:1], -1)], 0)
     adapter_term = (1.0 - decay_shift_mix) * grad_in + decay_shift_mix * grad_next

time: 147 us -> 146 us (level)
  starting transfers between devices: 35.6 us -> 33.7 us
    ppermute x2, waiting for transfers between devices: 14.5 us -> 1.43 us  [other_z(): return lax.ppermute(a, 'seq', route)]
    ppermute x3, waiting for transfers between devices: 0.15 us -> 9.2 us  [across(): return lax.ppermute(a, 'head', [(i, i ^ bit) for i in range(n_head)])]
    ppermute x5, waiting for transfers between devices: 2.05 us -> 8.02 us  [partner(): return lax.ppermute(a, 'seq', [(i, i ^ 1) for i in range(n_seq)])]
    ppermute x1, waiting for transfers between devices: 5.43 us -> 2.35 us  [per_device(): summed = lax.ppermute(total[:rows].astype(BF16), ('head', 'seq'), swap)]
    ppermute x1, starting transfers between devices: 4.99 us -> 3.12 us  [per_device(): edge = lax.ppermute(total[rows:rows + 1], ('head', 'seq'), back)]
  transfers between devices with their start and end apart: 29 -> 29, of which waited for: 16 -> 18; matrix products, arithmetic and copies ran while one was open for 2% -> 2% of each run, Pallas kernels for 32% -> 32%
where the time goes in v9:
time: 146 us; the launch traced here: 145 us
  waiting for transfers between devices  50.2 us (34%)
  Pallas kernels  46.5 us (32%)
  starting transfers between devices  33.7 us (23%)
  local copies, waits for them, and re-layouts  11.3 us (8%)
  other arithmetic  2.15 us (1%)
    ppermute x9, waiting for transfers between devices, around(): lax.ppermute(a, 'seq', [(i, (i + inner * step) % n_seq) for i in range(n_...  18.9 us
    ppermute x9, starting transfers between devices, around(): lax.ppermute(a, 'seq', [(i, (i + inner * step) % n_seq) for i in range(n_...  14.3 us
    pallas_call x2, Pallas kernels, project(): pl.pallas_call(lambda *refs: project_kernel(count, ring, final, *refs), i...  12.5 us
    pallas_call x2, Pallas kernels, inside(): pl.pallas_call(lambda *refs: inner_kernel(head, cut if extra else 0, *ref...  11.5 us
    ppermute x3, waiting for transfers between devices, across(): return lax.ppermute(a, 'head', [(i, i ^ bit) for i in range(n_head)])  9.2 us
    unnamed x54, local copies, waits for them, and re-layouts  8.69 us
    ppermute x6, waiting for transfers between devices, head_shift(): lax.ppermute(a, 'head', [(i, (i + d) % n_head) for i in range(n_head)])  8.4 us
    ppermute x5, waiting for transfers between devices, partner(): return lax.ppermute(a, 'seq', [(i, i ^ 1) for i in range(n_seq)])  8.02 us
  transfers between devices with their start and end apart: 29, of which 18 were waited for; matrix products, arithmetic and copies ran while one was open for 2% of the time, Pallas kernels for 32%

profile of v9, /device:TPU:4, one launch (start us, length us, event | category | flops | bytes accessed | tf_op | source)
XLA Modules:
  0.0 144.8 jit_solution(12071637383915161408)
XLA Ops:
  1.4 3.4 %collective-permute-start = (bf16[1,1024]{1,0:T(2,128)(2,1)S(1)}, bf16[1,1024]{1,0:T(2,128)(2,1)S(1)}, u32[]{:S(2)}, u32[]{:S(2)}) collective-permute-start(bf16[1,1024]{1,0:T(2,128)(2,1)S(1)} %slice.19), channel_id=1, source_target_pairs={{0,1},{1,2},{2,3},{3,4},{4,5},{5,6},{6,7},{8,9},{9,10},{10,11},{11... | collective-permute-start | bytes 6152 | tf_op jit(solution)/shard_map/ppermute | solution.py:423
  16.5 3.4 %decay_and_states.1 = (f32[128,128]{1,0:T(8,128)}, bf16[128,128]{1,0:T(8,128)(2,1)}, f32[128,1024]{1,0:T(8,128)}, f32[1,1024]{1,0:T(1,128)}, f32[64,1024]{1,0:T(8,128)}, /*index=5*/bf16[136,1024]{1,0:T(8,128)(2,1)}) custom-call(f32[128,128]{1,0:T(8,128)} %adapter_input.1.refs_0_, f32[128,128]{1,0:T(8,128)} %copy-done.21, f32[128,128]{1,0:T(8,128)} %copy-done.23, ...), custom_call_target="tpu_custom_call" | custom-call | bytes 10500000 | tf_op jit(solution)/shard_map/decay_and_states/pallas_call | solution.py:464
  21.1 6.4 %inside_chunk.2 = (f32[128,512]{1,0:T(8,128)}, f32[128,512]{1,0:T(8,128)}, f32[128,512]{1,0:T(8,128)}, f32[128,512]{1,0:T(8,128)}, f32[128,512]{1,0:T(8,128)}, /...) custom-call(bf16[128,1024]{1,0:T(8,128)(2,1)} %refs_0_.8, bf16[128,1024]{1,0:T(8,128)(2,1)} %refs_1_.7, ...), custom_call_target="tpu_custom_call" | custom-call | bytes 14000000 | tf_op jit(solution)/shard_map/inside_chunk/pallas_call | solution.py:490
  34.6 2.6 %collective-permute-start.7 = (bf16[72,1024]{1,0:T(8,128)(2,1)}, bf16[72,1024]{1,0:T(8,128)(2,1)S(1)}, u32[]{:S(2)}, u32[]{:S(2)}) collective-permute-start(bf16[72,1024]{1,0:T(8,128)(2,1)} %get-tuple-element.121), channel_id=1, source_target_pairs={{0,4},{1,5},{2,6},{3,7},{4,0},{5,1},{6,2},{7,3},{8,12},{9,13},{10,... | collective-permute-start | bytes 442376 | tf_op jit(solution)/shard_map/ppermute | solution.py:428
  38.6 5.1 %inside_chunk.3 = (f32[128,512]{1,0:T(8,128)}, f32[128,512]{1,0:T(8,128)}, f32[128,512]{1,0:T(8,128)}, f32[128,512]{1,0:T(8,128)}, f32[128,512]{1,0:T(8,128)}, /*index=5*/f32[128,512]{1,0:T(8,128)}, f32[1,512]{1,0:T(1,128)}) custom-call(bf16[128,1024]{1,0:T(8,128)(2,1)} %refs_0_.8, bf16[128,1024]{1,0:T(8,128)(2,1)} %refs_1_.7, bf16[128,1024]{1,0:T(8,128)(2,1)} %refs_2_.8, ...), custom_call_target="tpu_custom_call" | custom-call | bytes 14000000 | tf_op jit(solution)/shard_map/inside_chunk/pallas_call | solution.py:490
  43.7 3.4 %collective-permute-done.7.refs_15_ = bf16[72,1024]{1,0:T(8,128)(2,1)S(1)} collective-permute-done((bf16[72,1024]{1,0:T(8,128)(2,1)}, bf16[72,1024]{1,0:T(8,128)(2,1)S(1)}, u32[]{:S(2)}, u32[]{:S(2)}) %collective-permute-start.7) | collective-permute-done | bytes 147488 | tf_op jit(solution)/shard_map/ppermute | solution.py:428
  47.8 2.8 %across_chunks.2 = (bf16[3,128,512]{2,1,0:T(8,128)(2,1)}, f32[128,512]{1,0:T(8,128)}, f32[128,512]{1,0:T(8,128)}, f32[1,512]{1,0:T(1,128)}) custom-call(bf16[128,1024]{1,0:T(8,128)(2,1)} %refs_0_.8, bf16[128,1024]{1,0:T(8,128)(2,1)} %refs_1_.7, bf16[128,1024]{1,0:T(8,128)(2,1)} %refs_2_.8, bf16[128,1024]{1,0:T(8,128)(2,1)} %refs_3_.8, ...), custom_call_target="tpu_custom_call" | custom-call | bytes 10500000 | tf_op jit(solution)/shard_map/across_chunks/pallas_call | solution.py:524
  50.6 3.6 %collective-permute-start.9 = (bf16[3,128,512]{2,1,0:T(8,128)(2,1)}, bf16[3,128,512]{2,1,0:T(8,128)(2,1)S(1)}, u32[]{:S(2)}, u32[]{:S(2)}) collective-permute-start(bf16[3,128,512]{2,1,0:T(8,128)(2,1)} %get-tuple-element.126.refs_0_), channel_id=1, source_target_pairs={{0,2},{1,3},{2,4},{3,5},{4,6},{5,7},{6,0},{7,1},{8,10},{9,11},{10,... | collective-permute-start | bytes 1179656 | tf_op jit(solution)/shard_map/ppermute | solution.py:428
  54.2 2.9 %across_chunks.3 = (bf16[3,128,512]{2,1,0:T(8,128)(2,1)}, f32[128,512]{1,0:T(8,128)}, f32[128,512]{1,0:T(8,128)}, f32[1,512]{1,0:T(1,128)}) custom-call(bf16[128,1024]{1,0:T(8,128)(2,1)} %refs_0_.8, bf16[128,1024]{1,0:T(8,128)(2,1)} %refs_1_.7, bf16[128,1024]{1,0:T(8,128)(2,1)} %refs_2_.8, bf16[128,1024]{1,0:T(8,128)(2,1)} %refs_3_.8, ...), custom_call_target="tpu_custom_call" | custom-call | bytes 10500000 | tf_op jit(solution)/shard_map/across_chunks/pallas_call | solution.py:524
  57.2 2.6 %decay_gradient.3 = (f32[128,512]{1,0:T(8,128)}, f32[1,512]{1,0:T(1,128)}, f32[128,128]{1,0:T(8,128)}) custom-call(f32[128,1024]{1,0:T(8,128)} %get-tuple-element.95.refs_4_.w, f32[128,512]{1,0:T(8,128)} %get-tuple-element.138.r_gr, f32[128,512]{1,0:T(8,128)} %get-tuple-element.139.k_gk, f32[1,512]{1,0:T(1,128)} %get-tuple-element.140.at_end, ...), custom_call_target="tpu_custom_call" | custom-call | bytes 7000000 | tf_op jit(solution)/shard_map/decay_gradient/pallas_call | solution.py:544
  59.8 2.4 %decay_gradient.2 = (f32[128,512]{1,0:T(8,128)}, f32[1,512]{1,0:T(1,128)}, f32[128,128]{1,0:T(8,128)}) custom-call(f32[128,1024]{1,0:T(8,128)} %get-tuple-element.95.refs_4_.w, f32[128,512]{1,0:T(8,128)} %get-tuple-element.127.r_gr, f32[128,512]{1,0:T(8,128)} %get-tuple-element.128.k_gk, f32[1,512]{1,0:T(1,128)} %get-tuple-element.129.at_end, ...), custom_call_target="tpu_custom_call" | custom-call | bytes 7000000 | tf_op jit(solution)/shard_map/decay_gradient/pallas_call | solution.py:544
  63.0 2.6 %collective-permute-done.9.refs_1_ = bf16[3,128,512]{2,1,0:T(8,128)(2,1)S(1)} collective-permute-done((bf16[3,128,512]{2,1,0:T(8,128)(2,1)}, bf16[3,128,512]{2,1,0:T(8,128)(2,1)S(1)}, u32[]{:S(2)}, u32[]{:S(2)}) %collective-permute-start.9) | collective-permute-done | bytes 393248 | tf_op jit(solution)/shard_map/ppermute | solution.py:428
  67.7 3.3 %collective-permute-done.13.refs_6_ = f32[128,128]{1,0:T(8,128)S(1)} collective-permute-done((f32[128,128]{1,0:T(8,128)S(1)}, f32[128,128]{1,0:T(8,128)S(1)}, u32[]{:S(2)}, u32[]{:S(2)}) %collective-permute-start.13) | collective-permute-done | bytes 65568 | tf_op jit(solution)/shard_map/ppermute | solution.py:434
  73.5 3.0 %adapter_grads.1 = (bf16[272,512]{1,0:T(8,128)(2,1)}, bf16[272,512]{1,0:T(8,128)(2,1)}, f32[128,1024]{1,0:T(8,128)}) custom-call(bf16[128,1024]{1,0:T(8,128)(2,1)} %refs_0_.9, bf16[1,1024]{1,0:T(2,128)(2,1)} %copy-done.25, f32[1,1024]{1,0:T(1,128)} %bitcast.5, f32[1024,128]{1,0:T(8,128)} %refs_3_.9, f32[128,128]{1,0:T(8,128)} %get-tuple-element.144.refs_4_, ...), custom_call_target="tpu_custom_call" | custom-call | bytes 10500000 | tf_op jit(solution)/shard_map/adapter_grads/pallas_call | solution.py:562
  76.6 4.2 %collective-permute-done.10.refs_2_ = bf16[3,128,512]{2,1,0:T(8,128)(2,1)S(1)} collective-permute-done((bf16[3,128,512]{2,1,0:T(8,128)(2,1)S(1)}, bf16[3,128,512]{2,1,0:T(8,128)(2,1)S(1)}, u32[]{:S(2)}, u32[]{:S(2)}) %collective-permute-start.10) | collective-permute-done | bytes 393248 | tf_op jit(solution)/shard_map/ppermute | solution.py:428
  82.7 2.3 %collective-permute-start.11 = (bf16[3,128,512]{2,1,0:T(8,128)(2,1)}, bf16[3,128,512]{2,1,0:T(8,128)(2,1)S(1)}, u32[]{:S(2)}, u32[]{:S(2)}) collective-permute-start(bf16[3,128,512]{2,1,0:T(8,128)(2,1)} %copy-done.9), channel_id=1, source_target_pairs={{0,2},{1,3},{2,4},{3,5},{4,6},{5,7},{6,0},{7,1},{8,10},{9,11},{10,... | collective-permute-start | bytes 1179656 | tf_op jit(solution)/shard_map/ppermute | solution.py:428
  85.0 5.6 %collective-permute-done.16.refs_5_ = bf16[3,128,512]{2,1,0:T(8,128)(2,1)} collective-permute-done((bf16[3,128,512]{2,1,0:T(8,128)(2,1)}, bf16[3,128,512]{2,1,0:T(8,128)(2,1)}, u32[]{:S(2)}, u32[]{:S(2)}) %collective-permute-start.16) | collective-permute-done | bytes 393248 | tf_op jit(solution)/shard_map/ppermute | solution.py:428
  96.9 7.2 %projections.2 = (bf16[144,1024]{1,0:T(8,128)(2,1)S(1)}, bf16[144,1024]{1,0:T(8,128)(2,1)S(1)}, bf16[144,1024]{1,0:T(8,128)(2,1)S(1)}) custom-call(bf16[3,128,512]{2,1,0:T(8,128)(2,1)S(1)} %copy-done.5, bf16[3,128,512]{2,1,0:T(8,128)(2,1)S(1)} %copy-done.7, bf16[3,128,512]{2,1,0:T(8,128)(2,1)S(1)} %copy-done.10, bf16[3,128,512]{2,1,0:T(8,128)(2,1)S(1)} %copy-done.8, ...), custom_call_target="tpu_custom_call" | custom-call | bytes 17500000 | tf_op jit(solution)/shard_map/projections/pallas_call | solution.py:590
  104.3 3.2 %collective-permute-done.17.refs_1_ = bf16[3,128,512]{2,1,0:T(8,128)(2,1)S(1)} collective-permute-done((bf16[3,128,512]{2,1,0:T(8,128)(2,1)}, bf16[3,128,512]{2,1,0:T(8,128)(2,1)S(1)}, u32[]{:S(2)}, u32[]{:S(2)}) %collective-permute-start.17) | collective-permute-done | bytes 393248 | tf_op jit(solution)/shard_map/ppermute | solution.py:428
  107.5 5.3 %projections.3 = (bf16[144,1024]{1,0:T(8,128)(2,1)S(1)}, bf16[144,1024]{1,0:T(8,128)(2,1)S(1)}, bf16[144,1024]{1,0:T(8,128)(2,1)S(1)}, bf16[144,1024]{1,0:T(8,128)(2,1)S(1)}) custom-call(bf16[3,128,512]{2,1,0:T(8,128)(2,1)S(1)} %collective-permute-done.11.refs_0_, bf16[3,128,512]{2,1,0:T(8,128)(2,1)S(1)} %collective-permute-done.17.refs_1_, ...), custom_call_target="tpu_custom_call" | custom-call | bytes 17500000 | tf_op jit(solution)/shard_map/projections/pallas_call | solution.py:590
  115.4 8.2 %collective-permute-done.23 = bf16[144,1024]{1,0:T(8,128)(2,1)S(1)} collective-permute-done((bf16[144,1024]{1,0:T(8,128)(2,1)S(1)}, bf16[144,1024]{1,0:T(8,128)(2,1)S(1)}, u32[]{:S(2)}, u32[]{:S(2)}) %collective-permute-start.23) | collective-permute-done | bytes 294944 | tf_op jit(solution)/shard_map/ppermute | solution.py:616
  123.8 3.1 %collective-permute-start.26 = (f32[1,1024]{1,0:T(1,128)S(1)}, f32[1,1024]{1,0:T(1,128)S(1)}, u32[]{:S(2)}, u32[]{:S(2)}) collective-permute-start(f32[1,1024]{1,0:T(1,128)S(1)} %slice.26), channel_id=1, source_target_pairs={{1,0},{3,8},{5,16},{7,24},{8,1},{9,2},{10,9},{11,10},{12,17},{13,1... | collective-permute-start | bytes 12296 | tf_op jit(solution)/shard_map/ppermute | solution.py:638
  134.5 6.0 %collective-permute-done.27.refs_1_ = bf16[272,512]{1,0:T(8,128)(2,1)S(1)} collective-permute-done((bf16[272,512]{1,0:T(8,128)(2,1)S(1)}, bf16[272,512]{1,0:T(8,128)(2,1)S(1)}, u32[]{:S(2)}, u32[]{:S(2)}) %collective-permute-start.27) | collective-permute-done | bytes 278560 | tf_op jit(solution)/shard_map/ppermute | solution.py:431
  141.6 2.3 %collective-permute-done.24 = bf16[128,1024]{1,0:T(8,128)(2,1)S(1)} collective-permute-done((bf16[128,1024]{1,0:T(8,128)(2,1)S(1)}, bf16[128,1024]{1,0:T(8,128)(2,1)S(1)}, u32[]{:S(2)}, u32[]{:S(2)}) %collective-permute-start.24) | collective-permute-done | bytes 262176 | tf_op jit(solution)/shard_map/ppermute | solution.py:637
  (118 shorter events, 49.0 us)
Async XLA Ops:
  1.4 4.7 %collective-permute-start = (bf16[1,1024]{1,0:T(2,128)(2,1)S(1)}, bf16[1,1024]{1,0:T(2,128)(2,1)S(1)}, u32[]{:S(2)}, u32[]{:S(2)}) collective-permute-start(bf16[1,1024]{1,0:T(2,128)(2,1)S(1)} %slice.19), channel_id=1, source_target_pairs={{0,1},{1,2},{2,3},{3,4},{4,5},{5,6},{6,7},{8,9},{9,10},{10,11},{11... | collective-permute-start | bytes 6152 | tf_op jit(solution)/shard_map/ppermute | solution.py:423
  6.1 15.0 %collective-permute-start.5 = (bf16[3,96,1024]{2,1,0:T(8,128)(2,1)S(1)}, bf16[3,96,1024]{2,1,0:T(8,128)(2,1)S(1)}, u32[]{:S(2)}, u32[]{:S(2)}) collective-permute-start(bf16[3,96,1024]{2,1,0:T(8,128)(2,1)S(1)} %slice.20), channel_id=1, source_target_pairs={{0,1},{1,0},{2,3},{3,2},{4,5},{5,4},{6,7},{7,6},{8,9},{9,8},{10,11... | collective-permute-start | bytes 1769480 | tf_op jit(solution)/shard_map/ppermute | solution.py:431
  10.7 5.1 %collective-permute-start.2 = (f32[128,128]{1,0:T(8,128)}, f32[128,128]{1,0:T(8,128)S(1)}, u32[]{:S(2)}, u32[]{:S(2)}) collective-permute-start(f32[128,128]{1,0:T(8,128)} %adapter_input.1.refs_0_), channel_id=1, source_target_pairs={{0,16},{8,24},{16,0},{24,8},{1,17},{9,25},{17,1},{25,9},{2,18},{10... | collective-permute-start | bytes 196616 | tf_op jit(solution)/shard_map/ppermute | solution.py:434
  11.2 4.6 %collective-permute-start.3 = (f32[128,128]{1,0:T(8,128)}, f32[128,128]{1,0:T(8,128)S(1)}, u32[]{:S(2)}, u32[]{:S(2)}) collective-permute-start(f32[128,128]{1,0:T(8,128)} %adapter_input.1.refs_0_), channel_id=1, source_target_pairs={{0,24},{8,0},{16,8},{24,16},{1,25},{9,1},{17,9},{25,17},{2,26},{10... | collective-permute-start | bytes 196616 | tf_op jit(solution)/shard_map/ppermute | solution.py:434
  19.8 9.7 %collective-permute-start.4 = (bf16[136,1024]{1,0:T(8,128)(2,1)}, bf16[136,1024]{1,0:T(8,128)(2,1)S(1)}, u32[]{:S(2)}, u32[]{:S(2)}) collective-permute-start(bf16[136,1024]{1,0:T(8,128)(2,1)} %get-tuple-element.91.refs_0_), channel_id=1, source_target_pairs={{0,1},{1,0},{2,3},{3,2},{4,5},{5,4},{6,7},{7,6},{8,9},{9,8},{10,11... | collective-permute-start | bytes 835592 | tf_op jit(solution)/shard_map/ppermute | solution.py:431
  29.5 62.3 %collective-permute-start.18 = (bf16[3,416,1024]{2,1,0:T(8,128)(2,1)}, bf16[3,416,1024]{2,1,0:T(8,128)(2,1)}, u32[]{:S(2)}, u32[]{:S(2)}) collective-permute-start(bf16[3,416,1024]{2,1,0:T(8,128)(2,1)} %get-tuple-element.153), channel_id=1, source_target_pairs={{0,1},{1,0},{2,3},{3,2},{4,5},{5,4},{6,7},{7,6},{8,9},{9,8},{10,11... | collective-permute-start | bytes 7667720 | tf_op jit(solution)/shard_map/ppermute | solution.py:431
  32.3 11.4 %collective-permute-start.6 = (bf16[72,1024]{1,0:T(8,128)(2,1)}, bf16[72,1024]{1,0:T(8,128)(2,1)S(1)}, u32[]{:S(2)}, u32[]{:S(2)}) collective-permute-start(bf16[72,1024]{1,0:T(8,128)(2,1)} %get-tuple-element.120), channel_id=1, source_target_pairs={{0,2},{1,3},{2,4},{3,5},{4,6},{5,7},{6,0},{7,1},{8,10},{9,11},{10,... | collective-permute-start | bytes 442376 | tf_op jit(solution)/shard_map/ppermute | solution.py:428
  34.6 12.5 %collective-permute-start.7 = (bf16[72,1024]{1,0:T(8,128)(2,1)}, bf16[72,1024]{1,0:T(8,128)(2,1)S(1)}, u32[]{:S(2)}, u32[]{:S(2)}) collective-permute-start(bf16[72,1024]{1,0:T(8,128)(2,1)} %get-tuple-element.121), channel_id=1, source_target_pairs={{0,4},{1,5},{2,6},{3,7},{4,0},{5,1},{6,2},{7,3},{8,12},{9,13},{10,... | collective-permute-start | bytes 442376 | tf_op jit(solution)/shard_map/ppermute | solution.py:428
  37.2 9.9 %collective-permute-start.8 = (bf16[72,1024]{1,0:T(8,128)(2,1)}, bf16[72,1024]{1,0:T(8,128)(2,1)S(1)}, u32[]{:S(2)}, u32[]{:S(2)}) collective-permute-start(bf16[72,1024]{1,0:T(8,128)(2,1)} %get-tuple-element.122), channel_id=1, source_target_pairs={{0,6},{1,7},{2,0},{3,1},{4,2},{5,3},{6,4},{7,5},{8,14},{9,15},{10,... | collective-permute-start | bytes 442376 | tf_op jit(solution)/shard_map/ppermute | solution.py:428
  50.6 15.0 %collective-permute-start.9 = (bf16[3,128,512]{2,1,0:T(8,128)(2,1)}, bf16[3,128,512]{2,1,0:T(8,128)(2,1)S(1)}, u32[]{:S(2)}, u32[]{:S(2)}) collective-permute-start(bf16[3,128,512]{2,1,0:T(8,128)(2,1)} %get-tuple-element.126.refs_0_), channel_id=1, source_target_pairs={{0,2},{1,3},{2,4},{3,5},{4,6},{5,7},{6,0},{7,1},{8,10},{9,11},{10,... | collective-permute-start | bytes 1179656 | tf_op jit(solution)/shard_map/ppermute | solution.py:428
  57.1 19.4 %collective-permute-start.12 = (bf16[3,128,512]{2,1,0:T(8,128)(2,1)}, bf16[3,128,512]{2,1,0:T(8,128)(2,1)}, u32[]{:S(2)}, u32[]{:S(2)}) collective-permute-start(bf16[3,128,512]{2,1,0:T(8,128)(2,1)} %get-tuple-element.143.refs_3_), channel_id=1, source_target_pairs={{0,2},{1,3},{2,4},{3,5},{4,6},{5,7},{6,0},{7,1},{8,10},{9,11},{10,... | collective-permute-start | bytes 1179656 | tf_op jit(solution)/shard_map/ppermute | solution.py:428
  65.6 15.2 %collective-permute-start.10 = (bf16[3,128,512]{2,1,0:T(8,128)(2,1)S(1)}, bf16[3,128,512]{2,1,0:T(8,128)(2,1)S(1)}, u32[]{:S(2)}, u32[]{:S(2)}) collective-permute-start(bf16[3,128,512]{2,1,0:T(8,128)(2,1)S(1)} %collective-permute-done.9.refs_1_), channel_id=1, source_target_pairs={{0,2},{1,3},{2,4},{3,5},{4,6},{5,7},{6,0},{7,1},{8,10},{9,11},{10,... | collective-permute-start | bytes 1179656 | tf_op jit(solution)/shard_map/ppermute | solution.py:428
  67.2 4.9 %collective-permute-start.14 = (f32[128,128]{1,0:T(8,128)S(1)}, f32[128,128]{1,0:T(8,128)S(1)}, u32[]{:S(2)}, u32[]{:S(2)}) collective-permute-start(f32[128,128]{1,0:T(8,128)S(1)} %add.33.refs_5_), channel_id=1, source_target_pairs={{0,16},{8,24},{16,0},{24,8},{1,17},{9,25},{17,1},{25,9},{2,18},{10... | collective-permute-start | bytes 196616 | tf_op jit(solution)/shard_map/ppermute | solution.py:434
  76.5 14.1 %collective-permute-start.16 = (bf16[3,128,512]{2,1,0:T(8,128)(2,1)}, bf16[3,128,512]{2,1,0:T(8,128)(2,1)}, u32[]{:S(2)}, u32[]{:S(2)}) collective-permute-start(bf16[3,128,512]{2,1,0:T(8,128)(2,1)} %collective-permute-done.12.refs_4_), channel_id=1, source_target_pairs={{0,2},{1,3},{2,4},{3,5},{4,6},{5,7},{6,0},{7,1},{8,10},{9,11},{10,... | collective-permute-start | bytes 1179656 | tf_op jit(solution)/shard_map/ppermute | solution.py:428
  81.6 22.5 %collective-permute-start.20 = (bf16[272,512]{1,0:T(8,128)(2,1)}, bf16[272,512]{1,0:T(8,128)(2,1)S(1)}, u32[]{:S(2)}, u32[]{:S(2)}) collective-permute-start(bf16[272,512]{1,0:T(8,128)(2,1)} %get-tuple-element.161), channel_id=1, source_target_pairs={{0,1},{1,0},{2,3},{3,2},{4,5},{5,4},{6,7},{7,6},{8,9},{9,8},{10,11... | collective-permute-start | bytes 835592 | tf_op jit(solution)/shard_map/ppermute | solution.py:431
  82.7 24.7 %collective-permute-start.11 = (bf16[3,128,512]{2,1,0:T(8,128)(2,1)}, bf16[3,128,512]{2,1,0:T(8,128)(2,1)S(1)}, u32[]{:S(2)}, u32[]{:S(2)}) collective-permute-start(bf16[3,128,512]{2,1,0:T(8,128)(2,1)} %copy-done.9), channel_id=1, source_target_pairs={{0,2},{1,3},{2,4},{3,5},{4,6},{5,7},{6,0},{7,1},{8,10},{9,11},{10,... | collective-permute-start | bytes 1179656 | tf_op jit(solution)/shard_map/ppermute | solution.py:428
  90.6 16.8 %collective-permute-start.17 = (bf16[3,128,512]{2,1,0:T(8,128)(2,1)}, bf16[3,128,512]{2,1,0:T(8,128)(2,1)S(1)}, u32[]{:S(2)}, u32[]{:S(2)}) collective-permute-start(bf16[3,128,512]{2,1,0:T(8,128)(2,1)} %collective-permute-done.16.refs_5_), channel_id=1, source_target_pairs={{0,2},{1,3},{2,4},{3,5},{4,6},{5,7},{6,0},{7,1},{8,10},{9,11},{10,... | collective-permute-start | bytes 1179656 | tf_op jit(solution)/shard_map/ppermute | solution.py:428
  104.2 9.2 %collective-permute-start.21 = (bf16[272,512]{1,0:T(8,128)(2,1)S(1)}, bf16[272,512]{1,0:T(8,128)(2,1)S(1)}, u32[]{:S(2)}, u32[]{:S(2)}) collective-permute-start(bf16[272,512]{1,0:T(8,128)(2,1)S(1)} %add_convert_fusion.4), channel_id=1, source_target_pairs={{0,2},{1,3},{2,0},{3,1},{4,6},{5,7},{6,4},{7,5},{8,10},{9,11},{10,... | collective-permute-start | bytes 835592 | tf_op jit(solution)/shard_map/ppermute | solution.py:612
  114.5 9.1 %collective-permute-start.23 = (bf16[144,1024]{1,0:T(8,128)(2,1)S(1)}, bf16[144,1024]{1,0:T(8,128)(2,1)S(1)}, u32[]{:S(2)}, u32[]{:S(2)}) collective-permute-start(bf16[144,1024]{1,0:T(8,128)(2,1)S(1)} %add_convert_fusion), channel_id=1, source_target_pairs={{0,16},{8,24},{16,0},{24,8},{1,17},{9,25},{17,1},{25,9},{2,18},{10... | collective-permute-start | bytes 884744 | tf_op jit(solution)/shard_map/ppermute | solution.py:616
  114.6 15.7 %collective-permute-start.25 = (bf16[272,512]{1,0:T(8,128)(2,1)S(1)}, bf16[272,512]{1,0:T(8,128)(2,1)S(1)}, u32[]{:S(2)}, u32[]{:S(2)}) collective-permute-start(bf16[272,512]{1,0:T(8,128)(2,1)S(1)} %add_convert_fusion.3), channel_id=1, source_target_pairs={{0,4},{1,5},{2,6},{3,7},{4,0},{5,1},{6,2},{7,3},{8,12},{9,13},{10,... | collective-permute-start | bytes 835592 | tf_op jit(solution)/shard_map/ppermute | solution.py:612
  123.8 8.2 %collective-permute-start.26 = (f32[1,1024]{1,0:T(1,128)S(1)}, f32[1,1024]{1,0:T(1,128)S(1)}, u32[]{:S(2)}, u32[]{:S(2)}) collective-permute-start(f32[1,1024]{1,0:T(1,128)S(1)} %slice.26), channel_id=1, source_target_pairs={{1,0},{3,8},{5,16},{7,24},{8,1},{9,2},{10,9},{11,10},{12,17},{13,1... | collective-permute-start | bytes 12296 | tf_op jit(solution)/shard_map/ppermute | solution.py:638
  127.0 17.0 %collective-permute-start.24 = (bf16[128,1024]{1,0:T(8,128)(2,1)S(1)}, bf16[128,1024]{1,0:T(8,128)(2,1)S(1)}, u32[]{:S(2)}, u32[]{:S(2)}) collective-permute-start(bf16[128,1024]{1,0:T(8,128)(2,1)S(1)} %slice.28), channel_id=1, source_target_pairs={{0,0},{1,1},{2,8},{3,9},{4,16},{5,17},{6,24},{7,25},{8,2},{9,3},{1... | collective-permute-start | bytes 786440 | tf_op jit(solution)/shard_map/ppermute | solution.py:637
  132.1 8.4 %collective-permute-start.27 = (bf16[272,512]{1,0:T(8,128)(2,1)S(1)}, bf16[272,512]{1,0:T(8,128)(2,1)S(1)}, u32[]{:S(2)}, u32[]{:S(2)}) collective-permute-start(bf16[272,512]{1,0:T(8,128)(2,1)S(1)} %add_convert_fusion.2.refs_0_), channel_id=1, source_target_pairs={{0,1},{1,0},{2,3},{3,2},{4,5},{5,4},{6,7},{7,6},{8,9},{9,8},{10,11... | collective-permute-start | bytes 835592 | tf_op jit(solution)/shard_map/ppermute | solution.py:431
  133.1 10.8 %collective-permute-start.28 = (f32[1,1024]{1,0:T(1,128)S(1)}, f32[1,1024]{1,0:T(1,128)S(1)}, u32[]{:S(2)}, u32[]{:S(2)}) collective-permute-start(f32[1,1024]{1,0:T(1,128)S(1)} %slice.24), channel_id=1, source_target_pairs={{1,0},{2,1},{3,2},{4,3},{5,4},{6,5},{7,6},{9,8},{10,9},{11,10},{12... | collective-permute-start | bytes 12296 | tf_op jit(solution)/shard_map/ppermute | solution.py:423
  (32 other events, 245.3 us)

commit v10 on v9

--- a/solution.py
+++ b/solution.py
@@ -328,8 +328,8 @@
 
 def project_kernel(count, ring, final, *refs):
     place = position()
-    lows, highs, given, mix = refs[:count], refs[count : 2 * count], refs[2 * count : 2 * count + 3], refs[2 * count + 3]
-    rest, (low, high, weights, own, prior, sem) = refs[2 * count + 4 : -6], refs[-6:]
+    lows, highs, given, mix = refs[:count], refs[count : 2 * count], refs[2 * count : 2 * count + 2], refs[2 * count + 2]
+    rest, (low, high, weights, own, prior, sem) = refs[2 * count + 3 : -6], refs[-6:]
     done, outs = (rest[:-ring], rest[-ring:]) if final else ((), rest)
     rows, width = lows[0].shape[1:]
     n = weights.shape[2]
@@ -344,16 +344,7 @@
     weight_copies, block_copies = [], []
     for i in range(2):
         for m in range(3):
-            if i == 0:
-                weight_copies.append([fetch(given[0].at[m], weights.at[0, m])])
-            else:
-                first, cut = given[1].at[m], given[1].shape[1]
-                weight_copies.append(
-                    [
-                        fetch(first, weights.at[1, m, pl.ds(0, cut)]),
-                        fetch(given[2].at[m], weights.at[1, m, pl.ds(cut, n - cut)]),
-                    ]
-                )
+            weight_copies.append([fetch(given[i].at[m], weights.at[i, m])])
             if i == 0:
                 places = [pl.ds(q * rows, rows) for q in range(count)]
                 block_copies.append(
@@ -444,8 +435,7 @@
     anywhere = pl.BlockSpec(memory_space=pl.ANY)
     vmem = pl.BlockSpec(memory_space=pltpu.VMEM)
 
-    carried, piece = lax.optimization_barrier((shift(layer_input[rows - 1 :], 1), proj_weights[:, :cut]))
-    fars = [partner(piece)]
+    carried = shift(layer_input[rows - 1 :], 1)
     shift_mix = decay_shift_mix.reshape(1, cols)
     pre = pl.pallas_call(
         adapter_kernel,
@@ -486,7 +476,7 @@
 
     def inside(part):
         at = lambda n: col_block(n, block, part * steps)
-        extra = part == 0
+        extra = False
         return pl.pallas_call(
             lambda *refs: inner_kernel(head, cut if extra else 0, *refs),
             grid=(steps,),
@@ -500,13 +490,11 @@
             compiler_params=params,
             cost_estimate=work(4),
             name="inside_chunk",
-        )(r, k, v, dy, after_that(w, fars[0]) if extra else w, u, levels, sums, *[proj_weights] * extra)
+        )(r, k, v, dy, w, u, levels, sums, *[proj_weights] * extra)
 
     inner_parts = [inside(part) for part in range(parts)]
-    far, piece, inner_parts[0] = lax.optimization_barrier(
-        (partner(msg), inner_parts[0][7], inner_parts[0][:7])
-    )
-    fars.append(partner(piece))
+    far, weights, inner_parts[0] = lax.optimization_barrier((partner(msg), proj_weights, inner_parts[0]))
+    fars = [partner(weights)]
     out_msgs = pl.pallas_call(
         lambda *refs: pair_kernel(head, ring, *refs),
                 out_shape=[shape((head + 8, cols), BF16)] * (ring - 1),
@@ -589,7 +577,7 @@
         count, final = len(low), len(done) > 0
         return pl.pallas_call(
             lambda *refs: project_kernel(count, ring, final, *refs),
-            in_specs=[anywhere] * (2 * count + 3) + [vmem] * (1 + len(done)),
+            in_specs=[anywhere] * (2 * count + 2) + [vmem] * (1 + len(done)),
             out_shape=[shape((tall, cols), BF16)] * (ring if final else count),
             scratch_shapes=[
                 pltpu.VMEM((3, count * rows, part_cols), BF16),
@@ -597,7 +585,7 @@
                 pltpu.VMEM((inner, 3, weight_rows, cols), BF16),
                 pltpu.VMEM((count * rows, weight_rows), F32),
                 pltpu.VMEM((count * rows, weight_rows), F32),
-                pltpu.SemaphoreType.DMA((3 * (2 * count + 3),)),
+                pltpu.SemaphoreType.DMA((3 * (2 * count + 2),)),
             ],
             compiler_params=pltpu.CompilerParams(vmem_limit_bytes=24 * 2**20),
             cost_estimate=work(5),

time: 146 us -> 150 us (1.027)
  starting transfers between devices: 33.7 us -> 39.6 us
  Pallas kernels: 46.5 us -> 43.6 us
  waiting for transfers between devices: 50.2 us -> 52.4 us
    ppermute x5 -> x4, waiting for transfers between devices: 8.02 us -> 15.3 us  [partner(): return lax.ppermute(a, 'seq', [(i, i ^ 1) for i in range(n_seq)])]
    ppermute x2, starting transfers between devices: 0.86 us -> 5.4 us  [other_z(): return lax.ppermute(a, 'seq', route)]
    ppermute x9, waiting for transfers between devices: 18.9 us -> 15.8 us  [around(): lax.ppermute(a, 'seq', [(i, (i + inner * step) % n_seq) for i in range(n_...]
    ppermute x3, waiting for transfers between devices: 9.2 us -> 6.96 us  [across(): return lax.ppermute(a, 'head', [(i, i ^ bit) for i in range(n_head)])]
    pallas_call x2, Pallas kernels: 12.5 us -> 10.9 us  [project(): pl.pallas_call(lambda *refs: project_kernel(count, ring, final, *refs), i...]
    unnamed x54 -> x46, local copies, waits for them, and re-layouts: 8.69 us -> 8.1 us
    ppermute x5 -> x4, starting transfers between devices: 5.64 us -> 6.12 us  [partner(): return lax.ppermute(a, 'seq', [(i, i ^ 1) for i in range(n_seq)])]
  transfers between devices with their start and end apart: 29 -> 28, of which waited for: 18 -> 18; matrix products, arithmetic and copies ran while one was open for 2% -> 2% of each run, Pallas kernels for 32% -> 25%
where the time goes in v10:
time: 150 us; the launch traced here: 149 us
  waiting for transfers between devices  52.4 us (35%)
  Pallas kernels  43.6 us (29%)
  starting transfers between devices  39.6 us (26%)
  local copies, waits for them, and re-layouts  10.4 us (7%)
  other arithmetic  2.15 us (1%)
    ppermute x9, waiting for transfers between devices, around(): lax.ppermute(a, 'seq', [(i, (i + inner * step) % n_seq) for i in range(n_...  15.8 us
    ppermute x4, waiting for transfers between devices, partner(): return lax.ppermute(a, 'seq', [(i, i ^ 1) for i in range(n_seq)])  15.3 us
    ppermute x9, starting transfers between devices, around(): lax.ppermute(a, 'seq', [(i, (i + inner * step) % n_seq) for i in range(n_...  13.9 us
    pallas_call x2, Pallas kernels, project(): pl.pallas_call(lambda *refs: project_kernel(count, ring, final, *refs), i...  10.9 us
    pallas_call x2, Pallas kernels, inside(): pl.pallas_call(lambda *refs: inner_kernel(head, cut if extra else 0, *ref...  10.3 us
    ppermute x6, waiting for transfers between devices, head_shift(): lax.ppermute(a, 'head', [(i, (i + d) % n_head) for i in range(n_head)])  8.35 us
    unnamed x46, local copies, waits for them, and re-layouts  8.1 us
    ppermute x3, waiting for transfers between devices, across(): return lax.ppermute(a, 'head', [(i, i ^ bit) for i in range(n_head)])  6.96 us
  transfers between devices with their start and end apart: 28, of which 18 were waited for; matrix products, arithmetic and copies ran while one was open for 2% of the time, Pallas kernels for 25%

profile of v10, /device:TPU:4, one launch (start us, length us, event | category | flops | bytes accessed | tf_op | source)
XLA Modules:
  0.0 149.1 jit_solution(6759243310376122456)
XLA Ops:
  1.5 3.5 %collective-permute-start = (bf16[1,1024]{1,0:T(2,128)(2,1)S(1)}, bf16[1,1024]{1,0:T(2,128)(2,1)S(1)}, u32[]{:S(2)}, u32[]{:S(2)}) collective-permute-start(bf16[1,1024]{1,0:T(2,128)(2,1)S(1)} %slice.16), channel_id=1, source_target_pairs={{0,1},{1,2},{2,3},{3,4},{4,5},{5,6},{6,7},{8,9},{9,10},{10,11},{11... | collective-permute-start | bytes 6152 | tf_op jit(solution)/shard_map/ppermute | solution.py:414
  15.0 3.4 %decay_and_states.1 = (f32[128,128]{1,0:T(8,128)}, bf16[128,128]{1,0:T(8,128)(2,1)}, f32[128,1024]{1,0:T(8,128)}, f32[1,1024]{1,0:T(1,128)}, f32[64,1024]{1,0:T(8,128)}, /*index=5*/bf16[136,1024]{1,0:T(8,128)(2,1)}) custom-call(f32[128,128]{1,0:T(8,128)} %adapter_input.1.refs_0_, f32[128,128]{1,0:T(8,128)} %copy-done.18, f32[128,128]{1,0:T(8,128)} %copy-done.20, ...), custom_call_target="tpu_custom_call" | custom-call | bytes 10500000 | tf_op jit(solution)/shard_map/decay_and_states/pallas_call | solution.py:454
  22.0 5.2 %inside_chunk.2 = (f32[128,512]{1,0:T(8,128)}, f32[128,512]{1,0:T(8,128)}, f32[128,512]{1,0:T(8,128)}, f32[128,512]{1,0:T(8,128)}, f32[128,512]{1,0:T(8,128)}, /*index=5*/f32[128,512]{1,0:T(8,128)}, f32[1,512]{1,0:T(1,128)}) custom-call(bf16[128,1024]{1,0:T(8,128)(2,1)} %refs_0_.8, bf16[128,1024]{1,0:T(8,128)(2,1)} %refs_1_.7, bf16[128,1024]{1,0:T(8,128)(2,1)} %refs_2_.8, ...), custom_call_target="tpu_custom_call" | custom-call | bytes 14000000 | tf_op jit(solution)/shard_map/inside_chunk/pallas_call | solution.py:480
  33.9 2.6 %collective-permute-start.6 = (bf16[72,1024]{1,0:T(8,128)(2,1)}, bf16[72,1024]{1,0:T(8,128)(2,1)S(1)}, u32[]{:S(2)}, u32[]{:S(2)}) collective-permute-start(bf16[72,1024]{1,0:T(8,128)(2,1)} %get-tuple-element.113), channel_id=1, source_target_pairs={{0,4},{1,5},{2,6},{3,7},{4,0},{5,1},{6,2},{7,3},{8,12},{9,13},{10,... | collective-permute-start | bytes 442376 | tf_op jit(solution)/shard_map/ppermute | solution.py:419
  37.8 5.1 %inside_chunk.3 = (f32[128,512]{1,0:T(8,128)}, f32[128,512]{1,0:T(8,128)}, f32[128,512]{1,0:T(8,128)}, f32[128,512]{1,0:T(8,128)}, f32[128,512]{1,0:T(8,128)}, /*index=5*/f32[128,512]{1,0:T(8,128)}, f32[1,512]{1,0:T(1,128)}) custom-call(bf16[128,1024]{1,0:T(8,128)(2,1)} %refs_0_.8, bf16[128,1024]{1,0:T(8,128)(2,1)} %refs_1_.7, bf16[128,1024]{1,0:T(8,128)(2,1)} %refs_2_.8, ...), custom_call_target="tpu_custom_call" | custom-call | bytes 14000000 | tf_op jit(solution)/shard_map/inside_chunk/pallas_call | solution.py:480
  43.0 3.4 %collective-permute-done.6.refs_15_ = bf16[72,1024]{1,0:T(8,128)(2,1)S(1)} collective-permute-done((bf16[72,1024]{1,0:T(8,128)(2,1)}, bf16[72,1024]{1,0:T(8,128)(2,1)S(1)}, u32[]{:S(2)}, u32[]{:S(2)}) %collective-permute-start.6) | collective-permute-done | bytes 147488 | tf_op jit(solution)/shard_map/ppermute | solution.py:419
  47.1 2.8 %across_chunks.2 = (bf16[3,128,512]{2,1,0:T(8,128)(2,1)}, f32[128,512]{1,0:T(8,128)}, f32[128,512]{1,0:T(8,128)}, f32[1,512]{1,0:T(1,128)}) custom-call(bf16[128,1024]{1,0:T(8,128)(2,1)} %refs_0_.8, bf16[128,1024]{1,0:T(8,128)(2,1)} %refs_1_.7, bf16[128,1024]{1,0:T(8,128)(2,1)} %refs_2_.8, bf16[128,1024]{1,0:T(8,128)(2,1)} %refs_3_.8, ...), custom_call_target="tpu_custom_call" | custom-call | bytes 10500000 | tf_op jit(solution)/shard_map/across_chunks/pallas_call | solution.py:512
  49.9 3.6 %collective-permute-start.8 = (bf16[3,128,512]{2,1,0:T(8,128)(2,1)}, bf16[3,128,512]{2,1,0:T(8,128)(2,1)S(1)}, u32[]{:S(2)}, u32[]{:S(2)}) collective-permute-start(bf16[3,128,512]{2,1,0:T(8,128)(2,1)} %get-tuple-element.118.refs_0_), channel_id=1, source_target_pairs={{0,2},{1,3},{2,4},{3,5},{4,6},{5,7},{6,0},{7,1},{8,10},{9,11},{10,... | collective-permute-start | bytes 1179656 | tf_op jit(solution)/shard_map/ppermute | solution.py:419
  53.5 2.8 %across_chunks.3 = (bf16[3,128,512]{2,1,0:T(8,128)(2,1)}, f32[128,512]{1,0:T(8,128)}, f32[128,512]{1,0:T(8,128)}, f32[1,512]{1,0:T(1,128)}) custom-call(bf16[128,1024]{1,0:T(8,128)(2,1)} %refs_0_.8, bf16[128,1024]{1,0:T(8,128)(2,1)} %refs_1_.7, bf16[128,1024]{1,0:T(8,128)(2,1)} %refs_2_.8, bf16[128,1024]{1,0:T(8,128)(2,1)} %refs_3_.8, ...), custom_call_target="tpu_custom_call" | custom-call | bytes 10500000 | tf_op jit(solution)/shard_map/across_chunks/pallas_call | solution.py:512
  56.4 2.4 %decay_gradient.3 = (f32[128,512]{1,0:T(8,128)}, f32[1,512]{1,0:T(1,128)}, f32[128,128]{1,0:T(8,128)}) custom-call(f32[128,1024]{1,0:T(8,128)} %get-tuple-element.88.refs_4_.w, f32[128,512]{1,0:T(8,128)} %get-tuple-element.130.r_gr, f32[128,512]{1,0:T(8,128)} %get-tuple-element.131.k_gk, f32[1,512]{1,0:T(1,128)} %get-tuple-element.132.at_end, ...), custom_call_target="tpu_custom_call" | custom-call | bytes 7000000 | tf_op jit(solution)/shard_map/decay_gradient/pallas_call | solution.py:532
  62.1 2.8 %collective-permute-done.8.refs_1_ = bf16[3,128,512]{2,1,0:T(8,128)(2,1)S(1)} collective-permute-done((bf16[3,128,512]{2,1,0:T(8,128)(2,1)}, bf16[3,128,512]{2,1,0:T(8,128)(2,1)S(1)}, u32[]{:S(2)}, u32[]{:S(2)}) %collective-permute-start.8) | collective-permute-done | bytes 393248 | tf_op jit(solution)/shard_map/ppermute | solution.py:419
  67.0 3.3 %collective-permute-done.12.refs_6_ = f32[128,128]{1,0:T(8,128)S(1)} collective-permute-done((f32[128,128]{1,0:T(8,128)S(1)}, f32[128,128]{1,0:T(8,128)S(1)}, u32[]{:S(2)}, u32[]{:S(2)}) %collective-permute-start.12) | collective-permute-done | bytes 65568 | tf_op jit(solution)/shard_map/ppermute | solution.py:425
  72.8 3.0 %adapter_grads.1 = (bf16[272,512]{1,0:T(8,128)(2,1)}, bf16[272,512]{1,0:T(8,128)(2,1)}, f32[128,1024]{1,0:T(8,128)}) custom-call(bf16[128,1024]{1,0:T(8,128)(2,1)} %refs_0_.9, bf16[1,1024]{1,0:T(2,128)(2,1)} %copy-done.22, f32[1,1024]{1,0:T(1,128)} %bitcast.5, f32[1024,128]{1,0:T(8,128)} %refs_3_.9, f32[128,128]{1,0:T(8,128)} %get-tuple-element.136.refs_4_, ...), custom_call_target="tpu_custom_call" | custom-call | bytes 10500000 | tf_op jit(solution)/shard_map/adapter_grads/pallas_call | solution.py:550
  75.9 4.2 %collective-permute-done.9.refs_2_ = bf16[3,128,512]{2,1,0:T(8,128)(2,1)S(1)} collective-permute-done((bf16[3,128,512]{2,1,0:T(8,128)(2,1)S(1)}, bf16[3,128,512]{2,1,0:T(8,128)(2,1)S(1)}, u32[]{:S(2)}, u32[]{:S(2)}) %collective-permute-start.9) | collective-permute-done | bytes 393248 | tf_op jit(solution)/shard_map/ppermute | solution.py:419
  81.9 2.5 %collective-permute-start.10 = (bf16[3,128,512]{2,1,0:T(8,128)(2,1)}, bf16[3,128,512]{2,1,0:T(8,128)(2,1)S(1)}, u32[]{:S(2)}, u32[]{:S(2)}) collective-permute-start(bf16[3,128,512]{2,1,0:T(8,128)(2,1)} %copy-done.6), channel_id=1, source_target_pairs={{0,2},{1,3},{2,4},{3,5},{4,6},{5,7},{6,0},{7,1},{8,10},{9,11},{10,... | collective-permute-start | bytes 1179656 | tf_op jit(solution)/shard_map/ppermute | solution.py:419
  84.3 5.5 %collective-permute-done.15.refs_5_ = bf16[3,128,512]{2,1,0:T(8,128)(2,1)} collective-permute-done((bf16[3,128,512]{2,1,0:T(8,128)(2,1)}, bf16[3,128,512]{2,1,0:T(8,128)(2,1)}, u32[]{:S(2)}, u32[]{:S(2)}) %collective-permute-start.15) | collective-permute-done | bytes 393248 | tf_op jit(solution)/shard_map/ppermute | solution.py:419
  91.1 8.3 %collective-permute-done.17.refs_7_.refs_3_ = bf16[3,512,1024]{2,1,0:T(8,128)(2,1)} collective-permute-done((bf16[3,512,1024]{2,1,0:T(8,128)(2,1)S(1)}, bf16[3,512,1024]{2,1,0:T(8,128)(2,1)}, u32[]{:S(2)}, u32[]{:S(2)}) %collective-permute-start.17) | collective-permute-done | bytes 3145760 | tf_op jit(solution)/shard_map/ppermute | solution.py:422
  103.4 6.4 %projections.2 = (bf16[144,1024]{1,0:T(8,128)(2,1)S(1)}, bf16[144,1024]{1,0:T(8,128)(2,1)S(1)}, bf16[144,1024]{1,0:T(8,128)(2,1)S(1)}) custom-call(bf16[3,128,512]{2,1,0:T(8,128)(2,1)S(1)} %copy-done.2, bf16[3,128,512]{2,1,0:T(8,128)(2,1)S(1)} %copy-done.4, bf16[3,128,512]{2,1,0:T(8,128)(2,1)S(1)} %copy-done.7, bf16[3,128,512]{2,1,0:T(8,128)(2,1)S(1)} %copy-done.5, ...), custom_call_target="tpu_custom_call" | custom-call | bytes 17500000 | tf_op jit(solution)/shard_map/projections/pallas_call | solution.py:578
  109.9 2.8 %collective-permute-start.20 = (bf16[272,512]{1,0:T(8,128)(2,1)S(1)}, bf16[272,512]{1,0:T(8,128)(2,1)S(1)}, u32[]{:S(2)}, u32[]{:S(2)}) collective-permute-start(bf16[272,512]{1,0:T(8,128)(2,1)S(1)} %add_convert_fusion.4), channel_id=1, source_target_pairs={{0,2},{1,3},{2,0},{3,1},{4,6},{5,7},{6,4},{7,5},{8,10},{9,11},{10,... | collective-permute-start | bytes 835592 | tf_op jit(solution)/shard_map/ppermute | solution.py:600
  112.8 4.5 %projections.3 = (bf16[144,1024]{1,0:T(8,128)(2,1)S(1)}, bf16[144,1024]{1,0:T(8,128)(2,1)S(1)}, bf16[144,1024]{1,0:T(8,128)(2,1)S(1)}, bf16[144,1024]{1,0:T(8,128)(2,1)S(1)}) custom-call(bf16[3,128,512]{2,1,0:T(8,128)(2,1)S(1)} %collective-permute-done.10.refs_0_, bf16[3,128,512]{2,1,0:T(8,128)(2,1)S(1)} %collective-permute-done.16.refs_1_, ...), custom_call_target="tpu_custom_call" | custom-call | bytes 17500000 | tf_op jit(solution)/shard_map/projections/pallas_call | solution.py:578
  119.6 2.6 %collective-permute-start.24 = (bf16[272,512]{1,0:T(8,128)(2,1)S(1)}, bf16[272,512]{1,0:T(8,128)(2,1)S(1)}, u32[]{:S(2)}, u32[]{:S(2)}) collective-permute-start(bf16[272,512]{1,0:T(8,128)(2,1)S(1)} %add_convert_fusion.3), channel_id=1, source_target_pairs={{0,4},{1,5},{2,6},{3,7},{4,0},{5,1},{6,2},{7,3},{8,12},{9,13},{10,... | collective-permute-start | bytes 835592 | tf_op jit(solution)/shard_map/ppermute | solution.py:600
  122.2 6.0 %collective-permute-done.22 = bf16[144,1024]{1,0:T(8,128)(2,1)S(1)} collective-permute-done((bf16[144,1024]{1,0:T(8,128)(2,1)S(1)}, bf16[144,1024]{1,0:T(8,128)(2,1)S(1)}, u32[]{:S(2)}, u32[]{:S(2)}) %collective-permute-start.22) | collective-permute-done | bytes 294944 | tf_op jit(solution)/shard_map/ppermute | solution.py:604
  130.7 3.4 %collective-permute-start.23 = (bf16[128,1024]{1,0:T(8,128)(2,1)S(1)}, bf16[128,1024]{1,0:T(8,128)(2,1)S(1)}, u32[]{:S(2)}, u32[]{:S(2)}) collective-permute-start(bf16[128,1024]{1,0:T(8,128)(2,1)S(1)} %slice.24), channel_id=1, source_target_pairs={{0,0},{1,1},{2,8},{3,9},{4,16},{5,17},{6,24},{7,25},{8,2},{9,3},{1... | collective-permute-start | bytes 786440 | tf_op jit(solution)/shard_map/ppermute | solution.py:625
  139.0 5.9 %collective-permute-done.26.refs_1_ = bf16[272,512]{1,0:T(8,128)(2,1)S(1)} collective-permute-done((bf16[272,512]{1,0:T(8,128)(2,1)S(1)}, bf16[272,512]{1,0:T(8,128)(2,1)S(1)}, u32[]{:S(2)}, u32[]{:S(2)}) %collective-permute-start.26) | collective-permute-done | bytes 278560 | tf_op jit(solution)/shard_map/ppermute | solution.py:422
  (107 shorter events, 52.2 us)
Async XLA Ops:
  1.5 4.8 %collective-permute-start = (bf16[1,1024]{1,0:T(2,128)(2,1)S(1)}, bf16[1,1024]{1,0:T(2,128)(2,1)S(1)}, u32[]{:S(2)}, u32[]{:S(2)}) collective-permute-start(bf16[1,1024]{1,0:T(2,128)(2,1)S(1)} %slice.16), channel_id=1, source_target_pairs={{0,1},{1,2},{2,3},{3,4},{4,5},{5,6},{6,7},{8,9},{9,10},{10,11},{11... | collective-permute-start | bytes 6152 | tf_op jit(solution)/shard_map/ppermute | solution.py:414
  9.2 5.1 %collective-permute-start.2 = (f32[128,128]{1,0:T(8,128)}, f32[128,128]{1,0:T(8,128)S(1)}, u32[]{:S(2)}, u32[]{:S(2)}) collective-permute-start(f32[128,128]{1,0:T(8,128)} %adapter_input.1.refs_0_), channel_id=1, source_target_pairs={{0,16},{8,24},{16,0},{24,8},{1,17},{9,25},{17,1},{25,9},{2,18},{10... | collective-permute-start | bytes 196616 | tf_op jit(solution)/shard_map/ppermute | solution.py:425
  9.8 4.6 %collective-permute-start.3 = (f32[128,128]{1,0:T(8,128)}, f32[128,128]{1,0:T(8,128)S(1)}, u32[]{:S(2)}, u32[]{:S(2)}) collective-permute-start(f32[128,128]{1,0:T(8,128)} %adapter_input.1.refs_0_), channel_id=1, source_target_pairs={{0,24},{8,0},{16,8},{24,16},{1,25},{9,1},{17,9},{25,17},{2,26},{10... | collective-permute-start | bytes 196616 | tf_op jit(solution)/shard_map/ppermute | solution.py:425
  18.4 10.0 %collective-permute-start.4 = (bf16[136,1024]{1,0:T(8,128)(2,1)}, bf16[136,1024]{1,0:T(8,128)(2,1)S(1)}, u32[]{:S(2)}, u32[]{:S(2)}) collective-permute-start(bf16[136,1024]{1,0:T(8,128)(2,1)} %get-tuple-element.86.refs_0_), channel_id=1, source_target_pairs={{0,1},{1,0},{2,3},{3,2},{4,5},{5,4},{6,7},{7,6},{8,9},{9,8},{10,11... | collective-permute-start | bytes 835592 | tf_op jit(solution)/shard_map/ppermute | solution.py:422
  28.3 71.1 %collective-permute-start.17 = (bf16[3,512,1024]{2,1,0:T(8,128)(2,1)S(1)}, bf16[3,512,1024]{2,1,0:T(8,128)(2,1)}, u32[]{:S(2)}, u32[]{:S(2)}) collective-permute-start(bf16[3,512,1024]{2,1,0:T(8,128)(2,1)S(1)} %copy-done.1), channel_id=1, source_target_pairs={{0,1},{1,0},{2,3},{3,2},{4,5},{5,4},{6,7},{7,6},{8,9},{9,8},{10,11... | collective-permute-start | bytes 9437192 | tf_op jit(solution)/shard_map/ppermute | solution.py:422
  32.2 10.8 %collective-permute-start.5 = (bf16[72,1024]{1,0:T(8,128)(2,1)}, bf16[72,1024]{1,0:T(8,128)(2,1)S(1)}, u32[]{:S(2)}, u32[]{:S(2)}) collective-permute-start(bf16[72,1024]{1,0:T(8,128)(2,1)} %get-tuple-element.112), channel_id=1, source_target_pairs={{0,2},{1,3},{2,4},{3,5},{4,6},{5,7},{6,0},{7,1},{8,10},{9,11},{10,... | collective-permute-start | bytes 442376 | tf_op jit(solution)/shard_map/ppermute | solution.py:419
  33.9 12.5 %collective-permute-start.6 = (bf16[72,1024]{1,0:T(8,128)(2,1)}, bf16[72,1024]{1,0:T(8,128)(2,1)S(1)}, u32[]{:S(2)}, u32[]{:S(2)}) collective-permute-start(bf16[72,1024]{1,0:T(8,128)(2,1)} %get-tuple-element.113), channel_id=1, source_target_pairs={{0,4},{1,5},{2,6},{3,7},{4,0},{5,1},{6,2},{7,3},{8,12},{9,13},{10,... | collective-permute-start | bytes 442376 | tf_op jit(solution)/shard_map/ppermute | solution.py:419
  36.5 9.9 %collective-permute-start.7 = (bf16[72,1024]{1,0:T(8,128)(2,1)}, bf16[72,1024]{1,0:T(8,128)(2,1)S(1)}, u32[]{:S(2)}, u32[]{:S(2)}) collective-permute-start(bf16[72,1024]{1,0:T(8,128)(2,1)} %get-tuple-element.114), channel_id=1, source_target_pairs={{0,6},{1,7},{2,0},{3,1},{4,2},{5,3},{6,4},{7,5},{8,14},{9,15},{10,... | collective-permute-start | bytes 442376 | tf_op jit(solution)/shard_map/ppermute | solution.py:419
  49.9 15.0 %collective-permute-start.8 = (bf16[3,128,512]{2,1,0:T(8,128)(2,1)}, bf16[3,128,512]{2,1,0:T(8,128)(2,1)S(1)}, u32[]{:S(2)}, u32[]{:S(2)}) collective-permute-start(bf16[3,128,512]{2,1,0:T(8,128)(2,1)} %get-tuple-element.118.refs_0_), channel_id=1, source_target_pairs={{0,2},{1,3},{2,4},{3,5},{4,6},{5,7},{6,0},{7,1},{8,10},{9,11},{10,... | collective-permute-start | bytes 1179656 | tf_op jit(solution)/shard_map/ppermute | solution.py:419
  56.3 19.5 %collective-permute-start.11 = (bf16[3,128,512]{2,1,0:T(8,128)(2,1)}, bf16[3,128,512]{2,1,0:T(8,128)(2,1)}, u32[]{:S(2)}, u32[]{:S(2)}) collective-permute-start(bf16[3,128,512]{2,1,0:T(8,128)(2,1)} %get-tuple-element.135.refs_3_), channel_id=1, source_target_pairs={{0,2},{1,3},{2,4},{3,5},{4,6},{5,7},{6,0},{7,1},{8,10},{9,11},{10,... | collective-permute-start | bytes 1179656 | tf_op jit(solution)/shard_map/ppermute | solution.py:419
  64.9 15.2 %collective-permute-start.9 = (bf16[3,128,512]{2,1,0:T(8,128)(2,1)S(1)}, bf16[3,128,512]{2,1,0:T(8,128)(2,1)S(1)}, u32[]{:S(2)}, u32[]{:S(2)}) collective-permute-start(bf16[3,128,512]{2,1,0:T(8,128)(2,1)S(1)} %collective-permute-done.8.refs_1_), channel_id=1, source_target_pairs={{0,2},{1,3},{2,4},{3,5},{4,6},{5,7},{6,0},{7,1},{8,10},{9,11},{10,... | collective-permute-start | bytes 1179656 | tf_op jit(solution)/shard_map/ppermute | solution.py:419
  66.4 4.9 %collective-permute-start.13 = (f32[128,128]{1,0:T(8,128)S(1)}, f32[128,128]{1,0:T(8,128)S(1)}, u32[]{:S(2)}, u32[]{:S(2)}) collective-permute-start(f32[128,128]{1,0:T(8,128)S(1)} %add.33.refs_5_), channel_id=1, source_target_pairs={{0,16},{8,24},{16,0},{24,8},{1,17},{9,25},{17,1},{25,9},{2,18},{10... | collective-permute-start | bytes 196616 | tf_op jit(solution)/shard_map/ppermute | solution.py:425
  75.8 14.0 %collective-permute-start.15 = (bf16[3,128,512]{2,1,0:T(8,128)(2,1)}, bf16[3,128,512]{2,1,0:T(8,128)(2,1)}, u32[]{:S(2)}, u32[]{:S(2)}) collective-permute-start(bf16[3,128,512]{2,1,0:T(8,128)(2,1)} %collective-permute-done.11.refs_4_), channel_id=1, source_target_pairs={{0,2},{1,3},{2,4},{3,5},{4,6},{5,7},{6,0},{7,1},{8,10},{9,11},{10,... | collective-permute-start | bytes 1179656 | tf_op jit(solution)/shard_map/ppermute | solution.py:419
  80.8 29.0 %collective-permute-start.19 = (bf16[272,512]{1,0:T(8,128)(2,1)}, bf16[272,512]{1,0:T(8,128)(2,1)S(1)}, u32[]{:S(2)}, u32[]{:S(2)}) collective-permute-start(bf16[272,512]{1,0:T(8,128)(2,1)} %get-tuple-element.153), channel_id=1, source_target_pairs={{0,1},{1,0},{2,3},{3,2},{4,5},{5,4},{6,7},{7,6},{8,9},{9,8},{10,11... | collective-permute-start | bytes 835592 | tf_op jit(solution)/shard_map/ppermute | solution.py:422
  81.9 30.9 %collective-permute-start.10 = (bf16[3,128,512]{2,1,0:T(8,128)(2,1)}, bf16[3,128,512]{2,1,0:T(8,128)(2,1)S(1)}, u32[]{:S(2)}, u32[]{:S(2)}) collective-permute-start(bf16[3,128,512]{2,1,0:T(8,128)(2,1)} %copy-done.6), channel_id=1, source_target_pairs={{0,2},{1,3},{2,4},{3,5},{4,6},{5,7},{6,0},{7,1},{8,10},{9,11},{10,... | collective-permute-start | bytes 1179656 | tf_op jit(solution)/shard_map/ppermute | solution.py:419
  89.9 22.9 %collective-permute-start.16 = (bf16[3,128,512]{2,1,0:T(8,128)(2,1)}, bf16[3,128,512]{2,1,0:T(8,128)(2,1)S(1)}, u32[]{:S(2)}, u32[]{:S(2)}) collective-permute-start(bf16[3,128,512]{2,1,0:T(8,128)(2,1)} %collective-permute-done.15.refs_5_), channel_id=1, source_target_pairs={{0,2},{1,3},{2,4},{3,5},{4,6},{5,7},{6,0},{7,1},{8,10},{9,11},{10,... | collective-permute-start | bytes 1179656 | tf_op jit(solution)/shard_map/ppermute | solution.py:419
  109.9 8.0 %collective-permute-start.20 = (bf16[272,512]{1,0:T(8,128)(2,1)S(1)}, bf16[272,512]{1,0:T(8,128)(2,1)S(1)}, u32[]{:S(2)}, u32[]{:S(2)}) collective-permute-start(bf16[272,512]{1,0:T(8,128)(2,1)S(1)} %add_convert_fusion.4), channel_id=1, source_target_pairs={{0,2},{1,3},{2,0},{3,1},{4,6},{5,7},{6,4},{7,5},{8,10},{9,11},{10,... | collective-permute-start | bytes 835592 | tf_op jit(solution)/shard_map/ppermute | solution.py:600
  117.4 4.8 %collective-permute-start.18 = (bf16[144,1024]{1,0:T(8,128)(2,1)S(1)}, bf16[144,1024]{1,0:T(8,128)(2,1)S(1)}, u32[]{:S(2)}, u32[]{:S(2)}) collective-permute-start(bf16[144,1024]{1,0:T(8,128)(2,1)S(1)} %get-tuple-element.151), channel_id=1, source_target_pairs={{0,8},{8,0},{16,24},{24,16},{1,9},{9,1},{17,25},{25,17},{2,10},{10... | collective-permute-start | bytes 884744 | tf_op jit(solution)/shard_map/ppermute | solution.py:604
  119.0 9.1 %collective-permute-start.22 = (bf16[144,1024]{1,0:T(8,128)(2,1)S(1)}, bf16[144,1024]{1,0:T(8,128)(2,1)S(1)}, u32[]{:S(2)}, u32[]{:S(2)}) collective-permute-start(bf16[144,1024]{1,0:T(8,128)(2,1)S(1)} %add_convert_fusion), channel_id=1, source_target_pairs={{0,16},{8,24},{16,0},{24,8},{1,17},{9,25},{17,1},{25,9},{2,18},{10... | collective-permute-start | bytes 884744 | tf_op jit(solution)/shard_map/ppermute | solution.py:604
  119.6 15.1 %collective-permute-start.24 = (bf16[272,512]{1,0:T(8,128)(2,1)S(1)}, bf16[272,512]{1,0:T(8,128)(2,1)S(1)}, u32[]{:S(2)}, u32[]{:S(2)}) collective-permute-start(bf16[272,512]{1,0:T(8,128)(2,1)S(1)} %add_convert_fusion.3), channel_id=1, source_target_pairs={{0,4},{1,5},{2,6},{3,7},{4,0},{5,1},{6,2},{7,3},{8,12},{9,13},{10,... | collective-permute-start | bytes 835592 | tf_op jit(solution)/shard_map/ppermute | solution.py:600
  128.3 8.2 %collective-permute-start.25 = (f32[1,1024]{1,0:T(1,128)S(1)}, f32[1,1024]{1,0:T(1,128)S(1)}, u32[]{:S(2)}, u32[]{:S(2)}) collective-permute-start(f32[1,1024]{1,0:T(1,128)S(1)} %slice.22), channel_id=1, source_target_pairs={{1,0},{3,8},{5,16},{7,24},{8,1},{9,2},{10,9},{11,10},{12,17},{13,1... | collective-permute-start | bytes 12296 | tf_op jit(solution)/shard_map/ppermute | solution.py:626
  130.7 17.6 %collective-permute-start.23 = (bf16[128,1024]{1,0:T(8,128)(2,1)S(1)}, bf16[128,1024]{1,0:T(8,128)(2,1)S(1)}, u32[]{:S(2)}, u32[]{:S(2)}) collective-permute-start(bf16[128,1024]{1,0:T(8,128)(2,1)S(1)} %slice.24), channel_id=1, source_target_pairs={{0,0},{1,1},{2,8},{3,9},{4,16},{5,17},{6,24},{7,25},{8,2},{9,3},{1... | collective-permute-start | bytes 786440 | tf_op jit(solution)/shard_map/ppermute | solution.py:625
  136.6 8.3 %collective-permute-start.26 = (bf16[272,512]{1,0:T(8,128)(2,1)S(1)}, bf16[272,512]{1,0:T(8,128)(2,1)S(1)}, u32[]{:S(2)}, u32[]{:S(2)}) collective-permute-start(bf16[272,512]{1,0:T(8,128)(2,1)S(1)} %add_convert_fusion.2.refs_0_), channel_id=1, source_target_pairs={{0,1},{1,0},{2,3},{3,2},{4,5},{5,4},{6,7},{7,6},{8,9},{9,8},{10,11... | collective-permute-start | bytes 835592 | tf_op jit(solution)/shard_map/ppermute | solution.py:422
  137.6 10.6 %collective-permute-start.27 = (f32[1,1024]{1,0:T(1,128)S(1)}, f32[1,1024]{1,0:T(1,128)S(1)}, u32[]{:S(2)}, u32[]{:S(2)}) collective-permute-start(f32[1,1024]{1,0:T(1,128)S(1)} %slice.20), channel_id=1, source_target_pairs={{1,0},{2,1},{3,2},{4,3},{5,4},{6,5},{7,6},{9,8},{10,9},{11,10},{12... | collective-permute-start | bytes 12296 | tf_op jit(solution)/shard_map/ppermute | solution.py:414
  (27 other events, 195.9 us)
